TPU v7x, 32 devices: a whole 2x2x4 slice. The times are simulated.
32 devices in a mesh: tile: 16 (over z, x, core), freq: 2 (over y).
Axes of the slice: x: 2, y: 2, z: 4, core: 2. Of those that a mesh axis runs over, the one named last changes fastest.
Arguments:
- u_factors: bfloat16 [2, 4096, 8, 128], P('freq', 'tile'), may hold values from -0.25 to 0.25
- v_factors: bfloat16 [2, 4096, 8, 128], P('freq', 'tile'), may hold values from -0.1875 to 0.1875
- ranks: int32 [2, 8, 8], P('freq'), may hold values from 8 to 64, as said below
- observed: float32 [2, 4096, 128], P('freq', 'tile'), may hold values from -6 to 6
- start: float32 [2, 4096, 128], P('freq', 'tile'), may hold values from -6 to 6
Outputs:
- estimate: float32 [2, 4096, 128], P('freq', 'tile')
Inputs may be any that keep to these rules, and one draw needn't show every extreme that they name: `ranks`: every frequency has a tile of rank 64 and a tile of rank 64 // 8.
All inputs are finite; a program needn't handle non-finite values.
Results may differ from a plain program's by a relative error of at most 0.0031.
Values may be sent and summed in bfloat16 or wider, within the bound.
No kernel may reach another device: no remote copies, remote signals or barrier semaphores. Data moves between devices by JAX's collectives and lax.ppermute only.
A program may use at most 64 MiB of HBM per device.

v0:
```python
import functools
import math

import jax
import jax.numpy as jnp
from jax import lax
from jax.experimental import pallas as pl
from jax.experimental.pallas import tpu as pltpu
from jax.sharding import Mesh
from jax.sharding import PartitionSpec as P

STEP_SIZE = 0.2
LEVEL = 0.5
LANES = 128
F32 = jnp.float32
BF16 = jnp.bfloat16
VMEM_LIMIT = 32 * 1024 * 1024


def place():
    return lax.axis_index("chip"), lax.axis_index("core")


def signs(rows):
    lane = lax.broadcasted_iota(jnp.int32, (rows, LANES), 1)
    return jnp.where(lane < LANES // 2, 1.0, -1.0).astype(F32)


def separate(source, wide, target, masks=None):
    rows, columns = target.shape
    tiles = columns // LANES
    wide[...] = source[...].astype(F32)
    for tile in range(tiles):
        part = wide[pl.ds(tile, rows, stride=tiles), :]
        if masks is not None:
            part = jnp.where(masks[tile], part, 0.0)
        target[:, tile * LANES : (tile + 1) * LANES] = part.astype(BF16)


def adjoint_block(product, half, tile):
    columns = slice(tile * LANES, (tile + 1) * LANES)
    real, imaginary = product[:half, columns], product[half:, columns]
    return real * signs(half) + pltpu.roll(imaginary, LANES // 2, 1)


def spread_block(block, left, tile):
    half = block.shape[0]
    block = block.astype(F32)
    columns = slice(tile * LANES, (tile + 1) * LANES)
    left[:half, columns] = (block * signs(half)).astype(BF16)
    left[half:, columns] = pltpu.roll(block, LANES // 2, 1).astype(BF16)


def times_transposed(left, right):
    return lax.dot_general(left, right, (((1,), (1,)), ((), ())), preferred_element_type=F32)


def forward_kernel(start, factors, own, other, separated, wide, turned):
    _, core = place()
    tiles = own.shape[0]
    half = own.shape[1]
    separate(factors, wide, separated)
    turned[...] = start[...].T.astype(BF16).astype(F32)
    for side, out in ((core, own), (1 - core, other)):
        rows = pl.multiple_of(side * half, half)
        values = jnp.concatenate(
            [turned[pl.ds(rows, half), :], turned[pl.ds(rows + 2 * half, half), :]], axis=0
        ).astype(BF16)
        product = jnp.dot(values, separated[...], preferred_element_type=F32)
        for tile in range(tiles):
            out[tile] = adjoint_block(product, half, tile).astype(BF16)


def add_kernel(own, arrived, out):
    out[...] = (own[...].astype(F32) + arrived[...].astype(F32)).astype(BF16)


def rows_kernel(ranks, own, mate, observed, mate_observed, own_out, mate_out, observed_out, wide, turned):
    chip, core = place()
    half = observed_out.shape[1] // 2
    tiles = own_out.shape[1] // LANES
    lane = lax.broadcasted_iota(jnp.int32, (1, LANES), 1) % (LANES // 2)
    masks = [lane < ranks[0, chip, tile] for tile in range(tiles)]
    separate(own, wide, own_out, masks)
    separate(mate, wide, mate_out, masks)
    for index, values in enumerate((observed, mate_observed)):
        turned[...] = values[...].T
        rows = pl.multiple_of(core * half, half)
        observed_out[index, :half] = turned[pl.ds(rows, half), :]
        observed_out[index, half:] = turned[pl.ds(rows + 2 * half, half), :]


def columns_kernel(mate, mate_out, wide):
    separate(mate, wide, mate_out)


def image_kernel(blocks, own, mate, observed, out, left):
    chip, _ = place()
    tiles, half = out.shape[:2]
    for tile in range(tiles):
        spread_block(blocks[tile, chip], left, tile)
    products = []
    for index, factors in enumerate((own, mate)):
        misfit = times_transposed(left[...], factors[...]) - observed[index]
        products.append(jnp.dot(misfit.astype(BF16), factors[...], preferred_element_type=F32))
    for tile in range(tiles):
        parts = [adjoint_block(product, half, tile).astype(BF16).astype(F32) for product in products]
        out[tile] = (parts[0] + parts[1]).astype(BF16)


def gradient_kernel(blocks, own, mate, own_out, mate_out, left):
    for tile in range(blocks.shape[0]):
        spread_block(blocks[tile], left, tile)
    mate_out[...] = times_transposed(left[...], mate[...]).astype(BF16)
    own_out[...] = times_transposed(left[...], own[...]).astype(BF16)


def shrink_kernel(band, tables, *refs):
    starts, gradients, (out, spectra) = refs[:band], refs[band : 3 * band], refs[3 * band :]
    _, core = place()
    quarter = out.shape[1] // 4
    rows = out.shape[0]
    for index in range(band):
        for side, part in ((core, gradients[2 * index]), (1 - core, gradients[2 * index + 1])):
            at = pl.multiple_of(side * quarter, quarter)
            spectra[pl.ds(at, quarter), :] = part[:quarter].astype(F32)
            spectra[pl.ds(at + 2 * quarter, quarter), :] = part[quarter:].astype(F32)
        estimate = starts[index][...] - STEP_SIZE * spectra[...].T
        starts_real, starts_imaginary = estimate[:, : 2 * quarter], estimate[:, 2 * quarter :]
        if index == 0:
            real, imaginary = [starts_real], [starts_imaginary]
        else:
            real.append(starts_real)
            imaginary.append(starts_imaginary)
    scale = 1.0 / math.sqrt(band)

    def thin(values):
        return values - jnp.clip(values, -LEVEL, LEVEL)

    if band == 2:
        def both(parts):
            return (thin((parts[0] + parts[1]) * scale) + thin((parts[0] - parts[1]) * scale)) * scale

        out[...] = jnp.concatenate([both(real), both(imaginary)], axis=1)
        return
    total_real, total_imaginary = jnp.zeros_like(real[0]), jnp.zeros_like(real[0])
    for time in range(band):
        sample_real, sample_imaginary = jnp.zeros_like(real[0]), jnp.zeros_like(real[0])
        for index in range(band):
            cosine, sine = tables[0, index, time], tables[1, index, time]
            sample_real += cosine * real[index] - sine * imaginary[index]
            sample_imaginary += sine * real[index] + cosine * imaginary[index]
        thin_real, thin_imaginary = thin(sample_real * scale), thin(sample_imaginary * scale)
        cosine, sine = tables[0, 0, time], tables[1, 0, time]
        total_real += cosine * thin_real + sine * thin_imaginary
        total_imaginary += cosine * thin_imaginary - sine * thin_real
    out[...] = jnp.concatenate([total_real, total_imaginary], axis=1) * scale


def call(kernel, name, outs, inputs, scratch=(), flops=0, smem=0):
    vmem = pl.BlockSpec(memory_space=pltpu.VMEM)
    in_specs = [pl.BlockSpec(memory_space=pltpu.SMEM)] * smem + [vmem] * (len(inputs) - smem)
    moved = sum(x.size * x.dtype.itemsize for x in [*inputs, *outs])
    return pl.pallas_call(
        kernel,
        out_shape=outs,
        in_specs=in_specs,
        out_specs=[vmem] * len(outs),
        scratch_shapes=scratch,
        compiler_params=pltpu.CompilerParams(vmem_limit_bytes=VMEM_LIMIT),
        cost_estimate=pl.CostEstimate(flops=flops, bytes_accessed=moved, transcendentals=0),
        name=name,
    )(*inputs)


def body(u_factors, v_factors, ranks, observed, start):
    band = lax.axis_size("freq")
    rows, tiles, width = u_factors.shape[1:]
    sources = start.shape[2]
    half = sources // 4
    columns = tiles * width
    left_rows = u_factors.reshape(rows * tiles, width)
    right_rows = v_factors.reshape(rows * tiles, width)
    observed = observed.reshape(rows, sources)
    start = start.reshape(rows, sources)

    def shape(*dims, dtype=BF16):
        return jax.ShapeDtypeStruct(dims, dtype)

    def to_mate(value):
        return lax.ppermute(value, "core", [(0, 1), (1, 0)])

    def to_band(value, shift, flip):
        pairs = [
            (core * band + f, (core ^ flip) * band + (f - shift) % band) for core in range(2) for f in range(band)
        ]
        return lax.ppermute(value, ("core", "freq"), pairs)

    wide = pltpu.VMEM((rows * tiles, width), F32)
    turned = pltpu.VMEM((sources, rows), F32)
    factor = shape(rows, columns)
    blocks = shape(tiles, half, width)
    product = 2 * rows * columns * sources

    mate_left = to_mate(left_rows)
    mate_right = to_mate(right_rows)
    mate_observed = to_mate(observed)
    starts = [start] + [to_band(start, shift, 0) for shift in range(1, band)]

    own, other, own_right = call(
        forward_kernel, "forward", [blocks, blocks, factor], [start, right_rows], [wide, turned], product
    )
    (coeffs,) = call(add_kernel, "add", [blocks], [own, to_mate(other)])
    coeffs = lax.all_gather(coeffs, "chip")
    own_left, mate_left, turned_observed = call(
        rows_kernel,
        "rows",
        [factor, factor, shape(2, 2 * half, rows, dtype=F32)],
        [ranks, left_rows, mate_left, observed, mate_observed],
        [wide, turned],
        smem=1,
    )
    spread = pltpu.VMEM((2 * half, columns), BF16)
    (back,) = call(
        image_kernel, "image", [blocks], [coeffs, own_left, mate_left, turned_observed], [spread], 2 * product
    )
    back = lax.all_to_all(back, "chip", split_axis=0, concat_axis=0, tiled=True)
    (mate_right,) = call(columns_kernel, "columns", [factor], [mate_right], [wide])
    own_part, mate_part = call(
        gradient_kernel, "gradient", [shape(2 * half, rows)] * 2, [back, own_right, mate_right], [spread], product
    )
    gradients = [own_part, to_mate(mate_part)]
    for shift in range(1, band):
        gradients += [to_band(own_part, shift, 0), to_band(mate_part, shift, 1)]
    bands = jnp.arange(band, dtype=jnp.int32)
    phases = (2.0 * math.pi / band) * (
        (bands[:, None] + lax.axis_index("freq")) % band * bands[None, :] % band
    ).astype(F32)
    tables = jnp.stack([jnp.cos(phases), jnp.sin(phases)])
    (estimate,) = call(
        functools.partial(shrink_kernel, band),
        "shrink",
        [shape(rows, sources, dtype=F32)],
        [tables, *starts, *gradients],
        [turned],
        smem=1,
    )
    return estimate[None]


def solution(mesh):
    count, band = mesh.devices.shape
    cores = Mesh(mesh.devices.reshape(count // 2, 2, band), ("chip", "core", "freq"))
    tile = ("chip", "core")
    in_specs = (
        P("freq", tile, None, None),
        P("freq", tile, None, None),
        P("freq", None, None),
        P("freq", tile, None),
        P("freq", tile, None),
    )
    out_specs = P("freq", tile, None)
    return jax.shard_map(body, mesh=cores, in_specs=in_specs, out_specs=out_specs, check_vma=False)
```

profile of v0, /device:TPU:0, one launch (start us, length us, event | category | flops | bytes accessed | tf_op | source)
XLA Modules:
  0.0 61.3 jit_solution(9046514215369483752)
XLA Ops:
  0.0 0.5 collective-permute-start.2
  0.5 0.1 collective-permute-start.4
  0.5 3.0 %collective-permute-start = (f32[256,128]{1,0:T(8,128)}, f32[256,128]{1,0:T(8,128)S(1)}, u32[]{:S(2)}, u32[]{:S(2)}) collective-permute-start(f32[256,128]{1,0:T(8,128)} %bitcast.11), channel_id=1, source_target_pairs={{0,1},{1,0},{2,3},{3,2},{4,5},{5,4},{6,7},{7,6},{8,9},{9,8},{10,11... | collective-permute-start | bytes 393224 | tf_op jit(solution)/shard_map/ppermute | solution.py:197
  3.5 1.0 %copy-done = bf16[1,256,8,128]{3,2,1,0:T(8,128)(2,1)S(1)} copy-done((bf16[1,256,8,128]{3,2,1,0:T(8,128)(2,1)S(1)}, bf16[1,256,8,128]{3,2,1,0:T(8,128)(2,1)}, u32[]{:S(2)}) %copy-start) | copy-done | bytes 524312
  4.5 0.9 %copy-done.2 = f32[1,256,128]{2,1,0:T(8,128)S(1)} copy-done((f32[1,256,128]{2,1,0:T(8,128)S(1)}, f32[1,256,128]{2,1,0:T(8,128)}, u32[]{:S(2)}) %copy-start.2) | copy-done | bytes 131096
  5.4 0.6 %forward.1 = (bf16[8,32,128]{2,1,0:T(8,128)(2,1)S(1)}, bf16[8,32,128]{2,1,0:T(8,128)(2,1)S(1)}, bf16[256,1024]{1,0:T(8,128)(2,1)S(1)}) custom-call(f32[256,128]{1,0:T(8,128)S(1)} %bitcast.12, bf16[2048,128]{1,0:T(8,128)(2,1)S(1)} %bitcast.8), custom_call_target="tpu_custom_call" | custom-call | flops 67108864 | bytes 1310720 | tf_op jit(solution)/shard_map/forward/pallas_call | solution.py:164
  6.1 0.0 copy-start.1
  6.1 0.1 collective-permute-start.1
  6.2 0.2 copy-done.4
  6.3 0.3 collective-permute-start.3
  6.7 0.7 %collective-permute-done.1.arrived = bf16[8,32,128]{2,1,0:T(8,128)(2,1)S(1)} collective-permute-done((bf16[8,32,128]{2,1,0:T(8,128)(2,1)S(1)}, bf16[8,32,128]{2,1,0:T(8,128)(2,1)S(1)}, u32[]{:S(2)}, u32[]{:S(2)}) %collective-permute-start.1) | collective-permute-done | bytes 65568 | tf_op jit(solution)/shard_map/ppermute | solution.py:191
  7.4 0.0 copy-start.5
  7.4 31.8 %all-gather = bf16[64,32,128]{2,1,0:T(8,128)(2,1)S(1)} all-gather(bf16[8,32,128]{2,1,0:T(8,128)(2,1)S(1)} %add.56), channel_id=2, replica_groups=mesh['chip'=8,'core'=2,'freq'=2] {'chip'}, dimensions={0}, use_global_device_ids=true | all-gather | bytes 589824 | tf_op jit(solution)/shard_map/all_gather | solution.py:214
  39.2 0.0 collective-permute-done.3.mate_observed
  39.2 0.0 collective-permute-done.2.mate
  39.2 0.0 copy-done.1
  39.2 1.4 %rows.1 = (bf16[256,1024]{1,0:T(8,128)(2,1)S(1)}, bf16[256,1024]{1,0:T(8,128)(2,1)S(1)}, f32[2,64,256]{2,1,0:T(8,128)S(1)}) custom-call(s32[1,8,8]{2,1,0:T(8,128)S(1)} %copy-done.5, bf16[2048,128]{1,0:T(8,128)(2,1)S(1)} %bitcast.10, bf16[2048,128]{1,0:T(8,128)(2,1)S(1)} %collective-permute-done.2.mate, f32[256,128]{1,0:T(8,128)S(1)} %bitcast.15, ...), custom_call_target="tpu_custom_call" | custom-call | bytes 2490624 | tf_op jit(solution)/shard_map/rows/pallas_call | solution.py:164
  40.6 1.9 %image.1 = bf16[8,32,128]{2,1,0:T(8,128)(2,1)} custom-call(bf16[8,8,32,128]{3,2,1,0:T(8,128)(2,1)S(1)} %bitcast.6, bf16[256,1024]{1,0:T(8,128)(2,1)S(1)} %get-tuple-element.15.own, bf16[256,1024]{1,0:T(8,128)(2,1)S(1)} %get-tuple-element.16.mate, f32[2,64,256]{2,1,0:T(8,128)S(1)} %get-tuple-element.17.observed), custom_call_target="tpu_custom_call" | custom-call | flops 134217728 | bytes 1769472 | tf_op jit(solution)/shard_map/image/pallas_call | solution.py:164
  42.4 5.4 %all-to-all-start = ((bf16[8,32,128]{2,1,0:T(8,128)(2,1)}), bf16[8,32,128]{2,1,0:T(8,128)(2,1)S(1)}, u32[]{:S(2)}, u32[]{:S(2)}) async-start(bf16[8,32,128]{2,1,0:T(8,128)(2,1)} %image.1), calls=%async_computation | async-start | bytes 131072 | tf_op jit(solution)/shard_map/all_to_all | solution.py:227
  47.9 0.1 fusion.5
  48.0 0.0 collective-permute-done.4.mate
  48.0 0.3 columns.1.mate
  48.3 6.5 %all-to-all-done.blocks = bf16[8,32,128]{2,1,0:T(8,128)(2,1)S(1)} async-done(((bf16[8,32,128]{2,1,0:T(8,128)(2,1)}), bf16[8,32,128]{2,1,0:T(8,128)(2,1)S(1)}, u32[]{:S(2)}, u32[]{:S(2)}) %all-to-all-start) | async-done | bytes 65568 | tf_op jit(solution)/shard_map/all_to_all | solution.py:227
  54.8 0.5 gradient.1
  55.2 0.1 collective-permute-start.5
  55.3 0.6 %collective-permute-start.7 = (bf16[64,256]{1,0:T(8,128)(2,1)S(1)}, bf16[64,256]{1,0:T(8,128)(2,1)S(1)}, u32[]{:S(2)}, u32[]{:S(2)}) collective-permute-start(bf16[64,256]{1,0:T(8,128)(2,1)S(1)} %get-tuple-element.20), channel_id=1, source_target_pairs={{0,3},{1,2},{2,1},{3,0},{4,7},{5,6},{6,5},{7,4},{8,11},{9,10},{10,... | collective-permute-start | bytes 98312 | tf_op jit(solution)/shard_map/ppermute | solution.py:197
  55.9 1.5 %collective-permute-start.6 = (bf16[64,256]{1,0:T(8,128)(2,1)S(1)}, bf16[64,256]{1,0:T(8,128)(2,1)S(1)}, u32[]{:S(2)}, u32[]{:S(2)}) collective-permute-start(bf16[64,256]{1,0:T(8,128)(2,1)S(1)} %get-tuple-element.19.refs_2_), channel_id=1, source_target_pairs={{0,1},{1,0},{2,3},{3,2},{4,5},{5,4},{6,7},{7,6},{8,9},{9,8},{10,11... | collective-permute-start | bytes 98312 | tf_op jit(solution)/shard_map/ppermute | solution.py:197
  57.4 0.0 collective-permute-done.refs_1_
  57.5 0.0 collective-permute-done.5.refs_3_
  57.5 2.4 %collective-permute-done.6.refs_4_ = bf16[64,256]{1,0:T(8,128)(2,1)S(1)} collective-permute-done((bf16[64,256]{1,0:T(8,128)(2,1)S(1)}, bf16[64,256]{1,0:T(8,128)(2,1)S(1)}, u32[]{:S(2)}, u32[]{:S(2)}) %collective-permute-start.6) | collective-permute-done | bytes 32800 | tf_op jit(solution)/shard_map/ppermute | solution.py:197
  59.8 0.0 collective-permute-done.7.refs_5_
  59.8 1.4 %shrink.1 = f32[256,128]{1,0:T(8,128)} custom-call(f32[2,2,2]{2,1,0:T(2,128)S(1)} %pad_maximum_fusion.tables, f32[256,128]{1,0:T(8,128)S(1)} %bitcast.13, f32[256,128]{1,0:T(8,128)S(1)} %collective-permute-done.refs_1_, bf16[64,256]{1,0:T(8,128)(2,1)S(1)} %get-tuple-element.19.refs_2_, bf16[64,256]{1,0:T(8,128)(2,1)S(1)} %collective-permute-done.5.refs_3_, ...), custom_call_target="tpu_custom_call" | custom-call | bytes 524320 | tf_op jit(solution)/shard_map/shrink/pallas_call | solution.py:164
  (9 shorter events, 0.0 us)
Async XLA Ops:
  0.0 39.2 %collective-permute-start.2 = (bf16[2048,128]{1,0:T(8,128)(2,1)}, bf16[2048,128]{1,0:T(8,128)(2,1)S(1)}, u32[]{:S(2)}, u32[]{:S(2)}) collective-permute-start(bf16[2048,128]{1,0:T(8,128)(2,1)} %bitcast.9), channel_id=1, source_target_pairs={{0,2},{2,0},{1,3},{3,1},{4,6},{6,4},{5,7},{7,5},{8,10},{10,8},{9,1... | collective-permute-start | bytes 1572872 | tf_op jit(solution)/shard_map/ppermute | solution.py:191
  0.5 47.5 %collective-permute-start.4 = (bf16[2048,128]{1,0:T(8,128)(2,1)}, bf16[2048,128]{1,0:T(8,128)(2,1)S(1)}, u32[]{:S(2)}, u32[]{:S(2)}) collective-permute-start(bf16[2048,128]{1,0:T(8,128)(2,1)} %bitcast.7), channel_id=1, source_target_pairs={{0,2},{2,0},{1,3},{3,1},{4,6},{6,4},{5,7},{7,5},{8,10},{10,8},{9,1... | collective-permute-start | bytes 1572872 | tf_op jit(solution)/shard_map/ppermute | solution.py:191
  0.5 56.9 %collective-permute-start = (f32[256,128]{1,0:T(8,128)}, f32[256,128]{1,0:T(8,128)S(1)}, u32[]{:S(2)}, u32[]{:S(2)}) collective-permute-start(f32[256,128]{1,0:T(8,128)} %bitcast.11), channel_id=1, source_target_pairs={{0,1},{1,0},{2,3},{3,2},{4,5},{5,4},{6,7},{7,6},{8,9},{9,8},{10,11... | collective-permute-start | bytes 393224 | tf_op jit(solution)/shard_map/ppermute | solution.py:197
  3.5 1.0 %copy-start = (bf16[1,256,8,128]{3,2,1,0:T(8,128)(2,1)S(1)}, bf16[1,256,8,128]{3,2,1,0:T(8,128)(2,1)}, u32[]{:S(2)}) copy-start(bf16[1,256,8,128]{3,2,1,0:T(8,128)(2,1)} %param.6) | copy-start | bytes 1572868
  4.5 0.9 %copy-start.2 = (f32[1,256,128]{2,1,0:T(8,128)S(1)}, f32[1,256,128]{2,1,0:T(8,128)}, u32[]{:S(2)}) copy-start(f32[1,256,128]{2,1,0:T(8,128)} %param.9) | copy-start | bytes 393220
  5.4 0.9 %copy-start.4 = (f32[1,256,128]{2,1,0:T(8,128)S(1)}, f32[1,256,128]{2,1,0:T(8,128)}, u32[]{:S(2)}) copy-start(f32[1,256,128]{2,1,0:T(8,128)} %param.8) | copy-start | bytes 393220
  6.1 33.1 %copy-start.1 = (bf16[1,256,8,128]{3,2,1,0:T(8,128)(2,1)S(1)}, bf16[1,256,8,128]{3,2,1,0:T(8,128)(2,1)}, u32[]{:S(2)}) copy-start(bf16[1,256,8,128]{3,2,1,0:T(8,128)(2,1)} %param.5) | copy-start | bytes 1572868
  6.1 1.3 %collective-permute-start.1 = (bf16[8,32,128]{2,1,0:T(8,128)(2,1)S(1)}, bf16[8,32,128]{2,1,0:T(8,128)(2,1)S(1)}, u32[]{:S(2)}, u32[]{:S(2)}) collective-permute-start(bf16[8,32,128]{2,1,0:T(8,128)(2,1)S(1)} %get-tuple-element.14), channel_id=1, source_target_pairs={{0,2},{2,0},{1,3},{3,1},{4,6},{6,4},{5,7},{7,5},{8,10},{10,8},{9,1... | collective-permute-start | bytes 196616 | tf_op jit(solution)/shard_map/ppermute | solution.py:191
  6.3 32.9 %collective-permute-start.3 = (f32[256,128]{1,0:T(8,128)S(1)}, f32[256,128]{1,0:T(8,128)S(1)}, u32[]{:S(2)}, u32[]{:S(2)}) collective-permute-start(f32[256,128]{1,0:T(8,128)S(1)} %bitcast.14), channel_id=1, source_target_pairs={{0,2},{2,0},{1,3},{3,1},{4,6},{6,4},{5,7},{7,5},{8,10},{10,8},{9,1... | collective-permute-start | bytes 393224 | tf_op jit(solution)/shard_map/ppermute | solution.py:191
  7.4 31.8 %copy-start.5 = (s32[1,8,8]{2,1,0:T(8,128)S(1)}, s32[1,8,8]{2,1,0:T(8,128)}, u32[]{:S(2)}) copy-start(s32[1,8,8]{2,1,0:T(8,128)} %ranks.1) | copy-start | bytes 772
  42.4 12.3 %all-to-all-start = ((bf16[8,32,128]{2,1,0:T(8,128)(2,1)}), bf16[8,32,128]{2,1,0:T(8,128)(2,1)S(1)}, u32[]{:S(2)}, u32[]{:S(2)}) async-start(bf16[8,32,128]{2,1,0:T(8,128)(2,1)} %image.1), calls=%async_computation | async-start | bytes 131072 | tf_op jit(solution)/shard_map/all_to_all | solution.py:227
  54.8 5.1 %copy-start.3 = (f32[1,256,128]{2,1,0:T(8,128)S(1)}, f32[1,256,128]{2,1,0:T(8,128)}, u32[]{:S(2)}) copy-start(f32[1,256,128]{2,1,0:T(8,128)} %param.9) | copy-start | bytes 393220
  55.2 2.2 %collective-permute-start.5 = (bf16[64,256]{1,0:T(8,128)(2,1)S(1)}, bf16[64,256]{1,0:T(8,128)(2,1)S(1)}, u32[]{:S(2)}, u32[]{:S(2)}) collective-permute-start(bf16[64,256]{1,0:T(8,128)(2,1)S(1)} %get-tuple-element.20), channel_id=1, source_target_pairs={{0,2},{2,0},{1,3},{3,1},{4,6},{6,4},{5,7},{7,5},{8,10},{10,8},{9,1... | collective-permute-start | bytes 98312 | tf_op jit(solution)/shard_map/ppermute | solution.py:191
  55.3 4.5 %collective-permute-start.7 = (bf16[64,256]{1,0:T(8,128)(2,1)S(1)}, bf16[64,256]{1,0:T(8,128)(2,1)S(1)}, u32[]{:S(2)}, u32[]{:S(2)}) collective-permute-start(bf16[64,256]{1,0:T(8,128)(2,1)S(1)} %get-tuple-element.20), channel_id=1, source_target_pairs={{0,3},{1,2},{2,1},{3,0},{4,7},{5,6},{6,5},{7,4},{8,11},{9,10},{10,... | collective-permute-start | bytes 98312 | tf_op jit(solution)/shard_map/ppermute | solution.py:197
  55.9 3.9 %collective-permute-start.6 = (bf16[64,256]{1,0:T(8,128)(2,1)S(1)}, bf16[64,256]{1,0:T(8,128)(2,1)S(1)}, u32[]{:S(2)}, u32[]{:S(2)}) collective-permute-start(bf16[64,256]{1,0:T(8,128)(2,1)S(1)} %get-tuple-element.19.refs_2_), channel_id=1, source_target_pairs={{0,1},{1,0},{2,3},{3,2},{4,5},{5,4},{6,7},{7,6},{8,9},{9,8},{10,11... | collective-permute-start | bytes 98312 | tf_op jit(solution)/shard_map/ppermute | solution.py:197
where the time goes:
time: 61.5 us; the launch traced here: 61.3 us
  blocking collectives  31.8 us (52%)
  starting transfers between devices  11.5 us (19%)
  waiting for transfers between devices  9.63 us (16%)
  Pallas kernels  6.02 us (10%)
  local copies, waits for them, and re-layouts  2.14 us (3%)
    all_gather x1, blocking collectives, body(): coeffs = lax.all_gather(coeffs, 'chip')  31.8 us
    all_to_all x1, waiting for transfers between devices, body(): back = lax.all_to_all(back, 'chip', split_axis=0, concat_axis=0, tiled=True)  6.5 us
    pallas_call x7, Pallas kernels, call(): pl.pallas_call(kernel, out_shape=outs, in_specs=in_specs, out_specs=[vmem...  6.02 us
    all_to_all x1, starting transfers between devices, body(): back = lax.all_to_all(back, 'chip', split_axis=0, concat_axis=0, tiled=True)  5.4 us
    ppermute x3, starting transfers between devices, to_band(): return lax.ppermute(value, ('core', 'freq'), pairs)  5.11 us
    ppermute x3, waiting for transfers between devices, to_band(): return lax.ppermute(value, ('core', 'freq'), pairs)  2.39 us
    unnamed x12, local copies, waits for them, and re-layouts  2.14 us
  transfers between devices with their start and end apart: 9, of which 3 were waited for; matrix products, arithmetic and copies ran while one was open for 0% of the time, Pallas kernels for 8%

commit v1 on v0

v1 whole, which is shorter than its diff:
```python
import functools
import math

import jax
import jax.numpy as jnp
from jax import lax
from jax.experimental import pallas as pl
from jax.experimental.pallas import tpu as pltpu
from jax.sharding import Mesh
from jax.sharding import PartitionSpec as P

STEP_SIZE = 0.2
LEVEL = 0.5
LANES = 128
F32 = jnp.float32
BF16 = jnp.bfloat16
VMEM_LIMIT = 32 * 1024 * 1024
FIRST_LIMIT = 55090 * 1024


def place():
    return lax.axis_index("z"), lax.axis_index("x"), lax.axis_index("core")


def signs(rows):
    lane = lax.broadcasted_iota(jnp.int32, (rows, LANES), 1)
    return jnp.where(lane < LANES // 2, 1.0, -1.0).astype(F32)


def separate(source, wide, target, masks=None):
    rows, columns = target.shape
    tiles = columns // LANES
    wide[...] = source[...].astype(F32)
    for tile in range(tiles):
        part = wide[pl.ds(tile, rows, stride=tiles), :]
        if masks is not None:
            part = jnp.where(masks[tile], part, 0.0)
        target[:, tile * LANES : (tile + 1) * LANES] = part.astype(BF16)


def adjoint_block(real, imaginary):
    return real * signs(real.shape[0]) + pltpu.roll(imaginary, LANES // 2, 1)


def spread_block(block, left, tile):
    half = block.shape[0]
    block = block.astype(F32)
    columns = pl.ds(pl.multiple_of(tile * LANES, LANES), LANES)
    left[:half, columns] = (block * signs(half)).astype(BF16)
    left[half:, columns] = pltpu.roll(block, LANES // 2, 1).astype(BF16)


def spread_blocks(arrived, left):
    z, x, _ = place()
    near = len(arrived)
    for t, blocks in enumerate(arrived):
        for s in range(blocks.shape[0]):
            spread_block(blocks[s], left, (z ^ s) * near + (x ^ t))


def times_transposed(left, right):
    return lax.dot_general(left, right, (((1,), (1,)), ((), ())), preferred_element_type=F32)


def forward_kernel(start, factors, own, other, separated, start_here, factors_here, wide, product, sems):
    _, _, core = place()
    tiles, half = own.shape[:2]
    loads = [
        pltpu.make_async_copy(factors, factors_here, sems.at[0]),
        pltpu.make_async_copy(start, start_here, sems.at[1]),
    ]
    for load in loads:
        load.start()
    for load in loads:
        load.wait()
    separate(factors_here, wide, separated)
    values = start_here[...].T.astype(BF16)
    product[...] = jnp.dot(values, separated[...], preferred_element_type=F32)
    for side, out in ((core, own), (1 - core, other)):
        real = pl.ds(pl.multiple_of(side * half, half), half)
        imaginary = pl.ds(pl.multiple_of((side + 2) * half, half), half)
        for tile in range(tiles):
            columns = slice(tile * LANES, (tile + 1) * LANES)
            out[tile] = adjoint_block(product[real, columns], product[imaginary, columns]).astype(BF16)


def add_kernel(own, arrived, *outs):
    z, _, _ = place()
    near = outs[0].shape[0]
    for s, out in enumerate(outs):
        at = pl.ds((z ^ s) * near, near)
        out[...] = (own[at].astype(F32) + arrived[at].astype(F32)).astype(BF16)


def repack_kernel(far, *refs):
    blocks, outs = refs[:far], refs[far:]
    _, x, _ = place()
    for t, out in enumerate(outs):
        for s, block in enumerate(blocks):
            out[s] = block[x ^ t]


def rows_kernel(ranks, own, mate, observed, mate_observed, own_out, mate_out, observed_out, wide, turned):
    z, x, core = place()
    half = observed_out.shape[1] // 2
    tiles = own_out.shape[1] // LANES
    chip = z * lax.axis_size("x") + x
    lane = lax.broadcasted_iota(jnp.int32, (1, LANES), 1) % (LANES // 2)
    masks = [lane < ranks[0, chip, tile] for tile in range(tiles)]
    separate(own, wide, own_out, masks)
    separate(mate, wide, mate_out, masks)
    for index, values in enumerate((observed, mate_observed)):
        turned[...] = values[...].T
        observed_out[index, :half] = turned[pl.ds(pl.multiple_of(core * half, half), half), :]
        observed_out[index, half:] = turned[pl.ds(pl.multiple_of((core + 2) * half, half), half), :]


def columns_kernel(mate, mate_out, wide):
    separate(mate, wide, mate_out)


def image_kernel(near, *refs):
    blocks, (own, mate, observed), outs, (left,) = refs[:near], refs[near : near + 3], refs[near + 3 : -1], refs[-1:]
    z, _, _ = place()
    half = left.shape[0] // 2
    spread_blocks(blocks, left)
    products = []
    for index, factors in enumerate((own, mate)):
        misfit = times_transposed(left[...], factors[...]) - observed[index]
        products.append(jnp.dot(misfit.astype(BF16), factors[...], preferred_element_type=F32))
    for tile in range(left.shape[1] // LANES):
        columns = slice(tile * LANES, (tile + 1) * LANES)
        parts = [
            adjoint_block(product[:half, columns], product[half:, columns]).astype(BF16).astype(F32)
            for product in products
        ]
        left[:half, columns] = (parts[0] + parts[1]).astype(BF16)
    for s, out in enumerate(outs):
        for k in range(near):
            at = pl.multiple_of(((z ^ s) * near + k) * LANES, LANES)
            out[k] = left[:half, pl.ds(at, LANES)]


def gradient_kernel(near, *refs):
    blocks, (own, mate, own_out, mate_out, left) = refs[:near], refs[near:]
    spread_blocks(blocks, left)
    mate_out[...] = times_transposed(left[...], mate[...]).astype(BF16)
    own_out[...] = times_transposed(left[...], own[...]).astype(BF16)


def thin_out(values):
    return values - jnp.clip(values, -LEVEL, LEVEL)


def shrink_kernel(band, *refs):
    tables, starts, gradients, (out, spectra) = (
        refs[: -3 * band - 2],
        refs[-3 * band - 2 : -2 * band - 2],
        refs[-2 * band - 2 : -2],
        refs[-2:],
    )
    _, _, core = place()
    quarter = out.shape[1] // 4
    estimates = []
    for index in range(band):
        for side, part in ((core, gradients[2 * index]), (1 - core, gradients[2 * index + 1])):
            for row in (0, 2):
                at = pl.multiple_of((side + row) * quarter, quarter)
                spectra[index, pl.ds(at, quarter), :] = part[row // 2 * quarter : (row // 2 + 1) * quarter].astype(F32)
        estimates.append(starts[index][...] - STEP_SIZE * spectra[index].T)
    scale = 1.0 / math.sqrt(band)
    if band == 2:
        here, there = estimates
        out[...] = (thin_out((here + there) * scale) + thin_out((here - there) * scale)) * scale
        return
    (tables,) = tables
    lane = lax.broadcasted_iota(jnp.int32, (1, out.shape[1]), 1)
    turn = jnp.where(lane < 2 * quarter, -1.0, 1.0).astype(F32)
    turned = [pltpu.roll(estimate, 2 * quarter, 1) * turn for estimate in estimates]
    total = jnp.zeros_like(estimates[0])
    for time in range(band):
        sample = jnp.zeros_like(estimates[0])
        for index in range(band):
            sample += tables[0, index, time] * estimates[index] + tables[1, index, time] * turned[index]
        thinned = thin_out(sample * scale)
        total += tables[0, 0, time] * thinned - tables[1, 0, time] * (pltpu.roll(thinned, 2 * quarter, 1) * turn)
    out[...] = total * scale


def call(kernel, name, outs, inputs, scratch=(), flops=0, spaces=(), limit=VMEM_LIMIT):
    spaces = (*spaces, *[pltpu.VMEM] * (len(inputs) - len(spaces)))
    moved = sum(x.size * x.dtype.itemsize for x in [*inputs, *outs])
    return pl.pallas_call(
        kernel,
        out_shape=outs,
        in_specs=[pl.BlockSpec(memory_space=space) for space in spaces],
        out_specs=[pl.BlockSpec(memory_space=pltpu.VMEM)] * len(outs),
        scratch_shapes=scratch,
        compiler_params=pltpu.CompilerParams(vmem_limit_bytes=limit),
        cost_estimate=pl.CostEstimate(flops=flops, bytes_accessed=moved, transcendentals=0),
        name=name,
    )(*inputs)


def swap(value, axis, shift):
    return lax.ppermute(value, axis, [(i, i ^ shift) for i in range(lax.axis_size(axis))])


def to_band(value, shift, flip):
    band = lax.axis_size("freq")
    pairs = [(core * band + f, (core ^ flip) * band + (f - shift) % band) for core in range(2) for f in range(band)]
    return lax.ppermute(value, ("core", "freq"), pairs)


def after(value, *others):
    return lax.optimization_barrier((value, *others))[0]


def body(u_factors, v_factors, ranks, observed, start):
    band = lax.axis_size("freq")
    far, near = lax.axis_size("z"), lax.axis_size("x")
    rows, tiles, width = u_factors.shape[1:]
    sources = start.shape[2]
    half = sources // 4
    columns = tiles * width
    left_rows = u_factors.reshape(rows * tiles, width)
    right_rows = v_factors.reshape(rows * tiles, width)
    observed = observed.reshape(rows, sources)
    start = start.reshape(rows, sources)

    def shape(*dims, dtype=BF16):
        return jax.ShapeDtypeStruct(dims, dtype)

    wide = pltpu.VMEM((rows * tiles, width), F32)
    factor = shape(rows, columns)
    blocks = shape(tiles, half, width)
    product = 2 * rows * columns * sources
    along_z = [shape(near, half, width)] * far
    along_x = [shape(far, half, width)] * near

    own, other, own_right = call(
        forward_kernel,
        "forward",
        [blocks, blocks, factor],
        [start, right_rows],
        [
            pltpu.VMEM(start.shape, F32),
            pltpu.VMEM(right_rows.shape, BF16),
            wide,
            pltpu.VMEM((sources, columns), F32),
            pltpu.SemaphoreType.DMA((2,)),
        ],
        product,
        [pltpu.HBM] * 2,
        limit=FIRST_LIMIT,
    )
    mate_left = swap(after(left_rows, other), "core", 1)
    mate_observed = swap(after(observed, other), "core", 1)
    sends = call(add_kernel, "add", along_z, [own, swap(other, "core", 1)])
    arrived = [sends[0], *[swap(sends[s], "z", s) for s in reversed(range(1, far))][::-1]]
    mate_right = swap(after(right_rows, sends[0]), "core", 1)
    sends = call(functools.partial(repack_kernel, far), "repack", along_x, arrived)
    arrived = [sends[0], *[swap(sends[t], "x", t) for t in range(1, near)]]
    starts = [start] + [to_band(after(start, sends[0]), shift, 0) for shift in range(1, band)]
    own_left, mate_left, turned_observed = call(
        rows_kernel,
        "rows",
        [factor, factor, shape(2, 2 * half, rows, dtype=F32)],
        [ranks, left_rows, mate_left, observed, mate_observed],
        [wide, pltpu.VMEM((sources, rows), F32)],
        spaces=[pltpu.SMEM],
    )
    spread = pltpu.VMEM((2 * half, columns), BF16)
    sends = call(
        functools.partial(image_kernel, near),
        "image",
        along_z,
        [*arrived, own_left, mate_left, turned_observed],
        [spread],
        2 * product,
    )
    arrived = [sends[0], *[swap(sends[s], "z", s) for s in reversed(range(1, far))][::-1]]
    sends = call(functools.partial(repack_kernel, far), "repack", along_x, arrived)
    arrived = [sends[0], *[swap(sends[t], "x", t) for t in range(1, near)]]
    (mate_right,) = call(columns_kernel, "columns", [factor], [mate_right], [wide])
    own_part, mate_part = call(
        functools.partial(gradient_kernel, near),
        "gradient",
        [shape(2 * half, rows)] * 2,
        [*arrived, own_right, mate_right],
        [spread],
        product,
    )
    gradients = [own_part, swap(mate_part, "core", 1)]
    for shift in range(1, band):
        gradients += [to_band(own_part, shift, 0), to_band(mate_part, shift, 1)]
    inputs, spaces = [*starts, *gradients], []
    if band > 2:
        bands = jnp.arange(band, dtype=jnp.int32)
        phases = (bands[:, None] + lax.axis_index("freq")) * bands[None, :] % band
        phases = (2.0 * math.pi / band) * phases.astype(F32)
        inputs, spaces = [jnp.stack([jnp.cos(phases), jnp.sin(phases)]), *inputs], [pltpu.SMEM]
    (estimate,) = call(
        functools.partial(shrink_kernel, band),
        "shrink",
        [shape(rows, sources, dtype=F32)],
        inputs,
        [pltpu.VMEM((band, sources, rows), F32)],
        spaces=spaces,
    )
    return estimate[None]


def solution(mesh):
    count, band = mesh.devices.shape
    chips = count // 2
    near = 2 ** ((chips.bit_length() - 1) // 2)
    parts = Mesh(mesh.devices.reshape(chips // near, near, 2, band), ("z", "x", "core", "freq"))
    tile = ("z", "x", "core")
    in_specs = (
        P("freq", tile, None, None),
        P("freq", tile, None, None),
        P("freq", None, None),
        P("freq", tile, None),
        P("freq", tile, None),
    )
    out_specs = P("freq", tile, None)
    return jax.shard_map(body, mesh=parts, in_specs=in_specs, out_specs=out_specs, check_vma=False)
```

time: 61.5 us -> 39 us (0.63)
  blocking collectives: 31.8 us -> 0 us
  starting transfers between devices: 11.5 us -> 20.4 us
  waiting for transfers between devices: 9.63 us -> 11.8 us
  local copies, waits for them, and re-layouts: 2.14 us -> 0.02 us
    all_gather x1 -> x0, blocking collectives: 31.8 us -> none  [body(): coeffs = lax.all_gather(coeffs, 'chip')]
    ppermute x5 -> x13, starting transfers between devices: 0.98 us -> 17 us  [swap(): lax.ppermute(value, axis, [(i, i ^ shift) for i in range(lax.axis_size(ax...]
    ppermute x5 -> x13, waiting for transfers between devices: 0.74 us -> 9.26 us  [swap(): lax.ppermute(value, axis, [(i, i ^ shift) for i in range(lax.axis_size(ax...]
    all_to_all x1 -> x0, waiting for transfers between devices: 6.5 us -> none  [body(): back = lax.all_to_all(back, 'chip', split_axis=0, concat_axis=0, tiled=True)]
    all_to_all x1 -> x0, starting transfers between devices: 5.4 us -> none  [body(): back = lax.all_to_all(back, 'chip', split_axis=0, concat_axis=0, tiled=True)]
    unnamed x12 -> x10, local copies, waits for them, and re-layouts: 2.14 us -> 0.02 us
    ppermute x3, starting transfers between devices: 5.11 us -> 3.38 us  [to_band(): return lax.ppermute(value, ('core', 'freq'), pairs)]
    pallas_call x7 -> x9, Pallas kernels: 6.02 us -> 6.52 us  [call(): pl.pallas_call(kernel, out_shape=outs, in_specs=[pl.BlockSpec(memory_spac...]
  transfers between devices with their start and end apart: 9 -> 16, of which waited for: 3 -> 8; matrix products, arithmetic and copies ran while one was open for 0% -> 0% of each run, Pallas kernels for 8% -> 9%
where the time goes in v1:
time: 39 us; the launch traced here: 38.8 us
  starting transfers between devices  20.4 us (52%)
  waiting for transfers between devices  11.8 us (30%)
  Pallas kernels  6.52 us (17%)
    ppermute x13, starting transfers between devices, swap(): lax.ppermute(value, axis, [(i, i ^ shift) for i in range(lax.axis_size(ax...  17 us
    ppermute x13, waiting for transfers between devices, swap(): lax.ppermute(value, axis, [(i, i ^ shift) for i in range(lax.axis_size(ax...  9.26 us
    pallas_call x9, Pallas kernels, call(): pl.pallas_call(kernel, out_shape=outs, in_specs=[pl.BlockSpec(memory_spac...  6.52 us
    ppermute x3, starting transfers between devices, to_band(): return lax.ppermute(value, ('core', 'freq'), pairs)  3.38 us
    ppermute x3, waiting for transfers between devices, to_band(): return lax.ppermute(value, ('core', 'freq'), pairs)  2.55 us
  transfers between devices with their start and end apart: 16, of which 8 were waited for; matrix products, arithmetic and copies ran while one was open for 0% of the time, Pallas kernels for 9%

profile of v1, /device:TPU:0, one launch (start us, length us, event | category | flops | bytes accessed | tf_op | source)
XLA Modules:
  0.0 38.8 jit_solution(16087408106675533688)
XLA Ops:
  0.0 2.3 %forward.1 = (bf16[8,32,128]{2,1,0:T(8,128)(2,1)S(1)}, bf16[8,32,128]{2,1,0:T(8,128)(2,1)S(1)}, bf16[256,1024]{1,0:T(8,128)(2,1)}) custom-call(f32[256,128]{1,0:T(8,128)} %bitcast.7, bf16[2048,128]{1,0:T(8,128)(2,1)} %bitcast.12), custom_call_target="tpu_custom_call" | custom-call | flops 67108864 | bytes 1310720 | tf_op jit(solution)/shard_map/forward/pallas_call | solution.py:193
  2.3 0.0 copy-start.2
  2.3 0.5 %collective-permute-start = (bf16[8,32,128]{2,1,0:T(8,128)(2,1)S(1)}, bf16[8,32,128]{2,1,0:T(8,128)(2,1)S(1)}, u32[]{:S(2)}, u32[]{:S(2)}) collective-permute-start(bf16[8,32,128]{2,1,0:T(8,128)(2,1)S(1)} %get-tuple-element.30), channel_id=1, source_target_pairs={{0,2},{2,0},{1,3},{3,1},{4,6},{6,4},{5,7},{7,5},{8,10},{10,8},{9,1... | collective-permute-start | bytes 196616 | tf_op jit(solution)/shard_map/ppermute | solution.py:206
  2.8 0.1 collective-permute-start.6
  2.9 0.8 %collective-permute-done.arrived = bf16[8,32,128]{2,1,0:T(8,128)(2,1)S(1)} collective-permute-done((bf16[8,32,128]{2,1,0:T(8,128)(2,1)S(1)}, bf16[8,32,128]{2,1,0:T(8,128)(2,1)S(1)}, u32[]{:S(2)}, u32[]{:S(2)}) %collective-permute-start) | collective-permute-done | bytes 65568 | tf_op jit(solution)/shard_map/ppermute | solution.py:206
  3.7 0.4 %collective-permute-start.12 = (bf16[2048,128]{1,0:T(8,128)(2,1)}, bf16[2048,128]{1,0:T(8,128)(2,1)S(1)}, u32[]{:S(2)}, u32[]{:S(2)}) collective-permute-start(bf16[2048,128]{1,0:T(8,128)(2,1)} %bitcast.13), channel_id=1, source_target_pairs={{0,2},{2,0},{1,3},{3,1},{4,6},{6,4},{5,7},{7,5},{8,10},{10,8},{9,1... | collective-permute-start | bytes 1572872 | tf_op jit(solution)/shard_map/ppermute | solution.py:206
  4.2 0.2 collective-permute-start.7
  4.3 2.9 %collective-permute-start.1 = (bf16[2,32,128]{2,1,0:T(8,128)(2,1)S(1)}, bf16[2,32,128]{2,1,0:T(8,128)(2,1)S(1)}, u32[]{:S(2)}, u32[]{:S(2)}) collective-permute-start(bf16[2,32,128]{2,1,0:T(8,128)(2,1)S(1)} %get-tuple-element.32), channel_id=1, source_target_pairs={{0,8},{8,0},{16,24},{24,16},{1,9},{9,1},{17,25},{25,17},{2,10},{10... | collective-permute-start | bytes 49160 | tf_op jit(solution)/shard_map/ppermute | solution.py:206
  7.2 2.6 %collective-permute-start.2 = (bf16[2,32,128]{2,1,0:T(8,128)(2,1)S(1)}, bf16[2,32,128]{2,1,0:T(8,128)(2,1)S(1)}, u32[]{:S(2)}, u32[]{:S(2)}) collective-permute-start(bf16[2,32,128]{2,1,0:T(8,128)(2,1)S(1)} %get-tuple-element.33), channel_id=1, source_target_pairs={{0,16},{8,24},{16,0},{24,8},{1,17},{9,25},{17,1},{25,9},{2,18},{10... | collective-permute-start | bytes 49160 | tf_op jit(solution)/shard_map/ppermute | solution.py:206
  9.8 0.0 collective-permute-done.1.refs_1_
  9.8 3.2 %collective-permute-start.3 = (bf16[2,32,128]{2,1,0:T(8,128)(2,1)S(1)}, bf16[2,32,128]{2,1,0:T(8,128)(2,1)S(1)}, u32[]{:S(2)}, u32[]{:S(2)}) collective-permute-start(bf16[2,32,128]{2,1,0:T(8,128)(2,1)S(1)} %get-tuple-element.34), channel_id=1, source_target_pairs={{0,24},{8,16},{16,8},{24,0},{1,25},{9,17},{17,9},{25,1},{2,26},{10... | collective-permute-start | bytes 49160 | tf_op jit(solution)/shard_map/ppermute | solution.py:206
  13.0 0.0 collective-permute-done.2.refs_2_
  13.0 2.4 %collective-permute-done.3.refs_3_ = bf16[2,32,128]{2,1,0:T(8,128)(2,1)S(1)} collective-permute-done((bf16[2,32,128]{2,1,0:T(8,128)(2,1)S(1)}, bf16[2,32,128]{2,1,0:T(8,128)(2,1)S(1)}, u32[]{:S(2)}, u32[]{:S(2)}) %collective-permute-start.3) | collective-permute-done | bytes 16416 | tf_op jit(solution)/shard_map/ppermute | solution.py:206
  15.4 1.6 %collective-permute-start.5 = (bf16[4,32,128]{2,1,0:T(8,128)(2,1)S(1)}, bf16[4,32,128]{2,1,0:T(8,128)(2,1)S(1)}, u32[]{:S(2)}, u32[]{:S(2)}) collective-permute-start(bf16[4,32,128]{2,1,0:T(8,128)(2,1)S(1)} %get-tuple-element.37), channel_id=1, source_target_pairs={{0,4},{4,0},{1,5},{5,1},{2,6},{6,2},{3,7},{7,3},{8,12},{12,8},{9,1... | collective-permute-start | bytes 98312 | tf_op jit(solution)/shard_map/ppermute | solution.py:206
  16.9 1.5 %collective-permute-start.4 = (f32[256,128]{1,0:T(8,128)S(1)}, f32[256,128]{1,0:T(8,128)S(1)}, u32[]{:S(2)}, u32[]{:S(2)}) collective-permute-start(f32[256,128]{1,0:T(8,128)S(1)} %bitcast.8), channel_id=1, source_target_pairs={{0,1},{1,0},{2,3},{3,2},{4,5},{5,4},{6,7},{7,6},{8,9},{9,8},{10,11... | collective-permute-start | bytes 393224 | tf_op jit(solution)/shard_map/ppermute | solution.py:212
  18.5 1.4 %rows.1 = (bf16[256,1024]{1,0:T(8,128)(2,1)S(1)}, bf16[256,1024]{1,0:T(8,128)(2,1)S(1)}, f32[2,64,256]{2,1,0:T(8,128)S(1)}) custom-call(s32[1,8,8]{2,1,0:T(8,128)S(1)} %copy-done.4, bf16[2048,128]{1,0:T(8,128)(2,1)S(1)} %bitcast.6, bf16[2048,128]{1,0:T(8,128)(2,1)S(1)} %collective-permute-done.6.mate, f32[256,128]{1,0:T(8,128)S(1)} %bitcast.11, ...), custom_call_target="tpu_custom_call" | custom-call | bytes 2490624 | tf_op jit(solution)/shard_map/rows/pallas_call | solution.py:193
  19.9 1.3 %image.1 = (bf16[2,32,128]{2,1,0:T(8,128)(2,1)S(1)}, bf16[2,32,128]{2,1,0:T(8,128)(2,1)S(1)}, bf16[2,32,128]{2,1,0:T(8,128)(2,1)S(1)}, bf16[2,32,128]{2,1,0:T(8,128)(2,1)S(1)}) custom-call(bf16[4,32,128]{2,1,0:T(8,128)(2,1)S(1)} %get-tuple-element.35.refs_0_, bf16[4,32,128]{2,1,0:T(8,128)(2,1)S(1)} %collective-permute-done.5.refs_1_, ...), custom_call_target="tpu_custom_call" | custom-call | flops 134217728 | bytes 1310720 | tf_op jit(solution)/shard_map/image/pallas_call | solution.py:193
  21.1 3.2 %collective-permute-start.10 = (bf16[2,32,128]{2,1,0:T(8,128)(2,1)S(1)}, bf16[2,32,128]{2,1,0:T(8,128)(2,1)S(1)}, u32[]{:S(2)}, u32[]{:S(2)}) collective-permute-start(bf16[2,32,128]{2,1,0:T(8,128)(2,1)S(1)} %get-tuple-element.46), channel_id=1, source_target_pairs={{0,24},{8,16},{16,8},{24,0},{1,25},{9,17},{17,9},{25,1},{2,26},{10... | collective-permute-start | bytes 49160 | tf_op jit(solution)/shard_map/ppermute | solution.py:206
  24.4 1.2 %collective-permute-start.9 = (bf16[2,32,128]{2,1,0:T(8,128)(2,1)S(1)}, bf16[2,32,128]{2,1,0:T(8,128)(2,1)S(1)}, u32[]{:S(2)}, u32[]{:S(2)}) collective-permute-start(bf16[2,32,128]{2,1,0:T(8,128)(2,1)S(1)} %get-tuple-element.45), channel_id=1, source_target_pairs={{0,16},{8,24},{16,0},{24,8},{1,17},{9,25},{17,1},{25,9},{2,18},{10... | collective-permute-start | bytes 49160 | tf_op jit(solution)/shard_map/ppermute | solution.py:206
  25.6 1.1 %collective-permute-done.10.refs_3_ = bf16[2,32,128]{2,1,0:T(8,128)(2,1)S(1)} collective-permute-done((bf16[2,32,128]{2,1,0:T(8,128)(2,1)S(1)}, bf16[2,32,128]{2,1,0:T(8,128)(2,1)S(1)}, u32[]{:S(2)}, u32[]{:S(2)}) %collective-permute-start.10) | collective-permute-done | bytes 16416 | tf_op jit(solution)/shard_map/ppermute | solution.py:206
  26.7 1.4 %collective-permute-done.8.refs_1_ = bf16[2,32,128]{2,1,0:T(8,128)(2,1)S(1)} collective-permute-done((bf16[2,32,128]{2,1,0:T(8,128)(2,1)S(1)}, bf16[2,32,128]{2,1,0:T(8,128)(2,1)S(1)}, u32[]{:S(2)}, u32[]{:S(2)}) %collective-permute-start.8) | collective-permute-done | bytes 16416 | tf_op jit(solution)/shard_map/ppermute | solution.py:206
  28.1 0.9 %collective-permute-done.9.refs_2_ = bf16[2,32,128]{2,1,0:T(8,128)(2,1)S(1)} collective-permute-done((bf16[2,32,128]{2,1,0:T(8,128)(2,1)S(1)}, bf16[2,32,128]{2,1,0:T(8,128)(2,1)S(1)}, u32[]{:S(2)}, u32[]{:S(2)}) %collective-permute-start.9) | collective-permute-done | bytes 16416 | tf_op jit(solution)/shard_map/ppermute | solution.py:206
  29.0 1.1 %collective-permute-start.11 = (bf16[4,32,128]{2,1,0:T(8,128)(2,1)S(1)}, bf16[4,32,128]{2,1,0:T(8,128)(2,1)S(1)}, u32[]{:S(2)}, u32[]{:S(2)}) collective-permute-start(bf16[4,32,128]{2,1,0:T(8,128)(2,1)S(1)} %get-tuple-element.48), channel_id=1, source_target_pairs={{0,4},{4,0},{1,5},{5,1},{2,6},{6,2},{3,7},{7,3},{8,12},{12,8},{9,1... | collective-permute-start | bytes 98312 | tf_op jit(solution)/shard_map/ppermute | solution.py:206
  30.1 0.3 columns.1.refs_3_
  30.4 2.6 %collective-permute-done.11.refs_1_ = bf16[4,32,128]{2,1,0:T(8,128)(2,1)S(1)} collective-permute-done((bf16[4,32,128]{2,1,0:T(8,128)(2,1)S(1)}, bf16[4,32,128]{2,1,0:T(8,128)(2,1)S(1)}, u32[]{:S(2)}, u32[]{:S(2)}) %collective-permute-start.11) | collective-permute-done | bytes 32800 | tf_op jit(solution)/shard_map/ppermute | solution.py:206
  33.0 0.5 %gradient.1 = (bf16[64,256]{1,0:T(8,128)(2,1)S(1)}, bf16[64,256]{1,0:T(8,128)(2,1)S(1)}) custom-call(bf16[4,32,128]{2,1,0:T(8,128)(2,1)S(1)} %get-tuple-element.47.refs_0_, bf16[4,32,128]{2,1,0:T(8,128)(2,1)S(1)} %collective-permute-done.11.refs_1_, bf16[256,1024]{1,0:T(8,128)(2,1)S(1)} %copy-done.1, bf16[256,1024]{1,0:T(8,128)(2,1)S(1)} %columns.1.refs_3_), custom_call_target="tpu_custom_call" | custom-call | flops 67108864 | bytes 1179648 | tf_op jit(solution)/shard_map/gradient/pallas_call | solution.py:193
  33.5 0.1 collective-permute-start.13
  33.6 1.1 %collective-permute-start.14 = (bf16[64,256]{1,0:T(8,128)(2,1)S(1)}, bf16[64,256]{1,0:T(8,128)(2,1)S(1)}, u32[]{:S(2)}, u32[]{:S(2)}) collective-permute-start(bf16[64,256]{1,0:T(8,128)(2,1)S(1)} %get-tuple-element.51.refs_2_), channel_id=1, source_target_pairs={{0,1},{1,0},{2,3},{3,2},{4,5},{5,4},{6,7},{7,6},{8,9},{9,8},{10,11... | collective-permute-start | bytes 98312 | tf_op jit(solution)/shard_map/ppermute | solution.py:212
  34.6 0.8 %collective-permute-start.15 = (bf16[64,256]{1,0:T(8,128)(2,1)S(1)}, bf16[64,256]{1,0:T(8,128)(2,1)S(1)}, u32[]{:S(2)}, u32[]{:S(2)}) collective-permute-start(bf16[64,256]{1,0:T(8,128)(2,1)S(1)} %get-tuple-element.52), channel_id=1, source_target_pairs={{0,3},{1,2},{2,1},{3,0},{4,7},{5,6},{6,5},{7,4},{8,11},{9,10},{10,... | collective-permute-start | bytes 98312 | tf_op jit(solution)/shard_map/ppermute | solution.py:212
  35.4 2.1 %collective-permute-done.14.refs_4_ = bf16[64,256]{1,0:T(8,128)(2,1)S(1)} collective-permute-done((bf16[64,256]{1,0:T(8,128)(2,1)S(1)}, bf16[64,256]{1,0:T(8,128)(2,1)S(1)}, u32[]{:S(2)}, u32[]{:S(2)}) %collective-permute-start.14) | collective-permute-done | bytes 32800 | tf_op jit(solution)/shard_map/ppermute | solution.py:212
  37.5 0.4 %collective-permute-done.15.refs_5_ = bf16[64,256]{1,0:T(8,128)(2,1)S(1)} collective-permute-done((bf16[64,256]{1,0:T(8,128)(2,1)S(1)}, bf16[64,256]{1,0:T(8,128)(2,1)S(1)}, u32[]{:S(2)}, u32[]{:S(2)}) %collective-permute-start.15) | collective-permute-done | bytes 32800 | tf_op jit(solution)/shard_map/ppermute | solution.py:212
  38.0 0.8 %shrink.1 = f32[256,128]{1,0:T(8,128)} custom-call(f32[256,128]{1,0:T(8,128)S(1)} %bitcast.9, f32[256,128]{1,0:T(8,128)S(1)} %collective-permute-done.4.refs_1_, bf16[64,256]{1,0:T(8,128)(2,1)S(1)} %get-tuple-element.51.refs_2_, bf16[64,256]{1,0:T(8,128)(2,1)S(1)} %collective-permute-done.13.refs_3_, bf16[64,256]{1,0:T(8,128)(2,1)S(1)} %collective-permute-done.14.refs_4_, ...), custom_call_target="tpu_custom_call" | custom-call | bytes 524288 | tf_op jit(solution)/shard_map/shrink/pallas_call | solution.py:193
  (19 shorter events, 0.1 us)
Async XLA Ops:
  0.0 2.8 %copy-start = (bf16[1,256,8,128]{3,2,1,0:T(8,128)(2,1)S(1)}, bf16[1,256,8,128]{3,2,1,0:T(8,128)(2,1)}, u32[]{:S(2)}) copy-start(bf16[1,256,8,128]{3,2,1,0:T(8,128)(2,1)} %param.5) | copy-start | bytes 1572868
  0.0 4.2 %copy-start.3 = (f32[1,256,128]{2,1,0:T(8,128)S(1)}, f32[1,256,128]{2,1,0:T(8,128)}, u32[]{:S(2)}) copy-start(f32[1,256,128]{2,1,0:T(8,128)} %param.8) | copy-start | bytes 393220
  2.3 14.7 %copy-start.2 = (f32[1,256,128]{2,1,0:T(8,128)S(1)}, f32[1,256,128]{2,1,0:T(8,128)}, u32[]{:S(2)}) copy-start(f32[1,256,128]{2,1,0:T(8,128)} %param.9) | copy-start | bytes 393220
  2.3 1.4 %collective-permute-start = (bf16[8,32,128]{2,1,0:T(8,128)(2,1)S(1)}, bf16[8,32,128]{2,1,0:T(8,128)(2,1)S(1)}, u32[]{:S(2)}, u32[]{:S(2)}) collective-permute-start(bf16[8,32,128]{2,1,0:T(8,128)(2,1)S(1)} %get-tuple-element.30), channel_id=1, source_target_pairs={{0,2},{2,0},{1,3},{3,1},{4,6},{6,4},{5,7},{7,5},{8,10},{10,8},{9,1... | collective-permute-start | bytes 196616 | tf_op jit(solution)/shard_map/ppermute | solution.py:206
  2.8 15.7 %collective-permute-start.6 = (bf16[2048,128]{1,0:T(8,128)(2,1)S(1)}, bf16[2048,128]{1,0:T(8,128)(2,1)S(1)}, u32[]{:S(2)}, u32[]{:S(2)}) collective-permute-start(bf16[2048,128]{1,0:T(8,128)(2,1)S(1)} %bitcast.5), channel_id=1, source_target_pairs={{0,2},{2,0},{1,3},{3,1},{4,6},{6,4},{5,7},{7,5},{8,10},{10,8},{9,1... | collective-permute-start | bytes 1572872 | tf_op jit(solution)/shard_map/ppermute | solution.py:206
  3.7 26.4 %collective-permute-start.12 = (bf16[2048,128]{1,0:T(8,128)(2,1)}, bf16[2048,128]{1,0:T(8,128)(2,1)S(1)}, u32[]{:S(2)}, u32[]{:S(2)}) collective-permute-start(bf16[2048,128]{1,0:T(8,128)(2,1)} %bitcast.13), channel_id=1, source_target_pairs={{0,2},{2,0},{1,3},{3,1},{4,6},{6,4},{5,7},{7,5},{8,10},{10,8},{9,1... | collective-permute-start | bytes 1572872 | tf_op jit(solution)/shard_map/ppermute | solution.py:206
  4.2 14.3 %collective-permute-start.7 = (f32[256,128]{1,0:T(8,128)S(1)}, f32[256,128]{1,0:T(8,128)S(1)}, u32[]{:S(2)}, u32[]{:S(2)}) collective-permute-start(f32[256,128]{1,0:T(8,128)S(1)} %bitcast.10), channel_id=1, source_target_pairs={{0,2},{2,0},{1,3},{3,1},{4,6},{6,4},{5,7},{7,5},{8,10},{10,8},{9,1... | collective-permute-start | bytes 393224 | tf_op jit(solution)/shard_map/ppermute | solution.py:206
  4.3 5.5 %collective-permute-start.1 = (bf16[2,32,128]{2,1,0:T(8,128)(2,1)S(1)}, bf16[2,32,128]{2,1,0:T(8,128)(2,1)S(1)}, u32[]{:S(2)}, u32[]{:S(2)}) collective-permute-start(bf16[2,32,128]{2,1,0:T(8,128)(2,1)S(1)} %get-tuple-element.32), channel_id=1, source_target_pairs={{0,8},{8,0},{16,24},{24,16},{1,9},{9,1},{17,25},{25,17},{2,10},{10... | collective-permute-start | bytes 49160 | tf_op jit(solution)/shard_map/ppermute | solution.py:206
  7.2 5.8 %collective-permute-start.2 = (bf16[2,32,128]{2,1,0:T(8,128)(2,1)S(1)}, bf16[2,32,128]{2,1,0:T(8,128)(2,1)S(1)}, u32[]{:S(2)}, u32[]{:S(2)}) collective-permute-start(bf16[2,32,128]{2,1,0:T(8,128)(2,1)S(1)} %get-tuple-element.33), channel_id=1, source_target_pairs={{0,16},{8,24},{16,0},{24,8},{1,17},{9,25},{17,1},{25,9},{2,18},{10... | collective-permute-start | bytes 49160 | tf_op jit(solution)/shard_map/ppermute | solution.py:206
  9.8 5.5 %collective-permute-start.3 = (bf16[2,32,128]{2,1,0:T(8,128)(2,1)S(1)}, bf16[2,32,128]{2,1,0:T(8,128)(2,1)S(1)}, u32[]{:S(2)}, u32[]{:S(2)}) collective-permute-start(bf16[2,32,128]{2,1,0:T(8,128)(2,1)S(1)} %get-tuple-element.34), channel_id=1, source_target_pairs={{0,24},{8,16},{16,8},{24,0},{1,25},{9,17},{17,9},{25,1},{2,26},{10... | collective-permute-start | bytes 49160 | tf_op jit(solution)/shard_map/ppermute | solution.py:206
  15.4 3.1 %copy-start.4 = (s32[1,8,8]{2,1,0:T(8,128)S(1)}, s32[1,8,8]{2,1,0:T(8,128)}, u32[]{:S(2)}) copy-start(s32[1,8,8]{2,1,0:T(8,128)} %ranks.1) | copy-start | bytes 772
  15.4 4.5 %collective-permute-start.5 = (bf16[4,32,128]{2,1,0:T(8,128)(2,1)S(1)}, bf16[4,32,128]{2,1,0:T(8,128)(2,1)S(1)}, u32[]{:S(2)}, u32[]{:S(2)}) collective-permute-start(bf16[4,32,128]{2,1,0:T(8,128)(2,1)S(1)} %get-tuple-element.37), channel_id=1, source_target_pairs={{0,4},{4,0},{1,5},{5,1},{2,6},{6,2},{3,7},{7,3},{8,12},{12,8},{9,1... | collective-permute-start | bytes 98312 | tf_op jit(solution)/shard_map/ppermute | solution.py:206
  16.9 18.5 %collective-permute-start.4 = (f32[256,128]{1,0:T(8,128)S(1)}, f32[256,128]{1,0:T(8,128)S(1)}, u32[]{:S(2)}, u32[]{:S(2)}) collective-permute-start(f32[256,128]{1,0:T(8,128)S(1)} %bitcast.8), channel_id=1, source_target_pairs={{0,1},{1,0},{2,3},{3,2},{4,5},{5,4},{6,7},{7,6},{8,9},{9,8},{10,11... | collective-permute-start | bytes 393224 | tf_op jit(solution)/shard_map/ppermute | solution.py:212
  21.1 5.6 %collective-permute-start.10 = (bf16[2,32,128]{2,1,0:T(8,128)(2,1)S(1)}, bf16[2,32,128]{2,1,0:T(8,128)(2,1)S(1)}, u32[]{:S(2)}, u32[]{:S(2)}) collective-permute-start(bf16[2,32,128]{2,1,0:T(8,128)(2,1)S(1)} %get-tuple-element.46), channel_id=1, source_target_pairs={{0,24},{8,16},{16,8},{24,0},{1,25},{9,17},{17,9},{25,1},{2,26},{10... | collective-permute-start | bytes 49160 | tf_op jit(solution)/shard_map/ppermute | solution.py:206
  24.4 3.7 %collective-permute-start.8 = (bf16[2,32,128]{2,1,0:T(8,128)(2,1)S(1)}, bf16[2,32,128]{2,1,0:T(8,128)(2,1)S(1)}, u32[]{:S(2)}, u32[]{:S(2)}) collective-permute-start(bf16[2,32,128]{2,1,0:T(8,128)(2,1)S(1)} %get-tuple-element.44), channel_id=1, source_target_pairs={{0,8},{8,0},{16,24},{24,16},{1,9},{9,1},{17,25},{25,17},{2,10},{10... | collective-permute-start | bytes 49160 | tf_op jit(solution)/shard_map/ppermute | solution.py:206
  24.4 4.6 %collective-permute-start.9 = (bf16[2,32,128]{2,1,0:T(8,128)(2,1)S(1)}, bf16[2,32,128]{2,1,0:T(8,128)(2,1)S(1)}, u32[]{:S(2)}, u32[]{:S(2)}) collective-permute-start(bf16[2,32,128]{2,1,0:T(8,128)(2,1)S(1)} %get-tuple-element.45), channel_id=1, source_target_pairs={{0,16},{8,24},{16,0},{24,8},{1,17},{9,25},{17,1},{25,9},{2,18},{10... | collective-permute-start | bytes 49160 | tf_op jit(solution)/shard_map/ppermute | solution.py:206
  29.0 4.0 %copy-start.1 = (bf16[256,1024]{1,0:T(8,128)(2,1)S(1)}, bf16[256,1024]{1,0:T(8,128)(2,1)}, u32[]{:S(2)}) copy-start(bf16[256,1024]{1,0:T(8,128)(2,1)} %get-tuple-element.49.refs_2_) | copy-start | bytes 1572868
  29.0 4.0 %collective-permute-start.11 = (bf16[4,32,128]{2,1,0:T(8,128)(2,1)S(1)}, bf16[4,32,128]{2,1,0:T(8,128)(2,1)S(1)}, u32[]{:S(2)}, u32[]{:S(2)}) collective-permute-start(bf16[4,32,128]{2,1,0:T(8,128)(2,1)S(1)} %get-tuple-element.48), channel_id=1, source_target_pairs={{0,4},{4,0},{1,5},{5,1},{2,6},{6,2},{3,7},{7,3},{8,12},{12,8},{9,1... | collective-permute-start | bytes 98312 | tf_op jit(solution)/shard_map/ppermute | solution.py:206
  33.5 1.9 %collective-permute-start.13 = (bf16[64,256]{1,0:T(8,128)(2,1)S(1)}, bf16[64,256]{1,0:T(8,128)(2,1)S(1)}, u32[]{:S(2)}, u32[]{:S(2)}) collective-permute-start(bf16[64,256]{1,0:T(8,128)(2,1)S(1)} %get-tuple-element.52), channel_id=1, source_target_pairs={{0,2},{2,0},{1,3},{3,1},{4,6},{6,4},{5,7},{7,5},{8,10},{10,8},{9,1... | collective-permute-start | bytes 98312 | tf_op jit(solution)/shard_map/ppermute | solution.py:206
  33.6 4.0 %collective-permute-start.14 = (bf16[64,256]{1,0:T(8,128)(2,1)S(1)}, bf16[64,256]{1,0:T(8,128)(2,1)S(1)}, u32[]{:S(2)}, u32[]{:S(2)}) collective-permute-start(bf16[64,256]{1,0:T(8,128)(2,1)S(1)} %get-tuple-element.51.refs_2_), channel_id=1, source_target_pairs={{0,1},{1,0},{2,3},{3,2},{4,5},{5,4},{6,7},{7,6},{8,9},{9,8},{10,11... | collective-permute-start | bytes 98312 | tf_op jit(solution)/shard_map/ppermute | solution.py:212
  34.6 3.3 %collective-permute-start.15 = (bf16[64,256]{1,0:T(8,128)(2,1)S(1)}, bf16[64,256]{1,0:T(8,128)(2,1)S(1)}, u32[]{:S(2)}, u32[]{:S(2)}) collective-permute-start(bf16[64,256]{1,0:T(8,128)(2,1)S(1)} %get-tuple-element.52), channel_id=1, source_target_pairs={{0,3},{1,2},{2,1},{3,0},{4,7},{5,6},{6,5},{7,4},{8,11},{9,10},{10,... | collective-permute-start | bytes 98312 | tf_op jit(solution)/shard_map/ppermute | solution.py:212

commit v2 on v1

v2 whole, which is shorter than its diff:
```python
import functools
import math

import jax
import jax.numpy as jnp
from jax import lax
from jax.experimental import pallas as pl
from jax.experimental.pallas import tpu as pltpu
from jax.sharding import PartitionSpec as P

STEP_SIZE = 0.2
LEVEL = 0.5
LANES = 128
VMEM_LIMIT = 32 * 1024 * 1024
FIRST_LIMIT = 55050 * 1024
F32 = jnp.float32
BF16 = jnp.bfloat16


def shifts_of(chips):
    far_first = sorted(range(chips), key=lambda shift: (-shift.bit_count(), -shift))
    return [[far_first[at] for at in range(chips) if (at + 1) // 2 % 2 == core] for core in range(2)]


def place():
    position = lax.axis_index("tile")
    return position // 2, position % 2


def columns_of(tile):
    return pl.ds(pl.multiple_of(tile * LANES, LANES), LANES)


def both_shifts(shifts):
    chip, core = place()
    pairs = list(zip(*shifts))
    own = [chip ^ jnp.where(core == 0, first, second) for first, second in pairs]
    mate = [chip ^ jnp.where(core == 0, second, first) for first, second in pairs]
    return own, mate


def signs(rows):
    lane = lax.broadcasted_iota(jnp.int32, (rows, LANES), 1)
    return jnp.where(lane < LANES // 2, 1.0, -1.0).astype(F32)


def separate(source, wide, target, masks=None):
    rows, columns = target.shape
    tiles = columns // LANES
    wide[...] = source[...].astype(F32)
    for tile in range(tiles):
        part = wide[pl.ds(tile, rows, stride=tiles), :]
        if masks is not None:
            part = jnp.where(masks[tile], part, 0.0)
        target[:, tile * LANES : (tile + 1) * LANES] = part.astype(BF16)


def adjoint_blocks(product, shifts, keep, give):
    half = keep.shape[1]
    for out, tiles in zip((keep, give), both_shifts(shifts)):
        for index, tile in enumerate(tiles):
            real, imaginary = product[:half, columns_of(tile)], product[half:, columns_of(tile)]
            out[index] = (real * signs(half) + pltpu.roll(imaginary, LANES // 2, 1)).astype(BF16)


def spread_blocks(own, mate, shifts, left):
    half = own.shape[1]
    for blocks, tiles in zip((own, mate), both_shifts(shifts)):
        for index, tile in enumerate(tiles):
            block = blocks[index].astype(F32)
            left[:half, columns_of(tile)] = (block * signs(half)).astype(BF16)
            left[half:, columns_of(tile)] = pltpu.roll(block, LANES // 2, 1).astype(BF16)


def times_transposed(left, right):
    return lax.dot_general(left, right, (((1,), (1,)), ((), ())), preferred_element_type=F32)


def forward_kernel(shifts, start, factors, keep, give, start_here, factors_here, wide, separated, product, sems):
    loads = [
        pltpu.make_async_copy(factors, factors_here, sems.at[0]),
        pltpu.make_async_copy(start, start_here, sems.at[1]),
    ]
    for load in loads:
        load.start()
    for load in loads:
        load.wait()
    separate(factors_here, wide, separated)
    values = start_here[...].T.astype(BF16)
    product[...] = jnp.dot(values, separated[...], preferred_element_type=F32)
    adjoint_blocks(product, shifts, keep, give)


def add_kernel(keep, arrived, *outs):
    for index, out in enumerate(outs):
        out[...] = (keep[index].astype(F32) + arrived[index].astype(F32)).astype(BF16)


def pack_kernel(shifts, *refs):
    sent, arrived, packed = refs[0], refs[1:-1], refs[-1]
    _, core = place()
    for index, block in enumerate(arrived):
        values = block[...]
        for side in range(2):
            if shifts[side][index] == 0:
                values = jnp.where(core == side, sent[...], values)
        packed[index] = values


def rows_kernel(ranks, factors, observed, separated, turned, wide):
    chip, _ = place()
    tiles = separated.shape[1] // LANES
    lane = lax.broadcasted_iota(jnp.int32, (1, LANES), 1) % (LANES // 2)
    separate(factors, wide, separated, [lane < ranks[0, chip, tile] for tile in range(tiles)])
    turned[...] = observed[...].T


def columns_kernel(factors, separated, wide):
    separate(factors, wide, separated)


def image_kernel(shifts, own, mate, factors, observed, keep, give, left, product):
    spread_blocks(own, mate, shifts, left)
    misfit = times_transposed(left[...], factors[...]) - observed[...]
    product[...] = jnp.dot(misfit.astype(BF16), factors[...], preferred_element_type=F32)
    adjoint_blocks(product, shifts, keep, give)


def gradient_kernel(shifts, own, mate, factors, gradient, left):
    spread_blocks(own, mate, shifts, left)
    gradient[...] = times_transposed(left[...], factors[...]).astype(BF16)


def thin_out(values):
    return values - jnp.clip(values, -LEVEL, LEVEL)


def shrink_kernel(band, *refs):
    tables, starts, gradients, out = refs[: -2 * band - 1], refs[-2 * band - 1 : -band - 1], refs[-band - 1 : -1], refs[-1]
    estimates = [
        start[...] - STEP_SIZE * gradient[...].astype(F32).T for start, gradient in zip(starts, gradients)
    ]
    scale = 1.0 / math.sqrt(band)
    if band == 2:
        here, there = estimates
        out[...] = (thin_out((here + there) * scale) + thin_out((here - there) * scale)) * scale
        return
    (tables,) = tables
    half = out.shape[1] // 2
    lane = lax.broadcasted_iota(jnp.int32, (1, out.shape[1]), 1)
    turn = jnp.where(lane < half, -1.0, 1.0).astype(F32)
    turned = [pltpu.roll(estimate, half, 1) * turn for estimate in estimates]
    total = jnp.zeros_like(estimates[0])
    for time in range(band):
        sample = jnp.zeros_like(estimates[0])
        for index in range(band):
            sample += tables[0, index, time] * estimates[index] + tables[1, index, time] * turned[index]
        thinned = thin_out(sample * scale)
        total += tables[0, 0, time] * thinned - tables[1, 0, time] * (pltpu.roll(thinned, half, 1) * turn)
    out[...] = total * scale


def call(kernel, name, outs, inputs, scratch=(), flops=0, spaces=(), limit=VMEM_LIMIT):
    spaces = (*spaces, *[pltpu.VMEM] * (len(inputs) - len(spaces)))
    moved = sum(x.size * x.dtype.itemsize for x in [*inputs, *outs])
    return pl.pallas_call(
        kernel,
        out_shape=outs,
        in_specs=[pl.BlockSpec(memory_space=space) for space in spaces],
        out_specs=[pl.BlockSpec(memory_space=pltpu.VMEM)] * len(outs),
        scratch_shapes=scratch,
        compiler_params=pltpu.CompilerParams(vmem_limit_bytes=limit),
        cost_estimate=pl.CostEstimate(flops=flops, bytes_accessed=moved, transcendentals=0),
        name=name,
    )(*inputs)


def to_mate(value):
    return lax.ppermute(value, "tile", [(i, i ^ 1) for i in range(lax.axis_size("tile"))])


def after(value, *others):
    return lax.optimization_barrier((value, *others))[0]


def exchange(keep, give, shifts, beside):
    count = lax.axis_size("tile")
    members = len(shifts[0])
    block = jax.ShapeDtypeStruct(keep.shape[1:], keep.dtype)
    sends = call(add_kernel, "add", [block] * members, [keep, to_mate(give)])
    arrived = []
    for index, send in enumerate(sends):
        partners = [(i, i ^ 2 * shifts[i % 2][index]) for i in range(count)]
        arrived.append(lax.ppermute(send, "tile", [pair for pair in partners if pair[0] != pair[1]]))
    (own_index,) = [index for index in range(members) if 0 in (shifts[0][index], shifts[1][index])]
    arrived[0] = after(arrived[0], *beside)
    (own,) = call(functools.partial(pack_kernel, shifts), "pack", [keep], [sends[own_index], *arrived])
    return own, to_mate(own)


def body(u_factors, v_factors, ranks, observed, start):
    band = lax.axis_size("freq")
    rows, tiles, width = u_factors.shape[1:]
    sources = start.shape[2]
    columns = tiles * width
    left_rows = u_factors.reshape(rows * tiles, width)
    right_rows = v_factors.reshape(rows * tiles, width)
    observed = observed.reshape(rows, sources)
    start = start.reshape(rows, sources)
    shifts = shifts_of(tiles)

    def shape(*dims, dtype=BF16):
        return jax.ShapeDtypeStruct(dims, dtype)

    wide = pltpu.VMEM((rows * tiles, width), F32)
    factor = shape(rows, columns)
    blocks = shape(tiles // 2, sources // 2, width)
    product = pltpu.VMEM((sources, columns), F32)
    spread = pltpu.VMEM((sources, columns), BF16)
    spread_rows = pltpu.VMEM((rows, columns), BF16)
    flops = 2 * rows * columns * sources

    keep, give = call(
        functools.partial(forward_kernel, shifts),
        "forward",
        [blocks, blocks],
        [start, right_rows],
        [
            pltpu.VMEM(start.shape, F32),
            pltpu.VMEM(right_rows.shape, BF16),
            wide,
            spread_rows,
            product,
            pltpu.SemaphoreType.DMA((2,)),
        ],
        flops,
        [pltpu.HBM] * 2,
        FIRST_LIMIT,
    )
    left, turned = call(
        rows_kernel,
        "rows",
        [factor, shape(sources, rows, dtype=F32)],
        [ranks, after(left_rows, give), after(observed, give)],
        [wide],
        spaces=[pltpu.SMEM],
    )
    own, mate = exchange(keep, give, shifts, [left, turned])
    early = after(start, own)
    starts = [start]
    for shift in range(1, band):
        starts.append(lax.ppermute(early, "freq", [(f, (f - shift) % band) for f in range(band)]))
    keep, give = call(
        functools.partial(image_kernel, shifts),
        "image",
        [blocks, blocks],
        [own, mate, left, turned],
        [spread, product],
        2 * flops,
    )
    (right,) = call(columns_kernel, "columns", [factor], [after(right_rows, give)], [wide])
    own, mate = exchange(keep, give, shifts, [right])
    (gradient,) = call(
        functools.partial(gradient_kernel, shifts), "gradient", [shape(sources, rows)], [own, mate, right], [spread], flops
    )
    gradients = [gradient]
    for shift in range(1, band):
        gradients.append(lax.ppermute(gradient, "freq", [(f, (f - shift) % band) for f in range(band)]))
    inputs, spaces = [*starts, *gradients], []
    if band > 2:
        bands = jnp.arange(band, dtype=jnp.int32)
        phases = (bands[:, None] + lax.axis_index("freq")) * bands[None, :] % band
        phases = (2.0 * math.pi / band) * phases.astype(F32)
        inputs, spaces = [jnp.stack([jnp.cos(phases), jnp.sin(phases)]), *inputs], [pltpu.SMEM]
    (estimate,) = call(
        functools.partial(shrink_kernel, band), "shrink", [shape(rows, sources, dtype=F32)], inputs, spaces=spaces
    )
    return estimate[None]


def solution(mesh):
    in_specs = (
        P("freq", "tile", None, None),
        P("freq", "tile", None, None),
        P("freq", None, None),
        P("freq", "tile", None),
        P("freq", "tile", None),
    )
    out_specs = P("freq", "tile", None)
    return jax.shard_map(body, mesh=mesh, in_specs=in_specs, out_specs=out_specs, check_vma=False)
```

time: 39 us -> 34 us (0.87)
  starting transfers between devices: 20.4 us -> 17.2 us
  Pallas kernels: 6.52 us -> 5.07 us
  waiting for transfers between devices: 11.8 us -> 11.3 us
    ppermute x16 -> x14, starting transfers between devices: 20.4 us -> 17.2 us  [the longest x8 13.2 us: exchange(): lax.ppermute(send, 'tile', [pair for pair in partners if pair[0] != pair[...]
    pallas_call x9 -> x10, Pallas kernels: 6.52 us -> 5.07 us  [call(): pl.pallas_call(kernel, out_shape=outs, in_specs=[pl.BlockSpec(memory_spac...]
    ppermute x16 -> x14, waiting for transfers between devices: 11.8 us -> 11.3 us  [the longest x8 4.13 us: exchange(): lax.ppermute(send, 'tile', [pair for pair in partners if pair[0] != pair[...]
  transfers between devices with their start and end apart: 16 -> 14, of which waited for: 8 -> 9; matrix products, arithmetic and copies ran while one was open for 0% -> 0% of each run, Pallas kernels for 9% -> 5%
where the time goes in v2:
time: 34 us; the launch traced here: 33.8 us
  starting transfers between devices  17.2 us (51%)
  waiting for transfers between devices  11.3 us (33%)
  Pallas kernels  5.07 us (15%)
    ppermute x8, starting transfers between devices, exchange(): lax.ppermute(send, 'tile', [pair for pair in partners if pair[0] != pair[...  13.2 us
    pallas_call x10, Pallas kernels, call(): pl.pallas_call(kernel, out_shape=outs, in_specs=[pl.BlockSpec(memory_spac...  5.07 us
    ppermute x8, waiting for transfers between devices, exchange(): lax.ppermute(send, 'tile', [pair for pair in partners if pair[0] != pair[...  4.13 us
    ppermute x1, waiting for transfers between devices, body(): lax.ppermute(early, 'freq', [(f, (f - shift) % band) for f in range(band)])  3.33 us
    ppermute x4, waiting for transfers between devices, to_mate(): lax.ppermute(value, 'tile', [(i, i ^ 1) for i in range(lax.axis_size('til...  3.15 us
    ppermute x1, starting transfers between devices, body(): lax.ppermute(early, 'freq', [(f, (f - shift) % band) for f in range(band)])  1.52 us
    ppermute x4, starting transfers between devices, to_mate(): lax.ppermute(value, 'tile', [(i, i ^ 1) for i in range(lax.axis_size('til...  1.49 us
    ppermute x1, starting transfers between devices, body(): lax.ppermute(gradient, 'freq', [(f, (f - shift) % band) for f in range(ba...  0.97 us
  transfers between devices with their start and end apart: 14, of which 9 were waited for; matrix products, arithmetic and copies ran while one was open for 0% of the time, Pallas kernels for 5%

profile of v2, /device:TPU:0, one launch (start us, length us, event | category | flops | bytes accessed | tf_op | source)
XLA Modules:
  0.0 33.8 jit_solution(15664728664009231731)
XLA Ops:
  0.0 1.8 %forward.1 = (bf16[4,64,128]{2,1,0:T(8,128)(2,1)S(1)}, bf16[4,64,128]{2,1,0:T(8,128)(2,1)S(1)}) custom-call(f32[256,128]{1,0:T(8,128)} %bitcast.8, bf16[2048,128]{1,0:T(8,128)(2,1)} %bitcast.5), custom_call_target="tpu_custom_call" | custom-call | flops 67108864 | bytes 786432 | tf_op jit(solution)/shard_map/forward/pallas_call | solution.py:166
  1.8 0.0 copy-start.3
  1.8 0.5 %collective-permute-start = (bf16[4,64,128]{2,1,0:T(8,128)(2,1)S(1)}, bf16[4,64,128]{2,1,0:T(8,128)(2,1)S(1)}, u32[]{:S(2)}, u32[]{:S(2)}) collective-permute-start(bf16[4,64,128]{2,1,0:T(8,128)(2,1)S(1)} %get-tuple-element.26), channel_id=1, source_target_pairs={{0,2},{2,0},{4,6},{6,4},{8,10},{10,8},{12,14},{14,12},{16,18},{18,... | collective-permute-start | bytes 196616 | tf_op jit(solution)/shard_map/ppermute | solution.py:179
  2.3 0.9 %collective-permute-done.arrived = bf16[4,64,128]{2,1,0:T(8,128)(2,1)S(1)} collective-permute-done((bf16[4,64,128]{2,1,0:T(8,128)(2,1)S(1)}, bf16[4,64,128]{2,1,0:T(8,128)(2,1)S(1)}, u32[]{:S(2)}, u32[]{:S(2)}) %collective-permute-start) | collective-permute-done | bytes 65568 | tf_op jit(solution)/shard_map/ppermute | solution.py:179
  3.3 5.9 %collective-permute-start.1 = (bf16[64,128]{1,0:T(8,128)(2,1)S(1)}, bf16[64,128]{1,0:T(8,128)(2,1)S(1)}, u32[]{:S(2)}, u32[]{:S(2)}) collective-permute-start(bf16[64,128]{1,0:T(8,128)(2,1)S(1)} %get-tuple-element.28), channel_id=1, source_target_pairs={{0,28},{2,26},{4,24},{6,30},{8,20},{10,18},{12,16},{14,22},{16,12}... | collective-permute-start | bytes 49160 | tf_op jit(solution)/shard_map/ppermute | solution.py:194
  9.2 0.0 collective-permute-start.2
  9.2 0.6 %collective-permute-start.3 = (bf16[64,128]{1,0:T(8,128)(2,1)S(1)}, bf16[64,128]{1,0:T(8,128)(2,1)S(1)}, u32[]{:S(2)}, u32[]{:S(2)}) collective-permute-start(bf16[64,128]{1,0:T(8,128)(2,1)S(1)} %get-tuple-element.35), channel_id=1, source_target_pairs={{0,16},{2,10},{4,20},{6,14},{8,24},{10,2},{12,28},{14,6},{16,0},{1... | collective-permute-start | bytes 49160 | tf_op jit(solution)/shard_map/ppermute | solution.py:194
  9.9 0.7 %collective-permute-start.4 = (bf16[64,128]{1,0:T(8,128)(2,1)S(1)}, bf16[64,128]{1,0:T(8,128)(2,1)S(1)}, u32[]{:S(2)}, u32[]{:S(2)}) collective-permute-start(bf16[64,128]{1,0:T(8,128)(2,1)S(1)} %get-tuple-element.27.refs_0_), channel_id=1, source_target_pairs={{2,6},{6,2},{10,14},{14,10},{18,22},{22,18},{26,30},{30,26},{3,7},... | collective-permute-start | bytes 49160 | tf_op jit(solution)/shard_map/ppermute | solution.py:194
  10.5 1.0 %rows.1 = (bf16[256,1024]{1,0:T(8,128)(2,1)S(1)}, f32[128,256]{1,0:T(8,128)S(1)}) custom-call(s32[1,8,8]{2,1,0:T(8,128)S(1)} %copy-done.4, bf16[2048,128]{1,0:T(8,128)(2,1)S(1)} %bitcast.7, f32[256,128]{1,0:T(8,128)S(1)} %bitcast.11), custom_call_target="tpu_custom_call" | custom-call | bytes 1310976 | tf_op jit(solution)/shard_map/rows/pallas_call | solution.py:166
  11.5 0.0 copy-start
  11.6 2.3 %collective-permute-done.2.refs_2_ = bf16[64,128]{1,0:T(8,128)(2,1)S(1)} collective-permute-done((bf16[64,128]{1,0:T(8,128)(2,1)S(1)}, bf16[64,128]{1,0:T(8,128)(2,1)S(1)}, u32[]{:S(2)}, u32[]{:S(2)}) %collective-permute-start.2) | collective-permute-done | bytes 16416 | tf_op jit(solution)/shard_map/ppermute | solution.py:194
  13.9 0.2 collective-permute-start.6
  14.0 1.2 %collective-permute-done.6.mate = bf16[4,64,128]{2,1,0:T(8,128)(2,1)S(1)} collective-permute-done((bf16[4,64,128]{2,1,0:T(8,128)(2,1)S(1)}, bf16[4,64,128]{2,1,0:T(8,128)(2,1)S(1)}, u32[]{:S(2)}, u32[]{:S(2)}) %collective-permute-start.6) | collective-permute-done | bytes 65568 | tf_op jit(solution)/shard_map/ppermute | solution.py:179
  15.2 0.8 %image.1 = (bf16[4,64,128]{2,1,0:T(8,128)(2,1)S(1)}, bf16[4,64,128]{2,1,0:T(8,128)(2,1)S(1)}) custom-call(bf16[4,64,128]{2,1,0:T(8,128)(2,1)S(1)} %pack.2.own, bf16[4,64,128]{2,1,0:T(8,128)(2,1)S(1)} %collective-permute-done.6.mate, bf16[256,1024]{1,0:T(8,128)(2,1)S(1)} %get-tuple-element.31.factors, f32[128,256]{1,0:T(8,128)S(1)} %get-tuple-element.32.observed), custom_call_target="tpu_custom_call" | custom-call | flops 134217728 | bytes 917504 | tf_op jit(solution)/shard_map/image/pallas_call | solution.py:166
  16.0 0.2 collective-permute-start.7
  16.2 1.1 %collective-permute-done.7.arrived = bf16[4,64,128]{2,1,0:T(8,128)(2,1)S(1)} collective-permute-done((bf16[4,64,128]{2,1,0:T(8,128)(2,1)S(1)}, bf16[4,64,128]{2,1,0:T(8,128)(2,1)S(1)}, u32[]{:S(2)}, u32[]{:S(2)}) %collective-permute-start.7) | collective-permute-done | bytes 65568 | tf_op jit(solution)/shard_map/ppermute | solution.py:179
  17.3 3.2 %collective-permute-start.8 = (bf16[64,128]{1,0:T(8,128)(2,1)S(1)}, bf16[64,128]{1,0:T(8,128)(2,1)S(1)}, u32[]{:S(2)}, u32[]{:S(2)}) collective-permute-start(bf16[64,128]{1,0:T(8,128)(2,1)S(1)} %get-tuple-element.40), channel_id=1, source_target_pairs={{0,28},{2,26},{4,24},{6,30},{8,20},{10,18},{12,16},{14,22},{16,12}... | collective-permute-start | bytes 49160 | tf_op jit(solution)/shard_map/ppermute | solution.py:194
  20.5 0.3 collective-permute-start.9
  20.8 1.8 %collective-permute-start.10 = (bf16[64,128]{1,0:T(8,128)(2,1)S(1)}, bf16[64,128]{1,0:T(8,128)(2,1)S(1)}, u32[]{:S(2)}, u32[]{:S(2)}) collective-permute-start(bf16[64,128]{1,0:T(8,128)(2,1)S(1)} %get-tuple-element.44), channel_id=1, source_target_pairs={{0,16},{2,10},{4,20},{6,14},{8,24},{10,2},{12,28},{14,6},{16,0},{1... | collective-permute-start | bytes 49160 | tf_op jit(solution)/shard_map/ppermute | solution.py:194
  22.7 0.7 %collective-permute-start.11 = (bf16[64,128]{1,0:T(8,128)(2,1)S(1)}, bf16[64,128]{1,0:T(8,128)(2,1)S(1)}, u32[]{:S(2)}, u32[]{:S(2)}) collective-permute-start(bf16[64,128]{1,0:T(8,128)(2,1)S(1)} %get-tuple-element.39.refs_0_), channel_id=1, source_target_pairs={{2,6},{6,2},{10,14},{14,10},{18,22},{22,18},{26,30},{30,26},{3,7},... | collective-permute-start | bytes 49160 | tf_op jit(solution)/shard_map/ppermute | solution.py:194
  23.4 0.3 columns.1.factors
  23.6 0.0 copy-start.2
  23.6 0.2 collective-permute-done.8.refs_1_
  23.8 1.5 %collective-permute-done.9.refs_2_ = bf16[64,128]{1,0:T(8,128)(2,1)S(1)} collective-permute-done((bf16[64,128]{1,0:T(8,128)(2,1)S(1)}, bf16[64,128]{1,0:T(8,128)(2,1)S(1)}, u32[]{:S(2)}, u32[]{:S(2)}) %collective-permute-start.9) | collective-permute-done | bytes 16416 | tf_op jit(solution)/shard_map/ppermute | solution.py:194
  25.4 0.1 collective-permute-done.10.refs_3_
  25.5 0.6 %collective-permute-start.12 = (bf16[4,64,128]{2,1,0:T(8,128)(2,1)S(1)}, bf16[4,64,128]{2,1,0:T(8,128)(2,1)S(1)}, u32[]{:S(2)}, u32[]{:S(2)}) collective-permute-start(bf16[4,64,128]{2,1,0:T(8,128)(2,1)S(1)} %pack.3.own), channel_id=1, source_target_pairs={{0,2},{2,0},{4,6},{6,4},{8,10},{10,8},{12,14},{14,12},{16,18},{18,... | collective-permute-start | bytes 196616 | tf_op jit(solution)/shard_map/ppermute | solution.py:179
  26.1 1.5 %collective-permute-start.5 = (f32[256,128]{1,0:T(8,128)S(1)}, f32[256,128]{1,0:T(8,128)S(1)}, u32[]{:S(2)}, u32[]{:S(2)}) collective-permute-start(f32[256,128]{1,0:T(8,128)S(1)} %bitcast.9), channel_id=1, source_target_pairs={{0,1},{1,0},{2,3},{3,2},{4,5},{5,4},{6,7},{7,6},{8,9},{9,8},{10,11... | collective-permute-start | bytes 393224 | tf_op jit(solution)/shard_map/ppermute | solution.py:252
  27.6 0.4 %gradient.1.refs_2_ = bf16[128,256]{1,0:T(8,128)(2,1)S(1)} custom-call(bf16[4,64,128]{2,1,0:T(8,128)(2,1)S(1)} %pack.3.own, bf16[4,64,128]{2,1,0:T(8,128)(2,1)S(1)} %collective-permute-done.12.mate, bf16[256,1024]{1,0:T(8,128)(2,1)S(1)} %columns.1.factors), custom_call_target="tpu_custom_call" | custom-call | flops 67108864 | bytes 720896 | tf_op jit(solution)/shard_map/gradient/pallas_call | solution.py:166
  28.0 1.0 %collective-permute-start.13 = (bf16[128,256]{1,0:T(8,128)(2,1)S(1)}, bf16[128,256]{1,0:T(8,128)(2,1)S(1)}, u32[]{:S(2)}, u32[]{:S(2)}) collective-permute-start(bf16[128,256]{1,0:T(8,128)(2,1)S(1)} %gradient.1.refs_2_), channel_id=1, source_target_pairs={{0,1},{1,0},{2,3},{3,2},{4,5},{5,4},{6,7},{7,6},{8,9},{9,8},{10,11... | collective-permute-start | bytes 196616 | tf_op jit(solution)/shard_map/ppermute | solution.py:268
  29.0 3.3 %collective-permute-done.5.refs_1_ = f32[256,128]{1,0:T(8,128)S(1)} collective-permute-done((f32[256,128]{1,0:T(8,128)S(1)}, f32[256,128]{1,0:T(8,128)S(1)}, u32[]{:S(2)}, u32[]{:S(2)}) %collective-permute-start.5) | collective-permute-done | bytes 131104 | tf_op jit(solution)/shard_map/ppermute | solution.py:252
  32.3 0.7 %collective-permute-done.13.refs_3_ = bf16[128,256]{1,0:T(8,128)(2,1)S(1)} collective-permute-done((bf16[128,256]{1,0:T(8,128)(2,1)S(1)}, bf16[128,256]{1,0:T(8,128)(2,1)S(1)}, u32[]{:S(2)}, u32[]{:S(2)}) %collective-permute-start.13) | collective-permute-done | bytes 65568 | tf_op jit(solution)/shard_map/ppermute | solution.py:268
  33.0 0.8 %shrink.1 = f32[256,128]{1,0:T(8,128)} custom-call(f32[256,128]{1,0:T(8,128)S(1)} %bitcast.10, f32[256,128]{1,0:T(8,128)S(1)} %collective-permute-done.5.refs_1_, bf16[128,256]{1,0:T(8,128)(2,1)S(1)} %gradient.1.refs_2_, bf16[128,256]{1,0:T(8,128)(2,1)S(1)} %collective-permute-done.13.refs_3_), custom_call_target="tpu_custom_call" | custom-call | bytes 524288 | tf_op jit(solution)/shard_map/shrink/pallas_call | solution.py:166
  (16 shorter events, 0.1 us)
Async XLA Ops:
  0.0 10.5 %copy-start.1 = (bf16[1,256,8,128]{3,2,1,0:T(8,128)(2,1)S(1)}, bf16[1,256,8,128]{3,2,1,0:T(8,128)(2,1)}, u32[]{:S(2)}) copy-start(bf16[1,256,8,128]{3,2,1,0:T(8,128)(2,1)} %param.5) | copy-start | bytes 1572868
  1.8 8.7 %copy-start.3 = (f32[1,256,128]{2,1,0:T(8,128)S(1)}, f32[1,256,128]{2,1,0:T(8,128)}, u32[]{:S(2)}) copy-start(f32[1,256,128]{2,1,0:T(8,128)} %param.8) | copy-start | bytes 393220
  1.8 1.4 %collective-permute-start = (bf16[4,64,128]{2,1,0:T(8,128)(2,1)S(1)}, bf16[4,64,128]{2,1,0:T(8,128)(2,1)S(1)}, u32[]{:S(2)}, u32[]{:S(2)}) collective-permute-start(bf16[4,64,128]{2,1,0:T(8,128)(2,1)S(1)} %get-tuple-element.26), channel_id=1, source_target_pairs={{0,2},{2,0},{4,6},{6,4},{8,10},{10,8},{12,14},{14,12},{16,18},{18,... | collective-permute-start | bytes 196616 | tf_op jit(solution)/shard_map/ppermute | solution.py:179
  3.3 8.3 %collective-permute-start.1 = (bf16[64,128]{1,0:T(8,128)(2,1)S(1)}, bf16[64,128]{1,0:T(8,128)(2,1)S(1)}, u32[]{:S(2)}, u32[]{:S(2)}) collective-permute-start(bf16[64,128]{1,0:T(8,128)(2,1)S(1)} %get-tuple-element.28), channel_id=1, source_target_pairs={{0,28},{2,26},{4,24},{6,30},{8,20},{10,18},{12,16},{14,22},{16,12}... | collective-permute-start | bytes 49160 | tf_op jit(solution)/shard_map/ppermute | solution.py:194
  9.2 1.3 %copy-start.4 = (s32[1,8,8]{2,1,0:T(8,128)S(1)}, s32[1,8,8]{2,1,0:T(8,128)}, u32[]{:S(2)}) copy-start(s32[1,8,8]{2,1,0:T(8,128)} %ranks.1) | copy-start | bytes 772
  9.2 4.6 %collective-permute-start.2 = (bf16[64,128]{1,0:T(8,128)(2,1)S(1)}, bf16[64,128]{1,0:T(8,128)(2,1)S(1)}, u32[]{:S(2)}, u32[]{:S(2)}) collective-permute-start(bf16[64,128]{1,0:T(8,128)(2,1)S(1)} %get-tuple-element.34), channel_id=1, source_target_pairs={{0,12},{2,22},{4,8},{6,18},{8,4},{10,30},{12,0},{14,26},{16,28},{1... | collective-permute-start | bytes 49160 | tf_op jit(solution)/shard_map/ppermute | solution.py:194
  9.2 4.6 %collective-permute-start.3 = (bf16[64,128]{1,0:T(8,128)(2,1)S(1)}, bf16[64,128]{1,0:T(8,128)(2,1)S(1)}, u32[]{:S(2)}, u32[]{:S(2)}) collective-permute-start(bf16[64,128]{1,0:T(8,128)(2,1)S(1)} %get-tuple-element.35), channel_id=1, source_target_pairs={{0,16},{2,10},{4,20},{6,14},{8,24},{10,2},{12,28},{14,6},{16,0},{1... | collective-permute-start | bytes 49160 | tf_op jit(solution)/shard_map/ppermute | solution.py:194
  9.9 4.0 %collective-permute-start.4 = (bf16[64,128]{1,0:T(8,128)(2,1)S(1)}, bf16[64,128]{1,0:T(8,128)(2,1)S(1)}, u32[]{:S(2)}, u32[]{:S(2)}) collective-permute-start(bf16[64,128]{1,0:T(8,128)(2,1)S(1)} %get-tuple-element.27.refs_0_), channel_id=1, source_target_pairs={{2,6},{6,2},{10,14},{14,10},{18,22},{22,18},{26,30},{30,26},{3,7},... | collective-permute-start | bytes 49160 | tf_op jit(solution)/shard_map/ppermute | solution.py:194
  11.5 11.8 %copy-start = (bf16[1,256,8,128]{3,2,1,0:T(8,128)(2,1)S(1)}, bf16[1,256,8,128]{3,2,1,0:T(8,128)(2,1)}, u32[]{:S(2)}) copy-start(bf16[1,256,8,128]{3,2,1,0:T(8,128)(2,1)} %param.6) | copy-start | bytes 1572868
  13.9 1.3 %collective-permute-start.6 = (bf16[4,64,128]{2,1,0:T(8,128)(2,1)S(1)}, bf16[4,64,128]{2,1,0:T(8,128)(2,1)S(1)}, u32[]{:S(2)}, u32[]{:S(2)}) collective-permute-start(bf16[4,64,128]{2,1,0:T(8,128)(2,1)S(1)} %pack.2.own), channel_id=1, source_target_pairs={{0,2},{2,0},{4,6},{6,4},{8,10},{10,8},{12,14},{14,12},{16,18},{18,... | collective-permute-start | bytes 196616 | tf_op jit(solution)/shard_map/ppermute | solution.py:179
  16.0 1.3 %collective-permute-start.7 = (bf16[4,64,128]{2,1,0:T(8,128)(2,1)S(1)}, bf16[4,64,128]{2,1,0:T(8,128)(2,1)S(1)}, u32[]{:S(2)}, u32[]{:S(2)}) collective-permute-start(bf16[4,64,128]{2,1,0:T(8,128)(2,1)S(1)} %get-tuple-element.38), channel_id=1, source_target_pairs={{0,2},{2,0},{4,6},{6,4},{8,10},{10,8},{12,14},{14,12},{16,18},{18,... | collective-permute-start | bytes 196616 | tf_op jit(solution)/shard_map/ppermute | solution.py:179
  17.3 6.5 %collective-permute-start.8 = (bf16[64,128]{1,0:T(8,128)(2,1)S(1)}, bf16[64,128]{1,0:T(8,128)(2,1)S(1)}, u32[]{:S(2)}, u32[]{:S(2)}) collective-permute-start(bf16[64,128]{1,0:T(8,128)(2,1)S(1)} %get-tuple-element.40), channel_id=1, source_target_pairs={{0,28},{2,26},{4,24},{6,30},{8,20},{10,18},{12,16},{14,22},{16,12}... | collective-permute-start | bytes 49160 | tf_op jit(solution)/shard_map/ppermute | solution.py:194
  20.5 4.8 %collective-permute-start.9 = (bf16[64,128]{1,0:T(8,128)(2,1)S(1)}, bf16[64,128]{1,0:T(8,128)(2,1)S(1)}, u32[]{:S(2)}, u32[]{:S(2)}) collective-permute-start(bf16[64,128]{1,0:T(8,128)(2,1)S(1)} %get-tuple-element.43), channel_id=1, source_target_pairs={{0,12},{2,22},{4,8},{6,18},{8,4},{10,30},{12,0},{14,26},{16,28},{1... | collective-permute-start | bytes 49160 | tf_op jit(solution)/shard_map/ppermute | solution.py:194
  20.8 4.6 %collective-permute-start.10 = (bf16[64,128]{1,0:T(8,128)(2,1)S(1)}, bf16[64,128]{1,0:T(8,128)(2,1)S(1)}, u32[]{:S(2)}, u32[]{:S(2)}) collective-permute-start(bf16[64,128]{1,0:T(8,128)(2,1)S(1)} %get-tuple-element.44), channel_id=1, source_target_pairs={{0,16},{2,10},{4,20},{6,14},{8,24},{10,2},{12,28},{14,6},{16,0},{1... | collective-permute-start | bytes 49160 | tf_op jit(solution)/shard_map/ppermute | solution.py:194
  22.7 2.8 %collective-permute-start.11 = (bf16[64,128]{1,0:T(8,128)(2,1)S(1)}, bf16[64,128]{1,0:T(8,128)(2,1)S(1)}, u32[]{:S(2)}, u32[]{:S(2)}) collective-permute-start(bf16[64,128]{1,0:T(8,128)(2,1)S(1)} %get-tuple-element.39.refs_0_), channel_id=1, source_target_pairs={{2,6},{6,2},{10,14},{14,10},{18,22},{22,18},{26,30},{30,26},{3,7},... | collective-permute-start | bytes 49160 | tf_op jit(solution)/shard_map/ppermute | solution.py:194
  23.6 2.5 %copy-start.2 = (f32[1,256,128]{2,1,0:T(8,128)S(1)}, f32[1,256,128]{2,1,0:T(8,128)}, u32[]{:S(2)}) copy-start(f32[1,256,128]{2,1,0:T(8,128)} %param.9) | copy-start | bytes 393220
  25.5 2.1 %collective-permute-start.12 = (bf16[4,64,128]{2,1,0:T(8,128)(2,1)S(1)}, bf16[4,64,128]{2,1,0:T(8,128)(2,1)S(1)}, u32[]{:S(2)}, u32[]{:S(2)}) collective-permute-start(bf16[4,64,128]{2,1,0:T(8,128)(2,1)S(1)} %pack.3.own), channel_id=1, source_target_pairs={{0,2},{2,0},{4,6},{6,4},{8,10},{10,8},{12,14},{14,12},{16,18},{18,... | collective-permute-start | bytes 196616 | tf_op jit(solution)/shard_map/ppermute | solution.py:179
  26.1 6.2 %collective-permute-start.5 = (f32[256,128]{1,0:T(8,128)S(1)}, f32[256,128]{1,0:T(8,128)S(1)}, u32[]{:S(2)}, u32[]{:S(2)}) collective-permute-start(f32[256,128]{1,0:T(8,128)S(1)} %bitcast.9), channel_id=1, source_target_pairs={{0,1},{1,0},{2,3},{3,2},{4,5},{5,4},{6,7},{7,6},{8,9},{9,8},{10,11... | collective-permute-start | bytes 393224 | tf_op jit(solution)/shard_map/ppermute | solution.py:252
  28.0 5.0 %collective-permute-start.13 = (bf16[128,256]{1,0:T(8,128)(2,1)S(1)}, bf16[128,256]{1,0:T(8,128)(2,1)S(1)}, u32[]{:S(2)}, u32[]{:S(2)}) collective-permute-start(bf16[128,256]{1,0:T(8,128)(2,1)S(1)} %gradient.1.refs_2_), channel_id=1, source_target_pairs={{0,1},{1,0},{2,3},{3,2},{4,5},{5,4},{6,7},{7,6},{8,9},{9,8},{10,11... | collective-permute-start | bytes 196616 | tf_op jit(solution)/shard_map/ppermute | solution.py:268

commit v3 on v2

--- a/solution.py
+++ b/solution.py
@@ -13,6 +13,7 @@
 LANES = 128
 VMEM_LIMIT = 32 * 1024 * 1024
 FIRST_LIMIT = 55050 * 1024
+PIECES = 4
 F32 = jnp.float32
 BF16 = jnp.bfloat16
 
@@ -44,32 +45,37 @@
     return jnp.where(lane < LANES // 2, 1.0, -1.0).astype(F32)
 
 
-def separate(source, wide, target, masks=None):
-    rows, columns = target.shape
-    tiles = columns // LANES
+def separate(source, wide, target, chosen, masks=None):
+    rows = target.shape[0]
+    tiles = source.shape[0] // rows
     wide[...] = source[...].astype(F32)
-    for tile in range(tiles):
+    for index, tile in enumerate(chosen):
         part = wide[pl.ds(tile, rows, stride=tiles), :]
         if masks is not None:
-            part = jnp.where(masks[tile], part, 0.0)
-        target[:, tile * LANES : (tile + 1) * LANES] = part.astype(BF16)
-
-
-def adjoint_blocks(product, shifts, keep, give):
-    half = keep.shape[1]
-    for out, tiles in zip((keep, give), both_shifts(shifts)):
-        for index, tile in enumerate(tiles):
-            real, imaginary = product[:half, columns_of(tile)], product[half:, columns_of(tile)]
-            out[index] = (real * signs(half) + pltpu.roll(imaginary, LANES // 2, 1)).astype(BF16)
-
-
-def spread_blocks(own, mate, shifts, left):
-    half = own.shape[1]
-    for blocks, tiles in zip((own, mate), both_shifts(shifts)):
-        for index, tile in enumerate(tiles):
-            block = blocks[index].astype(F32)
-            left[:half, columns_of(tile)] = (block * signs(half)).astype(BF16)
-            left[half:, columns_of(tile)] = pltpu.roll(block, LANES // 2, 1).astype(BF16)
+            part = jnp.where(masks[index], part, 0.0)
+        target[:, index * LANES : (index + 1) * LANES] = part.astype(BF16)
+
+
+def adjoint_block(product, tile):
+    half = product.shape[0] // 2
+    real, imaginary = product[:half, columns_of(tile)], product[half:, columns_of(tile)]
+    return (real * signs(half) + pltpu.roll(imaginary, LANES // 2, 1)).astype(BF16)
+
+
+def spread_block(block, left, tile):
+    half = block.shape[0]
+    block = block.astype(F32)
+    left[:half, columns_of(tile)] = (block * signs(half)).astype(BF16)
+    left[half:, columns_of(tile)] = pltpu.roll(block, LANES // 2, 1).astype(BF16)
+
+
+def arrived_block(shifts, index, sent, arrived):
+    _, core = place()
+    values = arrived[...]
+    for side in range(2):
+        if shifts[side][index] == 0:
+            values = jnp.where(core == side, sent[...], values)
+    return values
 
 
 def times_transposed(left, right):
@@ -77,18 +83,28 @@
 
 
 def forward_kernel(shifts, start, factors, keep, give, start_here, factors_here, wide, separated, product, sems):
-    loads = [
-        pltpu.make_async_copy(factors, factors_here, sems.at[0]),
-        pltpu.make_async_copy(start, start_here, sems.at[1]),
-    ]
-    for load in loads:
-        load.start()
-    for load in loads:
+    pieces = sems.shape[0] - 1
+    rows, columns = separated.shape
+    tiles = columns // LANES
+    load_start = pltpu.make_async_copy(start, start_here, sems.at[pieces])
+    load_start.start()
+    loads = []
+    for piece in range(pieces):
+        at = pl.ds(piece * (rows * tiles // pieces), rows * tiles // pieces)
+        loads.append(pltpu.make_async_copy(factors.at[at], factors_here.at[at], sems.at[piece]))
+        loads[-1].start()
+    load_start.wait()
+    values = start_here[...].T.astype(BF16)
+    for piece, load in enumerate(loads):
+        at = pl.ds(piece * (rows * tiles // pieces), rows * tiles // pieces)
         load.wait()
-    separate(factors_here, wide, separated)
-    values = start_here[...].T.astype(BF16)
+        separate(
+            factors_here.at[at], wide.at[at], separated.at[pl.ds(piece * (rows // pieces), rows // pieces)], range(tiles)
+        )
     product[...] = jnp.dot(values, separated[...], preferred_element_type=F32)
-    adjoint_blocks(product, shifts, keep, give)
+    for out, chosen in zip((keep, give), both_shifts(shifts)):
+        for index, tile in enumerate(chosen):
+            out[index] = adjoint_block(product, tile)
 
 
 def add_kernel(keep, arrived, *outs):
@@ -96,38 +112,48 @@
         out[...] = (keep[index].astype(F32) + arrived[index].astype(F32)).astype(BF16)
 
 
-def pack_kernel(shifts, *refs):
-    sent, arrived, packed = refs[0], refs[1:-1], refs[-1]
-    _, core = place()
+def rows_kernel(shifts, ranks, own, mate, observed, own_out, mate_out, turned, wide):
+    chip, _ = place()
+    chosen, _ = both_shifts(shifts)
+    lane = lax.broadcasted_iota(jnp.int32, (1, LANES), 1) % (LANES // 2)
+    masks = [lane < ranks[0, chip, tile] for tile in chosen]
+    separate(own, wide, own_out, chosen, masks)
+    separate(mate, wide, mate_out, chosen, masks)
+    turned[...] = observed[...].T
+
+
+def columns_kernel(factors, separated, wide):
+    separate(factors, wide, separated, range(separated.shape[1] // LANES))
+
+
+def image_kernel(shifts, sent, *refs):
+    arrived, (own, mate, observed, misfit, left) = refs[:-5], refs[-5:]
     for index, block in enumerate(arrived):
-        values = block[...]
-        for side in range(2):
-            if shifts[side][index] == 0:
-                values = jnp.where(core == side, sent[...], values)
-        packed[index] = values
-
-
-def rows_kernel(ranks, factors, observed, separated, turned, wide):
-    chip, _ = place()
-    tiles = separated.shape[1] // LANES
-    lane = lax.broadcasted_iota(jnp.int32, (1, LANES), 1) % (LANES // 2)
-    separate(factors, wide, separated, [lane < ranks[0, chip, tile] for tile in range(tiles)])
-    turned[...] = observed[...].T
-
-
-def columns_kernel(factors, separated, wide):
-    separate(factors, wide, separated)
-
-
-def image_kernel(shifts, own, mate, factors, observed, keep, give, left, product):
-    spread_blocks(own, mate, shifts, left)
-    misfit = times_transposed(left[...], factors[...]) - observed[...]
-    product[...] = jnp.dot(misfit.astype(BF16), factors[...], preferred_element_type=F32)
-    adjoint_blocks(product, shifts, keep, give)
+        spread_block(arrived_block(shifts, index, sent, block), left, index)
+    misfit[0] = times_transposed(left[...], own[...]) - observed[...]
+    misfit[1] = times_transposed(left[...], mate[...])
+
+
+def back_kernel(here, there, own, mate, *refs):
+    outs, products = refs[:-1], refs[-1]
+    for rows, factors in ((0, own), (1, mate)):
+        misfit = (here[rows] + there[1 - rows]).astype(BF16)
+        products[rows] = jnp.dot(misfit, factors[...], preferred_element_type=F32)
+    for index, out in enumerate(outs):
+        parts = [adjoint_block(products.at[rows], index).astype(F32) for rows in range(2)]
+        out[...] = (parts[0] + parts[1]).astype(BF16)
+
+
+def pack_kernel(shifts, sent, *refs):
+    arrived, packed = refs[:-1], refs[-1]
+    for index, block in enumerate(arrived):
+        packed[index] = arrived_block(shifts, index, sent, block)
 
 
 def gradient_kernel(shifts, own, mate, factors, gradient, left):
-    spread_blocks(own, mate, shifts, left)
+    for blocks, chosen in zip((own, mate), both_shifts(shifts)):
+        for index, tile in enumerate(chosen):
+            spread_block(blocks[index], left, tile)
     gradient[...] = times_transposed(left[...], factors[...]).astype(BF16)
 
 
@@ -183,19 +209,15 @@
     return lax.optimization_barrier((value, *others))[0]
 
 
-def exchange(keep, give, shifts, beside):
+def exchange(sends, shifts, beside):
     count = lax.axis_size("tile")
-    members = len(shifts[0])
-    block = jax.ShapeDtypeStruct(keep.shape[1:], keep.dtype)
-    sends = call(add_kernel, "add", [block] * members, [keep, to_mate(give)])
     arrived = []
     for index, send in enumerate(sends):
         partners = [(i, i ^ 2 * shifts[i % 2][index]) for i in range(count)]
         arrived.append(lax.ppermute(send, "tile", [pair for pair in partners if pair[0] != pair[1]]))
-    (own_index,) = [index for index in range(members) if 0 in (shifts[0][index], shifts[1][index])]
     arrived[0] = after(arrived[0], *beside)
-    (own,) = call(functools.partial(pack_kernel, shifts), "pack", [keep], [sends[own_index], *arrived])
-    return own, to_mate(own)
+    (own,) = [send for index, send in enumerate(sends) if 0 in (shifts[0][index], shifts[1][index])]
+    return [own, *arrived]
 
 
 def body(u_factors, v_factors, ranks, observed, start):
@@ -212,12 +234,12 @@
     def shape(*dims, dtype=BF16):
         return jax.ShapeDtypeStruct(dims, dtype)
 
+    members = tiles // 2
     wide = pltpu.VMEM((rows * tiles, width), F32)
-    factor = shape(rows, columns)
-    blocks = shape(tiles // 2, sources // 2, width)
-    product = pltpu.VMEM((sources, columns), F32)
+    block = shape(sources // 2, width)
+    blocks = shape(members, sources // 2, width)
+    chosen = shape(rows, members * width)
     spread = pltpu.VMEM((sources, columns), BF16)
-    spread_rows = pltpu.VMEM((rows, columns), BF16)
     flops = 2 * rows * columns * sources
 
     keep, give = call(
@@ -229,39 +251,53 @@
             pltpu.VMEM(start.shape, F32),
             pltpu.VMEM(right_rows.shape, BF16),
             wide,
-            spread_rows,
-            product,
-            pltpu.SemaphoreType.DMA((2,)),
+            pltpu.VMEM((rows, columns), BF16),
+            pltpu.VMEM((sources, columns), F32),
+            pltpu.SemaphoreType.DMA((PIECES + 1,)),
         ],
         flops,
         [pltpu.HBM] * 2,
         FIRST_LIMIT,
     )
-    left, turned = call(
-        rows_kernel,
+    sends = call(add_kernel, "add", [block] * members, [keep, to_mate(give)])
+    left_rows = after(left_rows, sends[0])
+    own_left, mate_left, turned = call(
+        functools.partial(rows_kernel, shifts),
         "rows",
-        [factor, shape(sources, rows, dtype=F32)],
-        [ranks, after(left_rows, give), after(observed, give)],
+        [chosen, chosen, shape(sources, rows, dtype=F32)],
+        [ranks, left_rows, to_mate(left_rows), after(observed, give)],
         [wide],
         spaces=[pltpu.SMEM],
     )
-    own, mate = exchange(keep, give, shifts, [left, turned])
-    early = after(start, own)
+    early = after(start, own_left)
     starts = [start]
     for shift in range(1, band):
         starts.append(lax.ppermute(early, "freq", [(f, (f - shift) % band) for f in range(band)]))
-    keep, give = call(
+    (misfit,) = call(
         functools.partial(image_kernel, shifts),
         "image",
-        [blocks, blocks],
-        [own, mate, left, turned],
-        [spread, product],
-        2 * flops,
-    )
-    (right,) = call(columns_kernel, "columns", [factor], [after(right_rows, give)], [wide])
-    own, mate = exchange(keep, give, shifts, [right])
+        [shape(2, sources, rows, dtype=F32)],
+        [*exchange(sends, shifts, [own_left, mate_left, turned]), own_left, mate_left, turned],
+        [pltpu.VMEM((sources, members * width), BF16)],
+        flops,
+    )
+    sends = call(
+        back_kernel,
+        "back",
+        [block] * members,
+        [misfit, to_mate(misfit), own_left, mate_left],
+        [pltpu.VMEM((2, sources, members * width), F32)],
+        flops,
+    )
+    (right,) = call(columns_kernel, "columns", [shape(rows, columns)], [after(right_rows, sends[0])], [wide])
+    (own,) = call(functools.partial(pack_kernel, shifts), "pack", [blocks], exchange(sends, shifts, [right, *starts[1:]]))
     (gradient,) = call(
-        functools.partial(gradient_kernel, shifts), "gradient", [shape(sources, rows)], [own, mate, right], [spread], flops
+        functools.partial(gradient_kernel, shifts),
+        "gradient",
+        [shape(sources, rows)],
+        [own, to_mate(own), right],
+        [spread],
+        flops,
     )
     gradients = [gradient]
     for shift in range(1, band):

time: 34 us -> 33.9 us (level)
  starting transfers between devices: 17.2 us -> 18.4 us
  waiting for transfers between devices: 11.3 us -> 10.2 us
    ppermute x1, waiting for transfers between devices: 3.33 us -> 0.01 us  [body(): lax.ppermute(early, 'freq', [(f, (f - shift) % band) for f in range(band)])]
    ppermute x1, waiting for transfers between devices: 0.7 us -> 2.83 us  [body(): lax.ppermute(gradient, 'freq', [(f, (f - shift) % band) for f in range(ba...]
    ppermute x8, waiting for transfers between devices: 4.13 us -> 5.23 us  [exchange(): lax.ppermute(send, 'tile', [pair for pair in partners if pair[0] != pair[...]
    ppermute x4, waiting for transfers between devices: 3.15 us -> 2.15 us  [to_mate(): lax.ppermute(value, 'tile', [(i, i ^ 1) for i in range(lax.axis_size('til...]
    ppermute x4, starting transfers between devices: 1.49 us -> 2.35 us  [to_mate(): lax.ppermute(value, 'tile', [(i, i ^ 1) for i in range(lax.axis_size('til...]
    ppermute x1, starting transfers between devices: 0.97 us -> 1.5 us  [body(): lax.ppermute(gradient, 'freq', [(f, (f - shift) % band) for f in range(ba...]
    pallas_call x10 -> x9, Pallas kernels: 5.07 us -> 4.92 us  [call(): pl.pallas_call(kernel, out_shape=outs, in_specs=[pl.BlockSpec(memory_spac...]
  transfers between devices with their start and end apart: 14 -> 14, of which waited for: 9 -> 7; matrix products, arithmetic and copies ran while one was open for 0% -> 0% of each run, Pallas kernels for 5% -> 5%
where the time goes in v3:
time: 33.9 us; the launch traced here: 33.7 us
  starting transfers between devices  18.4 us (54%)
  waiting for transfers between devices  10.2 us (30%)
  Pallas kernels  4.92 us (15%)
    ppermute x8, starting transfers between devices, exchange(): lax.ppermute(send, 'tile', [pair for pair in partners if pair[0] != pair[...  13 us
    ppermute x8, waiting for transfers between devices, exchange(): lax.ppermute(send, 'tile', [pair for pair in partners if pair[0] != pair[...  5.23 us
    pallas_call x9, Pallas kernels, call(): pl.pallas_call(kernel, out_shape=outs, in_specs=[pl.BlockSpec(memory_spac...  4.92 us
    ppermute x1, waiting for transfers between devices, body(): lax.ppermute(gradient, 'freq', [(f, (f - shift) % band) for f in range(ba...  2.83 us
    ppermute x4, starting transfers between devices, to_mate(): lax.ppermute(value, 'tile', [(i, i ^ 1) for i in range(lax.axis_size('til...  2.35 us
    ppermute x4, waiting for transfers between devices, to_mate(): lax.ppermute(value, 'tile', [(i, i ^ 1) for i in range(lax.axis_size('til...  2.15 us
    ppermute x1, starting transfers between devices, body(): lax.ppermute(early, 'freq', [(f, (f - shift) % band) for f in range(band)])  1.52 us
    ppermute x1, starting transfers between devices, body(): lax.ppermute(gradient, 'freq', [(f, (f - shift) % band) for f in range(ba...  1.5 us
  transfers between devices with their start and end apart: 14, of which 7 were waited for; matrix products, arithmetic and copies ran while one was open for 0% of the time, Pallas kernels for 5%

profile of v3, /device:TPU:0, one launch (start us, length us, event | category | flops | bytes accessed | tf_op | source)
XLA Modules:
  0.0 33.7 jit_solution(11114436739492709722)
XLA Ops:
  0.0 1.7 %forward.1 = (bf16[4,64,128]{2,1,0:T(8,128)(2,1)S(1)}, bf16[4,64,128]{2,1,0:T(8,128)(2,1)S(1)}) custom-call(f32[256,128]{1,0:T(8,128)} %bitcast.9, bf16[2048,128]{1,0:T(8,128)(2,1)} %bitcast.5), custom_call_target="tpu_custom_call" | custom-call | flops 67108864 | bytes 786432 | tf_op jit(solution)/shard_map/forward/pallas_call | solution.py:192
  1.7 0.0 copy-start.3
  1.8 0.5 %collective-permute-start = (bf16[4,64,128]{2,1,0:T(8,128)(2,1)S(1)}, bf16[4,64,128]{2,1,0:T(8,128)(2,1)S(1)}, u32[]{:S(2)}, u32[]{:S(2)}) collective-permute-start(bf16[4,64,128]{2,1,0:T(8,128)(2,1)S(1)} %get-tuple-element.25), channel_id=1, source_target_pairs={{0,2},{2,0},{4,6},{6,4},{8,10},{10,8},{12,14},{14,12},{16,18},{18,... | collective-permute-start | bytes 196616 | tf_op jit(solution)/shard_map/ppermute | solution.py:205
  2.3 0.9 %collective-permute-done.arrived = bf16[4,64,128]{2,1,0:T(8,128)(2,1)S(1)} collective-permute-done((bf16[4,64,128]{2,1,0:T(8,128)(2,1)S(1)}, bf16[4,64,128]{2,1,0:T(8,128)(2,1)S(1)}, u32[]{:S(2)}, u32[]{:S(2)}) %collective-permute-start) | collective-permute-done | bytes 65568 | tf_op jit(solution)/shard_map/ppermute | solution.py:205
  3.2 0.0 copy-start.4
  3.2 0.4 %collective-permute-start.1 = (bf16[2048,128]{1,0:T(8,128)(2,1)S(1)}, bf16[2048,128]{1,0:T(8,128)(2,1)S(1)}, u32[]{:S(2)}, u32[]{:S(2)}) collective-permute-start(bf16[2048,128]{1,0:T(8,128)(2,1)S(1)} %bitcast.7), channel_id=1, source_target_pairs={{0,2},{2,0},{4,6},{6,4},{8,10},{10,8},{12,14},{14,12},{16,18},{18,... | collective-permute-start | bytes 1572872 | tf_op jit(solution)/shard_map/ppermute | solution.py:205
  3.6 5.7 %collective-permute-start.3 = (bf16[64,128]{1,0:T(8,128)(2,1)S(1)}, bf16[64,128]{1,0:T(8,128)(2,1)S(1)}, u32[]{:S(2)}, u32[]{:S(2)}) collective-permute-start(bf16[64,128]{1,0:T(8,128)(2,1)S(1)} %get-tuple-element.26), channel_id=1, source_target_pairs={{0,28},{2,26},{4,24},{6,30},{8,20},{10,18},{12,16},{14,22},{16,12}... | collective-permute-start | bytes 49160 | tf_op jit(solution)/shard_map/ppermute | solution.py:217
  9.3 0.7 %collective-permute-start.6 = (bf16[64,128]{1,0:T(8,128)(2,1)S(1)}, bf16[64,128]{1,0:T(8,128)(2,1)S(1)}, u32[]{:S(2)}, u32[]{:S(2)}) collective-permute-start(bf16[64,128]{1,0:T(8,128)(2,1)S(1)} %get-tuple-element.31.sent), channel_id=1, source_target_pairs={{2,6},{6,2},{10,14},{14,10},{18,22},{22,18},{26,30},{30,26},{3,7},... | collective-permute-start | bytes 49160 | tf_op jit(solution)/shard_map/ppermute | solution.py:217
  10.0 0.1 collective-permute-start.4
  10.1 0.6 %collective-permute-start.5 = (bf16[64,128]{1,0:T(8,128)(2,1)S(1)}, bf16[64,128]{1,0:T(8,128)(2,1)S(1)}, u32[]{:S(2)}, u32[]{:S(2)}) collective-permute-start(bf16[64,128]{1,0:T(8,128)(2,1)S(1)} %get-tuple-element.36), channel_id=1, source_target_pairs={{0,16},{2,10},{4,20},{6,14},{8,24},{10,2},{12,28},{14,6},{16,0},{1... | collective-permute-start | bytes 49160 | tf_op jit(solution)/shard_map/ppermute | solution.py:217
  10.6 1.1 %rows.1 = (bf16[256,512]{1,0:T(8,128)(2,1)S(1)}, bf16[256,512]{1,0:T(8,128)(2,1)S(1)}, f32[128,256]{1,0:T(8,128)S(1)}) custom-call(s32[1,8,8]{2,1,0:T(8,128)S(1)} %copy-done.4, bf16[2048,128]{1,0:T(8,128)(2,1)S(1)} %bitcast.8, bf16[2048,128]{1,0:T(8,128)(2,1)S(1)} %collective-permute-done.1.mate, f32[256,128]{1,0:T(8,128)S(1)} %bitcast.12), custom_call_target="tpu_custom_call" | custom-call | bytes 1835264 | tf_op jit(solution)/shard_map/rows/pallas_call | solution.py:192
  11.7 0.0 copy-start.2
  11.7 3.0 %collective-permute-done.4.refs_1_ = bf16[64,128]{1,0:T(8,128)(2,1)S(1)} collective-permute-done((bf16[64,128]{1,0:T(8,128)(2,1)S(1)}, bf16[64,128]{1,0:T(8,128)(2,1)S(1)}, u32[]{:S(2)}, u32[]{:S(2)}) %collective-permute-start.4) | collective-permute-done | bytes 16416 | tf_op jit(solution)/shard_map/ppermute | solution.py:217
  14.7 0.1 collective-permute-done.5.refs_2_
  14.8 0.3 image.1.here
  15.1 0.0 copy-start
  15.1 1.3 %collective-permute-start.7 = (f32[2,128,256]{2,1,0:T(8,128)S(1)}, f32[2,128,256]{2,1,0:T(8,128)S(1)}, u32[]{:S(2)}, u32[]{:S(2)}) collective-permute-start(f32[2,128,256]{2,1,0:T(8,128)S(1)} %image.1.here), channel_id=1, source_target_pairs={{0,2},{2,0},{4,6},{6,4},{8,10},{10,8},{12,14},{14,12},{16,18},{18,... | collective-permute-start | bytes 786440 | tf_op jit(solution)/shard_map/ppermute | solution.py:205
  16.4 1.5 %collective-permute-start.2 = (f32[256,128]{1,0:T(8,128)S(1)}, f32[256,128]{1,0:T(8,128)S(1)}, u32[]{:S(2)}, u32[]{:S(2)}) collective-permute-start(f32[256,128]{1,0:T(8,128)S(1)} %bitcast.10), channel_id=1, source_target_pairs={{0,1},{1,0},{2,3},{3,2},{4,5},{5,4},{6,7},{7,6},{8,9},{9,8},{10,11... | collective-permute-start | bytes 393224 | tf_op jit(solution)/shard_map/ppermute | solution.py:275
  18.0 0.3 back.1
  18.3 1.5 %collective-permute-start.8 = (bf16[64,128]{1,0:T(8,128)(2,1)S(1)}, bf16[64,128]{1,0:T(8,128)(2,1)S(1)}, u32[]{:S(2)}, u32[]{:S(2)}) collective-permute-start(bf16[64,128]{1,0:T(8,128)(2,1)S(1)} %get-tuple-element.38), channel_id=1, source_target_pairs={{0,28},{2,26},{4,24},{6,30},{8,20},{10,18},{12,16},{14,22},{16,12}... | collective-permute-start | bytes 49160 | tf_op jit(solution)/shard_map/ppermute | solution.py:217
  19.8 1.6 %collective-permute-start.10 = (bf16[64,128]{1,0:T(8,128)(2,1)S(1)}, bf16[64,128]{1,0:T(8,128)(2,1)S(1)}, u32[]{:S(2)}, u32[]{:S(2)}) collective-permute-start(bf16[64,128]{1,0:T(8,128)(2,1)S(1)} %get-tuple-element.42), channel_id=1, source_target_pairs={{0,16},{2,10},{4,20},{6,14},{8,24},{10,2},{12,28},{14,6},{16,0},{1... | collective-permute-start | bytes 49160 | tf_op jit(solution)/shard_map/ppermute | solution.py:217
  21.5 0.7 %collective-permute-start.11 = (bf16[64,128]{1,0:T(8,128)(2,1)S(1)}, bf16[64,128]{1,0:T(8,128)(2,1)S(1)}, u32[]{:S(2)}, u32[]{:S(2)}) collective-permute-start(bf16[64,128]{1,0:T(8,128)(2,1)S(1)} %get-tuple-element.37.sent), channel_id=1, source_target_pairs={{2,6},{6,2},{10,14},{14,10},{18,22},{22,18},{26,30},{30,26},{3,7},... | collective-permute-start | bytes 49160 | tf_op jit(solution)/shard_map/ppermute | solution.py:217
  22.2 2.2 %collective-permute-start.9 = (bf16[64,128]{1,0:T(8,128)(2,1)S(1)}, bf16[64,128]{1,0:T(8,128)(2,1)S(1)}, u32[]{:S(2)}, u32[]{:S(2)}) collective-permute-start(bf16[64,128]{1,0:T(8,128)(2,1)S(1)} %get-tuple-element.41), channel_id=1, source_target_pairs={{0,12},{2,22},{4,8},{6,18},{8,4},{10,30},{12,0},{14,26},{16,28},{1... | collective-permute-start | bytes 49160 | tf_op jit(solution)/shard_map/ppermute | solution.py:217
  24.4 0.3 columns.1.factors
  24.7 0.1 collective-permute-done.8.refs_0_
  24.8 2.1 %collective-permute-done.9.refs_1_ = bf16[64,128]{1,0:T(8,128)(2,1)S(1)} collective-permute-done((bf16[64,128]{1,0:T(8,128)(2,1)S(1)}, bf16[64,128]{1,0:T(8,128)(2,1)S(1)}, u32[]{:S(2)}, u32[]{:S(2)}) %collective-permute-start.9) | collective-permute-done | bytes 16416 | tf_op jit(solution)/shard_map/ppermute | solution.py:217
  26.9 0.1 collective-permute-start.12
  27.0 1.2 %collective-permute-done.12.mate = bf16[4,64,128]{2,1,0:T(8,128)(2,1)S(1)} collective-permute-done((bf16[4,64,128]{2,1,0:T(8,128)(2,1)S(1)}, bf16[4,64,128]{2,1,0:T(8,128)(2,1)S(1)}, u32[]{:S(2)}, u32[]{:S(2)}) %collective-permute-start.12) | collective-permute-done | bytes 65568 | tf_op jit(solution)/shard_map/ppermute | solution.py:205
  28.2 0.4 %gradient.1.refs_2_ = bf16[128,256]{1,0:T(8,128)(2,1)S(1)} custom-call(bf16[4,64,128]{2,1,0:T(8,128)(2,1)S(1)} %pack.1.own, bf16[4,64,128]{2,1,0:T(8,128)(2,1)S(1)} %collective-permute-done.12.mate, bf16[256,1024]{1,0:T(8,128)(2,1)S(1)} %columns.1.factors), custom_call_target="tpu_custom_call" | custom-call | flops 67108864 | bytes 720896 | tf_op jit(solution)/shard_map/gradient/pallas_call | solution.py:192
  28.6 1.5 %collective-permute-start.13 = (bf16[128,256]{1,0:T(8,128)(2,1)S(1)}, bf16[128,256]{1,0:T(8,128)(2,1)S(1)}, u32[]{:S(2)}, u32[]{:S(2)}) collective-permute-start(bf16[128,256]{1,0:T(8,128)(2,1)S(1)} %gradient.1.refs_2_), channel_id=1, source_target_pairs={{0,1},{1,0},{2,3},{3,2},{4,5},{5,4},{6,7},{7,6},{8,9},{9,8},{10,11... | collective-permute-start | bytes 196616 | tf_op jit(solution)/shard_map/ppermute | solution.py:304
  30.1 2.8 %collective-permute-done.13.refs_3_ = bf16[128,256]{1,0:T(8,128)(2,1)S(1)} collective-permute-done((bf16[128,256]{1,0:T(8,128)(2,1)S(1)}, bf16[128,256]{1,0:T(8,128)(2,1)S(1)}, u32[]{:S(2)}, u32[]{:S(2)}) %collective-permute-start.13) | collective-permute-done | bytes 65568 | tf_op jit(solution)/shard_map/ppermute | solution.py:304
  32.9 0.8 %shrink.1 = f32[256,128]{1,0:T(8,128)} custom-call(f32[256,128]{1,0:T(8,128)S(1)} %bitcast.11, f32[256,128]{1,0:T(8,128)S(1)} %collective-permute-done.2.refs_1_, bf16[128,256]{1,0:T(8,128)(2,1)S(1)} %gradient.1.refs_2_, bf16[128,256]{1,0:T(8,128)(2,1)S(1)} %collective-permute-done.13.refs_3_), custom_call_target="tpu_custom_call" | custom-call | bytes 524288 | tf_op jit(solution)/shard_map/shrink/pallas_call | solution.py:192
  (15 shorter events, 0.1 us)
Async XLA Ops:
  0.0 3.2 %copy-start.1 = (bf16[1,256,8,128]{3,2,1,0:T(8,128)(2,1)S(1)}, bf16[1,256,8,128]{3,2,1,0:T(8,128)(2,1)}, u32[]{:S(2)}) copy-start(bf16[1,256,8,128]{3,2,1,0:T(8,128)(2,1)} %param.5) | copy-start | bytes 1572868
  1.7 8.9 %copy-start.3 = (f32[1,256,128]{2,1,0:T(8,128)S(1)}, f32[1,256,128]{2,1,0:T(8,128)}, u32[]{:S(2)}) copy-start(f32[1,256,128]{2,1,0:T(8,128)} %param.8) | copy-start | bytes 393220
  1.8 1.4 %collective-permute-start = (bf16[4,64,128]{2,1,0:T(8,128)(2,1)S(1)}, bf16[4,64,128]{2,1,0:T(8,128)(2,1)S(1)}, u32[]{:S(2)}, u32[]{:S(2)}) collective-permute-start(bf16[4,64,128]{2,1,0:T(8,128)(2,1)S(1)} %get-tuple-element.25), channel_id=1, source_target_pairs={{0,2},{2,0},{4,6},{6,4},{8,10},{10,8},{12,14},{14,12},{16,18},{18,... | collective-permute-start | bytes 196616 | tf_op jit(solution)/shard_map/ppermute | solution.py:205
  3.2 7.4 %copy-start.4 = (s32[1,8,8]{2,1,0:T(8,128)S(1)}, s32[1,8,8]{2,1,0:T(8,128)}, u32[]{:S(2)}) copy-start(s32[1,8,8]{2,1,0:T(8,128)} %ranks.1) | copy-start | bytes 772
  3.2 7.4 %collective-permute-start.1 = (bf16[2048,128]{1,0:T(8,128)(2,1)S(1)}, bf16[2048,128]{1,0:T(8,128)(2,1)S(1)}, u32[]{:S(2)}, u32[]{:S(2)}) collective-permute-start(bf16[2048,128]{1,0:T(8,128)(2,1)S(1)} %bitcast.7), channel_id=1, source_target_pairs={{0,2},{2,0},{4,6},{6,4},{8,10},{10,8},{12,14},{14,12},{16,18},{18,... | collective-permute-start | bytes 1572872 | tf_op jit(solution)/shard_map/ppermute | solution.py:205
  3.6 8.1 %collective-permute-start.3 = (bf16[64,128]{1,0:T(8,128)(2,1)S(1)}, bf16[64,128]{1,0:T(8,128)(2,1)S(1)}, u32[]{:S(2)}, u32[]{:S(2)}) collective-permute-start(bf16[64,128]{1,0:T(8,128)(2,1)S(1)} %get-tuple-element.26), channel_id=1, source_target_pairs={{0,28},{2,26},{4,24},{6,30},{8,20},{10,18},{12,16},{14,22},{16,12}... | collective-permute-start | bytes 49160 | tf_op jit(solution)/shard_map/ppermute | solution.py:217
  9.3 2.4 %collective-permute-start.6 = (bf16[64,128]{1,0:T(8,128)(2,1)S(1)}, bf16[64,128]{1,0:T(8,128)(2,1)S(1)}, u32[]{:S(2)}, u32[]{:S(2)}) collective-permute-start(bf16[64,128]{1,0:T(8,128)(2,1)S(1)} %get-tuple-element.31.sent), channel_id=1, source_target_pairs={{2,6},{6,2},{10,14},{14,10},{18,22},{22,18},{26,30},{30,26},{3,7},... | collective-permute-start | bytes 49160 | tf_op jit(solution)/shard_map/ppermute | solution.py:217
  10.0 4.7 %collective-permute-start.4 = (bf16[64,128]{1,0:T(8,128)(2,1)S(1)}, bf16[64,128]{1,0:T(8,128)(2,1)S(1)}, u32[]{:S(2)}, u32[]{:S(2)}) collective-permute-start(bf16[64,128]{1,0:T(8,128)(2,1)S(1)} %get-tuple-element.35), channel_id=1, source_target_pairs={{0,12},{2,22},{4,8},{6,18},{8,4},{10,30},{12,0},{14,26},{16,28},{1... | collective-permute-start | bytes 49160 | tf_op jit(solution)/shard_map/ppermute | solution.py:217
  10.1 4.7 %collective-permute-start.5 = (bf16[64,128]{1,0:T(8,128)(2,1)S(1)}, bf16[64,128]{1,0:T(8,128)(2,1)S(1)}, u32[]{:S(2)}, u32[]{:S(2)}) collective-permute-start(bf16[64,128]{1,0:T(8,128)(2,1)S(1)} %get-tuple-element.36), channel_id=1, source_target_pairs={{0,16},{2,10},{4,20},{6,14},{8,24},{10,2},{12,28},{14,6},{16,0},{1... | collective-permute-start | bytes 49160 | tf_op jit(solution)/shard_map/ppermute | solution.py:217
  11.7 4.7 %copy-start.2 = (f32[1,256,128]{2,1,0:T(8,128)S(1)}, f32[1,256,128]{2,1,0:T(8,128)}, u32[]{:S(2)}) copy-start(f32[1,256,128]{2,1,0:T(8,128)} %param.9) | copy-start | bytes 393220
  15.1 9.3 %copy-start = (bf16[1,256,8,128]{3,2,1,0:T(8,128)(2,1)S(1)}, bf16[1,256,8,128]{3,2,1,0:T(8,128)(2,1)}, u32[]{:S(2)}) copy-start(bf16[1,256,8,128]{3,2,1,0:T(8,128)(2,1)} %param.6) | copy-start | bytes 1572868
  15.1 2.9 %collective-permute-start.7 = (f32[2,128,256]{2,1,0:T(8,128)S(1)}, f32[2,128,256]{2,1,0:T(8,128)S(1)}, u32[]{:S(2)}, u32[]{:S(2)}) collective-permute-start(f32[2,128,256]{2,1,0:T(8,128)S(1)} %image.1.here), channel_id=1, source_target_pairs={{0,2},{2,0},{4,6},{6,4},{8,10},{10,8},{12,14},{14,12},{16,18},{18,... | collective-permute-start | bytes 786440 | tf_op jit(solution)/shard_map/ppermute | solution.py:205
  16.4 8.2 %collective-permute-start.2 = (f32[256,128]{1,0:T(8,128)S(1)}, f32[256,128]{1,0:T(8,128)S(1)}, u32[]{:S(2)}, u32[]{:S(2)}) collective-permute-start(f32[256,128]{1,0:T(8,128)S(1)} %bitcast.10), channel_id=1, source_target_pairs={{0,1},{1,0},{2,3},{3,2},{4,5},{5,4},{6,7},{7,6},{8,9},{9,8},{10,11... | collective-permute-start | bytes 393224 | tf_op jit(solution)/shard_map/ppermute | solution.py:275
  18.3 6.5 %collective-permute-start.8 = (bf16[64,128]{1,0:T(8,128)(2,1)S(1)}, bf16[64,128]{1,0:T(8,128)(2,1)S(1)}, u32[]{:S(2)}, u32[]{:S(2)}) collective-permute-start(bf16[64,128]{1,0:T(8,128)(2,1)S(1)} %get-tuple-element.38), channel_id=1, source_target_pairs={{0,28},{2,26},{4,24},{6,30},{8,20},{10,18},{12,16},{14,22},{16,12}... | collective-permute-start | bytes 49160 | tf_op jit(solution)/shard_map/ppermute | solution.py:217
  19.8 5.0 %collective-permute-start.10 = (bf16[64,128]{1,0:T(8,128)(2,1)S(1)}, bf16[64,128]{1,0:T(8,128)(2,1)S(1)}, u32[]{:S(2)}, u32[]{:S(2)}) collective-permute-start(bf16[64,128]{1,0:T(8,128)(2,1)S(1)} %get-tuple-element.42), channel_id=1, source_target_pairs={{0,16},{2,10},{4,20},{6,14},{8,24},{10,2},{12,28},{14,6},{16,0},{1... | collective-permute-start | bytes 49160 | tf_op jit(solution)/shard_map/ppermute | solution.py:217
  21.5 3.3 %collective-permute-start.11 = (bf16[64,128]{1,0:T(8,128)(2,1)S(1)}, bf16[64,128]{1,0:T(8,128)(2,1)S(1)}, u32[]{:S(2)}, u32[]{:S(2)}) collective-permute-start(bf16[64,128]{1,0:T(8,128)(2,1)S(1)} %get-tuple-element.37.sent), channel_id=1, source_target_pairs={{2,6},{6,2},{10,14},{14,10},{18,22},{22,18},{26,30},{30,26},{3,7},... | collective-permute-start | bytes 49160 | tf_op jit(solution)/shard_map/ppermute | solution.py:217
  22.2 4.7 %collective-permute-start.9 = (bf16[64,128]{1,0:T(8,128)(2,1)S(1)}, bf16[64,128]{1,0:T(8,128)(2,1)S(1)}, u32[]{:S(2)}, u32[]{:S(2)}) collective-permute-start(bf16[64,128]{1,0:T(8,128)(2,1)S(1)} %get-tuple-element.41), channel_id=1, source_target_pairs={{0,12},{2,22},{4,8},{6,18},{8,4},{10,30},{12,0},{14,26},{16,28},{1... | collective-permute-start | bytes 49160 | tf_op jit(solution)/shard_map/ppermute | solution.py:217
  26.9 1.3 %collective-permute-start.12 = (bf16[4,64,128]{2,1,0:T(8,128)(2,1)S(1)}, bf16[4,64,128]{2,1,0:T(8,128)(2,1)S(1)}, u32[]{:S(2)}, u32[]{:S(2)}) collective-permute-start(bf16[4,64,128]{2,1,0:T(8,128)(2,1)S(1)} %pack.1.own), channel_id=1, source_target_pairs={{0,2},{2,0},{4,6},{6,4},{8,10},{10,8},{12,14},{14,12},{16,18},{18,... | collective-permute-start | bytes 196616 | tf_op jit(solution)/shard_map/ppermute | solution.py:205
  28.6 4.3 %collective-permute-start.13 = (bf16[128,256]{1,0:T(8,128)(2,1)S(1)}, bf16[128,256]{1,0:T(8,128)(2,1)S(1)}, u32[]{:S(2)}, u32[]{:S(2)}) collective-permute-start(bf16[128,256]{1,0:T(8,128)(2,1)S(1)} %gradient.1.refs_2_), channel_id=1, source_target_pairs={{0,1},{1,0},{2,3},{3,2},{4,5},{5,4},{6,7},{7,6},{8,9},{9,8},{10,11... | collective-permute-start | bytes 196616 | tf_op jit(solution)/shard_map/ppermute | solution.py:304

commit v4 on v3

--- a/solution.py
+++ b/solution.py
@@ -67,15 +67,6 @@
     block = block.astype(F32)
     left[:half, columns_of(tile)] = (block * signs(half)).astype(BF16)
     left[half:, columns_of(tile)] = pltpu.roll(block, LANES // 2, 1).astype(BF16)
-
-
-def arrived_block(shifts, index, sent, arrived):
-    _, core = place()
-    values = arrived[...]
-    for side in range(2):
-        if shifts[side][index] == 0:
-            values = jnp.where(core == side, sent[...], values)
-    return values
 
 
 def times_transposed(left, right):
@@ -126,10 +117,10 @@
     separate(factors, wide, separated, range(separated.shape[1] // LANES))
 
 
-def image_kernel(shifts, sent, *refs):
+def image_kernel(*refs):
     arrived, (own, mate, observed, misfit, left) = refs[:-5], refs[-5:]
     for index, block in enumerate(arrived):
-        spread_block(arrived_block(shifts, index, sent, block), left, index)
+        spread_block(block[...], left, index)
     misfit[0] = times_transposed(left[...], own[...]) - observed[...]
     misfit[1] = times_transposed(left[...], mate[...])
 
@@ -144,10 +135,9 @@
         out[...] = (parts[0] + parts[1]).astype(BF16)
 
 
-def pack_kernel(shifts, sent, *refs):
-    arrived, packed = refs[:-1], refs[-1]
-    for index, block in enumerate(arrived):
-        packed[index] = arrived_block(shifts, index, sent, block)
+def pack_kernel(*refs):
+    for index, block in enumerate(refs[:-1]):
+        refs[-1][index] = block[...]
 
 
 def gradient_kernel(shifts, own, mate, factors, gradient, left):
@@ -213,11 +203,8 @@
     count = lax.axis_size("tile")
     arrived = []
     for index, send in enumerate(sends):
-        partners = [(i, i ^ 2 * shifts[i % 2][index]) for i in range(count)]
-        arrived.append(lax.ppermute(send, "tile", [pair for pair in partners if pair[0] != pair[1]]))
-    arrived[0] = after(arrived[0], *beside)
-    (own,) = [send for index, send in enumerate(sends) if 0 in (shifts[0][index], shifts[1][index])]
-    return [own, *arrived]
+        arrived.append(lax.ppermute(send, "tile", [(i, i ^ 2 * shifts[i % 2][index]) for i in range(count)]))
+    return [after(arrived[0], *beside), *arrived[1:]]
 
 
 def body(u_factors, v_factors, ranks, observed, start):
@@ -274,7 +261,7 @@
     for shift in range(1, band):
         starts.append(lax.ppermute(early, "freq", [(f, (f - shift) % band) for f in range(band)]))
     (misfit,) = call(
-        functools.partial(image_kernel, shifts),
+        image_kernel,
         "image",
         [shape(2, sources, rows, dtype=F32)],
         [*exchange(sends, shifts, [own_left, mate_left, turned]), own_left, mate_left, turned],
@@ -290,7 +277,7 @@
         flops,
     )
     (right,) = call(columns_kernel, "columns", [shape(rows, columns)], [after(right_rows, sends[0])], [wide])
-    (own,) = call(functools.partial(pack_kernel, shifts), "pack", [blocks], exchange(sends, shifts, [right, *starts[1:]]))
+    (own,) = call(pack_kernel, "pack", [blocks], exchange(sends, shifts, [right, *starts[1:]]))
     (gradient,) = call(
         functools.partial(gradient_kernel, shifts),
         "gradient",

time: 33.9 us -> 31.9 us (0.941)
  starting transfers between devices: 18.4 us -> 16.9 us
  waiting for transfers between devices: 10.2 us -> 9.74 us
    ppermute x4, starting transfers between devices: 2.35 us -> 1.29 us  [to_mate(): lax.ppermute(value, 'tile', [(i, i ^ 1) for i in range(lax.axis_size('til...]
    ppermute x8, waiting for transfers between devices: 5.23 us -> 4.51 us  [exchange(): lax.ppermute(send, 'tile', [(i, i ^ 2 * shifts[i % 2][index]) for i in ra...]
where the time goes in v4:
time: 31.9 us; the launch traced here: 31.8 us
  starting transfers between devices  16.9 us (53%)
  waiting for transfers between devices  9.74 us (31%)
  Pallas kernels  4.91 us (15%)
    ppermute x8, starting transfers between devices, exchange(): lax.ppermute(send, 'tile', [(i, i ^ 2 * shifts[i % 2][index]) for i in ra...  12.9 us
    pallas_call x9, Pallas kernels, call(): pl.pallas_call(kernel, out_shape=outs, in_specs=[pl.BlockSpec(memory_spac...  4.91 us
    ppermute x8, waiting for transfers between devices, exchange(): lax.ppermute(send, 'tile', [(i, i ^ 2 * shifts[i % 2][index]) for i in ra...  4.51 us
    ppermute x1, waiting for transfers between devices, body(): lax.ppermute(gradient, 'freq', [(f, (f - shift) % band) for f in range(ba...  3.11 us
    ppermute x4, waiting for transfers between devices, to_mate(): lax.ppermute(value, 'tile', [(i, i ^ 1) for i in range(lax.axis_size('til...  2.12 us
    ppermute x1, starting transfers between devices, body(): lax.ppermute(early, 'freq', [(f, (f - shift) % band) for f in range(band)])  1.52 us
    ppermute x4, starting transfers between devices, to_mate(): lax.ppermute(value, 'tile', [(i, i ^ 1) for i in range(lax.axis_size('til...  1.29 us
    ppermute x1, starting transfers between devices, body(): lax.ppermute(gradient, 'freq', [(f, (f - shift) % band) for f in range(ba...  1.22 us
  transfers between devices with their start and end apart: 14, of which 7 were waited for; matrix products, arithmetic and copies ran while one was open for 0% of the time, Pallas kernels for 5%

profile of v4, /device:TPU:0, one launch (start us, length us, event | category | flops | bytes accessed | tf_op | source)
XLA Modules:
  0.0 31.8 jit_solution(16467078400574773848)
XLA Ops:
  0.0 1.7 %forward.1 = (bf16[4,64,128]{2,1,0:T(8,128)(2,1)S(1)}, bf16[4,64,128]{2,1,0:T(8,128)(2,1)S(1)}) custom-call(f32[256,128]{1,0:T(8,128)} %bitcast.9, bf16[2048,128]{1,0:T(8,128)(2,1)} %bitcast.5), custom_call_target="tpu_custom_call" | custom-call | flops 67108864 | bytes 786432 | tf_op jit(solution)/shard_map/forward/pallas_call | solution.py:182
  1.7 0.0 copy-start.3
  1.8 0.5 %collective-permute-start = (bf16[4,64,128]{2,1,0:T(8,128)(2,1)S(1)}, bf16[4,64,128]{2,1,0:T(8,128)(2,1)S(1)}, u32[]{:S(2)}, u32[]{:S(2)}) collective-permute-start(bf16[4,64,128]{2,1,0:T(8,128)(2,1)S(1)} %get-tuple-element.25), channel_id=1, source_target_pairs={{0,2},{2,0},{4,6},{6,4},{8,10},{10,8},{12,14},{14,12},{16,18},{18,... | collective-permute-start | bytes 196616 | tf_op jit(solution)/shard_map/ppermute | solution.py:195
  2.3 0.9 %collective-permute-done.arrived = bf16[4,64,128]{2,1,0:T(8,128)(2,1)S(1)} collective-permute-done((bf16[4,64,128]{2,1,0:T(8,128)(2,1)S(1)}, bf16[4,64,128]{2,1,0:T(8,128)(2,1)S(1)}, u32[]{:S(2)}, u32[]{:S(2)}) %collective-permute-start) | collective-permute-done | bytes 65568 | tf_op jit(solution)/shard_map/ppermute | solution.py:195
  3.2 0.0 copy-start.4
  3.2 0.4 %collective-permute-start.1 = (bf16[2048,128]{1,0:T(8,128)(2,1)S(1)}, bf16[2048,128]{1,0:T(8,128)(2,1)S(1)}, u32[]{:S(2)}, u32[]{:S(2)}) collective-permute-start(bf16[2048,128]{1,0:T(8,128)(2,1)S(1)} %bitcast.7), channel_id=1, source_target_pairs={{0,2},{2,0},{4,6},{6,4},{8,10},{10,8},{12,14},{14,12},{16,18},{18,... | collective-permute-start | bytes 1572872 | tf_op jit(solution)/shard_map/ppermute | solution.py:195
  3.6 5.7 %collective-permute-start.3 = (bf16[64,128]{1,0:T(8,128)(2,1)S(1)}, bf16[64,128]{1,0:T(8,128)(2,1)S(1)}, u32[]{:S(2)}, u32[]{:S(2)}) collective-permute-start(bf16[64,128]{1,0:T(8,128)(2,1)S(1)} %get-tuple-element.26), channel_id=1, source_target_pairs={{0,28},{2,26},{4,24},{6,30},{8,20},{10,18},{12,16},{14,22},{16,12}... | collective-permute-start | bytes 49160 | tf_op jit(solution)/shard_map/ppermute | solution.py:206
  9.3 0.0 collective-permute-start.4
  9.3 0.6 %collective-permute-start.5 = (bf16[64,128]{1,0:T(8,128)(2,1)S(1)}, bf16[64,128]{1,0:T(8,128)(2,1)S(1)}, u32[]{:S(2)}, u32[]{:S(2)}) collective-permute-start(bf16[64,128]{1,0:T(8,128)(2,1)S(1)} %get-tuple-element.35), channel_id=1, source_target_pairs={{0,16},{2,10},{4,20},{6,14},{8,24},{10,2},{12,28},{14,6},{16,0},{1... | collective-permute-start | bytes 49160 | tf_op jit(solution)/shard_map/ppermute | solution.py:206
  9.9 0.7 %collective-permute-start.6 = (bf16[64,128]{1,0:T(8,128)(2,1)S(1)}, bf16[64,128]{1,0:T(8,128)(2,1)S(1)}, u32[]{:S(2)}, u32[]{:S(2)}) collective-permute-start(bf16[64,128]{1,0:T(8,128)(2,1)S(1)} %get-tuple-element.36), channel_id=1, source_target_pairs={{0,0},{2,6},{4,4},{6,2},{8,8},{10,14},{12,12},{14,10},{16,16},{18,... | collective-permute-start | bytes 49160 | tf_op jit(solution)/shard_map/ppermute | solution.py:206
  10.6 1.1 %rows.1 = (bf16[256,512]{1,0:T(8,128)(2,1)S(1)}, bf16[256,512]{1,0:T(8,128)(2,1)S(1)}, f32[128,256]{1,0:T(8,128)S(1)}) custom-call(s32[1,8,8]{2,1,0:T(8,128)S(1)} %copy-done.4, bf16[2048,128]{1,0:T(8,128)(2,1)S(1)} %bitcast.8, bf16[2048,128]{1,0:T(8,128)(2,1)S(1)} %collective-permute-done.1.mate, f32[256,128]{1,0:T(8,128)S(1)} %bitcast.12), custom_call_target="tpu_custom_call" | custom-call | bytes 1835264 | tf_op jit(solution)/shard_map/rows/pallas_call | solution.py:182
  11.7 0.0 copy-start.2
  11.7 2.3 %collective-permute-done.4.refs_1_ = bf16[64,128]{1,0:T(8,128)(2,1)S(1)} collective-permute-done((bf16[64,128]{1,0:T(8,128)(2,1)S(1)}, bf16[64,128]{1,0:T(8,128)(2,1)S(1)}, u32[]{:S(2)}, u32[]{:S(2)}) %collective-permute-start.4) | collective-permute-done | bytes 16416 | tf_op jit(solution)/shard_map/ppermute | solution.py:206
  14.0 0.3 %image.1.here = f32[2,128,256]{2,1,0:T(8,128)S(1)} custom-call(bf16[64,128]{1,0:T(8,128)(2,1)S(1)} %collective-permute-done.3.refs_0_, bf16[64,128]{1,0:T(8,128)(2,1)S(1)} %collective-permute-done.4.refs_1_, bf16[64,128]{1,0:T(8,128)(2,1)S(1)} %collective-permute-done.5.refs_2_, bf16[64,128]{1,0:T(8,128)(2,1)S(1)} %collective-permute-done.6.refs_3_, ...), custom_call_target="tpu_custom_call" | custom-call | flops 67108864 | bytes 983040 | tf_op jit(solution)/shard_map/image/pallas_call | solution.py:182
  14.3 0.0 copy-start
  14.3 0.2 collective-permute-start.7
  14.6 1.5 %collective-permute-start.2 = (f32[256,128]{1,0:T(8,128)S(1)}, f32[256,128]{1,0:T(8,128)S(1)}, u32[]{:S(2)}, u32[]{:S(2)}) collective-permute-start(f32[256,128]{1,0:T(8,128)S(1)} %bitcast.10), channel_id=1, source_target_pairs={{0,1},{1,0},{2,3},{3,2},{4,5},{5,4},{6,7},{7,6},{8,9},{9,8},{10,11... | collective-permute-start | bytes 393224 | tf_op jit(solution)/shard_map/ppermute | solution.py:262
  16.1 0.3 %back.1 = (bf16[64,128]{1,0:T(8,128)(2,1)S(1)}, bf16[64,128]{1,0:T(8,128)(2,1)S(1)}, bf16[64,128]{1,0:T(8,128)(2,1)S(1)}, bf16[64,128]{1,0:T(8,128)(2,1)S(1)}) custom-call(f32[2,128,256]{2,1,0:T(8,128)S(1)} %image.1.here, f32[2,128,256]{2,1,0:T(8,128)S(1)} %collective-permute-done.7.there, bf16[256,512]{1,0:T(8,128)(2,1)S(1)} %get-tuple-element.29.refs_4_.own, ...), custom_call_target="tpu_custom_call" | custom-call | flops 67108864 | bytes 1114112 | tf_op jit(solution)/shard_map/back/pallas_call | solution.py:182
  16.4 3.6 %collective-permute-start.8 = (bf16[64,128]{1,0:T(8,128)(2,1)S(1)}, bf16[64,128]{1,0:T(8,128)(2,1)S(1)}, u32[]{:S(2)}, u32[]{:S(2)}) collective-permute-start(bf16[64,128]{1,0:T(8,128)(2,1)S(1)} %get-tuple-element.37), channel_id=1, source_target_pairs={{0,28},{2,26},{4,24},{6,30},{8,20},{10,18},{12,16},{14,22},{16,12}... | collective-permute-start | bytes 49160 | tf_op jit(solution)/shard_map/ppermute | solution.py:206
  20.0 0.3 collective-permute-start.9
  20.3 1.5 %collective-permute-start.10 = (bf16[64,128]{1,0:T(8,128)(2,1)S(1)}, bf16[64,128]{1,0:T(8,128)(2,1)S(1)}, u32[]{:S(2)}, u32[]{:S(2)}) collective-permute-start(bf16[64,128]{1,0:T(8,128)(2,1)S(1)} %get-tuple-element.41), channel_id=1, source_target_pairs={{0,16},{2,10},{4,20},{6,14},{8,24},{10,2},{12,28},{14,6},{16,0},{1... | collective-permute-start | bytes 49160 | tf_op jit(solution)/shard_map/ppermute | solution.py:206
  21.8 0.7 %collective-permute-start.11 = (bf16[64,128]{1,0:T(8,128)(2,1)S(1)}, bf16[64,128]{1,0:T(8,128)(2,1)S(1)}, u32[]{:S(2)}, u32[]{:S(2)}) collective-permute-start(bf16[64,128]{1,0:T(8,128)(2,1)S(1)} %get-tuple-element.42), channel_id=1, source_target_pairs={{0,0},{2,6},{4,4},{6,2},{8,8},{10,14},{12,12},{14,10},{16,16},{18,... | collective-permute-start | bytes 49160 | tf_op jit(solution)/shard_map/ppermute | solution.py:206
  22.4 0.3 columns.1.factors
  22.7 0.2 collective-permute-done.8.refs_0_
  22.9 1.7 %collective-permute-done.9.refs_1_ = bf16[64,128]{1,0:T(8,128)(2,1)S(1)} collective-permute-done((bf16[64,128]{1,0:T(8,128)(2,1)S(1)}, bf16[64,128]{1,0:T(8,128)(2,1)S(1)}, u32[]{:S(2)}, u32[]{:S(2)}) %collective-permute-start.9) | collective-permute-done | bytes 16416 | tf_op jit(solution)/shard_map/ppermute | solution.py:206
  24.6 0.3 collective-permute-done.10.refs_2_
  25.0 0.1 collective-permute-start.12
  25.1 1.2 %collective-permute-done.12.mate = bf16[4,64,128]{2,1,0:T(8,128)(2,1)S(1)} collective-permute-done((bf16[4,64,128]{2,1,0:T(8,128)(2,1)S(1)}, bf16[4,64,128]{2,1,0:T(8,128)(2,1)S(1)}, u32[]{:S(2)}, u32[]{:S(2)}) %collective-permute-start.12) | collective-permute-done | bytes 65568 | tf_op jit(solution)/shard_map/ppermute | solution.py:195
  26.3 0.4 %gradient.1.refs_2_ = bf16[128,256]{1,0:T(8,128)(2,1)S(1)} custom-call(bf16[4,64,128]{2,1,0:T(8,128)(2,1)S(1)} %pack.1.own, bf16[4,64,128]{2,1,0:T(8,128)(2,1)S(1)} %collective-permute-done.12.mate, bf16[256,1024]{1,0:T(8,128)(2,1)S(1)} %columns.1.factors), custom_call_target="tpu_custom_call" | custom-call | flops 67108864 | bytes 720896 | tf_op jit(solution)/shard_map/gradient/pallas_call | solution.py:182
  26.6 1.2 %collective-permute-start.13 = (bf16[128,256]{1,0:T(8,128)(2,1)S(1)}, bf16[128,256]{1,0:T(8,128)(2,1)S(1)}, u32[]{:S(2)}, u32[]{:S(2)}) collective-permute-start(bf16[128,256]{1,0:T(8,128)(2,1)S(1)} %gradient.1.refs_2_), channel_id=1, source_target_pairs={{0,1},{1,0},{2,3},{3,2},{4,5},{5,4},{6,7},{7,6},{8,9},{9,8},{10,11... | collective-permute-start | bytes 196616 | tf_op jit(solution)/shard_map/ppermute | solution.py:291
  27.9 3.1 %collective-permute-done.13.refs_3_ = bf16[128,256]{1,0:T(8,128)(2,1)S(1)} collective-permute-done((bf16[128,256]{1,0:T(8,128)(2,1)S(1)}, bf16[128,256]{1,0:T(8,128)(2,1)S(1)}, u32[]{:S(2)}, u32[]{:S(2)}) %collective-permute-start.13) | collective-permute-done | bytes 65568 | tf_op jit(solution)/shard_map/ppermute | solution.py:291
  31.0 0.8 %shrink.1 = f32[256,128]{1,0:T(8,128)} custom-call(f32[256,128]{1,0:T(8,128)S(1)} %bitcast.11, f32[256,128]{1,0:T(8,128)S(1)} %collective-permute-done.2.refs_1_, bf16[128,256]{1,0:T(8,128)(2,1)S(1)} %gradient.1.refs_2_, bf16[128,256]{1,0:T(8,128)(2,1)S(1)} %collective-permute-done.13.refs_3_), custom_call_target="tpu_custom_call" | custom-call | bytes 524288 | tf_op jit(solution)/shard_map/shrink/pallas_call | solution.py:182
  (15 shorter events, 0.1 us)
Async XLA Ops:
  0.0 3.2 %copy-start.1 = (bf16[1,256,8,128]{3,2,1,0:T(8,128)(2,1)S(1)}, bf16[1,256,8,128]{3,2,1,0:T(8,128)(2,1)}, u32[]{:S(2)}) copy-start(bf16[1,256,8,128]{3,2,1,0:T(8,128)(2,1)} %param.5) | copy-start | bytes 1572868
  1.7 8.8 %copy-start.3 = (f32[1,256,128]{2,1,0:T(8,128)S(1)}, f32[1,256,128]{2,1,0:T(8,128)}, u32[]{:S(2)}) copy-start(f32[1,256,128]{2,1,0:T(8,128)} %param.8) | copy-start | bytes 393220
  1.8 1.4 %collective-permute-start = (bf16[4,64,128]{2,1,0:T(8,128)(2,1)S(1)}, bf16[4,64,128]{2,1,0:T(8,128)(2,1)S(1)}, u32[]{:S(2)}, u32[]{:S(2)}) collective-permute-start(bf16[4,64,128]{2,1,0:T(8,128)(2,1)S(1)} %get-tuple-element.25), channel_id=1, source_target_pairs={{0,2},{2,0},{4,6},{6,4},{8,10},{10,8},{12,14},{14,12},{16,18},{18,... | collective-permute-start | bytes 196616 | tf_op jit(solution)/shard_map/ppermute | solution.py:195
  3.2 7.4 %copy-start.4 = (s32[1,8,8]{2,1,0:T(8,128)S(1)}, s32[1,8,8]{2,1,0:T(8,128)}, u32[]{:S(2)}) copy-start(s32[1,8,8]{2,1,0:T(8,128)} %ranks.1) | copy-start | bytes 772
  3.2 7.3 %collective-permute-start.1 = (bf16[2048,128]{1,0:T(8,128)(2,1)S(1)}, bf16[2048,128]{1,0:T(8,128)(2,1)S(1)}, u32[]{:S(2)}, u32[]{:S(2)}) collective-permute-start(bf16[2048,128]{1,0:T(8,128)(2,1)S(1)} %bitcast.7), channel_id=1, source_target_pairs={{0,2},{2,0},{4,6},{6,4},{8,10},{10,8},{12,14},{14,12},{16,18},{18,... | collective-permute-start | bytes 1572872 | tf_op jit(solution)/shard_map/ppermute | solution.py:195
  3.6 8.0 %collective-permute-start.3 = (bf16[64,128]{1,0:T(8,128)(2,1)S(1)}, bf16[64,128]{1,0:T(8,128)(2,1)S(1)}, u32[]{:S(2)}, u32[]{:S(2)}) collective-permute-start(bf16[64,128]{1,0:T(8,128)(2,1)S(1)} %get-tuple-element.26), channel_id=1, source_target_pairs={{0,28},{2,26},{4,24},{6,30},{8,20},{10,18},{12,16},{14,22},{16,12}... | collective-permute-start | bytes 49160 | tf_op jit(solution)/shard_map/ppermute | solution.py:206
  9.3 4.6 %collective-permute-start.4 = (bf16[64,128]{1,0:T(8,128)(2,1)S(1)}, bf16[64,128]{1,0:T(8,128)(2,1)S(1)}, u32[]{:S(2)}, u32[]{:S(2)}) collective-permute-start(bf16[64,128]{1,0:T(8,128)(2,1)S(1)} %get-tuple-element.34), channel_id=1, source_target_pairs={{0,12},{2,22},{4,8},{6,18},{8,4},{10,30},{12,0},{14,26},{16,28},{1... | collective-permute-start | bytes 49160 | tf_op jit(solution)/shard_map/ppermute | solution.py:206
  9.3 4.6 %collective-permute-start.5 = (bf16[64,128]{1,0:T(8,128)(2,1)S(1)}, bf16[64,128]{1,0:T(8,128)(2,1)S(1)}, u32[]{:S(2)}, u32[]{:S(2)}) collective-permute-start(bf16[64,128]{1,0:T(8,128)(2,1)S(1)} %get-tuple-element.35), channel_id=1, source_target_pairs={{0,16},{2,10},{4,20},{6,14},{8,24},{10,2},{12,28},{14,6},{16,0},{1... | collective-permute-start | bytes 49160 | tf_op jit(solution)/shard_map/ppermute | solution.py:206
  9.9 4.1 %collective-permute-start.6 = (bf16[64,128]{1,0:T(8,128)(2,1)S(1)}, bf16[64,128]{1,0:T(8,128)(2,1)S(1)}, u32[]{:S(2)}, u32[]{:S(2)}) collective-permute-start(bf16[64,128]{1,0:T(8,128)(2,1)S(1)} %get-tuple-element.36), channel_id=1, source_target_pairs={{0,0},{2,6},{4,4},{6,2},{8,8},{10,14},{12,12},{14,10},{16,16},{18,... | collective-permute-start | bytes 49160 | tf_op jit(solution)/shard_map/ppermute | solution.py:206
  11.7 2.9 %copy-start.2 = (f32[1,256,128]{2,1,0:T(8,128)S(1)}, f32[1,256,128]{2,1,0:T(8,128)}, u32[]{:S(2)}) copy-start(f32[1,256,128]{2,1,0:T(8,128)} %param.9) | copy-start | bytes 393220
  14.3 8.1 %copy-start = (bf16[1,256,8,128]{3,2,1,0:T(8,128)(2,1)S(1)}, bf16[1,256,8,128]{3,2,1,0:T(8,128)(2,1)}, u32[]{:S(2)}) copy-start(bf16[1,256,8,128]{3,2,1,0:T(8,128)(2,1)} %param.6) | copy-start | bytes 1572868
  14.3 1.8 %collective-permute-start.7 = (f32[2,128,256]{2,1,0:T(8,128)S(1)}, f32[2,128,256]{2,1,0:T(8,128)S(1)}, u32[]{:S(2)}, u32[]{:S(2)}) collective-permute-start(f32[2,128,256]{2,1,0:T(8,128)S(1)} %image.1.here), channel_id=1, source_target_pairs={{0,2},{2,0},{4,6},{6,4},{8,10},{10,8},{12,14},{14,12},{16,18},{18,... | collective-permute-start | bytes 786440 | tf_op jit(solution)/shard_map/ppermute | solution.py:195
  14.6 8.2 %collective-permute-start.2 = (f32[256,128]{1,0:T(8,128)S(1)}, f32[256,128]{1,0:T(8,128)S(1)}, u32[]{:S(2)}, u32[]{:S(2)}) collective-permute-start(f32[256,128]{1,0:T(8,128)S(1)} %bitcast.10), channel_id=1, source_target_pairs={{0,1},{1,0},{2,3},{3,2},{4,5},{5,4},{6,7},{7,6},{8,9},{9,8},{10,11... | collective-permute-start | bytes 393224 | tf_op jit(solution)/shard_map/ppermute | solution.py:262
  16.4 6.5 %collective-permute-start.8 = (bf16[64,128]{1,0:T(8,128)(2,1)S(1)}, bf16[64,128]{1,0:T(8,128)(2,1)S(1)}, u32[]{:S(2)}, u32[]{:S(2)}) collective-permute-start(bf16[64,128]{1,0:T(8,128)(2,1)S(1)} %get-tuple-element.37), channel_id=1, source_target_pairs={{0,28},{2,26},{4,24},{6,30},{8,20},{10,18},{12,16},{14,22},{16,12}... | collective-permute-start | bytes 49160 | tf_op jit(solution)/shard_map/ppermute | solution.py:206
  20.0 4.6 %collective-permute-start.9 = (bf16[64,128]{1,0:T(8,128)(2,1)S(1)}, bf16[64,128]{1,0:T(8,128)(2,1)S(1)}, u32[]{:S(2)}, u32[]{:S(2)}) collective-permute-start(bf16[64,128]{1,0:T(8,128)(2,1)S(1)} %get-tuple-element.40), channel_id=1, source_target_pairs={{0,12},{2,22},{4,8},{6,18},{8,4},{10,30},{12,0},{14,26},{16,28},{1... | collective-permute-start | bytes 49160 | tf_op jit(solution)/shard_map/ppermute | solution.py:206
  20.3 4.6 %collective-permute-start.10 = (bf16[64,128]{1,0:T(8,128)(2,1)S(1)}, bf16[64,128]{1,0:T(8,128)(2,1)S(1)}, u32[]{:S(2)}, u32[]{:S(2)}) collective-permute-start(bf16[64,128]{1,0:T(8,128)(2,1)S(1)} %get-tuple-element.41), channel_id=1, source_target_pairs={{0,16},{2,10},{4,20},{6,14},{8,24},{10,2},{12,28},{14,6},{16,0},{1... | collective-permute-start | bytes 49160 | tf_op jit(solution)/shard_map/ppermute | solution.py:206
  21.8 3.2 %collective-permute-start.11 = (bf16[64,128]{1,0:T(8,128)(2,1)S(1)}, bf16[64,128]{1,0:T(8,128)(2,1)S(1)}, u32[]{:S(2)}, u32[]{:S(2)}) collective-permute-start(bf16[64,128]{1,0:T(8,128)(2,1)S(1)} %get-tuple-element.42), channel_id=1, source_target_pairs={{0,0},{2,6},{4,4},{6,2},{8,8},{10,14},{12,12},{14,10},{16,16},{18,... | collective-permute-start | bytes 49160 | tf_op jit(solution)/shard_map/ppermute | solution.py:206
  25.0 1.3 %collective-permute-start.12 = (bf16[4,64,128]{2,1,0:T(8,128)(2,1)S(1)}, bf16[4,64,128]{2,1,0:T(8,128)(2,1)S(1)}, u32[]{:S(2)}, u32[]{:S(2)}) collective-permute-start(bf16[4,64,128]{2,1,0:T(8,128)(2,1)S(1)} %pack.1.own), channel_id=1, source_target_pairs={{0,2},{2,0},{4,6},{6,4},{8,10},{10,8},{12,14},{14,12},{16,18},{18,... | collective-permute-start | bytes 196616 | tf_op jit(solution)/shard_map/ppermute | solution.py:195
  26.6 4.3 %collective-permute-start.13 = (bf16[128,256]{1,0:T(8,128)(2,1)S(1)}, bf16[128,256]{1,0:T(8,128)(2,1)S(1)}, u32[]{:S(2)}, u32[]{:S(2)}) collective-permute-start(bf16[128,256]{1,0:T(8,128)(2,1)S(1)} %gradient.1.refs_2_), channel_id=1, source_target_pairs={{0,1},{1,0},{2,3},{3,2},{4,5},{5,4},{6,7},{7,6},{8,9},{9,8},{10,11... | collective-permute-start | bytes 196616 | tf_op jit(solution)/shard_map/ppermute | solution.py:291

commit v5 on v3

--- a/solution.py
+++ b/solution.py
@@ -145,32 +145,40 @@
 
 
 def pack_kernel(shifts, sent, *refs):
-    arrived, packed = refs[:-1], refs[-1]
-    for index, block in enumerate(arrived):
-        packed[index] = arrived_block(shifts, index, sent, block)
+    for index, block in enumerate(refs[:-1]):
+        refs[-1][index] = arrived_block(shifts, index, sent, block)
 
 
 def gradient_kernel(shifts, own, mate, factors, gradient, left):
     for blocks, chosen in zip((own, mate), both_shifts(shifts)):
         for index, tile in enumerate(chosen):
             spread_block(blocks[index], left, tile)
-    gradient[...] = times_transposed(left[...], factors[...]).astype(BF16)
+    gradient[...] = times_transposed(factors[...], left[...]).astype(BF16)
 
 
 def thin_out(values):
     return values - jnp.clip(values, -LEVEL, LEVEL)
+
+
+def pair_kernel(here, there, gradient, total, difference):
+    scale = 1.0 / math.sqrt(2)
+    estimate = here[...] - STEP_SIZE * gradient[...].astype(F32)
+    total[...] = (estimate + there[...]) * scale
+    difference[...] = (estimate - there[...]) * scale
+
+
+def shrink_pair_kernel(total, difference, gradient, out):
+    scale = 1.0 / math.sqrt(2)
+    step = (STEP_SIZE * scale) * gradient[...].astype(F32)
+    out[...] = (thin_out(total[...] - step) + thin_out(difference[...] + step)) * scale
 
 
 def shrink_kernel(band, *refs):
     tables, starts, gradients, out = refs[: -2 * band - 1], refs[-2 * band - 1 : -band - 1], refs[-band - 1 : -1], refs[-1]
     estimates = [
-        start[...] - STEP_SIZE * gradient[...].astype(F32).T for start, gradient in zip(starts, gradients)
+        start[...] - STEP_SIZE * gradient[...].astype(F32) for start, gradient in zip(starts, gradients)
     ]
     scale = 1.0 / math.sqrt(band)
-    if band == 2:
-        here, there = estimates
-        out[...] = (thin_out((here + there) * scale) + thin_out((here - there) * scale)) * scale
-        return
     (tables,) = tables
     half = out.shape[1] // 2
     lane = lax.broadcasted_iota(jnp.int32, (1, out.shape[1]), 1)
@@ -213,8 +221,8 @@
     count = lax.axis_size("tile")
     arrived = []
     for index, send in enumerate(sends):
-        partners = [(i, i ^ 2 * shifts[i % 2][index]) for i in range(count)]
-        arrived.append(lax.ppermute(send, "tile", [pair for pair in partners if pair[0] != pair[1]]))
+        pair = [shifts[core][index] or shifts[1 - core][index] for core in range(2)]
+        arrived.append(lax.ppermute(send, "tile", [(i, i ^ 2 * pair[i % 2]) for i in range(count)]))
     arrived[0] = after(arrived[0], *beside)
     (own,) = [send for index, send in enumerate(sends) if 0 in (shifts[0][index], shifts[1][index])]
     return [own, *arrived]
@@ -294,7 +302,7 @@
     (gradient,) = call(
         functools.partial(gradient_kernel, shifts),
         "gradient",
-        [shape(sources, rows)],
+        [shape(rows, sources)],
         [own, to_mate(own), right],
         [spread],
         flops,
@@ -302,14 +310,17 @@
     gradients = [gradient]
     for shift in range(1, band):
         gradients.append(lax.ppermute(gradient, "freq", [(f, (f - shift) % band) for f in range(band)]))
-    inputs, spaces = [*starts, *gradients], []
-    if band > 2:
-        bands = jnp.arange(band, dtype=jnp.int32)
-        phases = (bands[:, None] + lax.axis_index("freq")) * bands[None, :] % band
-        phases = (2.0 * math.pi / band) * phases.astype(F32)
-        inputs, spaces = [jnp.stack([jnp.cos(phases), jnp.sin(phases)]), *inputs], [pltpu.SMEM]
+    result = shape(rows, sources, dtype=F32)
+    if band == 2:
+        halves = call(pair_kernel, "pair", [result] * 2, [*starts, gradient])
+        (estimate,) = call(shrink_pair_kernel, "shrink", [result], [*halves, gradients[1]])
+        return estimate[None]
+    bands = jnp.arange(band, dtype=jnp.int32)
+    phases = (bands[:, None] + lax.axis_index("freq")) * bands[None, :] % band
+    phases = (2.0 * math.pi / band) * phases.astype(F32)
+    tables = jnp.stack([jnp.cos(phases), jnp.sin(phases)])
     (estimate,) = call(
-        functools.partial(shrink_kernel, band), "shrink", [shape(rows, sources, dtype=F32)], inputs, spaces=spaces
+        functools.partial(shrink_kernel, band), "shrink", [result], [tables, *starts, *gradients], spaces=[pltpu.SMEM]
     )
     return estimate[None]
 

time: 33.9 us -> 34.4 us (1.015)
  waiting for transfers between devices: 10.2 us -> 10.7 us
    ppermute x8, starting transfers between devices: 13 us -> 14.3 us  [exchange(): lax.ppermute(send, 'tile', [(i, i ^ 2 * pair[i % 2]) for i in range(count)])]
    ppermute x4, starting transfers between devices: 2.35 us -> 1.08 us  [to_mate(): lax.ppermute(value, 'tile', [(i, i ^ 1) for i in range(lax.axis_size('til...]
    ppermute x8, waiting for transfers between devices: 5.23 us -> 5.73 us  [exchange(): lax.ppermute(send, 'tile', [(i, i ^ 2 * pair[i % 2]) for i in range(count)])]
    pallas_call x9 -> x10, Pallas kernels: 4.92 us -> 4.91 us  [call(): pl.pallas_call(kernel, out_shape=outs, in_specs=[pl.BlockSpec(memory_spac...]
  transfers between devices with their start and end apart: 14 -> 14, of which waited for: 7 -> 9; matrix products, arithmetic and copies ran while one was open for 0% -> 0% of each run, Pallas kernels for 5% -> 5%
where the time goes in v5:
time: 34.4 us; the launch traced here: 34.2 us
  starting transfers between devices  18.5 us (54%)
  waiting for transfers between devices  10.7 us (31%)
  Pallas kernels  4.91 us (14%)
    ppermute x8, starting transfers between devices, exchange(): lax.ppermute(send, 'tile', [(i, i ^ 2 * pair[i % 2]) for i in range(count)])  14.3 us
    ppermute x8, waiting for transfers between devices, exchange(): lax.ppermute(send, 'tile', [(i, i ^ 2 * pair[i % 2]) for i in range(count)])  5.73 us
    pallas_call x10, Pallas kernels, call(): pl.pallas_call(kernel, out_shape=outs, in_specs=[pl.BlockSpec(memory_spac...  4.91 us
    ppermute x1, waiting for transfers between devices, body(): lax.ppermute(gradient, 'freq', [(f, (f - shift) % band) for f in range(ba...  2.78 us
    ppermute x4, waiting for transfers between devices, to_mate(): lax.ppermute(value, 'tile', [(i, i ^ 1) for i in range(lax.axis_size('til...  2.15 us
    ppermute x1, starting transfers between devices, body(): lax.ppermute(early, 'freq', [(f, (f - shift) % band) for f in range(band)])  1.58 us
    ppermute x1, starting transfers between devices, body(): lax.ppermute(gradient, 'freq', [(f, (f - shift) % band) for f in range(ba...  1.51 us
    ppermute x4, starting transfers between devices, to_mate(): lax.ppermute(value, 'tile', [(i, i ^ 1) for i in range(lax.axis_size('til...  1.08 us
  transfers between devices with their start and end apart: 14, of which 9 were waited for; matrix products, arithmetic and copies ran while one was open for 0% of the time, Pallas kernels for 5%

profile of v5, /device:TPU:0, one launch (start us, length us, event | category | flops | bytes accessed | tf_op | source)
XLA Modules:
  0.0 34.2 jit_solution(1539689648806383572)
XLA Ops:
  0.0 1.7 %forward.1 = (bf16[4,64,128]{2,1,0:T(8,128)(2,1)S(1)}, bf16[4,64,128]{2,1,0:T(8,128)(2,1)S(1)}) custom-call(f32[256,128]{1,0:T(8,128)} %bitcast.7, bf16[2048,128]{1,0:T(8,128)(2,1)} %bitcast.5), custom_call_target="tpu_custom_call" | custom-call | flops 67108864 | bytes 786432 | tf_op jit(solution)/shard_map/forward/pallas_call | solution.py:200
  1.7 0.0 copy-start.3
  1.8 0.5 %collective-permute-start = (bf16[4,64,128]{2,1,0:T(8,128)(2,1)S(1)}, bf16[4,64,128]{2,1,0:T(8,128)(2,1)S(1)}, u32[]{:S(2)}, u32[]{:S(2)}) collective-permute-start(bf16[4,64,128]{2,1,0:T(8,128)(2,1)S(1)} %get-tuple-element.27), channel_id=1, source_target_pairs={{0,2},{2,0},{4,6},{6,4},{8,10},{10,8},{12,14},{14,12},{16,18},{18,... | collective-permute-start | bytes 196616 | tf_op jit(solution)/shard_map/ppermute | solution.py:213
  2.3 0.9 %collective-permute-done.arrived = bf16[4,64,128]{2,1,0:T(8,128)(2,1)S(1)} collective-permute-done((bf16[4,64,128]{2,1,0:T(8,128)(2,1)S(1)}, bf16[4,64,128]{2,1,0:T(8,128)(2,1)S(1)}, u32[]{:S(2)}, u32[]{:S(2)}) %collective-permute-start) | collective-permute-done | bytes 65568 | tf_op jit(solution)/shard_map/ppermute | solution.py:213
  3.2 0.0 copy-start.4
  3.2 0.4 %collective-permute-start.1 = (bf16[2048,128]{1,0:T(8,128)(2,1)S(1)}, bf16[2048,128]{1,0:T(8,128)(2,1)S(1)}, u32[]{:S(2)}, u32[]{:S(2)}) collective-permute-start(bf16[2048,128]{1,0:T(8,128)(2,1)S(1)} %bitcast.10), channel_id=1, source_target_pairs={{0,2},{2,0},{4,6},{6,4},{8,10},{10,8},{12,14},{14,12},{16,18},{18,... | collective-permute-start | bytes 1572872 | tf_op jit(solution)/shard_map/ppermute | solution.py:213
  3.6 5.7 %collective-permute-start.3 = (bf16[64,128]{1,0:T(8,128)(2,1)S(1)}, bf16[64,128]{1,0:T(8,128)(2,1)S(1)}, u32[]{:S(2)}, u32[]{:S(2)}) collective-permute-start(bf16[64,128]{1,0:T(8,128)(2,1)S(1)} %get-tuple-element.28), channel_id=1, source_target_pairs={{0,28},{2,26},{4,24},{6,30},{8,20},{10,18},{12,16},{14,22},{16,12}... | collective-permute-start | bytes 49160 | tf_op jit(solution)/shard_map/ppermute | solution.py:225
  9.3 0.5 %collective-permute-start.6 = (bf16[64,128]{1,0:T(8,128)(2,1)S(1)}, bf16[64,128]{1,0:T(8,128)(2,1)S(1)}, u32[]{:S(2)}, u32[]{:S(2)}) collective-permute-start(bf16[64,128]{1,0:T(8,128)(2,1)S(1)} %get-tuple-element.33.sent), channel_id=1, source_target_pairs={{0,4},{2,6},{4,0},{6,2},{8,12},{10,14},{12,8},{14,10},{16,20},{18,... | collective-permute-start | bytes 49160 | tf_op jit(solution)/shard_map/ppermute | solution.py:225
  9.9 0.5 %collective-permute-start.4 = (bf16[64,128]{1,0:T(8,128)(2,1)S(1)}, bf16[64,128]{1,0:T(8,128)(2,1)S(1)}, u32[]{:S(2)}, u32[]{:S(2)}) collective-permute-start(bf16[64,128]{1,0:T(8,128)(2,1)S(1)} %get-tuple-element.37), channel_id=1, source_target_pairs={{0,12},{2,22},{4,8},{6,18},{8,4},{10,30},{12,0},{14,26},{16,28},{1... | collective-permute-start | bytes 49160 | tf_op jit(solution)/shard_map/ppermute | solution.py:225
  10.3 1.2 %collective-permute-start.5 = (bf16[64,128]{1,0:T(8,128)(2,1)S(1)}, bf16[64,128]{1,0:T(8,128)(2,1)S(1)}, u32[]{:S(2)}, u32[]{:S(2)}) collective-permute-start(bf16[64,128]{1,0:T(8,128)(2,1)S(1)} %get-tuple-element.38), channel_id=1, source_target_pairs={{0,16},{2,10},{4,20},{6,14},{8,24},{10,2},{12,28},{14,6},{16,0},{1... | collective-permute-start | bytes 49160 | tf_op jit(solution)/shard_map/ppermute | solution.py:225
  11.6 1.1 %rows.1 = (bf16[256,512]{1,0:T(8,128)(2,1)S(1)}, bf16[256,512]{1,0:T(8,128)(2,1)S(1)}, f32[128,256]{1,0:T(8,128)S(1)}) custom-call(s32[1,8,8]{2,1,0:T(8,128)S(1)} %copy-done.4, bf16[2048,128]{1,0:T(8,128)(2,1)S(1)} %bitcast.11, bf16[2048,128]{1,0:T(8,128)(2,1)S(1)} %collective-permute-done.1.mate, f32[256,128]{1,0:T(8,128)S(1)} %bitcast.12), custom_call_target="tpu_custom_call" | custom-call | bytes 1835264 | tf_op jit(solution)/shard_map/rows/pallas_call | solution.py:200
  12.7 0.4 %collective-permute-done.6.refs_3_ = bf16[64,128]{1,0:T(8,128)(2,1)S(1)} collective-permute-done((bf16[64,128]{1,0:T(8,128)(2,1)S(1)}, bf16[64,128]{1,0:T(8,128)(2,1)S(1)}, u32[]{:S(2)}, u32[]{:S(2)}) %collective-permute-start.6) | collective-permute-done | bytes 16416 | tf_op jit(solution)/shard_map/ppermute | solution.py:225
  13.1 1.4 %collective-permute-done.4.refs_1_ = bf16[64,128]{1,0:T(8,128)(2,1)S(1)} collective-permute-done((bf16[64,128]{1,0:T(8,128)(2,1)S(1)}, bf16[64,128]{1,0:T(8,128)(2,1)S(1)}, u32[]{:S(2)}, u32[]{:S(2)}) %collective-permute-start.4) | collective-permute-done | bytes 16416 | tf_op jit(solution)/shard_map/ppermute | solution.py:225
  14.5 0.5 %collective-permute-done.5.refs_2_ = bf16[64,128]{1,0:T(8,128)(2,1)S(1)} collective-permute-done((bf16[64,128]{1,0:T(8,128)(2,1)S(1)}, bf16[64,128]{1,0:T(8,128)(2,1)S(1)}, u32[]{:S(2)}, u32[]{:S(2)}) %collective-permute-start.5) | collective-permute-done | bytes 16416 | tf_op jit(solution)/shard_map/ppermute | solution.py:225
  15.0 0.3 image.1.here
  15.3 0.1 collective-permute-start.7
  15.4 1.6 %collective-permute-start.2 = (f32[256,128]{1,0:T(8,128)S(1)}, f32[256,128]{1,0:T(8,128)S(1)}, u32[]{:S(2)}, u32[]{:S(2)}) collective-permute-start(f32[256,128]{1,0:T(8,128)S(1)} %bitcast.8), channel_id=1, source_target_pairs={{0,1},{1,0},{2,3},{3,2},{4,5},{5,4},{6,7},{7,6},{8,9},{9,8},{10,11... | collective-permute-start | bytes 393224 | tf_op jit(solution)/shard_map/ppermute | solution.py:283
  17.0 0.3 back.1
  17.3 2.0 %collective-permute-start.8 = (bf16[64,128]{1,0:T(8,128)(2,1)S(1)}, bf16[64,128]{1,0:T(8,128)(2,1)S(1)}, u32[]{:S(2)}, u32[]{:S(2)}) collective-permute-start(bf16[64,128]{1,0:T(8,128)(2,1)S(1)} %get-tuple-element.40), channel_id=1, source_target_pairs={{0,28},{2,26},{4,24},{6,30},{8,20},{10,18},{12,16},{14,22},{16,12}... | collective-permute-start | bytes 49160 | tf_op jit(solution)/shard_map/ppermute | solution.py:225
  19.4 1.9 %collective-permute-start.10 = (bf16[64,128]{1,0:T(8,128)(2,1)S(1)}, bf16[64,128]{1,0:T(8,128)(2,1)S(1)}, u32[]{:S(2)}, u32[]{:S(2)}) collective-permute-start(bf16[64,128]{1,0:T(8,128)(2,1)S(1)} %get-tuple-element.44), channel_id=1, source_target_pairs={{0,16},{2,10},{4,20},{6,14},{8,24},{10,2},{12,28},{14,6},{16,0},{1... | collective-permute-start | bytes 49160 | tf_op jit(solution)/shard_map/ppermute | solution.py:225
  21.3 1.5 %collective-permute-start.11 = (bf16[64,128]{1,0:T(8,128)(2,1)S(1)}, bf16[64,128]{1,0:T(8,128)(2,1)S(1)}, u32[]{:S(2)}, u32[]{:S(2)}) collective-permute-start(bf16[64,128]{1,0:T(8,128)(2,1)S(1)} %get-tuple-element.39.sent), channel_id=1, source_target_pairs={{0,4},{2,6},{4,0},{6,2},{8,12},{10,14},{12,8},{14,10},{16,20},{18,... | collective-permute-start | bytes 49160 | tf_op jit(solution)/shard_map/ppermute | solution.py:225
  22.8 0.9 %collective-permute-start.9 = (bf16[64,128]{1,0:T(8,128)(2,1)S(1)}, bf16[64,128]{1,0:T(8,128)(2,1)S(1)}, u32[]{:S(2)}, u32[]{:S(2)}) collective-permute-start(bf16[64,128]{1,0:T(8,128)(2,1)S(1)} %get-tuple-element.43), channel_id=1, source_target_pairs={{0,12},{2,22},{4,8},{6,18},{8,4},{10,30},{12,0},{14,26},{16,28},{1... | collective-permute-start | bytes 49160 | tf_op jit(solution)/shard_map/ppermute | solution.py:225
  23.7 0.3 columns.1.factors
  24.0 0.2 collective-permute-done.10.refs_2_
  24.2 0.9 %collective-permute-done.11.refs_3_ = bf16[64,128]{1,0:T(8,128)(2,1)S(1)} collective-permute-done((bf16[64,128]{1,0:T(8,128)(2,1)S(1)}, bf16[64,128]{1,0:T(8,128)(2,1)S(1)}, u32[]{:S(2)}, u32[]{:S(2)}) %collective-permute-start.11) | collective-permute-done | bytes 16416 | tf_op jit(solution)/shard_map/ppermute | solution.py:225
  25.0 2.4 %collective-permute-done.9.refs_1_ = bf16[64,128]{1,0:T(8,128)(2,1)S(1)} collective-permute-done((bf16[64,128]{1,0:T(8,128)(2,1)S(1)}, bf16[64,128]{1,0:T(8,128)(2,1)S(1)}, u32[]{:S(2)}, u32[]{:S(2)}) %collective-permute-start.9) | collective-permute-done | bytes 16416 | tf_op jit(solution)/shard_map/ppermute | solution.py:225
  27.5 0.1 collective-permute-start.12
  27.5 1.2 %collective-permute-done.12.mate = bf16[4,64,128]{2,1,0:T(8,128)(2,1)S(1)} collective-permute-done((bf16[4,64,128]{2,1,0:T(8,128)(2,1)S(1)}, bf16[4,64,128]{2,1,0:T(8,128)(2,1)S(1)}, u32[]{:S(2)}, u32[]{:S(2)}) %collective-permute-start.12) | collective-permute-done | bytes 65568 | tf_op jit(solution)/shard_map/ppermute | solution.py:213
  28.8 0.4 %gradient.1 = bf16[256,128]{1,0:T(8,128)(2,1)S(1)} custom-call(bf16[4,64,128]{2,1,0:T(8,128)(2,1)S(1)} %pack.1.own, bf16[4,64,128]{2,1,0:T(8,128)(2,1)S(1)} %collective-permute-done.12.mate, bf16[256,1024]{1,0:T(8,128)(2,1)S(1)} %columns.1.factors), custom_call_target="tpu_custom_call" | custom-call | flops 67108864 | bytes 720896 | tf_op jit(solution)/shard_map/gradient/pallas_call | solution.py:200
  29.2 1.5 %collective-permute-start.13 = (bf16[256,128]{1,0:T(8,128)(2,1)S(1)}, bf16[256,128]{1,0:T(8,128)(2,1)S(1)}, u32[]{:S(2)}, u32[]{:S(2)}) collective-permute-start(bf16[256,128]{1,0:T(8,128)(2,1)S(1)} %gradient.1), channel_id=1, source_target_pairs={{0,1},{1,0},{2,3},{3,2},{4,5},{5,4},{6,7},{7,6},{8,9},{9,8},{10,11... | collective-permute-start | bytes 196616 | tf_op jit(solution)/shard_map/ppermute | solution.py:312
  30.7 2.8 %collective-permute-done.13.gradient = bf16[256,128]{1,0:T(8,128)(2,1)S(1)} collective-permute-done((bf16[256,128]{1,0:T(8,128)(2,1)S(1)}, bf16[256,128]{1,0:T(8,128)(2,1)S(1)}, u32[]{:S(2)}, u32[]{:S(2)}) %collective-permute-start.13) | collective-permute-done | bytes 65568 | tf_op jit(solution)/shard_map/ppermute | solution.py:312
  33.5 0.7 %shrink.1 = f32[256,128]{1,0:T(8,128)} custom-call(f32[256,128]{1,0:T(8,128)S(1)} %get-tuple-element.45.total, f32[256,128]{1,0:T(8,128)S(1)} %get-tuple-element.46.difference, bf16[256,128]{1,0:T(8,128)(2,1)S(1)} %collective-permute-done.13.gradient), custom_call_target="tpu_custom_call" | custom-call | bytes 458752 | tf_op jit(solution)/shard_map/shrink/pallas_call | solution.py:200
  (16 shorter events, 0.1 us)
Async XLA Ops:
  0.0 3.2 %copy-start.2 = (bf16[1,256,8,128]{3,2,1,0:T(8,128)(2,1)S(1)}, bf16[1,256,8,128]{3,2,1,0:T(8,128)(2,1)}, u32[]{:S(2)}) copy-start(bf16[1,256,8,128]{3,2,1,0:T(8,128)(2,1)} %param.5) | copy-start | bytes 1572868
  1.7 9.8 %copy-start.3 = (f32[1,256,128]{2,1,0:T(8,128)S(1)}, f32[1,256,128]{2,1,0:T(8,128)}, u32[]{:S(2)}) copy-start(f32[1,256,128]{2,1,0:T(8,128)} %param.8) | copy-start | bytes 393220
  1.8 1.4 %collective-permute-start = (bf16[4,64,128]{2,1,0:T(8,128)(2,1)S(1)}, bf16[4,64,128]{2,1,0:T(8,128)(2,1)S(1)}, u32[]{:S(2)}, u32[]{:S(2)}) collective-permute-start(bf16[4,64,128]{2,1,0:T(8,128)(2,1)S(1)} %get-tuple-element.27), channel_id=1, source_target_pairs={{0,2},{2,0},{4,6},{6,4},{8,10},{10,8},{12,14},{14,12},{16,18},{18,... | collective-permute-start | bytes 196616 | tf_op jit(solution)/shard_map/ppermute | solution.py:213
  3.2 8.4 %copy-start.4 = (s32[1,8,8]{2,1,0:T(8,128)S(1)}, s32[1,8,8]{2,1,0:T(8,128)}, u32[]{:S(2)}) copy-start(s32[1,8,8]{2,1,0:T(8,128)} %ranks.1) | copy-start | bytes 772
  3.2 8.4 %collective-permute-start.1 = (bf16[2048,128]{1,0:T(8,128)(2,1)S(1)}, bf16[2048,128]{1,0:T(8,128)(2,1)S(1)}, u32[]{:S(2)}, u32[]{:S(2)}) collective-permute-start(bf16[2048,128]{1,0:T(8,128)(2,1)S(1)} %bitcast.10), channel_id=1, source_target_pairs={{0,2},{2,0},{4,6},{6,4},{8,10},{10,8},{12,14},{14,12},{16,18},{18,... | collective-permute-start | bytes 1572872 | tf_op jit(solution)/shard_map/ppermute | solution.py:213
  3.6 9.0 %collective-permute-start.3 = (bf16[64,128]{1,0:T(8,128)(2,1)S(1)}, bf16[64,128]{1,0:T(8,128)(2,1)S(1)}, u32[]{:S(2)}, u32[]{:S(2)}) collective-permute-start(bf16[64,128]{1,0:T(8,128)(2,1)S(1)} %get-tuple-element.28), channel_id=1, source_target_pairs={{0,28},{2,26},{4,24},{6,30},{8,20},{10,18},{12,16},{14,22},{16,12}... | collective-permute-start | bytes 49160 | tf_op jit(solution)/shard_map/ppermute | solution.py:225
  9.3 3.7 %collective-permute-start.6 = (bf16[64,128]{1,0:T(8,128)(2,1)S(1)}, bf16[64,128]{1,0:T(8,128)(2,1)S(1)}, u32[]{:S(2)}, u32[]{:S(2)}) collective-permute-start(bf16[64,128]{1,0:T(8,128)(2,1)S(1)} %get-tuple-element.33.sent), channel_id=1, source_target_pairs={{0,4},{2,6},{4,0},{6,2},{8,12},{10,14},{12,8},{14,10},{16,20},{18,... | collective-permute-start | bytes 49160 | tf_op jit(solution)/shard_map/ppermute | solution.py:225
  9.9 4.6 %collective-permute-start.4 = (bf16[64,128]{1,0:T(8,128)(2,1)S(1)}, bf16[64,128]{1,0:T(8,128)(2,1)S(1)}, u32[]{:S(2)}, u32[]{:S(2)}) collective-permute-start(bf16[64,128]{1,0:T(8,128)(2,1)S(1)} %get-tuple-element.37), channel_id=1, source_target_pairs={{0,12},{2,22},{4,8},{6,18},{8,4},{10,30},{12,0},{14,26},{16,28},{1... | collective-permute-start | bytes 49160 | tf_op jit(solution)/shard_map/ppermute | solution.py:225
  10.3 4.6 %collective-permute-start.5 = (bf16[64,128]{1,0:T(8,128)(2,1)S(1)}, bf16[64,128]{1,0:T(8,128)(2,1)S(1)}, u32[]{:S(2)}, u32[]{:S(2)}) collective-permute-start(bf16[64,128]{1,0:T(8,128)(2,1)S(1)} %get-tuple-element.38), channel_id=1, source_target_pairs={{0,16},{2,10},{4,20},{6,14},{8,24},{10,2},{12,28},{14,6},{16,0},{1... | collective-permute-start | bytes 49160 | tf_op jit(solution)/shard_map/ppermute | solution.py:225
  12.7 2.7 %copy-start.1 = (f32[1,256,128]{2,1,0:T(8,128)S(1)}, f32[1,256,128]{2,1,0:T(8,128)}, u32[]{:S(2)}) copy-start(f32[1,256,128]{2,1,0:T(8,128)} %param.9) | copy-start | bytes 393220
  15.3 8.4 %copy-start = (bf16[1,256,8,128]{3,2,1,0:T(8,128)(2,1)S(1)}, bf16[1,256,8,128]{3,2,1,0:T(8,128)(2,1)}, u32[]{:S(2)}) copy-start(bf16[1,256,8,128]{3,2,1,0:T(8,128)(2,1)} %param.6) | copy-start | bytes 1572868
  15.3 1.7 %collective-permute-start.7 = (f32[2,128,256]{2,1,0:T(8,128)S(1)}, f32[2,128,256]{2,1,0:T(8,128)S(1)}, u32[]{:S(2)}, u32[]{:S(2)}) collective-permute-start(f32[2,128,256]{2,1,0:T(8,128)S(1)} %image.1.here), channel_id=1, source_target_pairs={{0,2},{2,0},{4,6},{6,4},{8,10},{10,8},{12,14},{14,12},{16,18},{18,... | collective-permute-start | bytes 786440 | tf_op jit(solution)/shard_map/ppermute | solution.py:213
  15.4 8.6 %collective-permute-start.2 = (f32[256,128]{1,0:T(8,128)S(1)}, f32[256,128]{1,0:T(8,128)S(1)}, u32[]{:S(2)}, u32[]{:S(2)}) collective-permute-start(f32[256,128]{1,0:T(8,128)S(1)} %bitcast.8), channel_id=1, source_target_pairs={{0,1},{1,0},{2,3},{3,2},{4,5},{5,4},{6,7},{7,6},{8,9},{9,8},{10,11... | collective-permute-start | bytes 393224 | tf_op jit(solution)/shard_map/ppermute | solution.py:283
  17.3 6.7 %collective-permute-start.8 = (bf16[64,128]{1,0:T(8,128)(2,1)S(1)}, bf16[64,128]{1,0:T(8,128)(2,1)S(1)}, u32[]{:S(2)}, u32[]{:S(2)}) collective-permute-start(bf16[64,128]{1,0:T(8,128)(2,1)S(1)} %get-tuple-element.40), channel_id=1, source_target_pairs={{0,28},{2,26},{4,24},{6,30},{8,20},{10,18},{12,16},{14,22},{16,12}... | collective-permute-start | bytes 49160 | tf_op jit(solution)/shard_map/ppermute | solution.py:225
  19.4 4.8 %collective-permute-start.10 = (bf16[64,128]{1,0:T(8,128)(2,1)S(1)}, bf16[64,128]{1,0:T(8,128)(2,1)S(1)}, u32[]{:S(2)}, u32[]{:S(2)}) collective-permute-start(bf16[64,128]{1,0:T(8,128)(2,1)S(1)} %get-tuple-element.44), channel_id=1, source_target_pairs={{0,16},{2,10},{4,20},{6,14},{8,24},{10,2},{12,28},{14,6},{16,0},{1... | collective-permute-start | bytes 49160 | tf_op jit(solution)/shard_map/ppermute | solution.py:225
  21.3 3.7 %collective-permute-start.11 = (bf16[64,128]{1,0:T(8,128)(2,1)S(1)}, bf16[64,128]{1,0:T(8,128)(2,1)S(1)}, u32[]{:S(2)}, u32[]{:S(2)}) collective-permute-start(bf16[64,128]{1,0:T(8,128)(2,1)S(1)} %get-tuple-element.39.sent), channel_id=1, source_target_pairs={{0,4},{2,6},{4,0},{6,2},{8,12},{10,14},{12,8},{14,10},{16,20},{18,... | collective-permute-start | bytes 49160 | tf_op jit(solution)/shard_map/ppermute | solution.py:225
  22.8 4.6 %collective-permute-start.9 = (bf16[64,128]{1,0:T(8,128)(2,1)S(1)}, bf16[64,128]{1,0:T(8,128)(2,1)S(1)}, u32[]{:S(2)}, u32[]{:S(2)}) collective-permute-start(bf16[64,128]{1,0:T(8,128)(2,1)S(1)} %get-tuple-element.43), channel_id=1, source_target_pairs={{0,12},{2,22},{4,8},{6,18},{8,4},{10,30},{12,0},{14,26},{16,28},{1... | collective-permute-start | bytes 49160 | tf_op jit(solution)/shard_map/ppermute | solution.py:225
  27.5 1.3 %collective-permute-start.12 = (bf16[4,64,128]{2,1,0:T(8,128)(2,1)S(1)}, bf16[4,64,128]{2,1,0:T(8,128)(2,1)S(1)}, u32[]{:S(2)}, u32[]{:S(2)}) collective-permute-start(bf16[4,64,128]{2,1,0:T(8,128)(2,1)S(1)} %pack.1.own), channel_id=1, source_target_pairs={{0,2},{2,0},{4,6},{6,4},{8,10},{10,8},{12,14},{14,12},{16,18},{18,... | collective-permute-start | bytes 196616 | tf_op jit(solution)/shard_map/ppermute | solution.py:213
  29.2 4.3 %collective-permute-start.13 = (bf16[256,128]{1,0:T(8,128)(2,1)S(1)}, bf16[256,128]{1,0:T(8,128)(2,1)S(1)}, u32[]{:S(2)}, u32[]{:S(2)}) collective-permute-start(bf16[256,128]{1,0:T(8,128)(2,1)S(1)} %gradient.1), channel_id=1, source_target_pairs={{0,1},{1,0},{2,3},{3,2},{4,5},{5,4},{6,7},{7,6},{8,9},{9,8},{10,11... | collective-permute-start | bytes 196616 | tf_op jit(solution)/shard_map/ppermute | solution.py:312

commit v6 on v5

--- a/solution.py
+++ b/solution.py
@@ -21,6 +21,11 @@
 def shifts_of(chips):
     far_first = sorted(range(chips), key=lambda shift: (-shift.bit_count(), -shift))
     return [[far_first[at] for at in range(chips) if (at + 1) // 2 % 2 == core] for core in range(2)]
+
+
+def own_index(shifts):
+    (index,) = [index for index, pair in enumerate(zip(*shifts)) if 0 in pair]
+    return index
 
 
 def place():
@@ -107,9 +112,11 @@
             out[index] = adjoint_block(product, tile)
 
 
-def add_kernel(keep, arrived, *outs):
+def add_kernel(shifts, keep, arrived, *outs):
+    outs, own = outs[:-1], outs[-1]
     for index, out in enumerate(outs):
         out[...] = (keep[index].astype(F32) + arrived[index].astype(F32)).astype(BF16)
+    own[...] = outs[own_index(shifts)][...]
 
 
 def rows_kernel(shifts, ranks, own, mate, observed, own_out, mate_out, turned, wide):
@@ -134,14 +141,15 @@
     misfit[1] = times_transposed(left[...], mate[...])
 
 
-def back_kernel(here, there, own, mate, *refs):
-    outs, products = refs[:-1], refs[-1]
+def back_kernel(shifts, here, there, own, mate, *refs):
+    outs, kept, products = refs[:-2], refs[-2], refs[-1]
     for rows, factors in ((0, own), (1, mate)):
         misfit = (here[rows] + there[1 - rows]).astype(BF16)
         products[rows] = jnp.dot(misfit, factors[...], preferred_element_type=F32)
     for index, out in enumerate(outs):
         parts = [adjoint_block(products.at[rows], index).astype(F32) for rows in range(2)]
         out[...] = (parts[0] + parts[1]).astype(BF16)
+    kept[...] = outs[own_index(shifts)][...]
 
 
 def pack_kernel(shifts, sent, *refs):
@@ -220,12 +228,11 @@
 def exchange(sends, shifts, beside):
     count = lax.axis_size("tile")
     arrived = []
-    for index, send in enumerate(sends):
+    for index, send in enumerate(sends[:-1]):
         pair = [shifts[core][index] or shifts[1 - core][index] for core in range(2)]
         arrived.append(lax.ppermute(send, "tile", [(i, i ^ 2 * pair[i % 2]) for i in range(count)]))
     arrived[0] = after(arrived[0], *beside)
-    (own,) = [send for index, send in enumerate(sends) if 0 in (shifts[0][index], shifts[1][index])]
-    return [own, *arrived]
+    return [sends[-1], *arrived]
 
 
 def body(u_factors, v_factors, ranks, observed, start):
@@ -267,7 +274,7 @@
         [pltpu.HBM] * 2,
         FIRST_LIMIT,
     )
-    sends = call(add_kernel, "add", [block] * members, [keep, to_mate(give)])
+    sends = call(functools.partial(add_kernel, shifts), "add", [block] * (members + 1), [keep, to_mate(give)])
     left_rows = after(left_rows, sends[0])
     own_left, mate_left, turned = call(
         functools.partial(rows_kernel, shifts),
@@ -290,9 +297,9 @@
         flops,
     )
     sends = call(
-        back_kernel,
+        functools.partial(back_kernel, shifts),
         "back",
-        [block] * members,
+        [block] * (members + 1),
         [misfit, to_mate(misfit), own_left, mate_left],
         [pltpu.VMEM((2, sources, members * width), F32)],
         flops,

time: 34.4 us -> 33 us (0.959)
  waiting for transfers between devices: 10.7 us -> 8.97 us
  local copies, waits for them, and re-layouts: 0.03 us -> 0.5 us
    ppermute x8, waiting for transfers between devices: 5.73 us -> 3.62 us  [exchange(): lax.ppermute(send, 'tile', [(i, i ^ 2 * pair[i % 2]) for i in range(count)])]
    unnamed x10, local copies, waits for them, and re-layouts: 0.03 us -> 0.5 us
    ppermute x1, starting transfers between devices: 1.51 us -> 1.09 us  [body(): lax.ppermute(gradient, 'freq', [(f, (f - shift) % band) for f in range(ba...]
    ppermute x1, waiting for transfers between devices: 2.78 us -> 3.2 us  [body(): lax.ppermute(gradient, 'freq', [(f, (f - shift) % band) for f in range(ba...]
  transfers between devices with their start and end apart: 14 -> 14, of which waited for: 9 -> 5; matrix products, arithmetic and copies ran while one was open for 0% -> 0% of each run, Pallas kernels for 5% -> 5%
where the time goes in v6:
time: 33 us; the launch traced here: 32.9 us
  starting transfers between devices  18.3 us (55%)
  waiting for transfers between devices  8.97 us (27%)
  Pallas kernels  4.94 us (15%)
  local copies, waits for them, and re-layouts  0.5 us (2%)
    ppermute x8, starting transfers between devices, exchange(): lax.ppermute(send, 'tile', [(i, i ^ 2 * pair[i % 2]) for i in range(count)])  14.6 us
    pallas_call x10, Pallas kernels, call(): pl.pallas_call(kernel, out_shape=outs, in_specs=[pl.BlockSpec(memory_spac...  4.94 us
    ppermute x8, waiting for transfers between devices, exchange(): lax.ppermute(send, 'tile', [(i, i ^ 2 * pair[i % 2]) for i in range(count)])  3.62 us
    ppermute x1, waiting for transfers between devices, body(): lax.ppermute(gradient, 'freq', [(f, (f - shift) % band) for f in range(ba...  3.2 us
    ppermute x4, waiting for transfers between devices, to_mate(): lax.ppermute(value, 'tile', [(i, i ^ 1) for i in range(lax.axis_size('til...  2.15 us
    ppermute x1, starting transfers between devices, body(): lax.ppermute(early, 'freq', [(f, (f - shift) % band) for f in range(band)])  1.56 us
    ppermute x1, starting transfers between devices, body(): lax.ppermute(gradient, 'freq', [(f, (f - shift) % band) for f in range(ba...  1.09 us
    ppermute x4, starting transfers between devices, to_mate(): lax.ppermute(value, 'tile', [(i, i ^ 1) for i in range(lax.axis_size('til...  1.08 us
  transfers between devices with their start and end apart: 14, of which 5 were waited for; matrix products, arithmetic and copies ran while one was open for 0% of the time, Pallas kernels for 5%

profile of v6, /device:TPU:0, one launch (start us, length us, event | category | flops | bytes accessed | tf_op | source)
XLA Modules:
  0.0 32.9 jit_solution(234524561123896990)
XLA Ops:
  0.0 1.7 %forward.1 = (bf16[4,64,128]{2,1,0:T(8,128)(2,1)S(1)}, bf16[4,64,128]{2,1,0:T(8,128)(2,1)S(1)}) custom-call(f32[256,128]{1,0:T(8,128)} %bitcast.7, bf16[2048,128]{1,0:T(8,128)(2,1)} %bitcast.5), custom_call_target="tpu_custom_call" | custom-call | flops 67108864 | bytes 786432 | tf_op jit(solution)/shard_map/forward/pallas_call | solution.py:208
  1.7 0.0 copy-start.3
  1.8 0.5 %collective-permute-start = (bf16[4,64,128]{2,1,0:T(8,128)(2,1)S(1)}, bf16[4,64,128]{2,1,0:T(8,128)(2,1)S(1)}, u32[]{:S(2)}, u32[]{:S(2)}) collective-permute-start(bf16[4,64,128]{2,1,0:T(8,128)(2,1)S(1)} %get-tuple-element.29), channel_id=1, source_target_pairs={{0,2},{2,0},{4,6},{6,4},{8,10},{10,8},{12,14},{14,12},{16,18},{18,... | collective-permute-start | bytes 196616 | tf_op jit(solution)/shard_map/ppermute | solution.py:221
  2.3 0.9 %collective-permute-done.arrived = bf16[4,64,128]{2,1,0:T(8,128)(2,1)S(1)} collective-permute-done((bf16[4,64,128]{2,1,0:T(8,128)(2,1)S(1)}, bf16[4,64,128]{2,1,0:T(8,128)(2,1)S(1)}, u32[]{:S(2)}, u32[]{:S(2)}) %collective-permute-start) | collective-permute-done | bytes 65568 | tf_op jit(solution)/shard_map/ppermute | solution.py:221
  3.2 0.0 copy-start.4
  3.2 0.4 %collective-permute-start.1 = (bf16[2048,128]{1,0:T(8,128)(2,1)S(1)}, bf16[2048,128]{1,0:T(8,128)(2,1)S(1)}, u32[]{:S(2)}, u32[]{:S(2)}) collective-permute-start(bf16[2048,128]{1,0:T(8,128)(2,1)S(1)} %bitcast.10), channel_id=1, source_target_pairs={{0,2},{2,0},{4,6},{6,4},{8,10},{10,8},{12,14},{14,12},{16,18},{18,... | collective-permute-start | bytes 1572872 | tf_op jit(solution)/shard_map/ppermute | solution.py:221
  3.6 5.7 %collective-permute-start.3 = (bf16[64,128]{1,0:T(8,128)(2,1)S(1)}, bf16[64,128]{1,0:T(8,128)(2,1)S(1)}, u32[]{:S(2)}, u32[]{:S(2)}) collective-permute-start(bf16[64,128]{1,0:T(8,128)(2,1)S(1)} %get-tuple-element.30), channel_id=1, source_target_pairs={{0,28},{2,26},{4,24},{6,30},{8,20},{10,18},{12,16},{14,22},{16,12}... | collective-permute-start | bytes 49160 | tf_op jit(solution)/shard_map/ppermute | solution.py:233
  9.3 0.0 collective-permute-start.4
  9.3 0.6 %collective-permute-start.5 = (bf16[64,128]{1,0:T(8,128)(2,1)S(1)}, bf16[64,128]{1,0:T(8,128)(2,1)S(1)}, u32[]{:S(2)}, u32[]{:S(2)}) collective-permute-start(bf16[64,128]{1,0:T(8,128)(2,1)S(1)} %get-tuple-element.40), channel_id=1, source_target_pairs={{0,16},{2,10},{4,20},{6,14},{8,24},{10,2},{12,28},{14,6},{16,0},{1... | collective-permute-start | bytes 49160 | tf_op jit(solution)/shard_map/ppermute | solution.py:233
  9.9 1.7 %collective-permute-start.6 = (bf16[64,128]{1,0:T(8,128)(2,1)S(1)}, bf16[64,128]{1,0:T(8,128)(2,1)S(1)}, u32[]{:S(2)}, u32[]{:S(2)}) collective-permute-start(bf16[64,128]{1,0:T(8,128)(2,1)S(1)} %get-tuple-element.41), channel_id=1, source_target_pairs={{0,4},{2,6},{4,0},{6,2},{8,12},{10,14},{12,8},{14,10},{16,20},{18,... | collective-permute-start | bytes 49160 | tf_op jit(solution)/shard_map/ppermute | solution.py:233
  11.6 1.1 %rows.1 = (bf16[256,512]{1,0:T(8,128)(2,1)S(1)}, bf16[256,512]{1,0:T(8,128)(2,1)S(1)}, f32[128,256]{1,0:T(8,128)S(1)}) custom-call(s32[1,8,8]{2,1,0:T(8,128)S(1)} %copy-done.4, bf16[2048,128]{1,0:T(8,128)(2,1)S(1)} %bitcast.11, bf16[2048,128]{1,0:T(8,128)(2,1)S(1)} %collective-permute-done.1.mate, f32[256,128]{1,0:T(8,128)S(1)} %bitcast.12), custom_call_target="tpu_custom_call" | custom-call | bytes 1835264 | tf_op jit(solution)/shard_map/rows/pallas_call | solution.py:208
  12.7 0.0 collective-permute-done.3.refs_0_
  12.7 1.3 %collective-permute-done.4.refs_1_ = bf16[64,128]{1,0:T(8,128)(2,1)S(1)} collective-permute-done((bf16[64,128]{1,0:T(8,128)(2,1)S(1)}, bf16[64,128]{1,0:T(8,128)(2,1)S(1)}, u32[]{:S(2)}, u32[]{:S(2)}) %collective-permute-start.4) | collective-permute-done | bytes 16416 | tf_op jit(solution)/shard_map/ppermute | solution.py:233
  14.0 0.3 image.1.here
  14.3 0.0 copy-start
  14.3 0.1 collective-permute-start.7
  14.4 0.5 %copy-done.1 = f32[1,256,128]{2,1,0:T(8,128)S(1)} copy-done((f32[1,256,128]{2,1,0:T(8,128)S(1)}, f32[1,256,128]{2,1,0:T(8,128)}, u32[]{:S(2)}) %copy-start.1) | copy-done | bytes 131096
  14.9 1.6 %collective-permute-start.2 = (f32[256,128]{1,0:T(8,128)S(1)}, f32[256,128]{1,0:T(8,128)S(1)}, u32[]{:S(2)}, u32[]{:S(2)}) collective-permute-start(f32[256,128]{1,0:T(8,128)S(1)} %bitcast.8), channel_id=1, source_target_pairs={{0,1},{1,0},{2,3},{3,2},{4,5},{5,4},{6,7},{7,6},{8,9},{9,8},{10,11... | collective-permute-start | bytes 393224 | tf_op jit(solution)/shard_map/ppermute | solution.py:290
  16.4 0.0 collective-permute-done.7.there
  16.4 0.3 %back.1 = (bf16[64,128]{1,0:T(8,128)(2,1)S(1)}, bf16[64,128]{1,0:T(8,128)(2,1)S(1)}, bf16[64,128]{1,0:T(8,128)(2,1)S(1)}, bf16[64,128]{1,0:T(8,128)(2,1)S(1)}, bf16[64,128]{1,0:T(8,128)(2,1)S(1)}) custom-call(f32[2,128,256]{2,1,0:T(8,128)S(1)} %image.1.here, f32[2,128,256]{2,1,0:T(8,128)S(1)} %collective-permute-done.7.there, ...), custom_call_target="tpu_custom_call" | custom-call | flops 67108864 | bytes 1130496 | tf_op jit(solution)/shard_map/back/pallas_call | solution.py:208
  16.8 4.4 %collective-permute-start.8 = (bf16[64,128]{1,0:T(8,128)(2,1)S(1)}, bf16[64,128]{1,0:T(8,128)(2,1)S(1)}, u32[]{:S(2)}, u32[]{:S(2)}) collective-permute-start(bf16[64,128]{1,0:T(8,128)(2,1)S(1)} %get-tuple-element.43), channel_id=1, source_target_pairs={{0,28},{2,26},{4,24},{6,30},{8,20},{10,18},{12,16},{14,22},{16,12}... | collective-permute-start | bytes 49160 | tf_op jit(solution)/shard_map/ppermute | solution.py:233
  21.2 0.9 %collective-permute-start.10 = (bf16[64,128]{1,0:T(8,128)(2,1)S(1)}, bf16[64,128]{1,0:T(8,128)(2,1)S(1)}, u32[]{:S(2)}, u32[]{:S(2)}) collective-permute-start(bf16[64,128]{1,0:T(8,128)(2,1)S(1)} %get-tuple-element.47), channel_id=1, source_target_pairs={{0,16},{2,10},{4,20},{6,14},{8,24},{10,2},{12,28},{14,6},{16,0},{1... | collective-permute-start | bytes 49160 | tf_op jit(solution)/shard_map/ppermute | solution.py:233
  22.1 1.3 %collective-permute-start.11 = (bf16[64,128]{1,0:T(8,128)(2,1)S(1)}, bf16[64,128]{1,0:T(8,128)(2,1)S(1)}, u32[]{:S(2)}, u32[]{:S(2)}) collective-permute-start(bf16[64,128]{1,0:T(8,128)(2,1)S(1)} %get-tuple-element.48), channel_id=1, source_target_pairs={{0,4},{2,6},{4,0},{6,2},{8,12},{10,14},{12,8},{14,10},{16,20},{18,... | collective-permute-start | bytes 49160 | tf_op jit(solution)/shard_map/ppermute | solution.py:233
  23.4 0.3 columns.1.factors
  23.7 0.0 collective-permute-done.8.refs_0_
  23.7 2.3 %collective-permute-done.9.refs_1_ = bf16[64,128]{1,0:T(8,128)(2,1)S(1)} collective-permute-done((bf16[64,128]{1,0:T(8,128)(2,1)S(1)}, bf16[64,128]{1,0:T(8,128)(2,1)S(1)}, u32[]{:S(2)}, u32[]{:S(2)}) %collective-permute-start.9) | collective-permute-done | bytes 16416 | tf_op jit(solution)/shard_map/ppermute | solution.py:233
  26.1 0.1 collective-permute-start.12
  26.2 1.2 %collective-permute-done.12.mate = bf16[4,64,128]{2,1,0:T(8,128)(2,1)S(1)} collective-permute-done((bf16[4,64,128]{2,1,0:T(8,128)(2,1)S(1)}, bf16[4,64,128]{2,1,0:T(8,128)(2,1)S(1)}, u32[]{:S(2)}, u32[]{:S(2)}) %collective-permute-start.12) | collective-permute-done | bytes 65568 | tf_op jit(solution)/shard_map/ppermute | solution.py:221
  27.4 0.4 %gradient.1 = bf16[256,128]{1,0:T(8,128)(2,1)S(1)} custom-call(bf16[4,64,128]{2,1,0:T(8,128)(2,1)S(1)} %pack.1.own, bf16[4,64,128]{2,1,0:T(8,128)(2,1)S(1)} %collective-permute-done.12.mate, bf16[256,1024]{1,0:T(8,128)(2,1)S(1)} %columns.1.factors), custom_call_target="tpu_custom_call" | custom-call | flops 67108864 | bytes 720896 | tf_op jit(solution)/shard_map/gradient/pallas_call | solution.py:208
  27.8 1.1 %collective-permute-start.13 = (bf16[256,128]{1,0:T(8,128)(2,1)S(1)}, bf16[256,128]{1,0:T(8,128)(2,1)S(1)}, u32[]{:S(2)}, u32[]{:S(2)}) collective-permute-start(bf16[256,128]{1,0:T(8,128)(2,1)S(1)} %gradient.1), channel_id=1, source_target_pairs={{0,1},{1,0},{2,3},{3,2},{4,5},{5,4},{6,7},{7,6},{8,9},{9,8},{10,11... | collective-permute-start | bytes 196616 | tf_op jit(solution)/shard_map/ppermute | solution.py:319
  29.0 3.2 %collective-permute-done.13.gradient = bf16[256,128]{1,0:T(8,128)(2,1)S(1)} collective-permute-done((bf16[256,128]{1,0:T(8,128)(2,1)S(1)}, bf16[256,128]{1,0:T(8,128)(2,1)S(1)}, u32[]{:S(2)}, u32[]{:S(2)}) %collective-permute-start.13) | collective-permute-done | bytes 65568 | tf_op jit(solution)/shard_map/ppermute | solution.py:319
  32.2 0.7 %shrink.1 = f32[256,128]{1,0:T(8,128)} custom-call(f32[256,128]{1,0:T(8,128)S(1)} %get-tuple-element.49.total, f32[256,128]{1,0:T(8,128)S(1)} %get-tuple-element.50.difference, bf16[256,128]{1,0:T(8,128)(2,1)S(1)} %collective-permute-done.13.gradient), custom_call_target="tpu_custom_call" | custom-call | bytes 458752 | tf_op jit(solution)/shard_map/shrink/pallas_call | solution.py:208
  (16 shorter events, 0.1 us)
Async XLA Ops:
  0.0 3.2 %copy-start.2 = (bf16[1,256,8,128]{3,2,1,0:T(8,128)(2,1)S(1)}, bf16[1,256,8,128]{3,2,1,0:T(8,128)(2,1)}, u32[]{:S(2)}) copy-start(bf16[1,256,8,128]{3,2,1,0:T(8,128)(2,1)} %param.5) | copy-start | bytes 1572868
  1.7 9.8 %copy-start.3 = (f32[1,256,128]{2,1,0:T(8,128)S(1)}, f32[1,256,128]{2,1,0:T(8,128)}, u32[]{:S(2)}) copy-start(f32[1,256,128]{2,1,0:T(8,128)} %param.8) | copy-start | bytes 393220
  1.8 1.4 %collective-permute-start = (bf16[4,64,128]{2,1,0:T(8,128)(2,1)S(1)}, bf16[4,64,128]{2,1,0:T(8,128)(2,1)S(1)}, u32[]{:S(2)}, u32[]{:S(2)}) collective-permute-start(bf16[4,64,128]{2,1,0:T(8,128)(2,1)S(1)} %get-tuple-element.29), channel_id=1, source_target_pairs={{0,2},{2,0},{4,6},{6,4},{8,10},{10,8},{12,14},{14,12},{16,18},{18,... | collective-permute-start | bytes 196616 | tf_op jit(solution)/shard_map/ppermute | solution.py:221
  3.2 8.4 %copy-start.4 = (s32[1,8,8]{2,1,0:T(8,128)S(1)}, s32[1,8,8]{2,1,0:T(8,128)}, u32[]{:S(2)}) copy-start(s32[1,8,8]{2,1,0:T(8,128)} %ranks.1) | copy-start | bytes 772
  3.2 8.4 %collective-permute-start.1 = (bf16[2048,128]{1,0:T(8,128)(2,1)S(1)}, bf16[2048,128]{1,0:T(8,128)(2,1)S(1)}, u32[]{:S(2)}, u32[]{:S(2)}) collective-permute-start(bf16[2048,128]{1,0:T(8,128)(2,1)S(1)} %bitcast.10), channel_id=1, source_target_pairs={{0,2},{2,0},{4,6},{6,4},{8,10},{10,8},{12,14},{14,12},{16,18},{18,... | collective-permute-start | bytes 1572872 | tf_op jit(solution)/shard_map/ppermute | solution.py:221
  3.6 9.0 %collective-permute-start.3 = (bf16[64,128]{1,0:T(8,128)(2,1)S(1)}, bf16[64,128]{1,0:T(8,128)(2,1)S(1)}, u32[]{:S(2)}, u32[]{:S(2)}) collective-permute-start(bf16[64,128]{1,0:T(8,128)(2,1)S(1)} %get-tuple-element.30), channel_id=1, source_target_pairs={{0,28},{2,26},{4,24},{6,30},{8,20},{10,18},{12,16},{14,22},{16,12}... | collective-permute-start | bytes 49160 | tf_op jit(solution)/shard_map/ppermute | solution.py:233
  9.3 4.6 %collective-permute-start.4 = (bf16[64,128]{1,0:T(8,128)(2,1)S(1)}, bf16[64,128]{1,0:T(8,128)(2,1)S(1)}, u32[]{:S(2)}, u32[]{:S(2)}) collective-permute-start(bf16[64,128]{1,0:T(8,128)(2,1)S(1)} %get-tuple-element.39), channel_id=1, source_target_pairs={{0,12},{2,22},{4,8},{6,18},{8,4},{10,30},{12,0},{14,26},{16,28},{1... | collective-permute-start | bytes 49160 | tf_op jit(solution)/shard_map/ppermute | solution.py:233
  9.3 4.6 %collective-permute-start.5 = (bf16[64,128]{1,0:T(8,128)(2,1)S(1)}, bf16[64,128]{1,0:T(8,128)(2,1)S(1)}, u32[]{:S(2)}, u32[]{:S(2)}) collective-permute-start(bf16[64,128]{1,0:T(8,128)(2,1)S(1)} %get-tuple-element.40), channel_id=1, source_target_pairs={{0,16},{2,10},{4,20},{6,14},{8,24},{10,2},{12,28},{14,6},{16,0},{1... | collective-permute-start | bytes 49160 | tf_op jit(solution)/shard_map/ppermute | solution.py:233
  9.9 4.1 %collective-permute-start.6 = (bf16[64,128]{1,0:T(8,128)(2,1)S(1)}, bf16[64,128]{1,0:T(8,128)(2,1)S(1)}, u32[]{:S(2)}, u32[]{:S(2)}) collective-permute-start(bf16[64,128]{1,0:T(8,128)(2,1)S(1)} %get-tuple-element.41), channel_id=1, source_target_pairs={{0,4},{2,6},{4,0},{6,2},{8,12},{10,14},{12,8},{14,10},{16,20},{18,... | collective-permute-start | bytes 49160 | tf_op jit(solution)/shard_map/ppermute | solution.py:233
  14.0 0.9 %copy-start.1 = (f32[1,256,128]{2,1,0:T(8,128)S(1)}, f32[1,256,128]{2,1,0:T(8,128)}, u32[]{:S(2)}) copy-start(f32[1,256,128]{2,1,0:T(8,128)} %param.9) | copy-start | bytes 393220
  14.3 9.1 %copy-start = (bf16[1,256,8,128]{3,2,1,0:T(8,128)(2,1)S(1)}, bf16[1,256,8,128]{3,2,1,0:T(8,128)(2,1)}, u32[]{:S(2)}) copy-start(bf16[1,256,8,128]{3,2,1,0:T(8,128)(2,1)} %param.6) | copy-start | bytes 1572868
  14.3 2.1 %collective-permute-start.7 = (f32[2,128,256]{2,1,0:T(8,128)S(1)}, f32[2,128,256]{2,1,0:T(8,128)S(1)}, u32[]{:S(2)}, u32[]{:S(2)}) collective-permute-start(f32[2,128,256]{2,1,0:T(8,128)S(1)} %image.1.here), channel_id=1, source_target_pairs={{0,2},{2,0},{4,6},{6,4},{8,10},{10,8},{12,14},{14,12},{16,18},{18,... | collective-permute-start | bytes 786440 | tf_op jit(solution)/shard_map/ppermute | solution.py:221
  14.9 8.8 %collective-permute-start.2 = (f32[256,128]{1,0:T(8,128)S(1)}, f32[256,128]{1,0:T(8,128)S(1)}, u32[]{:S(2)}, u32[]{:S(2)}) collective-permute-start(f32[256,128]{1,0:T(8,128)S(1)} %bitcast.8), channel_id=1, source_target_pairs={{0,1},{1,0},{2,3},{3,2},{4,5},{5,4},{6,7},{7,6},{8,9},{9,8},{10,11... | collective-permute-start | bytes 393224 | tf_op jit(solution)/shard_map/ppermute | solution.py:290
  16.8 6.9 %collective-permute-start.8 = (bf16[64,128]{1,0:T(8,128)(2,1)S(1)}, bf16[64,128]{1,0:T(8,128)(2,1)S(1)}, u32[]{:S(2)}, u32[]{:S(2)}) collective-permute-start(bf16[64,128]{1,0:T(8,128)(2,1)S(1)} %get-tuple-element.43), channel_id=1, source_target_pairs={{0,28},{2,26},{4,24},{6,30},{8,20},{10,18},{12,16},{14,22},{16,12}... | collective-permute-start | bytes 49160 | tf_op jit(solution)/shard_map/ppermute | solution.py:233
  21.2 4.9 %collective-permute-start.9 = (bf16[64,128]{1,0:T(8,128)(2,1)S(1)}, bf16[64,128]{1,0:T(8,128)(2,1)S(1)}, u32[]{:S(2)}, u32[]{:S(2)}) collective-permute-start(bf16[64,128]{1,0:T(8,128)(2,1)S(1)} %get-tuple-element.46), channel_id=1, source_target_pairs={{0,12},{2,22},{4,8},{6,18},{8,4},{10,30},{12,0},{14,26},{16,28},{1... | collective-permute-start | bytes 49160 | tf_op jit(solution)/shard_map/ppermute | solution.py:233
  21.2 4.9 %collective-permute-start.10 = (bf16[64,128]{1,0:T(8,128)(2,1)S(1)}, bf16[64,128]{1,0:T(8,128)(2,1)S(1)}, u32[]{:S(2)}, u32[]{:S(2)}) collective-permute-start(bf16[64,128]{1,0:T(8,128)(2,1)S(1)} %get-tuple-element.47), channel_id=1, source_target_pairs={{0,16},{2,10},{4,20},{6,14},{8,24},{10,2},{12,28},{14,6},{16,0},{1... | collective-permute-start | bytes 49160 | tf_op jit(solution)/shard_map/ppermute | solution.py:233
  22.1 3.9 %collective-permute-start.11 = (bf16[64,128]{1,0:T(8,128)(2,1)S(1)}, bf16[64,128]{1,0:T(8,128)(2,1)S(1)}, u32[]{:S(2)}, u32[]{:S(2)}) collective-permute-start(bf16[64,128]{1,0:T(8,128)(2,1)S(1)} %get-tuple-element.48), channel_id=1, source_target_pairs={{0,4},{2,6},{4,0},{6,2},{8,12},{10,14},{12,8},{14,10},{16,20},{18,... | collective-permute-start | bytes 49160 | tf_op jit(solution)/shard_map/ppermute | solution.py:233
  26.1 1.3 %collective-permute-start.12 = (bf16[4,64,128]{2,1,0:T(8,128)(2,1)S(1)}, bf16[4,64,128]{2,1,0:T(8,128)(2,1)S(1)}, u32[]{:S(2)}, u32[]{:S(2)}) collective-permute-start(bf16[4,64,128]{2,1,0:T(8,128)(2,1)S(1)} %pack.1.own), channel_id=1, source_target_pairs={{0,2},{2,0},{4,6},{6,4},{8,10},{10,8},{12,14},{14,12},{16,18},{18,... | collective-permute-start | bytes 196616 | tf_op jit(solution)/shard_map/ppermute | solution.py:221
  27.8 4.3 %collective-permute-start.13 = (bf16[256,128]{1,0:T(8,128)(2,1)S(1)}, bf16[256,128]{1,0:T(8,128)(2,1)S(1)}, u32[]{:S(2)}, u32[]{:S(2)}) collective-permute-start(bf16[256,128]{1,0:T(8,128)(2,1)S(1)} %gradient.1), channel_id=1, source_target_pairs={{0,1},{1,0},{2,3},{3,2},{4,5},{5,4},{6,7},{7,6},{8,9},{9,8},{10,11... | collective-permute-start | bytes 196616 | tf_op jit(solution)/shard_map/ppermute | solution.py:319

commit v7 on v6

--- a/solution.py
+++ b/solution.py
@@ -19,8 +19,9 @@
 
 
 def shifts_of(chips):
-    far_first = sorted(range(chips), key=lambda shift: (-shift.bit_count(), -shift))
-    return [[far_first[at] for at in range(chips) if (at + 1) // 2 % 2 == core] for core in range(2)]
+    upper = sorted(range(chips // 2, chips - 1), key=lambda shift: (shift % 2, shift))
+    lower = sorted(range(1, chips // 2), key=lambda shift: (-shift.bit_count(), shift))
+    return [[*upper, 0], [chips - 1, *lower]]
 
 
 def own_index(shifts):
@@ -119,7 +120,7 @@
     own[...] = outs[own_index(shifts)][...]
 
 
-def rows_kernel(shifts, ranks, own, mate, observed, own_out, mate_out, turned, wide):
+def rows_kernel(shifts, ranks, own, mate, observed, start, own_out, mate_out, turned, start_out, wide):
     chip, _ = place()
     chosen, _ = both_shifts(shifts)
     lane = lax.broadcasted_iota(jnp.int32, (1, LANES), 1) % (LANES // 2)
@@ -127,6 +128,7 @@
     separate(own, wide, own_out, chosen, masks)
     separate(mate, wide, mate_out, chosen, masks)
     turned[...] = observed[...].T
+    start_out[...] = start[...]
 
 
 def columns_kernel(factors, separated, wide):
@@ -276,18 +278,17 @@
     )
     sends = call(functools.partial(add_kernel, shifts), "add", [block] * (members + 1), [keep, to_mate(give)])
     left_rows = after(left_rows, sends[0])
-    own_left, mate_left, turned = call(
+    own_left, mate_left, turned, start = call(
         functools.partial(rows_kernel, shifts),
         "rows",
-        [chosen, chosen, shape(sources, rows, dtype=F32)],
-        [ranks, left_rows, to_mate(left_rows), after(observed, give)],
+        [chosen, chosen, shape(sources, rows, dtype=F32), shape(rows, sources, dtype=F32)],
+        [ranks, left_rows, to_mate(left_rows), after(observed, give), after(start, give)],
         [wide],
         spaces=[pltpu.SMEM],
     )
-    early = after(start, own_left)
     starts = [start]
     for shift in range(1, band):
-        starts.append(lax.ppermute(early, "freq", [(f, (f - shift) % band) for f in range(band)]))
+        starts.append(lax.ppermute(start, "freq", [(f, (f - shift) % band) for f in range(band)]))
     (misfit,) = call(
         functools.partial(image_kernel, shifts),
         "image",

time: 33 us -> 33.7 us (1.021)
  starting transfers between devices: 18.3 us -> 19.6 us
  local copies, waits for them, and re-layouts: 0.5 us -> 0.03 us
    ppermute x8, starting transfers between devices: 14.6 us -> 15.5 us  [exchange(): lax.ppermute(send, 'tile', [(i, i ^ 2 * pair[i % 2]) for i in range(count)])]
    unnamed x10, local copies, waits for them, and re-layouts: 0.5 us -> 0.03 us
    ppermute x1, starting transfers between devices: 1.09 us -> 1.51 us  [body(): lax.ppermute(gradient, 'freq', [(f, (f - shift) % band) for f in range(ba...]
    ppermute x1, waiting for transfers between devices: 3.2 us -> 2.78 us  [body(): lax.ppermute(gradient, 'freq', [(f, (f - shift) % band) for f in range(ba...]
  transfers between devices with their start and end apart: 14 -> 14, of which waited for: 5 -> 7; matrix products, arithmetic and copies ran while one was open for 0% -> 0% of each run, Pallas kernels for 5% -> 5%
where the time goes in v7:
time: 33.7 us; the launch traced here: 33.6 us
  starting transfers between devices  19.6 us (58%)
  waiting for transfers between devices  8.79 us (26%)
  Pallas kernels  4.94 us (15%)
    ppermute x8, starting transfers between devices, exchange(): lax.ppermute(send, 'tile', [(i, i ^ 2 * pair[i % 2]) for i in range(count)])  15.5 us
    pallas_call x10, Pallas kernels, call(): pl.pallas_call(kernel, out_shape=outs, in_specs=[pl.BlockSpec(memory_spac...  4.94 us
    ppermute x8, waiting for transfers between devices, exchange(): lax.ppermute(send, 'tile', [(i, i ^ 2 * pair[i % 2]) for i in range(count)])  3.86 us
    ppermute x1, waiting for transfers between devices, body(): lax.ppermute(gradient, 'freq', [(f, (f - shift) % band) for f in range(ba...  2.78 us
    ppermute x4, waiting for transfers between devices, to_mate(): lax.ppermute(value, 'tile', [(i, i ^ 1) for i in range(lax.axis_size('til...  2.15 us
    ppermute x1, starting transfers between devices, body(): lax.ppermute(start, 'freq', [(f, (f - shift) % band) for f in range(band)])  1.59 us
    ppermute x1, starting transfers between devices, body(): lax.ppermute(gradient, 'freq', [(f, (f - shift) % band) for f in range(ba...  1.51 us
    ppermute x4, starting transfers between devices, to_mate(): lax.ppermute(value, 'tile', [(i, i ^ 1) for i in range(lax.axis_size('til...  1.08 us
  transfers between devices with their start and end apart: 14, of which 7 were waited for; matrix products, arithmetic and copies ran while one was open for 0% of the time, Pallas kernels for 5%

profile of v7, /device:TPU:0, one launch (start us, length us, event | category | flops | bytes accessed | tf_op | source)
XLA Modules:
  0.0 33.6 jit_solution(15855696831118430765)
XLA Ops:
  0.0 1.7 %forward.1 = (bf16[4,64,128]{2,1,0:T(8,128)(2,1)S(1)}, bf16[4,64,128]{2,1,0:T(8,128)(2,1)S(1)}) custom-call(f32[256,128]{1,0:T(8,128)} %bitcast.7, bf16[2048,128]{1,0:T(8,128)(2,1)} %bitcast.5), custom_call_target="tpu_custom_call" | custom-call | flops 67108864 | bytes 786432 | tf_op jit(solution)/shard_map/forward/pallas_call | solution.py:210
  1.8 0.0 copy-start.1
  1.8 0.5 %collective-permute-start = (bf16[4,64,128]{2,1,0:T(8,128)(2,1)S(1)}, bf16[4,64,128]{2,1,0:T(8,128)(2,1)S(1)}, u32[]{:S(2)}, u32[]{:S(2)}) collective-permute-start(bf16[4,64,128]{2,1,0:T(8,128)(2,1)S(1)} %get-tuple-element.30), channel_id=1, source_target_pairs={{0,2},{2,0},{4,6},{6,4},{8,10},{10,8},{12,14},{14,12},{16,18},{18,... | collective-permute-start | bytes 196616 | tf_op jit(solution)/shard_map/ppermute | solution.py:223
  2.3 0.9 %collective-permute-done.arrived = bf16[4,64,128]{2,1,0:T(8,128)(2,1)S(1)} collective-permute-done((bf16[4,64,128]{2,1,0:T(8,128)(2,1)S(1)}, bf16[4,64,128]{2,1,0:T(8,128)(2,1)S(1)}, u32[]{:S(2)}, u32[]{:S(2)}) %collective-permute-start) | collective-permute-done | bytes 65568 | tf_op jit(solution)/shard_map/ppermute | solution.py:223
  3.2 0.0 copy-start.4
  3.2 0.4 %collective-permute-start.1 = (bf16[2048,128]{1,0:T(8,128)(2,1)S(1)}, bf16[2048,128]{1,0:T(8,128)(2,1)S(1)}, u32[]{:S(2)}, u32[]{:S(2)}) collective-permute-start(bf16[2048,128]{1,0:T(8,128)(2,1)S(1)} %bitcast.9), channel_id=1, source_target_pairs={{0,2},{2,0},{4,6},{6,4},{8,10},{10,8},{12,14},{14,12},{16,18},{18,... | collective-permute-start | bytes 1572872 | tf_op jit(solution)/shard_map/ppermute | solution.py:223
  3.6 3.7 %collective-permute-start.3 = (bf16[64,128]{1,0:T(8,128)(2,1)S(1)}, bf16[64,128]{1,0:T(8,128)(2,1)S(1)}, u32[]{:S(2)}, u32[]{:S(2)}) collective-permute-start(bf16[64,128]{1,0:T(8,128)(2,1)S(1)} %get-tuple-element.31), channel_id=1, source_target_pairs={{0,16},{2,30},{4,20},{6,26},{8,24},{10,22},{12,28},{14,18},{16,0},... | collective-permute-start | bytes 49160 | tf_op jit(solution)/shard_map/ppermute | solution.py:235
  7.4 1.4 %collective-permute-start.4 = (bf16[64,128]{1,0:T(8,128)(2,1)S(1)}, bf16[64,128]{1,0:T(8,128)(2,1)S(1)}, u32[]{:S(2)}, u32[]{:S(2)}) collective-permute-start(bf16[64,128]{1,0:T(8,128)(2,1)S(1)} %get-tuple-element.41), channel_id=1, source_target_pairs={{0,24},{2,14},{4,28},{6,10},{8,16},{10,6},{12,20},{14,2},{16,8},{1... | collective-permute-start | bytes 49160 | tf_op jit(solution)/shard_map/ppermute | solution.py:235
  8.7 2.6 %collective-permute-start.5 = (bf16[64,128]{1,0:T(8,128)(2,1)S(1)}, bf16[64,128]{1,0:T(8,128)(2,1)S(1)}, u32[]{:S(2)}, u32[]{:S(2)}) collective-permute-start(bf16[64,128]{1,0:T(8,128)(2,1)S(1)} %get-tuple-element.42), channel_id=1, source_target_pairs={{0,20},{2,6},{4,16},{6,2},{8,28},{10,14},{12,24},{14,10},{16,4},{1... | collective-permute-start | bytes 49160 | tf_op jit(solution)/shard_map/ppermute | solution.py:235
  11.4 1.3 %collective-permute-start.6 = (bf16[64,128]{1,0:T(8,128)(2,1)S(1)}, bf16[64,128]{1,0:T(8,128)(2,1)S(1)}, u32[]{:S(2)}, u32[]{:S(2)}) collective-permute-start(bf16[64,128]{1,0:T(8,128)(2,1)S(1)} %get-tuple-element.43), channel_id=1, source_target_pairs={{0,8},{2,10},{4,12},{6,14},{8,0},{10,2},{12,4},{14,6},{16,24},{18,... | collective-permute-start | bytes 49160 | tf_op jit(solution)/shard_map/ppermute | solution.py:235
  12.7 0.0 collective-permute-done.1.mate
  12.7 1.1 %rows.1 = (bf16[256,512]{1,0:T(8,128)(2,1)S(1)}, bf16[256,512]{1,0:T(8,128)(2,1)S(1)}, f32[128,256]{1,0:T(8,128)S(1)}, f32[256,128]{1,0:T(8,128)S(1)}) custom-call(s32[1,8,8]{2,1,0:T(8,128)S(1)} %copy-done.4, bf16[2048,128]{1,0:T(8,128)(2,1)S(1)} %bitcast.10, bf16[2048,128]{1,0:T(8,128)(2,1)S(1)} %collective-permute-done.1.mate, f32[256,128]{1,0:T(8,128)S(1)} %bitcast.11, ...), custom_call_target="tpu_custom_call" | custom-call | bytes 2097408 | tf_op jit(solution)/shard_map/rows/pallas_call | solution.py:210
  13.8 0.4 %collective-permute-done.5.refs_2_ = bf16[64,128]{1,0:T(8,128)(2,1)S(1)} collective-permute-done((bf16[64,128]{1,0:T(8,128)(2,1)S(1)}, bf16[64,128]{1,0:T(8,128)(2,1)S(1)}, u32[]{:S(2)}, u32[]{:S(2)}) %collective-permute-start.5) | collective-permute-done | bytes 16416 | tf_op jit(solution)/shard_map/ppermute | solution.py:235
  14.3 0.8 %collective-permute-done.6.refs_3_ = bf16[64,128]{1,0:T(8,128)(2,1)S(1)} collective-permute-done((bf16[64,128]{1,0:T(8,128)(2,1)S(1)}, bf16[64,128]{1,0:T(8,128)(2,1)S(1)}, u32[]{:S(2)}, u32[]{:S(2)}) %collective-permute-start.6) | collective-permute-done | bytes 16416 | tf_op jit(solution)/shard_map/ppermute | solution.py:235
  15.1 0.3 image.1.here
  15.4 0.1 collective-permute-start.7
  15.5 0.0 copy-start
  15.5 1.6 %collective-permute-start.2 = (f32[256,128]{1,0:T(8,128)S(1)}, f32[256,128]{1,0:T(8,128)S(1)}, u32[]{:S(2)}, u32[]{:S(2)}) collective-permute-start(f32[256,128]{1,0:T(8,128)S(1)} %get-tuple-element.35.here), channel_id=1, source_target_pairs={{0,1},{1,0},{2,3},{3,2},{4,5},{5,4},{6,7},{7,6},{8,9},{9,8},{10,11... | collective-permute-start | bytes 393224 | tf_op jit(solution)/shard_map/ppermute | solution.py:291
  17.1 0.3 %back.1 = (bf16[64,128]{1,0:T(8,128)(2,1)S(1)}, bf16[64,128]{1,0:T(8,128)(2,1)S(1)}, bf16[64,128]{1,0:T(8,128)(2,1)S(1)}, bf16[64,128]{1,0:T(8,128)(2,1)S(1)}, bf16[64,128]{1,0:T(8,128)(2,1)S(1)}) custom-call(f32[2,128,256]{2,1,0:T(8,128)S(1)} %image.1.here, f32[2,128,256]{2,1,0:T(8,128)S(1)} %collective-permute-done.7.there, ...), custom_call_target="tpu_custom_call" | custom-call | flops 67108864 | bytes 1130496 | tf_op jit(solution)/shard_map/back/pallas_call | solution.py:210
  17.5 1.3 %collective-permute-start.8 = (bf16[64,128]{1,0:T(8,128)(2,1)S(1)}, bf16[64,128]{1,0:T(8,128)(2,1)S(1)}, u32[]{:S(2)}, u32[]{:S(2)}) collective-permute-start(bf16[64,128]{1,0:T(8,128)(2,1)S(1)} %get-tuple-element.45), channel_id=1, source_target_pairs={{0,16},{2,30},{4,20},{6,26},{8,24},{10,22},{12,28},{14,18},{16,0},... | collective-permute-start | bytes 49160 | tf_op jit(solution)/shard_map/ppermute | solution.py:235
  18.8 2.5 %collective-permute-start.9 = (bf16[64,128]{1,0:T(8,128)(2,1)S(1)}, bf16[64,128]{1,0:T(8,128)(2,1)S(1)}, u32[]{:S(2)}, u32[]{:S(2)}) collective-permute-start(bf16[64,128]{1,0:T(8,128)(2,1)S(1)} %get-tuple-element.48), channel_id=1, source_target_pairs={{0,24},{2,14},{4,28},{6,10},{8,16},{10,6},{12,20},{14,2},{16,8},{1... | collective-permute-start | bytes 49160 | tf_op jit(solution)/shard_map/ppermute | solution.py:235
  21.2 0.9 %collective-permute-start.10 = (bf16[64,128]{1,0:T(8,128)(2,1)S(1)}, bf16[64,128]{1,0:T(8,128)(2,1)S(1)}, u32[]{:S(2)}, u32[]{:S(2)}) collective-permute-start(bf16[64,128]{1,0:T(8,128)(2,1)S(1)} %get-tuple-element.49), channel_id=1, source_target_pairs={{0,20},{2,6},{4,16},{6,2},{8,28},{10,14},{12,24},{14,10},{16,4},{1... | collective-permute-start | bytes 49160 | tf_op jit(solution)/shard_map/ppermute | solution.py:235
  22.1 1.7 %collective-permute-start.11 = (bf16[64,128]{1,0:T(8,128)(2,1)S(1)}, bf16[64,128]{1,0:T(8,128)(2,1)S(1)}, u32[]{:S(2)}, u32[]{:S(2)}) collective-permute-start(bf16[64,128]{1,0:T(8,128)(2,1)S(1)} %get-tuple-element.50), channel_id=1, source_target_pairs={{0,8},{2,10},{4,12},{6,14},{8,0},{10,2},{12,4},{14,6},{16,24},{18,... | collective-permute-start | bytes 49160 | tf_op jit(solution)/shard_map/ppermute | solution.py:235
  23.9 0.3 columns.1.factors
  24.2 0.1 collective-permute-done.9.refs_1_
  24.3 2.5 %collective-permute-done.10.refs_2_ = bf16[64,128]{1,0:T(8,128)(2,1)S(1)} collective-permute-done((bf16[64,128]{1,0:T(8,128)(2,1)S(1)}, bf16[64,128]{1,0:T(8,128)(2,1)S(1)}, u32[]{:S(2)}, u32[]{:S(2)}) %collective-permute-start.10) | collective-permute-done | bytes 16416 | tf_op jit(solution)/shard_map/ppermute | solution.py:235
  26.8 0.1 collective-permute-start.12
  26.9 1.2 %collective-permute-done.12.mate = bf16[4,64,128]{2,1,0:T(8,128)(2,1)S(1)} collective-permute-done((bf16[4,64,128]{2,1,0:T(8,128)(2,1)S(1)}, bf16[4,64,128]{2,1,0:T(8,128)(2,1)S(1)}, u32[]{:S(2)}, u32[]{:S(2)}) %collective-permute-start.12) | collective-permute-done | bytes 65568 | tf_op jit(solution)/shard_map/ppermute | solution.py:223
  28.1 0.4 %gradient.1 = bf16[256,128]{1,0:T(8,128)(2,1)S(1)} custom-call(bf16[4,64,128]{2,1,0:T(8,128)(2,1)S(1)} %pack.1.own, bf16[4,64,128]{2,1,0:T(8,128)(2,1)S(1)} %collective-permute-done.12.mate, bf16[256,1024]{1,0:T(8,128)(2,1)S(1)} %columns.1.factors), custom_call_target="tpu_custom_call" | custom-call | flops 67108864 | bytes 720896 | tf_op jit(solution)/shard_map/gradient/pallas_call | solution.py:210
  28.5 1.5 %collective-permute-start.13 = (bf16[256,128]{1,0:T(8,128)(2,1)S(1)}, bf16[256,128]{1,0:T(8,128)(2,1)S(1)}, u32[]{:S(2)}, u32[]{:S(2)}) collective-permute-start(bf16[256,128]{1,0:T(8,128)(2,1)S(1)} %gradient.1), channel_id=1, source_target_pairs={{0,1},{1,0},{2,3},{3,2},{4,5},{5,4},{6,7},{7,6},{8,9},{9,8},{10,11... | collective-permute-start | bytes 196616 | tf_op jit(solution)/shard_map/ppermute | solution.py:320
  30.1 2.8 %collective-permute-done.13.gradient = bf16[256,128]{1,0:T(8,128)(2,1)S(1)} collective-permute-done((bf16[256,128]{1,0:T(8,128)(2,1)S(1)}, bf16[256,128]{1,0:T(8,128)(2,1)S(1)}, u32[]{:S(2)}, u32[]{:S(2)}) %collective-permute-start.13) | collective-permute-done | bytes 65568 | tf_op jit(solution)/shard_map/ppermute | solution.py:320
  32.9 0.7 %shrink.1 = f32[256,128]{1,0:T(8,128)} custom-call(f32[256,128]{1,0:T(8,128)S(1)} %get-tuple-element.51.total, f32[256,128]{1,0:T(8,128)S(1)} %get-tuple-element.52.difference, bf16[256,128]{1,0:T(8,128)(2,1)S(1)} %collective-permute-done.13.gradient), custom_call_target="tpu_custom_call" | custom-call | bytes 458752 | tf_op jit(solution)/shard_map/shrink/pallas_call | solution.py:210
  (16 shorter events, 0.1 us)
Async XLA Ops:
  0.0 3.2 %copy-start.2 = (bf16[1,256,8,128]{3,2,1,0:T(8,128)(2,1)S(1)}, bf16[1,256,8,128]{3,2,1,0:T(8,128)(2,1)}, u32[]{:S(2)}) copy-start(bf16[1,256,8,128]{3,2,1,0:T(8,128)(2,1)} %param.5) | copy-start | bytes 1572868
  0.0 12.7 %copy-start.3 = (f32[1,256,128]{2,1,0:T(8,128)S(1)}, f32[1,256,128]{2,1,0:T(8,128)}, u32[]{:S(2)}) copy-start(f32[1,256,128]{2,1,0:T(8,128)} %param.8) | copy-start | bytes 393220
  1.8 11.0 %copy-start.1 = (f32[1,256,128]{2,1,0:T(8,128)S(1)}, f32[1,256,128]{2,1,0:T(8,128)}, u32[]{:S(2)}) copy-start(f32[1,256,128]{2,1,0:T(8,128)} %param.9) | copy-start | bytes 393220
  1.8 1.4 %collective-permute-start = (bf16[4,64,128]{2,1,0:T(8,128)(2,1)S(1)}, bf16[4,64,128]{2,1,0:T(8,128)(2,1)S(1)}, u32[]{:S(2)}, u32[]{:S(2)}) collective-permute-start(bf16[4,64,128]{2,1,0:T(8,128)(2,1)S(1)} %get-tuple-element.30), channel_id=1, source_target_pairs={{0,2},{2,0},{4,6},{6,4},{8,10},{10,8},{12,14},{14,12},{16,18},{18,... | collective-permute-start | bytes 196616 | tf_op jit(solution)/shard_map/ppermute | solution.py:223
  3.2 9.5 %copy-start.4 = (s32[1,8,8]{2,1,0:T(8,128)S(1)}, s32[1,8,8]{2,1,0:T(8,128)}, u32[]{:S(2)}) copy-start(s32[1,8,8]{2,1,0:T(8,128)} %ranks.1) | copy-start | bytes 772
  3.2 9.5 %collective-permute-start.1 = (bf16[2048,128]{1,0:T(8,128)(2,1)S(1)}, bf16[2048,128]{1,0:T(8,128)(2,1)S(1)}, u32[]{:S(2)}, u32[]{:S(2)}) collective-permute-start(bf16[2048,128]{1,0:T(8,128)(2,1)S(1)} %bitcast.9), channel_id=1, source_target_pairs={{0,2},{2,0},{4,6},{6,4},{8,10},{10,8},{12,14},{14,12},{16,18},{18,... | collective-permute-start | bytes 1572872 | tf_op jit(solution)/shard_map/ppermute | solution.py:223
  3.6 10.2 %collective-permute-start.3 = (bf16[64,128]{1,0:T(8,128)(2,1)S(1)}, bf16[64,128]{1,0:T(8,128)(2,1)S(1)}, u32[]{:S(2)}, u32[]{:S(2)}) collective-permute-start(bf16[64,128]{1,0:T(8,128)(2,1)S(1)} %get-tuple-element.31), channel_id=1, source_target_pairs={{0,16},{2,30},{4,20},{6,26},{8,24},{10,22},{12,28},{14,18},{16,0},... | collective-permute-start | bytes 49160 | tf_op jit(solution)/shard_map/ppermute | solution.py:235
  7.4 6.4 %collective-permute-start.4 = (bf16[64,128]{1,0:T(8,128)(2,1)S(1)}, bf16[64,128]{1,0:T(8,128)(2,1)S(1)}, u32[]{:S(2)}, u32[]{:S(2)}) collective-permute-start(bf16[64,128]{1,0:T(8,128)(2,1)S(1)} %get-tuple-element.41), channel_id=1, source_target_pairs={{0,24},{2,14},{4,28},{6,10},{8,16},{10,6},{12,20},{14,2},{16,8},{1... | collective-permute-start | bytes 49160 | tf_op jit(solution)/shard_map/ppermute | solution.py:235
  8.7 5.5 %collective-permute-start.5 = (bf16[64,128]{1,0:T(8,128)(2,1)S(1)}, bf16[64,128]{1,0:T(8,128)(2,1)S(1)}, u32[]{:S(2)}, u32[]{:S(2)}) collective-permute-start(bf16[64,128]{1,0:T(8,128)(2,1)S(1)} %get-tuple-element.42), channel_id=1, source_target_pairs={{0,20},{2,6},{4,16},{6,2},{8,28},{10,14},{12,24},{14,10},{16,4},{1... | collective-permute-start | bytes 49160 | tf_op jit(solution)/shard_map/ppermute | solution.py:235
  11.4 3.7 %collective-permute-start.6 = (bf16[64,128]{1,0:T(8,128)(2,1)S(1)}, bf16[64,128]{1,0:T(8,128)(2,1)S(1)}, u32[]{:S(2)}, u32[]{:S(2)}) collective-permute-start(bf16[64,128]{1,0:T(8,128)(2,1)S(1)} %get-tuple-element.43), channel_id=1, source_target_pairs={{0,8},{2,10},{4,12},{6,14},{8,0},{10,2},{12,4},{14,6},{16,24},{18,... | collective-permute-start | bytes 49160 | tf_op jit(solution)/shard_map/ppermute | solution.py:235
  15.4 1.7 %collective-permute-start.7 = (f32[2,128,256]{2,1,0:T(8,128)S(1)}, f32[2,128,256]{2,1,0:T(8,128)S(1)}, u32[]{:S(2)}, u32[]{:S(2)}) collective-permute-start(f32[2,128,256]{2,1,0:T(8,128)S(1)} %image.1.here), channel_id=1, source_target_pairs={{0,2},{2,0},{4,6},{6,4},{8,10},{10,8},{12,14},{14,12},{16,18},{18,... | collective-permute-start | bytes 786440 | tf_op jit(solution)/shard_map/ppermute | solution.py:223
  15.5 8.4 %copy-start = (bf16[1,256,8,128]{3,2,1,0:T(8,128)(2,1)S(1)}, bf16[1,256,8,128]{3,2,1,0:T(8,128)(2,1)}, u32[]{:S(2)}) copy-start(bf16[1,256,8,128]{3,2,1,0:T(8,128)(2,1)} %param.6) | copy-start | bytes 1572868
  15.5 8.6 %collective-permute-start.2 = (f32[256,128]{1,0:T(8,128)S(1)}, f32[256,128]{1,0:T(8,128)S(1)}, u32[]{:S(2)}, u32[]{:S(2)}) collective-permute-start(f32[256,128]{1,0:T(8,128)S(1)} %get-tuple-element.35.here), channel_id=1, source_target_pairs={{0,1},{1,0},{2,3},{3,2},{4,5},{5,4},{6,7},{7,6},{8,9},{9,8},{10,11... | collective-permute-start | bytes 393224 | tf_op jit(solution)/shard_map/ppermute | solution.py:291
  17.5 6.7 %collective-permute-start.8 = (bf16[64,128]{1,0:T(8,128)(2,1)S(1)}, bf16[64,128]{1,0:T(8,128)(2,1)S(1)}, u32[]{:S(2)}, u32[]{:S(2)}) collective-permute-start(bf16[64,128]{1,0:T(8,128)(2,1)S(1)} %get-tuple-element.45), channel_id=1, source_target_pairs={{0,16},{2,30},{4,20},{6,26},{8,24},{10,22},{12,28},{14,18},{16,0},... | collective-permute-start | bytes 49160 | tf_op jit(solution)/shard_map/ppermute | solution.py:235
  18.8 5.5 %collective-permute-start.9 = (bf16[64,128]{1,0:T(8,128)(2,1)S(1)}, bf16[64,128]{1,0:T(8,128)(2,1)S(1)}, u32[]{:S(2)}, u32[]{:S(2)}) collective-permute-start(bf16[64,128]{1,0:T(8,128)(2,1)S(1)} %get-tuple-element.48), channel_id=1, source_target_pairs={{0,24},{2,14},{4,28},{6,10},{8,16},{10,6},{12,20},{14,2},{16,8},{1... | collective-permute-start | bytes 49160 | tf_op jit(solution)/shard_map/ppermute | solution.py:235
  21.2 5.5 %collective-permute-start.10 = (bf16[64,128]{1,0:T(8,128)(2,1)S(1)}, bf16[64,128]{1,0:T(8,128)(2,1)S(1)}, u32[]{:S(2)}, u32[]{:S(2)}) collective-permute-start(bf16[64,128]{1,0:T(8,128)(2,1)S(1)} %get-tuple-element.49), channel_id=1, source_target_pairs={{0,20},{2,6},{4,16},{6,2},{8,28},{10,14},{12,24},{14,10},{16,4},{1... | collective-permute-start | bytes 49160 | tf_op jit(solution)/shard_map/ppermute | solution.py:235
  22.1 4.6 %collective-permute-start.11 = (bf16[64,128]{1,0:T(8,128)(2,1)S(1)}, bf16[64,128]{1,0:T(8,128)(2,1)S(1)}, u32[]{:S(2)}, u32[]{:S(2)}) collective-permute-start(bf16[64,128]{1,0:T(8,128)(2,1)S(1)} %get-tuple-element.50), channel_id=1, source_target_pairs={{0,8},{2,10},{4,12},{6,14},{8,0},{10,2},{12,4},{14,6},{16,24},{18,... | collective-permute-start | bytes 49160 | tf_op jit(solution)/shard_map/ppermute | solution.py:235
  26.8 1.3 %collective-permute-start.12 = (bf16[4,64,128]{2,1,0:T(8,128)(2,1)S(1)}, bf16[4,64,128]{2,1,0:T(8,128)(2,1)S(1)}, u32[]{:S(2)}, u32[]{:S(2)}) collective-permute-start(bf16[4,64,128]{2,1,0:T(8,128)(2,1)S(1)} %pack.1.own), channel_id=1, source_target_pairs={{0,2},{2,0},{4,6},{6,4},{8,10},{10,8},{12,14},{14,12},{16,18},{18,... | collective-permute-start | bytes 196616 | tf_op jit(solution)/shard_map/ppermute | solution.py:223
  28.5 4.3 %collective-permute-start.13 = (bf16[256,128]{1,0:T(8,128)(2,1)S(1)}, bf16[256,128]{1,0:T(8,128)(2,1)S(1)}, u32[]{:S(2)}, u32[]{:S(2)}) collective-permute-start(bf16[256,128]{1,0:T(8,128)(2,1)S(1)} %gradient.1), channel_id=1, source_target_pairs={{0,1},{1,0},{2,3},{3,2},{4,5},{5,4},{6,7},{7,6},{8,9},{9,8},{10,11... | collective-permute-start | bytes 196616 | tf_op jit(solution)/shard_map/ppermute | solution.py:320

commit v8 on v7

--- a/solution.py
+++ b/solution.py
@@ -19,9 +19,10 @@
 
 
 def shifts_of(chips):
-    upper = sorted(range(chips // 2, chips - 1), key=lambda shift: (shift % 2, shift))
-    lower = sorted(range(1, chips // 2), key=lambda shift: (-shift.bit_count(), shift))
-    return [[*upper, 0], [chips - 1, *lower]]
+    same_side_first = lambda shift: (shift % 2, shift)
+    upper = sorted(range(chips // 2, chips - 1), key=same_side_first)
+    lower = sorted(range(2, chips // 2), key=same_side_first)
+    return [[*upper, 1], [*lower[:1], chips - 1, *lower[1:], 0]]
 
 
 def own_index(shifts):

time: 33.7 us -> 33.7 us (level)
  waiting for transfers between devices: 8.79 us -> 10.8 us
  starting transfers between devices: 19.6 us -> 17.6 us
    ppermute x8, waiting for transfers between devices: 3.86 us -> 5.87 us  [exchange(): lax.ppermute(send, 'tile', [(i, i ^ 2 * pair[i % 2]) for i in range(count)])]
    ppermute x8, starting transfers between devices: 15.5 us -> 13.5 us  [exchange(): lax.ppermute(send, 'tile', [(i, i ^ 2 * pair[i % 2]) for i in range(count)])]
where the time goes in v8:
time: 33.7 us; the launch traced here: 33.6 us
  starting transfers between devices  17.6 us (52%)
  waiting for transfers between devices  10.8 us (32%)
  Pallas kernels  4.94 us (15%)
    ppermute x8, starting transfers between devices, exchange(): lax.ppermute(send, 'tile', [(i, i ^ 2 * pair[i % 2]) for i in range(count)])  13.5 us
    ppermute x8, waiting for transfers between devices, exchange(): lax.ppermute(send, 'tile', [(i, i ^ 2 * pair[i % 2]) for i in range(count)])  5.87 us
    pallas_call x10, Pallas kernels, call(): pl.pallas_call(kernel, out_shape=outs, in_specs=[pl.BlockSpec(memory_spac...  4.94 us
    ppermute x1, waiting for transfers between devices, body(): lax.ppermute(gradient, 'freq', [(f, (f - shift) % band) for f in range(ba...  2.78 us
    ppermute x4, waiting for transfers between devices, to_mate(): lax.ppermute(value, 'tile', [(i, i ^ 1) for i in range(lax.axis_size('til...  2.15 us
    ppermute x1, starting transfers between devices, body(): lax.ppermute(start, 'freq', [(f, (f - shift) % band) for f in range(band)])  1.59 us
    ppermute x1, starting transfers between devices, body(): lax.ppermute(gradient, 'freq', [(f, (f - shift) % band) for f in range(ba...  1.51 us
    ppermute x4, starting transfers between devices, to_mate(): lax.ppermute(value, 'tile', [(i, i ^ 1) for i in range(lax.axis_size('til...  1.07 us
  transfers between devices with their start and end apart: 14, of which 7 were waited for; matrix products, arithmetic and copies ran while one was open for 0% of the time, Pallas kernels for 5%

profile of v8, /device:TPU:0, one launch (start us, length us, event | category | flops | bytes accessed | tf_op | source)
XLA Modules:
  0.0 33.6 jit_solution(6212159760615969059)
XLA Ops:
  0.0 1.7 %forward.1 = (bf16[4,64,128]{2,1,0:T(8,128)(2,1)S(1)}, bf16[4,64,128]{2,1,0:T(8,128)(2,1)S(1)}) custom-call(f32[256,128]{1,0:T(8,128)} %bitcast.7, bf16[2048,128]{1,0:T(8,128)(2,1)} %bitcast.5), custom_call_target="tpu_custom_call" | custom-call | flops 67108864 | bytes 786432 | tf_op jit(solution)/shard_map/forward/pallas_call | solution.py:211
  1.8 0.0 copy-start.1
  1.8 0.5 %collective-permute-start = (bf16[4,64,128]{2,1,0:T(8,128)(2,1)S(1)}, bf16[4,64,128]{2,1,0:T(8,128)(2,1)S(1)}, u32[]{:S(2)}, u32[]{:S(2)}) collective-permute-start(bf16[4,64,128]{2,1,0:T(8,128)(2,1)S(1)} %get-tuple-element.30), channel_id=1, source_target_pairs={{0,2},{2,0},{4,6},{6,4},{8,10},{10,8},{12,14},{14,12},{16,18},{18,... | collective-permute-start | bytes 196616 | tf_op jit(solution)/shard_map/ppermute | solution.py:224
  2.3 0.9 %collective-permute-done.arrived = bf16[4,64,128]{2,1,0:T(8,128)(2,1)S(1)} collective-permute-done((bf16[4,64,128]{2,1,0:T(8,128)(2,1)S(1)}, bf16[4,64,128]{2,1,0:T(8,128)(2,1)S(1)}, u32[]{:S(2)}, u32[]{:S(2)}) %collective-permute-start) | collective-permute-done | bytes 65568 | tf_op jit(solution)/shard_map/ppermute | solution.py:224
  3.2 0.0 copy-start.4
  3.2 0.4 %collective-permute-start.1 = (bf16[2048,128]{1,0:T(8,128)(2,1)S(1)}, bf16[2048,128]{1,0:T(8,128)(2,1)S(1)}, u32[]{:S(2)}, u32[]{:S(2)}) collective-permute-start(bf16[2048,128]{1,0:T(8,128)(2,1)S(1)} %bitcast.9), channel_id=1, source_target_pairs={{0,2},{2,0},{4,6},{6,4},{8,10},{10,8},{12,14},{14,12},{16,18},{18,... | collective-permute-start | bytes 1572872 | tf_op jit(solution)/shard_map/ppermute | solution.py:224
  3.6 3.7 %collective-permute-start.3 = (bf16[64,128]{1,0:T(8,128)(2,1)S(1)}, bf16[64,128]{1,0:T(8,128)(2,1)S(1)}, u32[]{:S(2)}, u32[]{:S(2)}) collective-permute-start(bf16[64,128]{1,0:T(8,128)(2,1)S(1)} %get-tuple-element.31), channel_id=1, source_target_pairs={{0,16},{2,10},{4,20},{6,14},{8,24},{10,2},{12,28},{14,6},{16,0},{1... | collective-permute-start | bytes 49160 | tf_op jit(solution)/shard_map/ppermute | solution.py:236
  7.4 1.4 %collective-permute-start.4 = (bf16[64,128]{1,0:T(8,128)(2,1)S(1)}, bf16[64,128]{1,0:T(8,128)(2,1)S(1)}, u32[]{:S(2)}, u32[]{:S(2)}) collective-permute-start(bf16[64,128]{1,0:T(8,128)(2,1)S(1)} %get-tuple-element.41), channel_id=1, source_target_pairs={{0,24},{2,30},{4,28},{6,26},{8,16},{10,22},{12,20},{14,18},{16,8},... | collective-permute-start | bytes 49160 | tf_op jit(solution)/shard_map/ppermute | solution.py:236
  8.7 2.6 %collective-permute-start.5 = (bf16[64,128]{1,0:T(8,128)(2,1)S(1)}, bf16[64,128]{1,0:T(8,128)(2,1)S(1)}, u32[]{:S(2)}, u32[]{:S(2)}) collective-permute-start(bf16[64,128]{1,0:T(8,128)(2,1)S(1)} %get-tuple-element.42), channel_id=1, source_target_pairs={{0,20},{2,14},{4,16},{6,10},{8,28},{10,6},{12,24},{14,2},{16,4},{1... | collective-permute-start | bytes 49160 | tf_op jit(solution)/shard_map/ppermute | solution.py:236
  11.4 0.5 %collective-permute-start.6 = (bf16[64,128]{1,0:T(8,128)(2,1)S(1)}, bf16[64,128]{1,0:T(8,128)(2,1)S(1)}, u32[]{:S(2)}, u32[]{:S(2)}) collective-permute-start(bf16[64,128]{1,0:T(8,128)(2,1)S(1)} %get-tuple-element.43), channel_id=1, source_target_pairs={{0,4},{2,6},{4,0},{6,2},{8,12},{10,14},{12,8},{14,10},{16,20},{18,... | collective-permute-start | bytes 49160 | tf_op jit(solution)/shard_map/ppermute | solution.py:236
  11.9 0.0 collective-permute-done.1.mate
  11.9 1.1 %rows.1 = (bf16[256,512]{1,0:T(8,128)(2,1)S(1)}, bf16[256,512]{1,0:T(8,128)(2,1)S(1)}, f32[128,256]{1,0:T(8,128)S(1)}, f32[256,128]{1,0:T(8,128)S(1)}) custom-call(s32[1,8,8]{2,1,0:T(8,128)S(1)} %copy-done.4, bf16[2048,128]{1,0:T(8,128)(2,1)S(1)} %bitcast.10, bf16[2048,128]{1,0:T(8,128)(2,1)S(1)} %collective-permute-done.1.mate, f32[256,128]{1,0:T(8,128)S(1)} %bitcast.11, ...), custom_call_target="tpu_custom_call" | custom-call | bytes 2097408 | tf_op jit(solution)/shard_map/rows/pallas_call | solution.py:211
  13.0 1.3 %collective-permute-done.5.refs_2_ = bf16[64,128]{1,0:T(8,128)(2,1)S(1)} collective-permute-done((bf16[64,128]{1,0:T(8,128)(2,1)S(1)}, bf16[64,128]{1,0:T(8,128)(2,1)S(1)}, u32[]{:S(2)}, u32[]{:S(2)}) %collective-permute-start.5) | collective-permute-done | bytes 16416 | tf_op jit(solution)/shard_map/ppermute | solution.py:236
  14.3 0.8 %collective-permute-done.6.refs_3_ = bf16[64,128]{1,0:T(8,128)(2,1)S(1)} collective-permute-done((bf16[64,128]{1,0:T(8,128)(2,1)S(1)}, bf16[64,128]{1,0:T(8,128)(2,1)S(1)}, u32[]{:S(2)}, u32[]{:S(2)}) %collective-permute-start.6) | collective-permute-done | bytes 16416 | tf_op jit(solution)/shard_map/ppermute | solution.py:236
  15.1 0.3 image.1.here
  15.4 0.1 collective-permute-start.7
  15.5 0.0 copy-start
  15.5 1.6 %collective-permute-start.2 = (f32[256,128]{1,0:T(8,128)S(1)}, f32[256,128]{1,0:T(8,128)S(1)}, u32[]{:S(2)}, u32[]{:S(2)}) collective-permute-start(f32[256,128]{1,0:T(8,128)S(1)} %get-tuple-element.35.here), channel_id=1, source_target_pairs={{0,1},{1,0},{2,3},{3,2},{4,5},{5,4},{6,7},{7,6},{8,9},{9,8},{10,11... | collective-permute-start | bytes 393224 | tf_op jit(solution)/shard_map/ppermute | solution.py:292
  17.1 0.3 %back.1 = (bf16[64,128]{1,0:T(8,128)(2,1)S(1)}, bf16[64,128]{1,0:T(8,128)(2,1)S(1)}, bf16[64,128]{1,0:T(8,128)(2,1)S(1)}, bf16[64,128]{1,0:T(8,128)(2,1)S(1)}, bf16[64,128]{1,0:T(8,128)(2,1)S(1)}) custom-call(f32[2,128,256]{2,1,0:T(8,128)S(1)} %image.1.here, f32[2,128,256]{2,1,0:T(8,128)S(1)} %collective-permute-done.7.there, ...), custom_call_target="tpu_custom_call" | custom-call | flops 67108864 | bytes 1130496 | tf_op jit(solution)/shard_map/back/pallas_call | solution.py:211
  17.5 1.3 %collective-permute-start.8 = (bf16[64,128]{1,0:T(8,128)(2,1)S(1)}, bf16[64,128]{1,0:T(8,128)(2,1)S(1)}, u32[]{:S(2)}, u32[]{:S(2)}) collective-permute-start(bf16[64,128]{1,0:T(8,128)(2,1)S(1)} %get-tuple-element.45), channel_id=1, source_target_pairs={{0,16},{2,10},{4,20},{6,14},{8,24},{10,2},{12,28},{14,6},{16,0},{1... | collective-permute-start | bytes 49160 | tf_op jit(solution)/shard_map/ppermute | solution.py:236
  18.8 2.5 %collective-permute-start.9 = (bf16[64,128]{1,0:T(8,128)(2,1)S(1)}, bf16[64,128]{1,0:T(8,128)(2,1)S(1)}, u32[]{:S(2)}, u32[]{:S(2)}) collective-permute-start(bf16[64,128]{1,0:T(8,128)(2,1)S(1)} %get-tuple-element.48), channel_id=1, source_target_pairs={{0,24},{2,30},{4,28},{6,26},{8,16},{10,22},{12,20},{14,18},{16,8},... | collective-permute-start | bytes 49160 | tf_op jit(solution)/shard_map/ppermute | solution.py:236
  21.2 0.9 %collective-permute-start.10 = (bf16[64,128]{1,0:T(8,128)(2,1)S(1)}, bf16[64,128]{1,0:T(8,128)(2,1)S(1)}, u32[]{:S(2)}, u32[]{:S(2)}) collective-permute-start(bf16[64,128]{1,0:T(8,128)(2,1)S(1)} %get-tuple-element.49), channel_id=1, source_target_pairs={{0,20},{2,14},{4,16},{6,10},{8,28},{10,6},{12,24},{14,2},{16,4},{1... | collective-permute-start | bytes 49160 | tf_op jit(solution)/shard_map/ppermute | solution.py:236
  22.1 0.5 %collective-permute-start.11 = (bf16[64,128]{1,0:T(8,128)(2,1)S(1)}, bf16[64,128]{1,0:T(8,128)(2,1)S(1)}, u32[]{:S(2)}, u32[]{:S(2)}) collective-permute-start(bf16[64,128]{1,0:T(8,128)(2,1)S(1)} %get-tuple-element.50), channel_id=1, source_target_pairs={{0,4},{2,6},{4,0},{6,2},{8,12},{10,14},{12,8},{14,10},{16,20},{18,... | collective-permute-start | bytes 49160 | tf_op jit(solution)/shard_map/ppermute | solution.py:236
  22.7 0.3 columns.1.factors
  23.0 1.3 %collective-permute-done.9.refs_1_ = bf16[64,128]{1,0:T(8,128)(2,1)S(1)} collective-permute-done((bf16[64,128]{1,0:T(8,128)(2,1)S(1)}, bf16[64,128]{1,0:T(8,128)(2,1)S(1)}, u32[]{:S(2)}, u32[]{:S(2)}) %collective-permute-start.9) | collective-permute-done | bytes 16416 | tf_op jit(solution)/shard_map/ppermute | solution.py:236
  24.3 2.5 %collective-permute-done.10.refs_2_ = bf16[64,128]{1,0:T(8,128)(2,1)S(1)} collective-permute-done((bf16[64,128]{1,0:T(8,128)(2,1)S(1)}, bf16[64,128]{1,0:T(8,128)(2,1)S(1)}, u32[]{:S(2)}, u32[]{:S(2)}) %collective-permute-start.10) | collective-permute-done | bytes 16416 | tf_op jit(solution)/shard_map/ppermute | solution.py:236
  26.8 0.1 collective-permute-start.12
  26.9 1.2 %collective-permute-done.12.mate = bf16[4,64,128]{2,1,0:T(8,128)(2,1)S(1)} collective-permute-done((bf16[4,64,128]{2,1,0:T(8,128)(2,1)S(1)}, bf16[4,64,128]{2,1,0:T(8,128)(2,1)S(1)}, u32[]{:S(2)}, u32[]{:S(2)}) %collective-permute-start.12) | collective-permute-done | bytes 65568 | tf_op jit(solution)/shard_map/ppermute | solution.py:224
  28.1 0.4 %gradient.1 = bf16[256,128]{1,0:T(8,128)(2,1)S(1)} custom-call(bf16[4,64,128]{2,1,0:T(8,128)(2,1)S(1)} %pack.1.own, bf16[4,64,128]{2,1,0:T(8,128)(2,1)S(1)} %collective-permute-done.12.mate, bf16[256,1024]{1,0:T(8,128)(2,1)S(1)} %columns.1.factors), custom_call_target="tpu_custom_call" | custom-call | flops 67108864 | bytes 720896 | tf_op jit(solution)/shard_map/gradient/pallas_call | solution.py:211
  28.5 1.5 %collective-permute-start.13 = (bf16[256,128]{1,0:T(8,128)(2,1)S(1)}, bf16[256,128]{1,0:T(8,128)(2,1)S(1)}, u32[]{:S(2)}, u32[]{:S(2)}) collective-permute-start(bf16[256,128]{1,0:T(8,128)(2,1)S(1)} %gradient.1), channel_id=1, source_target_pairs={{0,1},{1,0},{2,3},{3,2},{4,5},{5,4},{6,7},{7,6},{8,9},{9,8},{10,11... | collective-permute-start | bytes 196616 | tf_op jit(solution)/shard_map/ppermute | solution.py:321
  30.1 2.8 %collective-permute-done.13.gradient = bf16[256,128]{1,0:T(8,128)(2,1)S(1)} collective-permute-done((bf16[256,128]{1,0:T(8,128)(2,1)S(1)}, bf16[256,128]{1,0:T(8,128)(2,1)S(1)}, u32[]{:S(2)}, u32[]{:S(2)}) %collective-permute-start.13) | collective-permute-done | bytes 65568 | tf_op jit(solution)/shard_map/ppermute | solution.py:321
  32.9 0.7 %shrink.1 = f32[256,128]{1,0:T(8,128)} custom-call(f32[256,128]{1,0:T(8,128)S(1)} %get-tuple-element.51.total, f32[256,128]{1,0:T(8,128)S(1)} %get-tuple-element.52.difference, bf16[256,128]{1,0:T(8,128)(2,1)S(1)} %collective-permute-done.13.gradient), custom_call_target="tpu_custom_call" | custom-call | bytes 458752 | tf_op jit(solution)/shard_map/shrink/pallas_call | solution.py:211
  (16 shorter events, 0.1 us)
Async XLA Ops:
  0.0 3.2 %copy-start.2 = (bf16[1,256,8,128]{3,2,1,0:T(8,128)(2,1)S(1)}, bf16[1,256,8,128]{3,2,1,0:T(8,128)(2,1)}, u32[]{:S(2)}) copy-start(bf16[1,256,8,128]{3,2,1,0:T(8,128)(2,1)} %param.5) | copy-start | bytes 1572868
  0.0 11.9 %copy-start.3 = (f32[1,256,128]{2,1,0:T(8,128)S(1)}, f32[1,256,128]{2,1,0:T(8,128)}, u32[]{:S(2)}) copy-start(f32[1,256,128]{2,1,0:T(8,128)} %param.8) | copy-start | bytes 393220
  1.8 10.1 %copy-start.1 = (f32[1,256,128]{2,1,0:T(8,128)S(1)}, f32[1,256,128]{2,1,0:T(8,128)}, u32[]{:S(2)}) copy-start(f32[1,256,128]{2,1,0:T(8,128)} %param.9) | copy-start | bytes 393220
  1.8 1.4 %collective-permute-start = (bf16[4,64,128]{2,1,0:T(8,128)(2,1)S(1)}, bf16[4,64,128]{2,1,0:T(8,128)(2,1)S(1)}, u32[]{:S(2)}, u32[]{:S(2)}) collective-permute-start(bf16[4,64,128]{2,1,0:T(8,128)(2,1)S(1)} %get-tuple-element.30), channel_id=1, source_target_pairs={{0,2},{2,0},{4,6},{6,4},{8,10},{10,8},{12,14},{14,12},{16,18},{18,... | collective-permute-start | bytes 196616 | tf_op jit(solution)/shard_map/ppermute | solution.py:224
  3.2 8.7 %copy-start.4 = (s32[1,8,8]{2,1,0:T(8,128)S(1)}, s32[1,8,8]{2,1,0:T(8,128)}, u32[]{:S(2)}) copy-start(s32[1,8,8]{2,1,0:T(8,128)} %ranks.1) | copy-start | bytes 772
  3.2 8.7 %collective-permute-start.1 = (bf16[2048,128]{1,0:T(8,128)(2,1)S(1)}, bf16[2048,128]{1,0:T(8,128)(2,1)S(1)}, u32[]{:S(2)}, u32[]{:S(2)}) collective-permute-start(bf16[2048,128]{1,0:T(8,128)(2,1)S(1)} %bitcast.9), channel_id=1, source_target_pairs={{0,2},{2,0},{4,6},{6,4},{8,10},{10,8},{12,14},{14,12},{16,18},{18,... | collective-permute-start | bytes 1572872 | tf_op jit(solution)/shard_map/ppermute | solution.py:224
  3.6 9.4 %collective-permute-start.3 = (bf16[64,128]{1,0:T(8,128)(2,1)S(1)}, bf16[64,128]{1,0:T(8,128)(2,1)S(1)}, u32[]{:S(2)}, u32[]{:S(2)}) collective-permute-start(bf16[64,128]{1,0:T(8,128)(2,1)S(1)} %get-tuple-element.31), channel_id=1, source_target_pairs={{0,16},{2,10},{4,20},{6,14},{8,24},{10,2},{12,28},{14,6},{16,0},{1... | collective-permute-start | bytes 49160 | tf_op jit(solution)/shard_map/ppermute | solution.py:236
  7.4 5.6 %collective-permute-start.4 = (bf16[64,128]{1,0:T(8,128)(2,1)S(1)}, bf16[64,128]{1,0:T(8,128)(2,1)S(1)}, u32[]{:S(2)}, u32[]{:S(2)}) collective-permute-start(bf16[64,128]{1,0:T(8,128)(2,1)S(1)} %get-tuple-element.41), channel_id=1, source_target_pairs={{0,24},{2,30},{4,28},{6,26},{8,16},{10,22},{12,20},{14,18},{16,8},... | collective-permute-start | bytes 49160 | tf_op jit(solution)/shard_map/ppermute | solution.py:236
  8.7 5.5 %collective-permute-start.5 = (bf16[64,128]{1,0:T(8,128)(2,1)S(1)}, bf16[64,128]{1,0:T(8,128)(2,1)S(1)}, u32[]{:S(2)}, u32[]{:S(2)}) collective-permute-start(bf16[64,128]{1,0:T(8,128)(2,1)S(1)} %get-tuple-element.42), channel_id=1, source_target_pairs={{0,20},{2,14},{4,16},{6,10},{8,28},{10,6},{12,24},{14,2},{16,4},{1... | collective-permute-start | bytes 49160 | tf_op jit(solution)/shard_map/ppermute | solution.py:236
  11.4 3.7 %collective-permute-start.6 = (bf16[64,128]{1,0:T(8,128)(2,1)S(1)}, bf16[64,128]{1,0:T(8,128)(2,1)S(1)}, u32[]{:S(2)}, u32[]{:S(2)}) collective-permute-start(bf16[64,128]{1,0:T(8,128)(2,1)S(1)} %get-tuple-element.43), channel_id=1, source_target_pairs={{0,4},{2,6},{4,0},{6,2},{8,12},{10,14},{12,8},{14,10},{16,20},{18,... | collective-permute-start | bytes 49160 | tf_op jit(solution)/shard_map/ppermute | solution.py:236
  15.4 1.7 %collective-permute-start.7 = (f32[2,128,256]{2,1,0:T(8,128)S(1)}, f32[2,128,256]{2,1,0:T(8,128)S(1)}, u32[]{:S(2)}, u32[]{:S(2)}) collective-permute-start(f32[2,128,256]{2,1,0:T(8,128)S(1)} %image.1.here), channel_id=1, source_target_pairs={{0,2},{2,0},{4,6},{6,4},{8,10},{10,8},{12,14},{14,12},{16,18},{18,... | collective-permute-start | bytes 786440 | tf_op jit(solution)/shard_map/ppermute | solution.py:224
  15.5 7.2 %copy-start = (bf16[1,256,8,128]{3,2,1,0:T(8,128)(2,1)S(1)}, bf16[1,256,8,128]{3,2,1,0:T(8,128)(2,1)}, u32[]{:S(2)}) copy-start(bf16[1,256,8,128]{3,2,1,0:T(8,128)(2,1)} %param.6) | copy-start | bytes 1572868
  15.5 7.4 %collective-permute-start.2 = (f32[256,128]{1,0:T(8,128)S(1)}, f32[256,128]{1,0:T(8,128)S(1)}, u32[]{:S(2)}, u32[]{:S(2)}) collective-permute-start(f32[256,128]{1,0:T(8,128)S(1)} %get-tuple-element.35.here), channel_id=1, source_target_pairs={{0,1},{1,0},{2,3},{3,2},{4,5},{5,4},{6,7},{7,6},{8,9},{9,8},{10,11... | collective-permute-start | bytes 393224 | tf_op jit(solution)/shard_map/ppermute | solution.py:292
  17.5 5.5 %collective-permute-start.8 = (bf16[64,128]{1,0:T(8,128)(2,1)S(1)}, bf16[64,128]{1,0:T(8,128)(2,1)S(1)}, u32[]{:S(2)}, u32[]{:S(2)}) collective-permute-start(bf16[64,128]{1,0:T(8,128)(2,1)S(1)} %get-tuple-element.45), channel_id=1, source_target_pairs={{0,16},{2,10},{4,20},{6,14},{8,24},{10,2},{12,28},{14,6},{16,0},{1... | collective-permute-start | bytes 49160 | tf_op jit(solution)/shard_map/ppermute | solution.py:236
  18.8 5.5 %collective-permute-start.9 = (bf16[64,128]{1,0:T(8,128)(2,1)S(1)}, bf16[64,128]{1,0:T(8,128)(2,1)S(1)}, u32[]{:S(2)}, u32[]{:S(2)}) collective-permute-start(bf16[64,128]{1,0:T(8,128)(2,1)S(1)} %get-tuple-element.48), channel_id=1, source_target_pairs={{0,24},{2,30},{4,28},{6,26},{8,16},{10,22},{12,20},{14,18},{16,8},... | collective-permute-start | bytes 49160 | tf_op jit(solution)/shard_map/ppermute | solution.py:236
  21.2 5.5 %collective-permute-start.10 = (bf16[64,128]{1,0:T(8,128)(2,1)S(1)}, bf16[64,128]{1,0:T(8,128)(2,1)S(1)}, u32[]{:S(2)}, u32[]{:S(2)}) collective-permute-start(bf16[64,128]{1,0:T(8,128)(2,1)S(1)} %get-tuple-element.49), channel_id=1, source_target_pairs={{0,20},{2,14},{4,16},{6,10},{8,28},{10,6},{12,24},{14,2},{16,4},{1... | collective-permute-start | bytes 49160 | tf_op jit(solution)/shard_map/ppermute | solution.py:236
  22.1 4.6 %collective-permute-start.11 = (bf16[64,128]{1,0:T(8,128)(2,1)S(1)}, bf16[64,128]{1,0:T(8,128)(2,1)S(1)}, u32[]{:S(2)}, u32[]{:S(2)}) collective-permute-start(bf16[64,128]{1,0:T(8,128)(2,1)S(1)} %get-tuple-element.50), channel_id=1, source_target_pairs={{0,4},{2,6},{4,0},{6,2},{8,12},{10,14},{12,8},{14,10},{16,20},{18,... | collective-permute-start | bytes 49160 | tf_op jit(solution)/shard_map/ppermute | solution.py:236
  26.8 1.3 %collective-permute-start.12 = (bf16[4,64,128]{2,1,0:T(8,128)(2,1)S(1)}, bf16[4,64,128]{2,1,0:T(8,128)(2,1)S(1)}, u32[]{:S(2)}, u32[]{:S(2)}) collective-permute-start(bf16[4,64,128]{2,1,0:T(8,128)(2,1)S(1)} %pack.1.own), channel_id=1, source_target_pairs={{0,2},{2,0},{4,6},{6,4},{8,10},{10,8},{12,14},{14,12},{16,18},{18,... | collective-permute-start | bytes 196616 | tf_op jit(solution)/shard_map/ppermute | solution.py:224
  28.5 4.3 %collective-permute-start.13 = (bf16[256,128]{1,0:T(8,128)(2,1)S(1)}, bf16[256,128]{1,0:T(8,128)(2,1)S(1)}, u32[]{:S(2)}, u32[]{:S(2)}) collective-permute-start(bf16[256,128]{1,0:T(8,128)(2,1)S(1)} %gradient.1), channel_id=1, source_target_pairs={{0,1},{1,0},{2,3},{3,2},{4,5},{5,4},{6,7},{7,6},{8,9},{9,8},{10,11... | collective-permute-start | bytes 196616 | tf_op jit(solution)/shard_map/ppermute | solution.py:321

commit v9 on v7

--- a/solution.py
+++ b/solution.py
@@ -19,9 +19,8 @@
 
 
 def shifts_of(chips):
-    upper = sorted(range(chips // 2, chips - 1), key=lambda shift: (shift % 2, shift))
-    lower = sorted(range(1, chips // 2), key=lambda shift: (-shift.bit_count(), shift))
-    return [[*upper, 0], [chips - 1, *lower]]
+    order = sorted(range(0, chips, 2), key=lambda shift: -(shift ^ shift >> 1))
+    return [order, [shift + 1 for shift in order]]
 
 
 def own_index(shifts):

time: 33.7 us -> 30.7 us (0.911)
  starting transfers between devices: 19.6 us -> 16.8 us
    ppermute x8, starting transfers between devices: 15.5 us -> 11.5 us  [exchange(): lax.ppermute(send, 'tile', [(i, i ^ 2 * pair[i % 2]) for i in range(count)])]
    ppermute x4, starting transfers between devices: 1.08 us -> 2.28 us  [to_mate(): lax.ppermute(value, 'tile', [(i, i ^ 1) for i in range(lax.axis_size('til...]
    ppermute x4, waiting for transfers between devices: 2.15 us -> 1.81 us  [to_mate(): lax.ppermute(value, 'tile', [(i, i ^ 1) for i in range(lax.axis_size('til...]
  transfers between devices with their start and end apart: 14 -> 14, of which waited for: 7 -> 5; matrix products, arithmetic and copies ran while one was open for 0% -> 0% of each run, Pallas kernels for 5% -> 6%
where the time goes in v9:
time: 30.7 us; the launch traced here: 30.6 us
  starting transfers between devices  16.8 us (55%)
  waiting for transfers between devices  8.73 us (28%)
  Pallas kernels  4.93 us (16%)
    ppermute x8, starting transfers between devices, exchange(): lax.ppermute(send, 'tile', [(i, i ^ 2 * pair[i % 2]) for i in range(count)])  11.5 us
    pallas_call x10, Pallas kernels, call(): pl.pallas_call(kernel, out_shape=outs, in_specs=[pl.BlockSpec(memory_spac...  4.93 us
    ppermute x8, waiting for transfers between devices, exchange(): lax.ppermute(send, 'tile', [(i, i ^ 2 * pair[i % 2]) for i in range(count)])  4.03 us
    ppermute x1, waiting for transfers between devices, body(): lax.ppermute(gradient, 'freq', [(f, (f - shift) % band) for f in range(ba...  2.89 us
    ppermute x4, starting transfers between devices, to_mate(): lax.ppermute(value, 'tile', [(i, i ^ 1) for i in range(lax.axis_size('til...  2.28 us
    ppermute x4, waiting for transfers between devices, to_mate(): lax.ppermute(value, 'tile', [(i, i ^ 1) for i in range(lax.axis_size('til...  1.81 us
    ppermute x1, starting transfers between devices, body(): lax.ppermute(start, 'freq', [(f, (f - shift) % band) for f in range(band)])  1.52 us
    ppermute x1, starting transfers between devices, body(): lax.ppermute(gradient, 'freq', [(f, (f - shift) % band) for f in range(ba...  1.5 us
  transfers between devices with their start and end apart: 14, of which 5 were waited for; matrix products, arithmetic and copies ran while one was open for 0% of the time, Pallas kernels for 6%

profile of v9, /device:TPU:0, one launch (start us, length us, event | category | flops | bytes accessed | tf_op | source)
XLA Modules:
  0.0 30.6 jit_solution(12127253791746448208)
XLA Ops:
  0.0 1.7 %forward.1 = (bf16[4,64,128]{2,1,0:T(8,128)(2,1)S(1)}, bf16[4,64,128]{2,1,0:T(8,128)(2,1)S(1)}) custom-call(f32[256,128]{1,0:T(8,128)} %bitcast.7, bf16[2048,128]{1,0:T(8,128)(2,1)} %bitcast.5), custom_call_target="tpu_custom_call" | custom-call | flops 67108864 | bytes 786432 | tf_op jit(solution)/shard_map/forward/pallas_call | solution.py:209
  1.8 0.0 copy-start.1
  1.8 0.5 %collective-permute-start = (bf16[4,64,128]{2,1,0:T(8,128)(2,1)S(1)}, bf16[4,64,128]{2,1,0:T(8,128)(2,1)S(1)}, u32[]{:S(2)}, u32[]{:S(2)}) collective-permute-start(bf16[4,64,128]{2,1,0:T(8,128)(2,1)S(1)} %get-tuple-element.30), channel_id=1, source_target_pairs={{0,2},{2,0},{4,6},{6,4},{8,10},{10,8},{12,14},{14,12},{16,18},{18,... | collective-permute-start | bytes 196616 | tf_op jit(solution)/shard_map/ppermute | solution.py:222
  2.3 0.9 %collective-permute-done.arrived = bf16[4,64,128]{2,1,0:T(8,128)(2,1)S(1)} collective-permute-done((bf16[4,64,128]{2,1,0:T(8,128)(2,1)S(1)}, bf16[4,64,128]{2,1,0:T(8,128)(2,1)S(1)}, u32[]{:S(2)}, u32[]{:S(2)}) %collective-permute-start) | collective-permute-done | bytes 65568 | tf_op jit(solution)/shard_map/ppermute | solution.py:222
  3.2 0.0 copy-start.4
  3.2 0.4 %collective-permute-start.1 = (bf16[2048,128]{1,0:T(8,128)(2,1)S(1)}, bf16[2048,128]{1,0:T(8,128)(2,1)S(1)}, u32[]{:S(2)}, u32[]{:S(2)}) collective-permute-start(bf16[2048,128]{1,0:T(8,128)(2,1)S(1)} %bitcast.9), channel_id=1, source_target_pairs={{0,2},{2,0},{4,6},{6,4},{8,10},{10,8},{12,14},{14,12},{16,18},{18,... | collective-permute-start | bytes 1572872 | tf_op jit(solution)/shard_map/ppermute | solution.py:222
  3.6 3.7 %collective-permute-start.3 = (bf16[64,128]{1,0:T(8,128)(2,1)S(1)}, bf16[64,128]{1,0:T(8,128)(2,1)S(1)}, u32[]{:S(2)}, u32[]{:S(2)}) collective-permute-start(bf16[64,128]{1,0:T(8,128)(2,1)S(1)} %get-tuple-element.31), channel_id=1, source_target_pairs={{0,16},{2,22},{4,20},{6,18},{8,24},{10,30},{12,28},{14,26},{16,0},... | collective-permute-start | bytes 49160 | tf_op jit(solution)/shard_map/ppermute | solution.py:234
  7.4 1.4 %collective-permute-start.4 = (bf16[64,128]{1,0:T(8,128)(2,1)S(1)}, bf16[64,128]{1,0:T(8,128)(2,1)S(1)}, u32[]{:S(2)}, u32[]{:S(2)}) collective-permute-start(bf16[64,128]{1,0:T(8,128)(2,1)S(1)} %get-tuple-element.41), channel_id=1, source_target_pairs={{0,24},{2,30},{4,28},{6,26},{8,16},{10,22},{12,20},{14,18},{16,8},... | collective-permute-start | bytes 49160 | tf_op jit(solution)/shard_map/ppermute | solution.py:234
  8.7 0.2 collective-permute-start.5
  9.0 1.5 %collective-permute-start.6 = (bf16[64,128]{1,0:T(8,128)(2,1)S(1)}, bf16[64,128]{1,0:T(8,128)(2,1)S(1)}, u32[]{:S(2)}, u32[]{:S(2)}) collective-permute-start(bf16[64,128]{1,0:T(8,128)(2,1)S(1)} %get-tuple-element.43), channel_id=1, source_target_pairs={{0,4},{2,6},{4,0},{6,2},{8,12},{10,14},{12,8},{14,10},{16,20},{18,... | collective-permute-start | bytes 49160 | tf_op jit(solution)/shard_map/ppermute | solution.py:234
  10.5 0.0 collective-permute-done.1.mate
  10.5 1.1 %rows.1 = (bf16[256,512]{1,0:T(8,128)(2,1)S(1)}, bf16[256,512]{1,0:T(8,128)(2,1)S(1)}, f32[128,256]{1,0:T(8,128)S(1)}, f32[256,128]{1,0:T(8,128)S(1)}) custom-call(s32[1,8,8]{2,1,0:T(8,128)S(1)} %copy-done.4, bf16[2048,128]{1,0:T(8,128)(2,1)S(1)} %bitcast.10, bf16[2048,128]{1,0:T(8,128)(2,1)S(1)} %collective-permute-done.1.mate, f32[256,128]{1,0:T(8,128)S(1)} %bitcast.11, ...), custom_call_target="tpu_custom_call" | custom-call | bytes 2097408 | tf_op jit(solution)/shard_map/rows/pallas_call | solution.py:209
  11.6 0.0 collective-permute-done.3.refs_0_
  11.6 1.5 %collective-permute-done.4.refs_1_ = bf16[64,128]{1,0:T(8,128)(2,1)S(1)} collective-permute-done((bf16[64,128]{1,0:T(8,128)(2,1)S(1)}, bf16[64,128]{1,0:T(8,128)(2,1)S(1)}, u32[]{:S(2)}, u32[]{:S(2)}) %collective-permute-start.4) | collective-permute-done | bytes 16416 | tf_op jit(solution)/shard_map/ppermute | solution.py:234
  13.1 0.0 collective-permute-done.5.refs_2_
  13.1 0.3 %image.1.here = f32[2,128,256]{2,1,0:T(8,128)S(1)} custom-call(bf16[64,128]{1,0:T(8,128)(2,1)S(1)} %get-tuple-element.36.sent, bf16[64,128]{1,0:T(8,128)(2,1)S(1)} %collective-permute-done.3.refs_0_, bf16[64,128]{1,0:T(8,128)(2,1)S(1)} %collective-permute-done.4.refs_1_, bf16[64,128]{1,0:T(8,128)(2,1)S(1)} %collective-permute-done.5.refs_2_, ...), custom_call_target="tpu_custom_call" | custom-call | flops 67108864 | bytes 999424 | tf_op jit(solution)/shard_map/image/pallas_call | solution.py:209
  13.4 0.8 %collective-permute-start.7 = (f32[2,128,256]{2,1,0:T(8,128)S(1)}, f32[2,128,256]{2,1,0:T(8,128)S(1)}, u32[]{:S(2)}, u32[]{:S(2)}) collective-permute-start(f32[2,128,256]{2,1,0:T(8,128)S(1)} %image.1.here), channel_id=1, source_target_pairs={{0,2},{2,0},{4,6},{6,4},{8,10},{10,8},{12,14},{14,12},{16,18},{18,... | collective-permute-start | bytes 786440 | tf_op jit(solution)/shard_map/ppermute | solution.py:222
  14.3 1.5 %collective-permute-start.2 = (f32[256,128]{1,0:T(8,128)S(1)}, f32[256,128]{1,0:T(8,128)S(1)}, u32[]{:S(2)}, u32[]{:S(2)}) collective-permute-start(f32[256,128]{1,0:T(8,128)S(1)} %get-tuple-element.35.here), channel_id=1, source_target_pairs={{0,1},{1,0},{2,3},{3,2},{4,5},{5,4},{6,7},{7,6},{8,9},{9,8},{10,11... | collective-permute-start | bytes 393224 | tf_op jit(solution)/shard_map/ppermute | solution.py:290
  15.8 0.3 %back.1 = (bf16[64,128]{1,0:T(8,128)(2,1)S(1)}, bf16[64,128]{1,0:T(8,128)(2,1)S(1)}, bf16[64,128]{1,0:T(8,128)(2,1)S(1)}, bf16[64,128]{1,0:T(8,128)(2,1)S(1)}, bf16[64,128]{1,0:T(8,128)(2,1)S(1)}) custom-call(f32[2,128,256]{2,1,0:T(8,128)S(1)} %image.1.here, f32[2,128,256]{2,1,0:T(8,128)S(1)} %collective-permute-done.7.there, ...), custom_call_target="tpu_custom_call" | custom-call | flops 67108864 | bytes 1130496 | tf_op jit(solution)/shard_map/back/pallas_call | solution.py:209
  16.1 1.9 %collective-permute-start.8 = (bf16[64,128]{1,0:T(8,128)(2,1)S(1)}, bf16[64,128]{1,0:T(8,128)(2,1)S(1)}, u32[]{:S(2)}, u32[]{:S(2)}) collective-permute-start(bf16[64,128]{1,0:T(8,128)(2,1)S(1)} %get-tuple-element.45), channel_id=1, source_target_pairs={{0,16},{2,22},{4,20},{6,18},{8,24},{10,30},{12,28},{14,26},{16,0},... | collective-permute-start | bytes 49160 | tf_op jit(solution)/shard_map/ppermute | solution.py:234
  18.0 1.3 %collective-permute-start.9 = (bf16[64,128]{1,0:T(8,128)(2,1)S(1)}, bf16[64,128]{1,0:T(8,128)(2,1)S(1)}, u32[]{:S(2)}, u32[]{:S(2)}) collective-permute-start(bf16[64,128]{1,0:T(8,128)(2,1)S(1)} %get-tuple-element.48), channel_id=1, source_target_pairs={{0,24},{2,30},{4,28},{6,26},{8,16},{10,22},{12,20},{14,18},{16,8},... | collective-permute-start | bytes 49160 | tf_op jit(solution)/shard_map/ppermute | solution.py:234
  19.4 0.3 collective-permute-start.10
  19.7 1.1 %collective-permute-start.11 = (bf16[64,128]{1,0:T(8,128)(2,1)S(1)}, bf16[64,128]{1,0:T(8,128)(2,1)S(1)}, u32[]{:S(2)}, u32[]{:S(2)}) collective-permute-start(bf16[64,128]{1,0:T(8,128)(2,1)S(1)} %get-tuple-element.50), channel_id=1, source_target_pairs={{0,4},{2,6},{4,0},{6,2},{8,12},{10,14},{12,8},{14,10},{16,20},{18,... | collective-permute-start | bytes 49160 | tf_op jit(solution)/shard_map/ppermute | solution.py:234
  20.8 0.3 columns.1.factors
  21.1 2.5 %collective-permute-done.9.refs_1_ = bf16[64,128]{1,0:T(8,128)(2,1)S(1)} collective-permute-done((bf16[64,128]{1,0:T(8,128)(2,1)S(1)}, bf16[64,128]{1,0:T(8,128)(2,1)S(1)}, u32[]{:S(2)}, u32[]{:S(2)}) %collective-permute-start.9) | collective-permute-done | bytes 16416 | tf_op jit(solution)/shard_map/ppermute | solution.py:234
  23.6 0.0 collective-permute-done.11.refs_3_
  23.6 0.5 %collective-permute-start.12 = (bf16[4,64,128]{2,1,0:T(8,128)(2,1)S(1)}, bf16[4,64,128]{2,1,0:T(8,128)(2,1)S(1)}, u32[]{:S(2)}, u32[]{:S(2)}) collective-permute-start(bf16[4,64,128]{2,1,0:T(8,128)(2,1)S(1)} %pack.1.own), channel_id=1, source_target_pairs={{0,2},{2,0},{4,6},{6,4},{8,10},{10,8},{12,14},{14,12},{16,18},{18,... | collective-permute-start | bytes 196616 | tf_op jit(solution)/shard_map/ppermute | solution.py:222
  24.1 0.9 %collective-permute-done.12.mate = bf16[4,64,128]{2,1,0:T(8,128)(2,1)S(1)} collective-permute-done((bf16[4,64,128]{2,1,0:T(8,128)(2,1)S(1)}, bf16[4,64,128]{2,1,0:T(8,128)(2,1)S(1)}, u32[]{:S(2)}, u32[]{:S(2)}) %collective-permute-start.12) | collective-permute-done | bytes 65568 | tf_op jit(solution)/shard_map/ppermute | solution.py:222
  25.0 0.4 %gradient.1 = bf16[256,128]{1,0:T(8,128)(2,1)S(1)} custom-call(bf16[4,64,128]{2,1,0:T(8,128)(2,1)S(1)} %pack.1.own, bf16[4,64,128]{2,1,0:T(8,128)(2,1)S(1)} %collective-permute-done.12.mate, bf16[256,1024]{1,0:T(8,128)(2,1)S(1)} %columns.1.factors), custom_call_target="tpu_custom_call" | custom-call | flops 67108864 | bytes 720896 | tf_op jit(solution)/shard_map/gradient/pallas_call | solution.py:209
  25.5 1.5 %collective-permute-start.13 = (bf16[256,128]{1,0:T(8,128)(2,1)S(1)}, bf16[256,128]{1,0:T(8,128)(2,1)S(1)}, u32[]{:S(2)}, u32[]{:S(2)}) collective-permute-start(bf16[256,128]{1,0:T(8,128)(2,1)S(1)} %gradient.1), channel_id=1, source_target_pairs={{0,1},{1,0},{2,3},{3,2},{4,5},{5,4},{6,7},{7,6},{8,9},{9,8},{10,11... | collective-permute-start | bytes 196616 | tf_op jit(solution)/shard_map/ppermute | solution.py:319
  27.0 2.9 %collective-permute-done.13.gradient = bf16[256,128]{1,0:T(8,128)(2,1)S(1)} collective-permute-done((bf16[256,128]{1,0:T(8,128)(2,1)S(1)}, bf16[256,128]{1,0:T(8,128)(2,1)S(1)}, u32[]{:S(2)}, u32[]{:S(2)}) %collective-permute-start.13) | collective-permute-done | bytes 65568 | tf_op jit(solution)/shard_map/ppermute | solution.py:319
  29.9 0.7 %shrink.1 = f32[256,128]{1,0:T(8,128)} custom-call(f32[256,128]{1,0:T(8,128)S(1)} %get-tuple-element.51.total, f32[256,128]{1,0:T(8,128)S(1)} %get-tuple-element.52.difference, bf16[256,128]{1,0:T(8,128)(2,1)S(1)} %collective-permute-done.13.gradient), custom_call_target="tpu_custom_call" | custom-call | bytes 458752 | tf_op jit(solution)/shard_map/shrink/pallas_call | solution.py:209
  (16 shorter events, 0.1 us)
Async XLA Ops:
  0.0 3.2 %copy-start.2 = (bf16[1,256,8,128]{3,2,1,0:T(8,128)(2,1)S(1)}, bf16[1,256,8,128]{3,2,1,0:T(8,128)(2,1)}, u32[]{:S(2)}) copy-start(bf16[1,256,8,128]{3,2,1,0:T(8,128)(2,1)} %param.5) | copy-start | bytes 1572868
  0.0 10.5 %copy-start.3 = (f32[1,256,128]{2,1,0:T(8,128)S(1)}, f32[1,256,128]{2,1,0:T(8,128)}, u32[]{:S(2)}) copy-start(f32[1,256,128]{2,1,0:T(8,128)} %param.8) | copy-start | bytes 393220
  1.8 8.7 %copy-start.1 = (f32[1,256,128]{2,1,0:T(8,128)S(1)}, f32[1,256,128]{2,1,0:T(8,128)}, u32[]{:S(2)}) copy-start(f32[1,256,128]{2,1,0:T(8,128)} %param.9) | copy-start | bytes 393220
  1.8 1.4 %collective-permute-start = (bf16[4,64,128]{2,1,0:T(8,128)(2,1)S(1)}, bf16[4,64,128]{2,1,0:T(8,128)(2,1)S(1)}, u32[]{:S(2)}, u32[]{:S(2)}) collective-permute-start(bf16[4,64,128]{2,1,0:T(8,128)(2,1)S(1)} %get-tuple-element.30), channel_id=1, source_target_pairs={{0,2},{2,0},{4,6},{6,4},{8,10},{10,8},{12,14},{14,12},{16,18},{18,... | collective-permute-start | bytes 196616 | tf_op jit(solution)/shard_map/ppermute | solution.py:222
  3.2 7.3 %copy-start.4 = (s32[1,8,8]{2,1,0:T(8,128)S(1)}, s32[1,8,8]{2,1,0:T(8,128)}, u32[]{:S(2)}) copy-start(s32[1,8,8]{2,1,0:T(8,128)} %ranks.1) | copy-start | bytes 772
  3.2 7.2 %collective-permute-start.1 = (bf16[2048,128]{1,0:T(8,128)(2,1)S(1)}, bf16[2048,128]{1,0:T(8,128)(2,1)S(1)}, u32[]{:S(2)}, u32[]{:S(2)}) collective-permute-start(bf16[2048,128]{1,0:T(8,128)(2,1)S(1)} %bitcast.9), channel_id=1, source_target_pairs={{0,2},{2,0},{4,6},{6,4},{8,10},{10,8},{12,14},{14,12},{16,18},{18,... | collective-permute-start | bytes 1572872 | tf_op jit(solution)/shard_map/ppermute | solution.py:222
  3.6 7.9 %collective-permute-start.3 = (bf16[64,128]{1,0:T(8,128)(2,1)S(1)}, bf16[64,128]{1,0:T(8,128)(2,1)S(1)}, u32[]{:S(2)}, u32[]{:S(2)}) collective-permute-start(bf16[64,128]{1,0:T(8,128)(2,1)S(1)} %get-tuple-element.31), channel_id=1, source_target_pairs={{0,16},{2,22},{4,20},{6,18},{8,24},{10,30},{12,28},{14,26},{16,0},... | collective-permute-start | bytes 49160 | tf_op jit(solution)/shard_map/ppermute | solution.py:234
  7.4 5.7 %collective-permute-start.4 = (bf16[64,128]{1,0:T(8,128)(2,1)S(1)}, bf16[64,128]{1,0:T(8,128)(2,1)S(1)}, u32[]{:S(2)}, u32[]{:S(2)}) collective-permute-start(bf16[64,128]{1,0:T(8,128)(2,1)S(1)} %get-tuple-element.41), channel_id=1, source_target_pairs={{0,24},{2,30},{4,28},{6,26},{8,16},{10,22},{12,20},{14,18},{16,8},... | collective-permute-start | bytes 49160 | tf_op jit(solution)/shard_map/ppermute | solution.py:234
  8.7 4.4 %collective-permute-start.5 = (bf16[64,128]{1,0:T(8,128)(2,1)S(1)}, bf16[64,128]{1,0:T(8,128)(2,1)S(1)}, u32[]{:S(2)}, u32[]{:S(2)}) collective-permute-start(bf16[64,128]{1,0:T(8,128)(2,1)S(1)} %get-tuple-element.42), channel_id=1, source_target_pairs={{0,8},{2,14},{4,12},{6,10},{8,0},{10,6},{12,4},{14,2},{16,24},{18,... | collective-permute-start | bytes 49160 | tf_op jit(solution)/shard_map/ppermute | solution.py:234
  9.0 4.1 %collective-permute-start.6 = (bf16[64,128]{1,0:T(8,128)(2,1)S(1)}, bf16[64,128]{1,0:T(8,128)(2,1)S(1)}, u32[]{:S(2)}, u32[]{:S(2)}) collective-permute-start(bf16[64,128]{1,0:T(8,128)(2,1)S(1)} %get-tuple-element.43), channel_id=1, source_target_pairs={{0,4},{2,6},{4,0},{6,2},{8,12},{10,14},{12,8},{14,10},{16,20},{18,... | collective-permute-start | bytes 49160 | tf_op jit(solution)/shard_map/ppermute | solution.py:234
  13.4 2.3 %collective-permute-start.7 = (f32[2,128,256]{2,1,0:T(8,128)S(1)}, f32[2,128,256]{2,1,0:T(8,128)S(1)}, u32[]{:S(2)}, u32[]{:S(2)}) collective-permute-start(f32[2,128,256]{2,1,0:T(8,128)S(1)} %image.1.here), channel_id=1, source_target_pairs={{0,2},{2,0},{4,6},{6,4},{8,10},{10,8},{12,14},{14,12},{16,18},{18,... | collective-permute-start | bytes 786440 | tf_op jit(solution)/shard_map/ppermute | solution.py:222
  14.3 6.5 %copy-start = (bf16[1,256,8,128]{3,2,1,0:T(8,128)(2,1)S(1)}, bf16[1,256,8,128]{3,2,1,0:T(8,128)(2,1)}, u32[]{:S(2)}) copy-start(bf16[1,256,8,128]{3,2,1,0:T(8,128)(2,1)} %param.6) | copy-start | bytes 1572868
  14.3 6.8 %collective-permute-start.2 = (f32[256,128]{1,0:T(8,128)S(1)}, f32[256,128]{1,0:T(8,128)S(1)}, u32[]{:S(2)}, u32[]{:S(2)}) collective-permute-start(f32[256,128]{1,0:T(8,128)S(1)} %get-tuple-element.35.here), channel_id=1, source_target_pairs={{0,1},{1,0},{2,3},{3,2},{4,5},{5,4},{6,7},{7,6},{8,9},{9,8},{10,11... | collective-permute-start | bytes 393224 | tf_op jit(solution)/shard_map/ppermute | solution.py:290
  16.1 5.0 %collective-permute-start.8 = (bf16[64,128]{1,0:T(8,128)(2,1)S(1)}, bf16[64,128]{1,0:T(8,128)(2,1)S(1)}, u32[]{:S(2)}, u32[]{:S(2)}) collective-permute-start(bf16[64,128]{1,0:T(8,128)(2,1)S(1)} %get-tuple-element.45), channel_id=1, source_target_pairs={{0,16},{2,22},{4,20},{6,18},{8,24},{10,30},{12,28},{14,26},{16,0},... | collective-permute-start | bytes 49160 | tf_op jit(solution)/shard_map/ppermute | solution.py:234
  18.0 5.5 %collective-permute-start.9 = (bf16[64,128]{1,0:T(8,128)(2,1)S(1)}, bf16[64,128]{1,0:T(8,128)(2,1)S(1)}, u32[]{:S(2)}, u32[]{:S(2)}) collective-permute-start(bf16[64,128]{1,0:T(8,128)(2,1)S(1)} %get-tuple-element.48), channel_id=1, source_target_pairs={{0,24},{2,30},{4,28},{6,26},{8,16},{10,22},{12,20},{14,18},{16,8},... | collective-permute-start | bytes 49160 | tf_op jit(solution)/shard_map/ppermute | solution.py:234
  19.4 4.2 %collective-permute-start.10 = (bf16[64,128]{1,0:T(8,128)(2,1)S(1)}, bf16[64,128]{1,0:T(8,128)(2,1)S(1)}, u32[]{:S(2)}, u32[]{:S(2)}) collective-permute-start(bf16[64,128]{1,0:T(8,128)(2,1)S(1)} %get-tuple-element.49), channel_id=1, source_target_pairs={{0,8},{2,14},{4,12},{6,10},{8,0},{10,6},{12,4},{14,2},{16,24},{18,... | collective-permute-start | bytes 49160 | tf_op jit(solution)/shard_map/ppermute | solution.py:234
  19.7 3.9 %collective-permute-start.11 = (bf16[64,128]{1,0:T(8,128)(2,1)S(1)}, bf16[64,128]{1,0:T(8,128)(2,1)S(1)}, u32[]{:S(2)}, u32[]{:S(2)}) collective-permute-start(bf16[64,128]{1,0:T(8,128)(2,1)S(1)} %get-tuple-element.50), channel_id=1, source_target_pairs={{0,4},{2,6},{4,0},{6,2},{8,12},{10,14},{12,8},{14,10},{16,20},{18,... | collective-permute-start | bytes 49160 | tf_op jit(solution)/shard_map/ppermute | solution.py:234
  23.6 1.4 %collective-permute-start.12 = (bf16[4,64,128]{2,1,0:T(8,128)(2,1)S(1)}, bf16[4,64,128]{2,1,0:T(8,128)(2,1)S(1)}, u32[]{:S(2)}, u32[]{:S(2)}) collective-permute-start(bf16[4,64,128]{2,1,0:T(8,128)(2,1)S(1)} %pack.1.own), channel_id=1, source_target_pairs={{0,2},{2,0},{4,6},{6,4},{8,10},{10,8},{12,14},{14,12},{16,18},{18,... | collective-permute-start | bytes 196616 | tf_op jit(solution)/shard_map/ppermute | solution.py:222
  25.5 4.4 %collective-permute-start.13 = (bf16[256,128]{1,0:T(8,128)(2,1)S(1)}, bf16[256,128]{1,0:T(8,128)(2,1)S(1)}, u32[]{:S(2)}, u32[]{:S(2)}) collective-permute-start(bf16[256,128]{1,0:T(8,128)(2,1)S(1)} %gradient.1), channel_id=1, source_target_pairs={{0,1},{1,0},{2,3},{3,2},{4,5},{5,4},{6,7},{7,6},{8,9},{9,8},{10,11... | collective-permute-start | bytes 196616 | tf_op jit(solution)/shard_map/ppermute | solution.py:319

commit v10 on v5

--- a/solution.py
+++ b/solution.py
@@ -19,8 +19,10 @@
 
 
 def shifts_of(chips):
-    far_first = sorted(range(chips), key=lambda shift: (-shift.bit_count(), -shift))
-    return [[far_first[at] for at in range(chips) if (at + 1) // 2 % 2 == core] for core in range(2)]
+    even = list(range(chips - 2, -1, -2))
+    odd = [shift + 1 for shift in even]
+    even[-2], odd[-1] = odd[-1], even[-2]
+    return [even, odd]
 
 
 def place():
@@ -67,15 +69,6 @@
     block = block.astype(F32)
     left[:half, columns_of(tile)] = (block * signs(half)).astype(BF16)
     left[half:, columns_of(tile)] = pltpu.roll(block, LANES // 2, 1).astype(BF16)
-
-
-def arrived_block(shifts, index, sent, arrived):
-    _, core = place()
-    values = arrived[...]
-    for side in range(2):
-        if shifts[side][index] == 0:
-            values = jnp.where(core == side, sent[...], values)
-    return values
 
 
 def times_transposed(left, right):
@@ -112,24 +105,25 @@
         out[...] = (keep[index].astype(F32) + arrived[index].astype(F32)).astype(BF16)
 
 
-def rows_kernel(shifts, ranks, own, mate, observed, own_out, mate_out, turned, wide):
+def rows_kernel(shifts, ranks, own, mate, observed, start, own_out, mate_out, turned, start_out, wide):
     chip, _ = place()
-    chosen, _ = both_shifts(shifts)
+    _, chosen = both_shifts(shifts)
     lane = lax.broadcasted_iota(jnp.int32, (1, LANES), 1) % (LANES // 2)
     masks = [lane < ranks[0, chip, tile] for tile in chosen]
     separate(own, wide, own_out, chosen, masks)
     separate(mate, wide, mate_out, chosen, masks)
     turned[...] = observed[...].T
+    start_out[...] = start[...]
 
 
 def columns_kernel(factors, separated, wide):
     separate(factors, wide, separated, range(separated.shape[1] // LANES))
 
 
-def image_kernel(shifts, sent, *refs):
+def image_kernel(*refs):
     arrived, (own, mate, observed, misfit, left) = refs[:-5], refs[-5:]
     for index, block in enumerate(arrived):
-        spread_block(arrived_block(shifts, index, sent, block), left, index)
+        spread_block(block[...], left, index)
     misfit[0] = times_transposed(left[...], own[...]) - observed[...]
     misfit[1] = times_transposed(left[...], mate[...])
 
@@ -144,9 +138,9 @@
         out[...] = (parts[0] + parts[1]).astype(BF16)
 
 
-def pack_kernel(shifts, sent, *refs):
+def pack_kernel(*refs):
     for index, block in enumerate(refs[:-1]):
-        refs[-1][index] = arrived_block(shifts, index, sent, block)
+        refs[-1][index] = block[...]
 
 
 def gradient_kernel(shifts, own, mate, factors, gradient, left):
@@ -221,11 +215,9 @@
     count = lax.axis_size("tile")
     arrived = []
     for index, send in enumerate(sends):
-        pair = [shifts[core][index] or shifts[1 - core][index] for core in range(2)]
-        arrived.append(lax.ppermute(send, "tile", [(i, i ^ 2 * pair[i % 2]) for i in range(count)]))
-    arrived[0] = after(arrived[0], *beside)
-    (own,) = [send for index, send in enumerate(sends) if 0 in (shifts[0][index], shifts[1][index])]
-    return [own, *arrived]
+        pairs = [(i, i ^ 2 * shifts[i % 2][index] ^ 1) for i in range(count)]
+        arrived.append(lax.ppermute(send, "tile", pairs))
+    return [after(arrived[0], *beside), *arrived[1:]]
 
 
 def body(u_factors, v_factors, ranks, observed, start):
@@ -269,20 +261,19 @@
     )
     sends = call(add_kernel, "add", [block] * members, [keep, to_mate(give)])
     left_rows = after(left_rows, sends[0])
-    own_left, mate_left, turned = call(
+    own_left, mate_left, turned, start = call(
         functools.partial(rows_kernel, shifts),
         "rows",
-        [chosen, chosen, shape(sources, rows, dtype=F32)],
-        [ranks, left_rows, to_mate(left_rows), after(observed, give)],
+        [chosen, chosen, shape(sources, rows, dtype=F32), shape(rows, sources, dtype=F32)],
+        [ranks, left_rows, to_mate(left_rows), after(observed, give), after(start, give)],
         [wide],
         spaces=[pltpu.SMEM],
     )
-    early = after(start, own_left)
     starts = [start]
     for shift in range(1, band):
-        starts.append(lax.ppermute(early, "freq", [(f, (f - shift) % band) for f in range(band)]))
+        starts.append(lax.ppermute(start, "freq", [(f, (f - shift) % band) for f in range(band)]))
     (misfit,) = call(
-        functools.partial(image_kernel, shifts),
+        image_kernel,
         "image",
         [shape(2, sources, rows, dtype=F32)],
         [*exchange(sends, shifts, [own_left, mate_left, turned]), own_left, mate_left, turned],
@@ -298,7 +289,7 @@
         flops,
     )
     (right,) = call(columns_kernel, "columns", [shape(rows, columns)], [after(right_rows, sends[0])], [wide])
-    (own,) = call(functools.partial(pack_kernel, shifts), "pack", [blocks], exchange(sends, shifts, [right, *starts[1:]]))
+    (own,) = call(pack_kernel, "pack", [blocks], exchange(sends, shifts[::-1], [right, *starts[1:]]))
     (gradient,) = call(
         functools.partial(gradient_kernel, shifts),
         "gradient",

time: 34.4 us -> 29.6 us (0.86)
  waiting for transfers between devices: 10.7 us -> 8.09 us
  starting transfers between devices: 18.5 us -> 16.3 us
    ppermute x9, starting transfers between devices: 15.9 us -> 13.2 us  [the longest x8 11.7 us: exchange(): arrived.append(lax.ppermute(send, 'tile', pairs))]
    ppermute x9, waiting for transfers between devices: 5.74 us -> 3.39 us  [the longest x8 3.39 us: exchange(): arrived.append(lax.ppermute(send, 'tile', pairs))]
    ppermute x4, starting transfers between devices: 1.08 us -> 1.63 us  [to_mate(): lax.ppermute(value, 'tile', [(i, i ^ 1) for i in range(lax.axis_size('til...]
  transfers between devices with their start and end apart: 14 -> 14, of which waited for: 9 -> 6; matrix products, arithmetic and copies ran while one was open for 0% -> 0% of each run, Pallas kernels for 5% -> 6%
where the time goes in v10:
time: 29.6 us; the launch traced here: 29.5 us
  starting transfers between devices  16.3 us (55%)
  waiting for transfers between devices  8.09 us (27%)
  Pallas kernels  4.91 us (17%)
    ppermute x8, starting transfers between devices, exchange(): arrived.append(lax.ppermute(send, 'tile', pairs))  11.7 us
    pallas_call x10, Pallas kernels, call(): pl.pallas_call(kernel, out_shape=outs, in_specs=[pl.BlockSpec(memory_spac...  4.91 us
    ppermute x8, waiting for transfers between devices, exchange(): arrived.append(lax.ppermute(send, 'tile', pairs))  3.39 us
    ppermute x1, waiting for transfers between devices, body(): lax.ppermute(gradient, 'freq', [(f, (f - shift) % band) for f in range(ba...  2.89 us
    ppermute x4, waiting for transfers between devices, to_mate(): lax.ppermute(value, 'tile', [(i, i ^ 1) for i in range(lax.axis_size('til...  1.81 us
    ppermute x4, starting transfers between devices, to_mate(): lax.ppermute(value, 'tile', [(i, i ^ 1) for i in range(lax.axis_size('til...  1.63 us
    ppermute x1, starting transfers between devices, body(): lax.ppermute(start, 'freq', [(f, (f - shift) % band) for f in range(band)])  1.52 us
    ppermute x1, starting transfers between devices, body(): lax.ppermute(gradient, 'freq', [(f, (f - shift) % band) for f in range(ba...  1.5 us
  transfers between devices with their start and end apart: 14, of which 6 were waited for; matrix products, arithmetic and copies ran while one was open for 0% of the time, Pallas kernels for 6%

profile of v10, /device:TPU:0, one launch (start us, length us, event | category | flops | bytes accessed | tf_op | source)
XLA Modules:
  0.0 29.5 jit_solution(8458569828022459567)
XLA Ops:
  0.0 1.7 %forward.1 = (bf16[4,64,128]{2,1,0:T(8,128)(2,1)S(1)}, bf16[4,64,128]{2,1,0:T(8,128)(2,1)S(1)}) custom-call(f32[256,128]{1,0:T(8,128)} %bitcast.7, bf16[2048,128]{1,0:T(8,128)(2,1)} %bitcast.5), custom_call_target="tpu_custom_call" | custom-call | flops 67108864 | bytes 786432 | tf_op jit(solution)/shard_map/forward/pallas_call | solution.py:194
  1.8 0.0 copy-start.1
  1.8 0.5 %collective-permute-start = (bf16[4,64,128]{2,1,0:T(8,128)(2,1)S(1)}, bf16[4,64,128]{2,1,0:T(8,128)(2,1)S(1)}, u32[]{:S(2)}, u32[]{:S(2)}) collective-permute-start(bf16[4,64,128]{2,1,0:T(8,128)(2,1)S(1)} %get-tuple-element.28), channel_id=1, source_target_pairs={{0,2},{2,0},{4,6},{6,4},{8,10},{10,8},{12,14},{14,12},{16,18},{18,... | collective-permute-start | bytes 196616 | tf_op jit(solution)/shard_map/ppermute | solution.py:207
  2.3 0.9 %collective-permute-done.arrived = bf16[4,64,128]{2,1,0:T(8,128)(2,1)S(1)} collective-permute-done((bf16[4,64,128]{2,1,0:T(8,128)(2,1)S(1)}, bf16[4,64,128]{2,1,0:T(8,128)(2,1)S(1)}, u32[]{:S(2)}, u32[]{:S(2)}) %collective-permute-start) | collective-permute-done | bytes 65568 | tf_op jit(solution)/shard_map/ppermute | solution.py:207
  3.2 0.0 copy-start.4
  3.2 0.4 %collective-permute-start.1 = (bf16[2048,128]{1,0:T(8,128)(2,1)S(1)}, bf16[2048,128]{1,0:T(8,128)(2,1)S(1)}, u32[]{:S(2)}, u32[]{:S(2)}) collective-permute-start(bf16[2048,128]{1,0:T(8,128)(2,1)S(1)} %bitcast.9), channel_id=1, source_target_pairs={{0,2},{2,0},{4,6},{6,4},{8,10},{10,8},{12,14},{14,12},{16,18},{18,... | collective-permute-start | bytes 1572872 | tf_op jit(solution)/shard_map/ppermute | solution.py:207
  3.6 4.7 %collective-permute-start.3 = (bf16[64,128]{1,0:T(8,128)(2,1)S(1)}, bf16[64,128]{1,0:T(8,128)(2,1)S(1)}, u32[]{:S(2)}, u32[]{:S(2)}) collective-permute-start(bf16[64,128]{1,0:T(8,128)(2,1)S(1)} %get-tuple-element.29), channel_id=1, source_target_pairs={{0,26},{2,28},{4,30},{6,24},{8,18},{10,20},{12,22},{14,16},{16,10}... | collective-permute-start | bytes 49160 | tf_op jit(solution)/shard_map/ppermute | solution.py:219
  8.4 0.1 collective-permute-start.4
  8.5 1.1 %collective-permute-start.5 = (bf16[64,128]{1,0:T(8,128)(2,1)S(1)}, bf16[64,128]{1,0:T(8,128)(2,1)S(1)}, u32[]{:S(2)}, u32[]{:S(2)}) collective-permute-start(bf16[64,128]{1,0:T(8,128)(2,1)S(1)} %get-tuple-element.39), channel_id=1, source_target_pairs={{0,6},{2,12},{4,2},{6,8},{8,14},{10,4},{12,10},{14,0},{16,22},{18,... | collective-permute-start | bytes 49160 | tf_op jit(solution)/shard_map/ppermute | solution.py:219
  9.6 0.4 %collective-permute-start.6 = (bf16[64,128]{1,0:T(8,128)(2,1)S(1)}, bf16[64,128]{1,0:T(8,128)(2,1)S(1)}, u32[]{:S(2)}, u32[]{:S(2)}) collective-permute-start(bf16[64,128]{1,0:T(8,128)(2,1)S(1)} %get-tuple-element.40), channel_id=1, source_target_pairs={{0,2},{2,8},{4,6},{6,12},{8,10},{10,0},{12,14},{14,4},{16,18},{18,... | collective-permute-start | bytes 49160 | tf_op jit(solution)/shard_map/ppermute | solution.py:219
  10.0 0.0 collective-permute-done.1.mate
  10.0 1.1 %rows.1 = (bf16[256,512]{1,0:T(8,128)(2,1)S(1)}, bf16[256,512]{1,0:T(8,128)(2,1)S(1)}, f32[128,256]{1,0:T(8,128)S(1)}, f32[256,128]{1,0:T(8,128)S(1)}) custom-call(s32[1,8,8]{2,1,0:T(8,128)S(1)} %copy-done.4, bf16[2048,128]{1,0:T(8,128)(2,1)S(1)} %bitcast.10, bf16[2048,128]{1,0:T(8,128)(2,1)S(1)} %collective-permute-done.1.mate, f32[256,128]{1,0:T(8,128)S(1)} %bitcast.11, ...), custom_call_target="tpu_custom_call" | custom-call | bytes 2097408 | tf_op jit(solution)/shard_map/rows/pallas_call | solution.py:194
  11.1 2.2 %collective-permute-done.4.refs_1_ = bf16[64,128]{1,0:T(8,128)(2,1)S(1)} collective-permute-done((bf16[64,128]{1,0:T(8,128)(2,1)S(1)}, bf16[64,128]{1,0:T(8,128)(2,1)S(1)}, u32[]{:S(2)}, u32[]{:S(2)}) %collective-permute-start.4) | collective-permute-done | bytes 16416 | tf_op jit(solution)/shard_map/ppermute | solution.py:219
  13.3 0.0 collective-permute-done.5.refs_2_
  13.3 0.0 collective-permute-done.6.refs_3_
  13.3 0.3 %image.1.here = f32[2,128,256]{2,1,0:T(8,128)S(1)} custom-call(bf16[64,128]{1,0:T(8,128)(2,1)S(1)} %collective-permute-done.3.refs_0_, bf16[64,128]{1,0:T(8,128)(2,1)S(1)} %collective-permute-done.4.refs_1_, bf16[64,128]{1,0:T(8,128)(2,1)S(1)} %collective-permute-done.5.refs_2_, bf16[64,128]{1,0:T(8,128)(2,1)S(1)} %collective-permute-done.6.refs_3_, ...), custom_call_target="tpu_custom_call" | custom-call | flops 67108864 | bytes 983040 | tf_op jit(solution)/shard_map/image/pallas_call | solution.py:194
  13.7 0.2 collective-permute-start.7
  13.9 1.5 %collective-permute-start.2 = (f32[256,128]{1,0:T(8,128)S(1)}, f32[256,128]{1,0:T(8,128)S(1)}, u32[]{:S(2)}, u32[]{:S(2)}) collective-permute-start(f32[256,128]{1,0:T(8,128)S(1)} %get-tuple-element.33.here), channel_id=1, source_target_pairs={{0,1},{1,0},{2,3},{3,2},{4,5},{5,4},{6,7},{7,6},{8,9},{9,8},{10,11... | collective-permute-start | bytes 393224 | tf_op jit(solution)/shard_map/ppermute | solution.py:274
  15.4 0.3 %back.1 = (bf16[64,128]{1,0:T(8,128)(2,1)S(1)}, bf16[64,128]{1,0:T(8,128)(2,1)S(1)}, bf16[64,128]{1,0:T(8,128)(2,1)S(1)}, bf16[64,128]{1,0:T(8,128)(2,1)S(1)}) custom-call(f32[2,128,256]{2,1,0:T(8,128)S(1)} %image.1.here, f32[2,128,256]{2,1,0:T(8,128)S(1)} %collective-permute-done.7.there, bf16[256,512]{1,0:T(8,128)(2,1)S(1)} %get-tuple-element.34.refs_4_.own, ...), custom_call_target="tpu_custom_call" | custom-call | flops 67108864 | bytes 1114112 | tf_op jit(solution)/shard_map/back/pallas_call | solution.py:194
  15.8 2.3 %collective-permute-start.8 = (bf16[64,128]{1,0:T(8,128)(2,1)S(1)}, bf16[64,128]{1,0:T(8,128)(2,1)S(1)}, u32[]{:S(2)}, u32[]{:S(2)}) collective-permute-start(bf16[64,128]{1,0:T(8,128)(2,1)S(1)} %get-tuple-element.41), channel_id=1, source_target_pairs={{0,30},{2,24},{4,26},{6,28},{8,22},{10,16},{12,18},{14,20},{16,14}... | collective-permute-start | bytes 49160 | tf_op jit(solution)/shard_map/ppermute | solution.py:219
  18.0 0.7 %collective-permute-start.9 = (bf16[64,128]{1,0:T(8,128)(2,1)S(1)}, bf16[64,128]{1,0:T(8,128)(2,1)S(1)}, u32[]{:S(2)}, u32[]{:S(2)}) collective-permute-start(bf16[64,128]{1,0:T(8,128)(2,1)S(1)} %get-tuple-element.44), channel_id=1, source_target_pairs={{0,22},{2,16},{4,18},{6,20},{8,30},{10,24},{12,26},{14,28},{16,6},... | collective-permute-start | bytes 49160 | tf_op jit(solution)/shard_map/ppermute | solution.py:219
  18.8 1.7 %collective-permute-start.10 = (bf16[64,128]{1,0:T(8,128)(2,1)S(1)}, bf16[64,128]{1,0:T(8,128)(2,1)S(1)}, u32[]{:S(2)}, u32[]{:S(2)}) collective-permute-start(bf16[64,128]{1,0:T(8,128)(2,1)S(1)} %get-tuple-element.45), channel_id=1, source_target_pairs={{0,14},{2,4},{4,10},{6,0},{8,6},{10,12},{12,2},{14,8},{16,30},{18,... | collective-permute-start | bytes 49160 | tf_op jit(solution)/shard_map/ppermute | solution.py:219
  20.5 0.6 %collective-permute-start.11 = (bf16[64,128]{1,0:T(8,128)(2,1)S(1)}, bf16[64,128]{1,0:T(8,128)(2,1)S(1)}, u32[]{:S(2)}, u32[]{:S(2)}) collective-permute-start(bf16[64,128]{1,0:T(8,128)(2,1)S(1)} %get-tuple-element.46), channel_id=1, source_target_pairs={{0,10},{2,0},{4,14},{6,4},{8,2},{10,8},{12,6},{14,12},{16,26},{18,... | collective-permute-start | bytes 49160 | tf_op jit(solution)/shard_map/ppermute | solution.py:219
  21.1 0.3 columns.1.factors
  21.4 0.7 %collective-permute-done.9.refs_1_ = bf16[64,128]{1,0:T(8,128)(2,1)S(1)} collective-permute-done((bf16[64,128]{1,0:T(8,128)(2,1)S(1)}, bf16[64,128]{1,0:T(8,128)(2,1)S(1)}, u32[]{:S(2)}, u32[]{:S(2)}) %collective-permute-start.9) | collective-permute-done | bytes 16416 | tf_op jit(solution)/shard_map/ppermute | solution.py:219
  22.1 0.4 %collective-permute-done.11.refs_3_ = bf16[64,128]{1,0:T(8,128)(2,1)S(1)} collective-permute-done((bf16[64,128]{1,0:T(8,128)(2,1)S(1)}, bf16[64,128]{1,0:T(8,128)(2,1)S(1)}, u32[]{:S(2)}, u32[]{:S(2)}) %collective-permute-start.11) | collective-permute-done | bytes 16416 | tf_op jit(solution)/shard_map/ppermute | solution.py:219
  22.6 0.4 %collective-permute-start.12 = (bf16[4,64,128]{2,1,0:T(8,128)(2,1)S(1)}, bf16[4,64,128]{2,1,0:T(8,128)(2,1)S(1)}, u32[]{:S(2)}, u32[]{:S(2)}) collective-permute-start(bf16[4,64,128]{2,1,0:T(8,128)(2,1)S(1)} %pack.1.own), channel_id=1, source_target_pairs={{0,2},{2,0},{4,6},{6,4},{8,10},{10,8},{12,14},{14,12},{16,18},{18,... | collective-permute-start | bytes 196616 | tf_op jit(solution)/shard_map/ppermute | solution.py:207
  23.0 0.9 %collective-permute-done.12.mate = bf16[4,64,128]{2,1,0:T(8,128)(2,1)S(1)} collective-permute-done((bf16[4,64,128]{2,1,0:T(8,128)(2,1)S(1)}, bf16[4,64,128]{2,1,0:T(8,128)(2,1)S(1)}, u32[]{:S(2)}, u32[]{:S(2)}) %collective-permute-start.12) | collective-permute-done | bytes 65568 | tf_op jit(solution)/shard_map/ppermute | solution.py:207
  23.9 0.4 %gradient.1 = bf16[256,128]{1,0:T(8,128)(2,1)S(1)} custom-call(bf16[4,64,128]{2,1,0:T(8,128)(2,1)S(1)} %pack.1.own, bf16[4,64,128]{2,1,0:T(8,128)(2,1)S(1)} %collective-permute-done.12.mate, bf16[256,1024]{1,0:T(8,128)(2,1)S(1)} %columns.1.factors), custom_call_target="tpu_custom_call" | custom-call | flops 67108864 | bytes 720896 | tf_op jit(solution)/shard_map/gradient/pallas_call | solution.py:194
  24.3 1.5 %collective-permute-start.13 = (bf16[256,128]{1,0:T(8,128)(2,1)S(1)}, bf16[256,128]{1,0:T(8,128)(2,1)S(1)}, u32[]{:S(2)}, u32[]{:S(2)}) collective-permute-start(bf16[256,128]{1,0:T(8,128)(2,1)S(1)} %gradient.1), channel_id=1, source_target_pairs={{0,1},{1,0},{2,3},{3,2},{4,5},{5,4},{6,7},{7,6},{8,9},{9,8},{10,11... | collective-permute-start | bytes 196616 | tf_op jit(solution)/shard_map/ppermute | solution.py:303
  25.9 2.9 %collective-permute-done.13.gradient = bf16[256,128]{1,0:T(8,128)(2,1)S(1)} collective-permute-done((bf16[256,128]{1,0:T(8,128)(2,1)S(1)}, bf16[256,128]{1,0:T(8,128)(2,1)S(1)}, u32[]{:S(2)}, u32[]{:S(2)}) %collective-permute-start.13) | collective-permute-done | bytes 65568 | tf_op jit(solution)/shard_map/ppermute | solution.py:303
  28.8 0.7 %shrink.1 = f32[256,128]{1,0:T(8,128)} custom-call(f32[256,128]{1,0:T(8,128)S(1)} %get-tuple-element.47.total, f32[256,128]{1,0:T(8,128)S(1)} %get-tuple-element.48.difference, bf16[256,128]{1,0:T(8,128)(2,1)S(1)} %collective-permute-done.13.gradient), custom_call_target="tpu_custom_call" | custom-call | bytes 458752 | tf_op jit(solution)/shard_map/shrink/pallas_call | solution.py:194
  (16 shorter events, 0.1 us)
Async XLA Ops:
  0.0 3.2 %copy-start.2 = (bf16[1,256,8,128]{3,2,1,0:T(8,128)(2,1)S(1)}, bf16[1,256,8,128]{3,2,1,0:T(8,128)(2,1)}, u32[]{:S(2)}) copy-start(bf16[1,256,8,128]{3,2,1,0:T(8,128)(2,1)} %param.5) | copy-start | bytes 1572868
  0.0 10.0 %copy-start.3 = (f32[1,256,128]{2,1,0:T(8,128)S(1)}, f32[1,256,128]{2,1,0:T(8,128)}, u32[]{:S(2)}) copy-start(f32[1,256,128]{2,1,0:T(8,128)} %param.8) | copy-start | bytes 393220
  1.8 8.2 %copy-start.1 = (f32[1,256,128]{2,1,0:T(8,128)S(1)}, f32[1,256,128]{2,1,0:T(8,128)}, u32[]{:S(2)}) copy-start(f32[1,256,128]{2,1,0:T(8,128)} %param.9) | copy-start | bytes 393220
  1.8 1.4 %collective-permute-start = (bf16[4,64,128]{2,1,0:T(8,128)(2,1)S(1)}, bf16[4,64,128]{2,1,0:T(8,128)(2,1)S(1)}, u32[]{:S(2)}, u32[]{:S(2)}) collective-permute-start(bf16[4,64,128]{2,1,0:T(8,128)(2,1)S(1)} %get-tuple-element.28), channel_id=1, source_target_pairs={{0,2},{2,0},{4,6},{6,4},{8,10},{10,8},{12,14},{14,12},{16,18},{18,... | collective-permute-start | bytes 196616 | tf_op jit(solution)/shard_map/ppermute | solution.py:207
  3.2 6.8 %copy-start.4 = (s32[1,8,8]{2,1,0:T(8,128)S(1)}, s32[1,8,8]{2,1,0:T(8,128)}, u32[]{:S(2)}) copy-start(s32[1,8,8]{2,1,0:T(8,128)} %ranks.1) | copy-start | bytes 772
  3.2 6.7 %collective-permute-start.1 = (bf16[2048,128]{1,0:T(8,128)(2,1)S(1)}, bf16[2048,128]{1,0:T(8,128)(2,1)S(1)}, u32[]{:S(2)}, u32[]{:S(2)}) collective-permute-start(bf16[2048,128]{1,0:T(8,128)(2,1)S(1)} %bitcast.9), channel_id=1, source_target_pairs={{0,2},{2,0},{4,6},{6,4},{8,10},{10,8},{12,14},{14,12},{16,18},{18,... | collective-permute-start | bytes 1572872 | tf_op jit(solution)/shard_map/ppermute | solution.py:207
  3.6 7.4 %collective-permute-start.3 = (bf16[64,128]{1,0:T(8,128)(2,1)S(1)}, bf16[64,128]{1,0:T(8,128)(2,1)S(1)}, u32[]{:S(2)}, u32[]{:S(2)}) collective-permute-start(bf16[64,128]{1,0:T(8,128)(2,1)S(1)} %get-tuple-element.29), channel_id=1, source_target_pairs={{0,26},{2,28},{4,30},{6,24},{8,18},{10,20},{12,22},{14,16},{16,10}... | collective-permute-start | bytes 49160 | tf_op jit(solution)/shard_map/ppermute | solution.py:219
  8.4 5.0 %collective-permute-start.4 = (bf16[64,128]{1,0:T(8,128)(2,1)S(1)}, bf16[64,128]{1,0:T(8,128)(2,1)S(1)}, u32[]{:S(2)}, u32[]{:S(2)}) collective-permute-start(bf16[64,128]{1,0:T(8,128)(2,1)S(1)} %get-tuple-element.38), channel_id=1, source_target_pairs={{0,18},{2,20},{4,22},{6,16},{8,26},{10,28},{12,30},{14,24},{16,2},... | collective-permute-start | bytes 49160 | tf_op jit(solution)/shard_map/ppermute | solution.py:219
  8.5 4.8 %collective-permute-start.5 = (bf16[64,128]{1,0:T(8,128)(2,1)S(1)}, bf16[64,128]{1,0:T(8,128)(2,1)S(1)}, u32[]{:S(2)}, u32[]{:S(2)}) collective-permute-start(bf16[64,128]{1,0:T(8,128)(2,1)S(1)} %get-tuple-element.39), channel_id=1, source_target_pairs={{0,6},{2,12},{4,2},{6,8},{8,14},{10,4},{12,10},{14,0},{16,22},{18,... | collective-permute-start | bytes 49160 | tf_op jit(solution)/shard_map/ppermute | solution.py:219
  9.6 3.7 %collective-permute-start.6 = (bf16[64,128]{1,0:T(8,128)(2,1)S(1)}, bf16[64,128]{1,0:T(8,128)(2,1)S(1)}, u32[]{:S(2)}, u32[]{:S(2)}) collective-permute-start(bf16[64,128]{1,0:T(8,128)(2,1)S(1)} %get-tuple-element.40), channel_id=1, source_target_pairs={{0,2},{2,8},{4,6},{6,12},{8,10},{10,0},{12,14},{14,4},{16,18},{18,... | collective-permute-start | bytes 49160 | tf_op jit(solution)/shard_map/ppermute | solution.py:219
  13.7 1.8 %collective-permute-start.7 = (f32[2,128,256]{2,1,0:T(8,128)S(1)}, f32[2,128,256]{2,1,0:T(8,128)S(1)}, u32[]{:S(2)}, u32[]{:S(2)}) collective-permute-start(f32[2,128,256]{2,1,0:T(8,128)S(1)} %image.1.here), channel_id=1, source_target_pairs={{0,2},{2,0},{4,6},{6,4},{8,10},{10,8},{12,14},{14,12},{16,18},{18,... | collective-permute-start | bytes 786440 | tf_op jit(solution)/shard_map/ppermute | solution.py:207
  13.9 7.2 %copy-start = (bf16[1,256,8,128]{3,2,1,0:T(8,128)(2,1)S(1)}, bf16[1,256,8,128]{3,2,1,0:T(8,128)(2,1)}, u32[]{:S(2)}) copy-start(bf16[1,256,8,128]{3,2,1,0:T(8,128)(2,1)} %param.6) | copy-start | bytes 1572868
  13.9 7.5 %collective-permute-start.2 = (f32[256,128]{1,0:T(8,128)S(1)}, f32[256,128]{1,0:T(8,128)S(1)}, u32[]{:S(2)}, u32[]{:S(2)}) collective-permute-start(f32[256,128]{1,0:T(8,128)S(1)} %get-tuple-element.33.here), channel_id=1, source_target_pairs={{0,1},{1,0},{2,3},{3,2},{4,5},{5,4},{6,7},{7,6},{8,9},{9,8},{10,11... | collective-permute-start | bytes 393224 | tf_op jit(solution)/shard_map/ppermute | solution.py:274
  15.8 5.6 %collective-permute-start.8 = (bf16[64,128]{1,0:T(8,128)(2,1)S(1)}, bf16[64,128]{1,0:T(8,128)(2,1)S(1)}, u32[]{:S(2)}, u32[]{:S(2)}) collective-permute-start(bf16[64,128]{1,0:T(8,128)(2,1)S(1)} %get-tuple-element.41), channel_id=1, source_target_pairs={{0,30},{2,24},{4,26},{6,28},{8,22},{10,16},{12,18},{14,20},{16,14}... | collective-permute-start | bytes 49160 | tf_op jit(solution)/shard_map/ppermute | solution.py:219
  18.0 4.1 %collective-permute-start.9 = (bf16[64,128]{1,0:T(8,128)(2,1)S(1)}, bf16[64,128]{1,0:T(8,128)(2,1)S(1)}, u32[]{:S(2)}, u32[]{:S(2)}) collective-permute-start(bf16[64,128]{1,0:T(8,128)(2,1)S(1)} %get-tuple-element.44), channel_id=1, source_target_pairs={{0,22},{2,16},{4,18},{6,20},{8,30},{10,24},{12,26},{14,28},{16,6},... | collective-permute-start | bytes 49160 | tf_op jit(solution)/shard_map/ppermute | solution.py:219
  18.8 3.4 %collective-permute-start.10 = (bf16[64,128]{1,0:T(8,128)(2,1)S(1)}, bf16[64,128]{1,0:T(8,128)(2,1)S(1)}, u32[]{:S(2)}, u32[]{:S(2)}) collective-permute-start(bf16[64,128]{1,0:T(8,128)(2,1)S(1)} %get-tuple-element.45), channel_id=1, source_target_pairs={{0,14},{2,4},{4,10},{6,0},{8,6},{10,12},{12,2},{14,8},{16,30},{18,... | collective-permute-start | bytes 49160 | tf_op jit(solution)/shard_map/ppermute | solution.py:219
  20.5 2.1 %collective-permute-start.11 = (bf16[64,128]{1,0:T(8,128)(2,1)S(1)}, bf16[64,128]{1,0:T(8,128)(2,1)S(1)}, u32[]{:S(2)}, u32[]{:S(2)}) collective-permute-start(bf16[64,128]{1,0:T(8,128)(2,1)S(1)} %get-tuple-element.46), channel_id=1, source_target_pairs={{0,10},{2,0},{4,14},{6,4},{8,2},{10,8},{12,6},{14,12},{16,26},{18,... | collective-permute-start | bytes 49160 | tf_op jit(solution)/shard_map/ppermute | solution.py:219
  22.6 1.4 %collective-permute-start.12 = (bf16[4,64,128]{2,1,0:T(8,128)(2,1)S(1)}, bf16[4,64,128]{2,1,0:T(8,128)(2,1)S(1)}, u32[]{:S(2)}, u32[]{:S(2)}) collective-permute-start(bf16[4,64,128]{2,1,0:T(8,128)(2,1)S(1)} %pack.1.own), channel_id=1, source_target_pairs={{0,2},{2,0},{4,6},{6,4},{8,10},{10,8},{12,14},{14,12},{16,18},{18,... | collective-permute-start | bytes 196616 | tf_op jit(solution)/shard_map/ppermute | solution.py:207
  24.3 4.4 %collective-permute-start.13 = (bf16[256,128]{1,0:T(8,128)(2,1)S(1)}, bf16[256,128]{1,0:T(8,128)(2,1)S(1)}, u32[]{:S(2)}, u32[]{:S(2)}) collective-permute-start(bf16[256,128]{1,0:T(8,128)(2,1)S(1)} %gradient.1), channel_id=1, source_target_pairs={{0,1},{1,0},{2,3},{3,2},{4,5},{5,4},{6,7},{7,6},{8,9},{9,8},{10,11... | collective-permute-start | bytes 196616 | tf_op jit(solution)/shard_map/ppermute | solution.py:303

commit v11 on v10

--- a/solution.py
+++ b/solution.py
@@ -75,10 +75,16 @@
     return lax.dot_general(left, right, (((1,), (1,)), ((), ())), preferred_element_type=F32)
 
 
-def forward_kernel(shifts, start, factors, keep, give, start_here, factors_here, wide, separated, product, sems):
+def block_parts(shifts, start, separated, product):
+    product[...] = jnp.dot(start[...].T.astype(BF16), separated[...], preferred_element_type=F32)
+    return [adjoint_block(product, index) for index in range(len(shifts[0]))]
+
+
+def forward_kernel(shifts, start, factors, parts, start_here, factors_here, sems, wide, separated, product):
     pieces = sems.shape[0] - 1
-    rows, columns = separated.shape
-    tiles = columns // LANES
+    rows = start.shape[0]
+    tiles = factors.shape[0] // rows
+    chosen, _ = both_shifts(shifts)
     load_start = pltpu.make_async_copy(start, start_here, sems.at[pieces])
     load_start.start()
     loads = []
@@ -87,22 +93,22 @@
         loads.append(pltpu.make_async_copy(factors.at[at], factors_here.at[at], sems.at[piece]))
         loads[-1].start()
     load_start.wait()
-    values = start_here[...].T.astype(BF16)
     for piece, load in enumerate(loads):
         at = pl.ds(piece * (rows * tiles // pieces), rows * tiles // pieces)
         load.wait()
         separate(
-            factors_here.at[at], wide.at[at], separated.at[pl.ds(piece * (rows // pieces), rows // pieces)], range(tiles)
+            factors_here.at[at], wide.at[at], separated.at[pl.ds(piece * (rows // pieces), rows // pieces)], chosen
         )
-    product[...] = jnp.dot(values, separated[...], preferred_element_type=F32)
-    for out, chosen in zip((keep, give), both_shifts(shifts)):
-        for index, tile in enumerate(chosen):
-            out[index] = adjoint_block(product, tile)
-
-
-def add_kernel(keep, arrived, *outs):
-    for index, out in enumerate(outs):
-        out[...] = (keep[index].astype(F32) + arrived[index].astype(F32)).astype(BF16)
+    for index, block in enumerate(block_parts(shifts, start_here, separated, product)):
+        parts[index] = block
+
+
+def join_kernel(shifts, parts, start, factors, *refs):
+    outs, (wide, separated, product) = refs[:-3], refs[-3:]
+    chosen, _ = both_shifts(shifts)
+    separate(factors, wide, separated, chosen)
+    for index, block in enumerate(block_parts(shifts, start, separated, product)):
+        outs[index][...] = (parts[index].astype(F32) + block.astype(F32)).astype(BF16)
 
 
 def rows_kernel(shifts, ranks, own, mate, observed, start, own_out, mate_out, turned, start_out, wide):
@@ -150,13 +156,17 @@
     gradient[...] = times_transposed(factors[...], left[...]).astype(BF16)
 
 
+def step_kernel(factors, left, start, estimate):
+    estimate[...] = start[...] - STEP_SIZE * times_transposed(factors[...], left[...])
+
+
 def thin_out(values):
     return values - jnp.clip(values, -LEVEL, LEVEL)
 
 
-def pair_kernel(here, there, gradient, total, difference):
+def pair_kernel(factors, left, here, there, total, difference):
     scale = 1.0 / math.sqrt(2)
-    estimate = here[...] - STEP_SIZE * gradient[...].astype(F32)
+    estimate = here[...] - STEP_SIZE * times_transposed(factors[...], left[...])
     total[...] = (estimate + there[...]) * scale
     difference[...] = (estimate - there[...]) * scale
 
@@ -168,12 +178,10 @@
 
 
 def shrink_kernel(band, *refs):
-    tables, starts, gradients, out = refs[: -2 * band - 1], refs[-2 * band - 1 : -band - 1], refs[-band - 1 : -1], refs[-1]
-    estimates = [
-        start[...] - STEP_SIZE * gradient[...].astype(F32) for start, gradient in zip(starts, gradients)
-    ]
+    tables, own, starts, gradients, out = refs[0], refs[1], refs[2 : band + 1], refs[band + 1 : -1], refs[-1]
+    others = [start[...] - STEP_SIZE * gradient[...].astype(F32) for start, gradient in zip(starts, gradients)]
+    estimates = [own[...], *others]
     scale = 1.0 / math.sqrt(band)
-    (tables,) = tables
     half = out.shape[1] // 2
     lane = lax.broadcasted_iota(jnp.int32, (1, out.shape[1]), 1)
     turn = jnp.where(lane < half, -1.0, 1.0).astype(F32)
@@ -190,7 +198,7 @@
 
 def call(kernel, name, outs, inputs, scratch=(), flops=0, spaces=(), limit=VMEM_LIMIT):
     spaces = (*spaces, *[pltpu.VMEM] * (len(inputs) - len(spaces)))
-    moved = sum(x.size * x.dtype.itemsize for x in [*inputs, *outs])
+    moved = sum(x.size * x.dtype.itemsize for x in [*inputs, *outs]) if flops else 0
     return pl.pallas_call(
         kernel,
         out_shape=outs,
@@ -221,7 +229,7 @@
 
 
 def body(u_factors, v_factors, ranks, observed, start):
-    band = lax.axis_size("freq")
+    count, band = lax.axis_size("tile"), lax.axis_size("freq")
     rows, tiles, width = u_factors.shape[1:]
     sources = start.shape[2]
     columns = tiles * width
@@ -239,33 +247,39 @@
     block = shape(sources // 2, width)
     blocks = shape(members, sources // 2, width)
     chosen = shape(rows, members * width)
-    spread = pltpu.VMEM((sources, columns), BF16)
+    factor = shape(rows, columns)
     flops = 2 * rows * columns * sources
 
-    keep, give = call(
+    raw_right, raw_start = to_mate(right_rows), to_mate(start)
+    scratch = [wide, pltpu.VMEM((rows, members * width), BF16), pltpu.VMEM((sources, members * width), F32)]
+    (parts,) = call(
         functools.partial(forward_kernel, shifts),
         "forward",
-        [blocks, blocks],
+        [blocks],
         [start, right_rows],
         [
             pltpu.VMEM(start.shape, F32),
             pltpu.VMEM(right_rows.shape, BF16),
-            wide,
-            pltpu.VMEM((rows, columns), BF16),
-            pltpu.VMEM((sources, columns), F32),
             pltpu.SemaphoreType.DMA((PIECES + 1,)),
+            *scratch,
         ],
-        flops,
-        [pltpu.HBM] * 2,
-        FIRST_LIMIT,
-    )
-    sends = call(add_kernel, "add", [block] * members, [keep, to_mate(give)])
+        spaces=[pltpu.HBM] * 2,
+        limit=FIRST_LIMIT,
+    )
+    sends = call(
+        functools.partial(join_kernel, shifts),
+        "join",
+        [block] * members,
+        [parts, raw_start, raw_right],
+        scratch,
+        flops // 2,
+    )
     left_rows = after(left_rows, sends[0])
     own_left, mate_left, turned, start = call(
         functools.partial(rows_kernel, shifts),
         "rows",
         [chosen, chosen, shape(sources, rows, dtype=F32), shape(rows, sources, dtype=F32)],
-        [ranks, left_rows, to_mate(left_rows), after(observed, give), after(start, give)],
+        [ranks, left_rows, to_mate(left_rows), after(observed, parts), after(start, parts)],
         [wide],
         spaces=[pltpu.SMEM],
     )
@@ -280,6 +294,7 @@
         [pltpu.VMEM((sources, members * width), BF16)],
         flops,
     )
+    (mate_right,) = call(columns_kernel, "columns", [factor], [after(raw_right, misfit)], [wide])
     sends = call(
         back_kernel,
         "back",
@@ -288,30 +303,35 @@
         [pltpu.VMEM((2, sources, members * width), F32)],
         flops,
     )
-    (right,) = call(columns_kernel, "columns", [shape(rows, columns)], [after(right_rows, sends[0])], [wide])
-    (own,) = call(pack_kernel, "pack", [blocks], exchange(sends, shifts[::-1], [right, *starts[1:]]))
-    (gradient,) = call(
+    (right,) = call(columns_kernel, "columns", [factor], [after(right_rows, sends[0])], [wide])
+    (own,) = call(pack_kernel, "pack", [blocks], exchange(sends, shifts[::-1], [right, mate_right, *starts[1:]]))
+    gradient, left = call(
         functools.partial(gradient_kernel, shifts),
         "gradient",
-        [shape(rows, sources)],
-        [own, to_mate(own), right],
-        [spread],
-        flops,
-    )
-    gradients = [gradient]
+        [shape(rows, sources), shape(sources, columns)],
+        [own, to_mate(own), mate_right],
+        flops=flops,
+    )
+    gradients = []
     for shift in range(1, band):
-        gradients.append(lax.ppermute(gradient, "freq", [(f, (f - shift) % band) for f in range(band)]))
+        pairs = [(i * band + f, (i ^ 1) * band + (f - shift) % band) for i in range(count) for f in range(band)]
+        gradients.append(lax.ppermute(gradient, ("tile", "freq"), pairs))
     result = shape(rows, sources, dtype=F32)
     if band == 2:
-        halves = call(pair_kernel, "pair", [result] * 2, [*starts, gradient])
-        (estimate,) = call(shrink_pair_kernel, "shrink", [result], [*halves, gradients[1]])
+        halves = call(pair_kernel, "pair", [result] * 2, [right, left, *starts], flops=flops)
+        (estimate,) = call(shrink_pair_kernel, "shrink", [result], [*halves, *gradients])
         return estimate[None]
     bands = jnp.arange(band, dtype=jnp.int32)
     phases = (bands[:, None] + lax.axis_index("freq")) * bands[None, :] % band
     phases = (2.0 * math.pi / band) * phases.astype(F32)
     tables = jnp.stack([jnp.cos(phases), jnp.sin(phases)])
+    (estimate,) = call(step_kernel, "step", [result], [right, left, start], flops=flops)
     (estimate,) = call(
-        functools.partial(shrink_kernel, band), "shrink", [result], [tables, *starts, *gradients], spaces=[pltpu.SMEM]
+        functools.partial(shrink_kernel, band),
+        "shrink",
+        [result],
+        [tables, estimate, *starts[1:], *gradients],
+        spaces=[pltpu.SMEM],
     )
     return estimate[None]
 

time: 29.6 us -> 29.2 us (0.986)
  waiting for transfers between devices: 8.09 us -> 6.4 us
  Pallas kernels: 4.91 us -> 5.84 us
  local copies, waits for them, and re-layouts: 0.02 us -> 0.47 us
    pallas_call x10 -> x11, Pallas kernels: 4.91 us -> 5.84 us  [call(): pl.pallas_call(kernel, out_shape=outs, in_specs=[pl.BlockSpec(memory_spac...]
    ppermute x4 -> x5, waiting for transfers between devices: 1.81 us -> 1.16 us  [to_mate(): lax.ppermute(value, 'tile', [(i, i ^ 1) for i in range(lax.axis_size('til...]
    ppermute x1, waiting for transfers between devices: 2.89 us -> 2.36 us  [body(): gradients.append(lax.ppermute(gradient, ('tile', 'freq'), pairs))]
    ppermute x8, waiting for transfers between devices: 3.39 us -> 2.88 us  [exchange(): arrived.append(lax.ppermute(send, 'tile', pairs))]
    unnamed x10, local copies, waits for them, and re-layouts: 0.02 us -> 0.47 us
    ppermute x4 -> x5, starting transfers between devices: 1.63 us -> 1.6 us  [to_mate(): lax.ppermute(value, 'tile', [(i, i ^ 1) for i in range(lax.axis_size('til...]
  transfers between devices with their start and end apart: 14 -> 15, of which waited for: 6 -> 6; matrix products, arithmetic and copies ran while one was open for 0% -> 0% of each run, Pallas kernels for 6% -> 13%
where the time goes in v11:
time: 29.2 us; the launch traced here: 29 us
  starting transfers between devices  16.1 us (55%)
  waiting for transfers between devices  6.4 us (22%)
  Pallas kernels  5.84 us (20%)
  local copies, waits for them, and re-layouts  0.47 us (2%)
    ppermute x8, starting transfers between devices, exchange(): arrived.append(lax.ppermute(send, 'tile', pairs))  11.7 us
    pallas_call x11, Pallas kernels, call(): pl.pallas_call(kernel, out_shape=outs, in_specs=[pl.BlockSpec(memory_spac...  5.84 us
    ppermute x8, waiting for transfers between devices, exchange(): arrived.append(lax.ppermute(send, 'tile', pairs))  2.88 us
    ppermute x1, waiting for transfers between devices, body(): gradients.append(lax.ppermute(gradient, ('tile', 'freq'), pairs))  2.36 us
    ppermute x5, starting transfers between devices, to_mate(): lax.ppermute(value, 'tile', [(i, i ^ 1) for i in range(lax.axis_size('til...  1.6 us
    ppermute x1, starting transfers between devices, body(): lax.ppermute(start, 'freq', [(f, (f - shift) % band) for f in range(band)])  1.52 us
    ppermute x1, starting transfers between devices, body(): gradients.append(lax.ppermute(gradient, ('tile', 'freq'), pairs))  1.35 us
    ppermute x5, waiting for transfers between devices, to_mate(): lax.ppermute(value, 'tile', [(i, i ^ 1) for i in range(lax.axis_size('til...  1.16 us
  transfers between devices with their start and end apart: 15, of which 6 were waited for; matrix products, arithmetic and copies ran while one was open for 0% of the time, Pallas kernels for 13%

profile of v11, /device:TPU:0, one launch (start us, length us, event | category | flops | bytes accessed | tf_op | source)
XLA Modules:
  0.0 29.0 jit_solution(17784605049342685238)
XLA Ops:
  0.0 0.5 %collective-permute-start.1 = (bf16[2048,128]{1,0:T(8,128)(2,1)}, bf16[2048,128]{1,0:T(8,128)(2,1)S(1)}, u32[]{:S(2)}, u32[]{:S(2)}) collective-permute-start(bf16[2048,128]{1,0:T(8,128)(2,1)} %bitcast.5), channel_id=1, source_target_pairs={{0,2},{2,0},{4,6},{6,4},{8,10},{10,8},{12,14},{14,12},{16,18},{18,... | collective-permute-start | bytes 1572872 | tf_op jit(solution)/shard_map/ppermute | solution.py:215
  0.5 0.1 collective-permute-start
  0.5 1.6 %forward.1.parts = bf16[4,64,128]{2,1,0:T(8,128)(2,1)S(1)} custom-call(f32[256,128]{1,0:T(8,128)} %bitcast.11, bf16[2048,128]{1,0:T(8,128)(2,1)} %bitcast.6), custom_call_target="tpu_custom_call" | custom-call | tf_op jit(solution)/shard_map/forward/pallas_call | solution.py:202
  2.1 0.2 collective-permute-done.start
  2.4 0.5 %join.1 = (bf16[64,128]{1,0:T(8,128)(2,1)S(1)}, bf16[64,128]{1,0:T(8,128)(2,1)S(1)}, bf16[64,128]{1,0:T(8,128)(2,1)S(1)}, bf16[64,128]{1,0:T(8,128)(2,1)S(1)}) custom-call(bf16[4,64,128]{2,1,0:T(8,128)(2,1)S(1)} %forward.1.parts, f32[256,128]{1,0:T(8,128)S(1)} %collective-permute-done.start, bf16[2048,128]{1,0:T(8,128)(2,1)S(1)} %collective-permute-done.1.factors), custom_call_target="tpu_custom_call" | custom-call | flops 33554432 | bytes 786432 | tf_op jit(solution)/shard_map/join/pallas_call | solution.py:202
  2.9 0.2 copy-done.1
  3.2 0.5 %collective-permute-start.3 = (bf16[2048,128]{1,0:T(8,128)(2,1)S(1)}, bf16[2048,128]{1,0:T(8,128)(2,1)S(1)}, u32[]{:S(2)}, u32[]{:S(2)}) collective-permute-start(bf16[2048,128]{1,0:T(8,128)(2,1)S(1)} %bitcast.8), channel_id=1, source_target_pairs={{0,2},{2,0},{4,6},{6,4},{8,10},{10,8},{12,14},{14,12},{16,18},{18,... | collective-permute-start | bytes 1572872 | tf_op jit(solution)/shard_map/ppermute | solution.py:215
  3.6 4.7 %collective-permute-start.2 = (bf16[64,128]{1,0:T(8,128)(2,1)S(1)}, bf16[64,128]{1,0:T(8,128)(2,1)S(1)}, u32[]{:S(2)}, u32[]{:S(2)}) collective-permute-start(bf16[64,128]{1,0:T(8,128)(2,1)S(1)} %get-tuple-element.28), channel_id=1, source_target_pairs={{0,26},{2,28},{4,30},{6,24},{8,18},{10,20},{12,22},{14,16},{16,10}... | collective-permute-start | bytes 49160 | tf_op jit(solution)/shard_map/ppermute | solution.py:227
  8.3 1.1 %collective-permute-start.5 = (bf16[64,128]{1,0:T(8,128)(2,1)S(1)}, bf16[64,128]{1,0:T(8,128)(2,1)S(1)}, u32[]{:S(2)}, u32[]{:S(2)}) collective-permute-start(bf16[64,128]{1,0:T(8,128)(2,1)S(1)} %get-tuple-element.37), channel_id=1, source_target_pairs={{0,6},{2,12},{4,2},{6,8},{8,14},{10,4},{12,10},{14,0},{16,22},{18,... | collective-permute-start | bytes 49160 | tf_op jit(solution)/shard_map/ppermute | solution.py:227
  9.4 0.5 %collective-permute-start.6 = (bf16[64,128]{1,0:T(8,128)(2,1)S(1)}, bf16[64,128]{1,0:T(8,128)(2,1)S(1)}, u32[]{:S(2)}, u32[]{:S(2)}) collective-permute-start(bf16[64,128]{1,0:T(8,128)(2,1)S(1)} %get-tuple-element.38), channel_id=1, source_target_pairs={{0,2},{2,8},{4,6},{6,12},{8,10},{10,0},{12,14},{14,4},{16,18},{18,... | collective-permute-start | bytes 49160 | tf_op jit(solution)/shard_map/ppermute | solution.py:227
  10.0 1.1 %rows.1 = (bf16[256,512]{1,0:T(8,128)(2,1)S(1)}, bf16[256,512]{1,0:T(8,128)(2,1)S(1)}, f32[128,256]{1,0:T(8,128)S(1)}, f32[256,128]{1,0:T(8,128)S(1)}) custom-call(s32[1,8,8]{2,1,0:T(8,128)S(1)} %copy-done.4, bf16[2048,128]{1,0:T(8,128)(2,1)S(1)} %bitcast.9, bf16[2048,128]{1,0:T(8,128)(2,1)S(1)} %collective-permute-done.3.mate, f32[256,128]{1,0:T(8,128)S(1)} %bitcast.13, ...), custom_call_target="tpu_custom_call" | custom-call | tf_op jit(solution)/shard_map/rows/pallas_call | solution.py:202
  11.1 2.2 %collective-permute-done.4.refs_1_ = bf16[64,128]{1,0:T(8,128)(2,1)S(1)} collective-permute-done((bf16[64,128]{1,0:T(8,128)(2,1)S(1)}, bf16[64,128]{1,0:T(8,128)(2,1)S(1)}, u32[]{:S(2)}, u32[]{:S(2)}) %collective-permute-start.4) | collective-permute-done | bytes 16416 | tf_op jit(solution)/shard_map/ppermute | solution.py:227
  13.3 0.3 %image.1.here = f32[2,128,256]{2,1,0:T(8,128)S(1)} custom-call(bf16[64,128]{1,0:T(8,128)(2,1)S(1)} %collective-permute-done.2.refs_0_, bf16[64,128]{1,0:T(8,128)(2,1)S(1)} %collective-permute-done.4.refs_1_, bf16[64,128]{1,0:T(8,128)(2,1)S(1)} %collective-permute-done.5.refs_2_, bf16[64,128]{1,0:T(8,128)(2,1)S(1)} %collective-permute-done.6.refs_3_, ...), custom_call_target="tpu_custom_call" | custom-call | flops 67108864 | bytes 983040 | tf_op jit(solution)/shard_map/image/pallas_call | solution.py:202
  13.6 0.2 collective-permute-start.7
  13.8 1.5 %collective-permute-start.9 = (f32[256,128]{1,0:T(8,128)S(1)}, f32[256,128]{1,0:T(8,128)S(1)}, u32[]{:S(2)}, u32[]{:S(2)}) collective-permute-start(f32[256,128]{1,0:T(8,128)S(1)} %get-tuple-element.42.here), channel_id=1, source_target_pairs={{0,1},{1,0},{2,3},{3,2},{4,5},{5,4},{6,7},{7,6},{8,9},{9,8},{10,11... | collective-permute-start | bytes 393224 | tf_op jit(solution)/shard_map/ppermute | solution.py:288
  15.3 0.3 %back.1 = (bf16[64,128]{1,0:T(8,128)(2,1)S(1)}, bf16[64,128]{1,0:T(8,128)(2,1)S(1)}, bf16[64,128]{1,0:T(8,128)(2,1)S(1)}, bf16[64,128]{1,0:T(8,128)(2,1)S(1)}) custom-call(f32[2,128,256]{2,1,0:T(8,128)S(1)} %image.1.here, f32[2,128,256]{2,1,0:T(8,128)S(1)} %collective-permute-done.7.there, bf16[256,512]{1,0:T(8,128)(2,1)S(1)} %get-tuple-element.32.refs_4_.own, ...), custom_call_target="tpu_custom_call" | custom-call | flops 67108864 | bytes 1114112 | tf_op jit(solution)/shard_map/back/pallas_call | solution.py:202
  15.7 2.3 %collective-permute-start.8 = (bf16[64,128]{1,0:T(8,128)(2,1)S(1)}, bf16[64,128]{1,0:T(8,128)(2,1)S(1)}, u32[]{:S(2)}, u32[]{:S(2)}) collective-permute-start(bf16[64,128]{1,0:T(8,128)(2,1)S(1)} %get-tuple-element.39), channel_id=1, source_target_pairs={{0,30},{2,24},{4,26},{6,28},{8,22},{10,16},{12,18},{14,20},{16,14}... | collective-permute-start | bytes 49160 | tf_op jit(solution)/shard_map/ppermute | solution.py:227
  18.0 0.7 %collective-permute-start.10 = (bf16[64,128]{1,0:T(8,128)(2,1)S(1)}, bf16[64,128]{1,0:T(8,128)(2,1)S(1)}, u32[]{:S(2)}, u32[]{:S(2)}) collective-permute-start(bf16[64,128]{1,0:T(8,128)(2,1)S(1)} %get-tuple-element.44), channel_id=1, source_target_pairs={{0,22},{2,16},{4,18},{6,20},{8,30},{10,24},{12,26},{14,28},{16,6},... | collective-permute-start | bytes 49160 | tf_op jit(solution)/shard_map/ppermute | solution.py:227
  18.7 1.7 %collective-permute-start.11 = (bf16[64,128]{1,0:T(8,128)(2,1)S(1)}, bf16[64,128]{1,0:T(8,128)(2,1)S(1)}, u32[]{:S(2)}, u32[]{:S(2)}) collective-permute-start(bf16[64,128]{1,0:T(8,128)(2,1)S(1)} %get-tuple-element.45), channel_id=1, source_target_pairs={{0,14},{2,4},{4,10},{6,0},{8,6},{10,12},{12,2},{14,8},{16,30},{18,... | collective-permute-start | bytes 49160 | tf_op jit(solution)/shard_map/ppermute | solution.py:227
  20.5 0.5 %collective-permute-start.12 = (bf16[64,128]{1,0:T(8,128)(2,1)S(1)}, bf16[64,128]{1,0:T(8,128)(2,1)S(1)}, u32[]{:S(2)}, u32[]{:S(2)}) collective-permute-start(bf16[64,128]{1,0:T(8,128)(2,1)S(1)} %get-tuple-element.46), channel_id=1, source_target_pairs={{0,10},{2,0},{4,14},{6,4},{8,2},{10,8},{12,6},{14,12},{16,26},{18,... | collective-permute-start | bytes 49160 | tf_op jit(solution)/shard_map/ppermute | solution.py:227
  21.0 0.3 columns.3.factors
  21.3 0.2 copy-done
  21.5 0.3 columns.2.factors
  21.8 0.3 collective-permute-done.10.refs_1_
  22.1 0.4 %collective-permute-done.12.refs_3_ = bf16[64,128]{1,0:T(8,128)(2,1)S(1)} collective-permute-done((bf16[64,128]{1,0:T(8,128)(2,1)S(1)}, bf16[64,128]{1,0:T(8,128)(2,1)S(1)}, u32[]{:S(2)}, u32[]{:S(2)}) %collective-permute-start.12) | collective-permute-done | bytes 16416 | tf_op jit(solution)/shard_map/ppermute | solution.py:227
  22.5 0.5 %collective-permute-start.13 = (bf16[4,64,128]{2,1,0:T(8,128)(2,1)S(1)}, bf16[4,64,128]{2,1,0:T(8,128)(2,1)S(1)}, u32[]{:S(2)}, u32[]{:S(2)}) collective-permute-start(bf16[4,64,128]{2,1,0:T(8,128)(2,1)S(1)} %pack.1.own), channel_id=1, source_target_pairs={{0,2},{2,0},{4,6},{6,4},{8,10},{10,8},{12,14},{14,12},{16,18},{18,... | collective-permute-start | bytes 196616 | tf_op jit(solution)/shard_map/ppermute | solution.py:215
  22.9 0.9 %collective-permute-done.13.mate = bf16[4,64,128]{2,1,0:T(8,128)(2,1)S(1)} collective-permute-done((bf16[4,64,128]{2,1,0:T(8,128)(2,1)S(1)}, bf16[4,64,128]{2,1,0:T(8,128)(2,1)S(1)}, u32[]{:S(2)}, u32[]{:S(2)}) %collective-permute-start.13) | collective-permute-done | bytes 65568 | tf_op jit(solution)/shard_map/ppermute | solution.py:215
  23.8 0.4 %gradient.1 = (bf16[256,128]{1,0:T(8,128)(2,1)S(1)}, bf16[128,1024]{1,0:T(8,128)(2,1)S(1)}) custom-call(bf16[4,64,128]{2,1,0:T(8,128)(2,1)S(1)} %pack.1.own, bf16[4,64,128]{2,1,0:T(8,128)(2,1)S(1)} %collective-permute-done.13.mate, bf16[256,1024]{1,0:T(8,128)(2,1)S(1)} %columns.3.factors), custom_call_target="tpu_custom_call" | custom-call | flops 67108864 | bytes 983040 | tf_op jit(solution)/shard_map/gradient/pallas_call | solution.py:202
  24.2 1.4 %collective-permute-start.14 = (bf16[256,128]{1,0:T(8,128)(2,1)S(1)}, bf16[256,128]{1,0:T(8,128)(2,1)S(1)}, u32[]{:S(2)}, u32[]{:S(2)}) collective-permute-start(bf16[256,128]{1,0:T(8,128)(2,1)S(1)} %get-tuple-element.50), channel_id=1, source_target_pairs={{0,3},{1,2},{2,1},{3,0},{4,7},{5,6},{6,5},{7,4},{8,11},{9,10},{10,... | collective-permute-start | bytes 196616 | tf_op jit(solution)/shard_map/ppermute | solution.py:318
  25.6 0.3 %pair.1 = (f32[256,128]{1,0:T(8,128)S(1)}, f32[256,128]{1,0:T(8,128)S(1)}) custom-call(bf16[256,1024]{1,0:T(8,128)(2,1)S(1)} %columns.2.factors, bf16[128,1024]{1,0:T(8,128)(2,1)S(1)} %get-tuple-element.47.left, f32[256,128]{1,0:T(8,128)S(1)} %get-tuple-element.42.here, f32[256,128]{1,0:T(8,128)S(1)} %collective-permute-done.9.there), custom_call_target="tpu_custom_call" | custom-call | flops 67108864 | bytes 1310720 | tf_op jit(solution)/shard_map/pair/pallas_call | solution.py:202
  25.9 2.4 %collective-permute-done.14.gradient = bf16[256,128]{1,0:T(8,128)(2,1)S(1)} collective-permute-done((bf16[256,128]{1,0:T(8,128)(2,1)S(1)}, bf16[256,128]{1,0:T(8,128)(2,1)S(1)}, u32[]{:S(2)}, u32[]{:S(2)}) %collective-permute-start.14) | collective-permute-done | bytes 65568 | tf_op jit(solution)/shard_map/ppermute | solution.py:318
  28.3 0.7 %shrink.1 = f32[256,128]{1,0:T(8,128)} custom-call(f32[256,128]{1,0:T(8,128)S(1)} %get-tuple-element.48.total, f32[256,128]{1,0:T(8,128)S(1)} %get-tuple-element.49.difference, bf16[256,128]{1,0:T(8,128)(2,1)S(1)} %collective-permute-done.14.gradient), custom_call_target="tpu_custom_call" | custom-call | tf_op jit(solution)/shard_map/shrink/pallas_call | solution.py:202
  (19 shorter events, 0.1 us)
Async XLA Ops:
  0.0 2.4 %collective-permute-start.1 = (bf16[2048,128]{1,0:T(8,128)(2,1)}, bf16[2048,128]{1,0:T(8,128)(2,1)S(1)}, u32[]{:S(2)}, u32[]{:S(2)}) collective-permute-start(bf16[2048,128]{1,0:T(8,128)(2,1)} %bitcast.5), channel_id=1, source_target_pairs={{0,2},{2,0},{4,6},{6,4},{8,10},{10,8},{12,14},{14,12},{16,18},{18,... | collective-permute-start | bytes 1572872 | tf_op jit(solution)/shard_map/ppermute | solution.py:215
  0.5 1.9 %collective-permute-start = (f32[256,128]{1,0:T(8,128)}, f32[256,128]{1,0:T(8,128)S(1)}, u32[]{:S(2)}, u32[]{:S(2)}) collective-permute-start(f32[256,128]{1,0:T(8,128)} %bitcast.10), channel_id=1, source_target_pairs={{0,2},{2,0},{4,6},{6,4},{8,10},{10,8},{12,14},{14,12},{16,18},{18,... | collective-permute-start | bytes 393224 | tf_op jit(solution)/shard_map/ppermute | solution.py:215
  0.5 9.4 %copy-start.3 = (f32[1,256,128]{2,1,0:T(8,128)S(1)}, f32[1,256,128]{2,1,0:T(8,128)}, u32[]{:S(2)}) copy-start(f32[1,256,128]{2,1,0:T(8,128)} %param.8) | copy-start | bytes 393220
  2.1 1.0 %copy-start.1 = (bf16[1,256,8,128]{3,2,1,0:T(8,128)(2,1)S(1)}, bf16[1,256,8,128]{3,2,1,0:T(8,128)(2,1)}, u32[]{:S(2)}) copy-start(bf16[1,256,8,128]{3,2,1,0:T(8,128)(2,1)} %param.5) | copy-start | bytes 1572868
  2.1 7.8 %copy-start.2 = (f32[1,256,128]{2,1,0:T(8,128)S(1)}, f32[1,256,128]{2,1,0:T(8,128)}, u32[]{:S(2)}) copy-start(f32[1,256,128]{2,1,0:T(8,128)} %param.9) | copy-start | bytes 393220
  3.2 6.8 %copy-start.4 = (s32[1,8,8]{2,1,0:T(8,128)S(1)}, s32[1,8,8]{2,1,0:T(8,128)}, u32[]{:S(2)}) copy-start(s32[1,8,8]{2,1,0:T(8,128)} %ranks.1) | copy-start | bytes 772
  3.2 6.8 %collective-permute-start.3 = (bf16[2048,128]{1,0:T(8,128)(2,1)S(1)}, bf16[2048,128]{1,0:T(8,128)(2,1)S(1)}, u32[]{:S(2)}, u32[]{:S(2)}) collective-permute-start(bf16[2048,128]{1,0:T(8,128)(2,1)S(1)} %bitcast.8), channel_id=1, source_target_pairs={{0,2},{2,0},{4,6},{6,4},{8,10},{10,8},{12,14},{14,12},{16,18},{18,... | collective-permute-start | bytes 1572872 | tf_op jit(solution)/shard_map/ppermute | solution.py:215
  3.6 7.4 %collective-permute-start.2 = (bf16[64,128]{1,0:T(8,128)(2,1)S(1)}, bf16[64,128]{1,0:T(8,128)(2,1)S(1)}, u32[]{:S(2)}, u32[]{:S(2)}) collective-permute-start(bf16[64,128]{1,0:T(8,128)(2,1)S(1)} %get-tuple-element.28), channel_id=1, source_target_pairs={{0,26},{2,28},{4,30},{6,24},{8,18},{10,20},{12,22},{14,16},{16,10}... | collective-permute-start | bytes 49160 | tf_op jit(solution)/shard_map/ppermute | solution.py:227
  8.3 5.0 %collective-permute-start.4 = (bf16[64,128]{1,0:T(8,128)(2,1)S(1)}, bf16[64,128]{1,0:T(8,128)(2,1)S(1)}, u32[]{:S(2)}, u32[]{:S(2)}) collective-permute-start(bf16[64,128]{1,0:T(8,128)(2,1)S(1)} %get-tuple-element.36), channel_id=1, source_target_pairs={{0,18},{2,20},{4,22},{6,16},{8,26},{10,28},{12,30},{14,24},{16,2},... | collective-permute-start | bytes 49160 | tf_op jit(solution)/shard_map/ppermute | solution.py:227
  8.3 5.0 %collective-permute-start.5 = (bf16[64,128]{1,0:T(8,128)(2,1)S(1)}, bf16[64,128]{1,0:T(8,128)(2,1)S(1)}, u32[]{:S(2)}, u32[]{:S(2)}) collective-permute-start(bf16[64,128]{1,0:T(8,128)(2,1)S(1)} %get-tuple-element.37), channel_id=1, source_target_pairs={{0,6},{2,12},{4,2},{6,8},{8,14},{10,4},{12,10},{14,0},{16,22},{18,... | collective-permute-start | bytes 49160 | tf_op jit(solution)/shard_map/ppermute | solution.py:227
  9.4 3.9 %collective-permute-start.6 = (bf16[64,128]{1,0:T(8,128)(2,1)S(1)}, bf16[64,128]{1,0:T(8,128)(2,1)S(1)}, u32[]{:S(2)}, u32[]{:S(2)}) collective-permute-start(bf16[64,128]{1,0:T(8,128)(2,1)S(1)} %get-tuple-element.38), channel_id=1, source_target_pairs={{0,2},{2,8},{4,6},{6,12},{8,10},{10,0},{12,14},{14,4},{16,18},{18,... | collective-permute-start | bytes 49160 | tf_op jit(solution)/shard_map/ppermute | solution.py:227
  13.6 1.7 %collective-permute-start.7 = (f32[2,128,256]{2,1,0:T(8,128)S(1)}, f32[2,128,256]{2,1,0:T(8,128)S(1)}, u32[]{:S(2)}, u32[]{:S(2)}) collective-permute-start(f32[2,128,256]{2,1,0:T(8,128)S(1)} %image.1.here), channel_id=1, source_target_pairs={{0,2},{2,0},{4,6},{6,4},{8,10},{10,8},{12,14},{14,12},{16,18},{18,... | collective-permute-start | bytes 786440 | tf_op jit(solution)/shard_map/ppermute | solution.py:215
  13.8 8.0 %collective-permute-start.9 = (f32[256,128]{1,0:T(8,128)S(1)}, f32[256,128]{1,0:T(8,128)S(1)}, u32[]{:S(2)}, u32[]{:S(2)}) collective-permute-start(f32[256,128]{1,0:T(8,128)S(1)} %get-tuple-element.42.here), channel_id=1, source_target_pairs={{0,1},{1,0},{2,3},{3,2},{4,5},{5,4},{6,7},{7,6},{8,9},{9,8},{10,11... | collective-permute-start | bytes 393224 | tf_op jit(solution)/shard_map/ppermute | solution.py:288
  15.7 6.1 %collective-permute-start.8 = (bf16[64,128]{1,0:T(8,128)(2,1)S(1)}, bf16[64,128]{1,0:T(8,128)(2,1)S(1)}, u32[]{:S(2)}, u32[]{:S(2)}) collective-permute-start(bf16[64,128]{1,0:T(8,128)(2,1)S(1)} %get-tuple-element.39), channel_id=1, source_target_pairs={{0,30},{2,24},{4,26},{6,28},{8,22},{10,16},{12,18},{14,20},{16,14}... | collective-permute-start | bytes 49160 | tf_op jit(solution)/shard_map/ppermute | solution.py:227
  18.0 4.1 %collective-permute-start.10 = (bf16[64,128]{1,0:T(8,128)(2,1)S(1)}, bf16[64,128]{1,0:T(8,128)(2,1)S(1)}, u32[]{:S(2)}, u32[]{:S(2)}) collective-permute-start(bf16[64,128]{1,0:T(8,128)(2,1)S(1)} %get-tuple-element.44), channel_id=1, source_target_pairs={{0,22},{2,16},{4,18},{6,20},{8,30},{10,24},{12,26},{14,28},{16,6},... | collective-permute-start | bytes 49160 | tf_op jit(solution)/shard_map/ppermute | solution.py:227
  18.7 3.4 %collective-permute-start.11 = (bf16[64,128]{1,0:T(8,128)(2,1)S(1)}, bf16[64,128]{1,0:T(8,128)(2,1)S(1)}, u32[]{:S(2)}, u32[]{:S(2)}) collective-permute-start(bf16[64,128]{1,0:T(8,128)(2,1)S(1)} %get-tuple-element.45), channel_id=1, source_target_pairs={{0,14},{2,4},{4,10},{6,0},{8,6},{10,12},{12,2},{14,8},{16,30},{18,... | collective-permute-start | bytes 49160 | tf_op jit(solution)/shard_map/ppermute | solution.py:227
  20.5 1.0 %copy-start = (bf16[1,256,8,128]{3,2,1,0:T(8,128)(2,1)S(1)}, bf16[1,256,8,128]{3,2,1,0:T(8,128)(2,1)}, u32[]{:S(2)}) copy-start(bf16[1,256,8,128]{3,2,1,0:T(8,128)(2,1)} %param.6) | copy-start | bytes 1572868
  20.5 2.0 %collective-permute-start.12 = (bf16[64,128]{1,0:T(8,128)(2,1)S(1)}, bf16[64,128]{1,0:T(8,128)(2,1)S(1)}, u32[]{:S(2)}, u32[]{:S(2)}) collective-permute-start(bf16[64,128]{1,0:T(8,128)(2,1)S(1)} %get-tuple-element.46), channel_id=1, source_target_pairs={{0,10},{2,0},{4,14},{6,4},{8,2},{10,8},{12,6},{14,12},{16,26},{18,... | collective-permute-start | bytes 49160 | tf_op jit(solution)/shard_map/ppermute | solution.py:227
  22.5 1.4 %collective-permute-start.13 = (bf16[4,64,128]{2,1,0:T(8,128)(2,1)S(1)}, bf16[4,64,128]{2,1,0:T(8,128)(2,1)S(1)}, u32[]{:S(2)}, u32[]{:S(2)}) collective-permute-start(bf16[4,64,128]{2,1,0:T(8,128)(2,1)S(1)} %pack.1.own), channel_id=1, source_target_pairs={{0,2},{2,0},{4,6},{6,4},{8,10},{10,8},{12,14},{14,12},{16,18},{18,... | collective-permute-start | bytes 196616 | tf_op jit(solution)/shard_map/ppermute | solution.py:215
  24.2 4.0 %collective-permute-start.14 = (bf16[256,128]{1,0:T(8,128)(2,1)S(1)}, bf16[256,128]{1,0:T(8,128)(2,1)S(1)}, u32[]{:S(2)}, u32[]{:S(2)}) collective-permute-start(bf16[256,128]{1,0:T(8,128)(2,1)S(1)} %get-tuple-element.50), channel_id=1, source_target_pairs={{0,3},{1,2},{2,1},{3,0},{4,7},{5,6},{6,5},{7,4},{8,11},{9,10},{10,... | collective-permute-start | bytes 196616 | tf_op jit(solution)/shard_map/ppermute | solution.py:318

commit v12 on v11

--- a/solution.py
+++ b/solution.py
@@ -111,7 +111,7 @@
         outs[index][...] = (parts[index].astype(F32) + block.astype(F32)).astype(BF16)
 
 
-def rows_kernel(shifts, ranks, own, mate, observed, start, own_out, mate_out, turned, start_out, wide):
+def rows_kernel(shifts, ranks, own, mate, observed, own_out, mate_out, turned, wide):
     chip, _ = place()
     _, chosen = both_shifts(shifts)
     lane = lax.broadcasted_iota(jnp.int32, (1, LANES), 1) % (LANES // 2)
@@ -119,7 +119,6 @@
     separate(own, wide, own_out, chosen, masks)
     separate(mate, wide, mate_out, chosen, masks)
     turned[...] = observed[...].T
-    start_out[...] = start[...]
 
 
 def columns_kernel(factors, separated, wide):
@@ -127,17 +126,18 @@
 
 
 def image_kernel(*refs):
-    arrived, (own, mate, observed, misfit, left) = refs[:-5], refs[-5:]
+    arrived, (own, mate, observed, misfit, sent, left) = refs[:-6], refs[-6:]
     for index, block in enumerate(arrived):
         spread_block(block[...], left, index)
     misfit[0] = times_transposed(left[...], own[...]) - observed[...]
     misfit[1] = times_transposed(left[...], mate[...])
+    sent[...] = misfit[...].astype(BF16)
 
 
 def back_kernel(here, there, own, mate, *refs):
     outs, products = refs[:-1], refs[-1]
     for rows, factors in ((0, own), (1, mate)):
-        misfit = (here[rows] + there[1 - rows]).astype(BF16)
+        misfit = (here[rows] + there[1 - rows].astype(F32)).astype(BF16)
         products[rows] = jnp.dot(misfit, factors[...], preferred_element_type=F32)
     for index, out in enumerate(outs):
         parts = [adjoint_block(products.at[rows], index).astype(F32) for rows in range(2)]
@@ -215,6 +215,12 @@
     return lax.ppermute(value, "tile", [(i, i ^ 1) for i in range(lax.axis_size("tile"))])
 
 
+def across(value, shift):
+    count, band = lax.axis_size("tile"), lax.axis_size("freq")
+    pairs = [(i * band + f, (i ^ 1) * band + (f - shift) % band) for i in range(count) for f in range(band)]
+    return lax.ppermute(value, ("tile", "freq"), pairs)
+
+
 def after(value, *others):
     return lax.optimization_barrier((value, *others))[0]
 
@@ -229,7 +235,7 @@
 
 
 def body(u_factors, v_factors, ranks, observed, start):
-    count, band = lax.axis_size("tile"), lax.axis_size("freq")
+    band = lax.axis_size("freq")
     rows, tiles, width = u_factors.shape[1:]
     sources = start.shape[2]
     columns = tiles * width
@@ -275,36 +281,35 @@
         flops // 2,
     )
     left_rows = after(left_rows, sends[0])
-    own_left, mate_left, turned, start = call(
+    own_left, mate_left, turned = call(
         functools.partial(rows_kernel, shifts),
         "rows",
-        [chosen, chosen, shape(sources, rows, dtype=F32), shape(rows, sources, dtype=F32)],
-        [ranks, left_rows, to_mate(left_rows), after(observed, parts), after(start, parts)],
+        [chosen, chosen, shape(sources, rows, dtype=F32)],
+        [ranks, left_rows, to_mate(left_rows), after(observed, parts)],
         [wide],
         spaces=[pltpu.SMEM],
     )
-    starts = [start]
-    for shift in range(1, band):
-        starts.append(lax.ppermute(start, "freq", [(f, (f - shift) % band) for f in range(band)]))
-    (misfit,) = call(
+    misfit, sent = call(
         image_kernel,
         "image",
-        [shape(2, sources, rows, dtype=F32)],
+        [shape(2, sources, rows, dtype=F32), shape(2, sources, rows)],
         [*exchange(sends, shifts, [own_left, mate_left, turned]), own_left, mate_left, turned],
         [pltpu.VMEM((sources, members * width), BF16)],
         flops,
     )
-    (mate_right,) = call(columns_kernel, "columns", [factor], [after(raw_right, misfit)], [wide])
+    starts = [start]
+    for shift in range(1, band):
+        starts.append(across(after(raw_start, own_left), shift))
+    (mate_right,) = call(columns_kernel, "columns", [factor], [after(raw_right, sends[0])], [wide])
     sends = call(
         back_kernel,
         "back",
         [block] * members,
-        [misfit, to_mate(misfit), own_left, mate_left],
+        [misfit, to_mate(sent), own_left, mate_left],
         [pltpu.VMEM((2, sources, members * width), F32)],
         flops,
     )
-    (right,) = call(columns_kernel, "columns", [factor], [after(right_rows, sends[0])], [wide])
-    (own,) = call(pack_kernel, "pack", [blocks], exchange(sends, shifts[::-1], [right, mate_right, *starts[1:]]))
+    (own,) = call(pack_kernel, "pack", [blocks], exchange(sends, shifts[::-1], [mate_right, *starts[1:]]))
     gradient, left = call(
         functools.partial(gradient_kernel, shifts),
         "gradient",
@@ -312,10 +317,10 @@
         [own, to_mate(own), mate_right],
         flops=flops,
     )
+    (right,) = call(columns_kernel, "columns", [factor], [after(right_rows, gradient)], [wide])
     gradients = []
     for shift in range(1, band):
-        pairs = [(i * band + f, (i ^ 1) * band + (f - shift) % band) for i in range(count) for f in range(band)]
-        gradients.append(lax.ppermute(gradient, ("tile", "freq"), pairs))
+        gradients.append(across(gradient, shift))
     result = shape(rows, sources, dtype=F32)
     if band == 2:
         halves = call(pair_kernel, "pair", [result] * 2, [right, left, *starts], flops=flops)

time: 29.2 us -> 29.1 us (level)
  waiting for transfers between devices: 6.4 us -> 6.87 us
    ppermute x8, waiting for transfers between devices: 2.88 us -> 3.4 us  [exchange(): arrived.append(lax.ppermute(send, 'tile', pairs))]
where the time goes in v12:
time: 29.1 us; the launch traced here: 28.9 us
  starting transfers between devices  15.9 us (55%)
  waiting for transfers between devices  6.87 us (24%)
  Pallas kernels  5.79 us (20%)
    ppermute x8, starting transfers between devices, exchange(): arrived.append(lax.ppermute(send, 'tile', pairs))  11.7 us
    pallas_call x11, Pallas kernels, call(): pl.pallas_call(kernel, out_shape=outs, in_specs=[pl.BlockSpec(memory_spac...  5.79 us
    ppermute x8, waiting for transfers between devices, exchange(): arrived.append(lax.ppermute(send, 'tile', pairs))  3.4 us
    ppermute x2, starting transfers between devices, across(): return lax.ppermute(value, ('tile', 'freq'), pairs)  2.81 us
    ppermute x2, waiting for transfers between devices, across(): return lax.ppermute(value, ('tile', 'freq'), pairs)  2.21 us
    ppermute x5, starting transfers between devices, to_mate(): lax.ppermute(value, 'tile', [(i, i ^ 1) for i in range(lax.axis_size('til...  1.43 us
    ppermute x5, waiting for transfers between devices, to_mate(): lax.ppermute(value, 'tile', [(i, i ^ 1) for i in range(lax.axis_size('til...  1.26 us
  transfers between devices with their start and end apart: 15, of which 6 were waited for; matrix products, arithmetic and copies ran while one was open for 0% of the time, Pallas kernels for 13%

profile of v12, /device:TPU:0, one launch (start us, length us, event | category | flops | bytes accessed | tf_op | source)
XLA Modules:
  0.0 28.9 jit_solution(11965846517555034965)
XLA Ops:
  0.0 0.5 %collective-permute-start.1 = (bf16[2048,128]{1,0:T(8,128)(2,1)}, bf16[2048,128]{1,0:T(8,128)(2,1)S(1)}, u32[]{:S(2)}, u32[]{:S(2)}) collective-permute-start(bf16[2048,128]{1,0:T(8,128)(2,1)} %bitcast.5), channel_id=1, source_target_pairs={{0,2},{2,0},{4,6},{6,4},{8,10},{10,8},{12,14},{14,12},{16,18},{18,... | collective-permute-start | bytes 1572872 | tf_op jit(solution)/shard_map/ppermute | solution.py:215
  0.5 0.1 collective-permute-start
  0.5 1.6 %forward.1.parts = bf16[4,64,128]{2,1,0:T(8,128)(2,1)S(1)} custom-call(f32[256,128]{1,0:T(8,128)} %bitcast.11, bf16[2048,128]{1,0:T(8,128)(2,1)} %bitcast.6), custom_call_target="tpu_custom_call" | custom-call | tf_op jit(solution)/shard_map/forward/pallas_call | solution.py:202
  2.1 0.0 copy-start.1
  2.1 0.3 collective-permute-done.start
  2.4 0.5 %join.1 = (bf16[64,128]{1,0:T(8,128)(2,1)S(1)}, bf16[64,128]{1,0:T(8,128)(2,1)S(1)}, bf16[64,128]{1,0:T(8,128)(2,1)S(1)}, bf16[64,128]{1,0:T(8,128)(2,1)S(1)}) custom-call(bf16[4,64,128]{2,1,0:T(8,128)(2,1)S(1)} %forward.1.parts, f32[256,128]{1,0:T(8,128)S(1)} %collective-permute-done.start, bf16[2048,128]{1,0:T(8,128)(2,1)S(1)} %collective-permute-done.1.factors), custom_call_target="tpu_custom_call" | custom-call | flops 33554432 | bytes 786432 | tf_op jit(solution)/shard_map/join/pallas_call | solution.py:202
  2.9 0.2 copy-done.1
  3.1 0.5 %collective-permute-start.3 = (bf16[2048,128]{1,0:T(8,128)(2,1)S(1)}, bf16[2048,128]{1,0:T(8,128)(2,1)S(1)}, u32[]{:S(2)}, u32[]{:S(2)}) collective-permute-start(bf16[2048,128]{1,0:T(8,128)(2,1)S(1)} %bitcast.8), channel_id=1, source_target_pairs={{0,2},{2,0},{4,6},{6,4},{8,10},{10,8},{12,14},{14,12},{16,18},{18,... | collective-permute-start | bytes 1572872 | tf_op jit(solution)/shard_map/ppermute | solution.py:215
  3.6 4.7 %collective-permute-start.2 = (bf16[64,128]{1,0:T(8,128)(2,1)S(1)}, bf16[64,128]{1,0:T(8,128)(2,1)S(1)}, u32[]{:S(2)}, u32[]{:S(2)}) collective-permute-start(bf16[64,128]{1,0:T(8,128)(2,1)S(1)} %get-tuple-element.29), channel_id=1, source_target_pairs={{0,26},{2,28},{4,30},{6,24},{8,18},{10,20},{12,22},{14,16},{16,10}... | collective-permute-start | bytes 49160 | tf_op jit(solution)/shard_map/ppermute | solution.py:233
  8.3 1.1 %collective-permute-start.5 = (bf16[64,128]{1,0:T(8,128)(2,1)S(1)}, bf16[64,128]{1,0:T(8,128)(2,1)S(1)}, u32[]{:S(2)}, u32[]{:S(2)}) collective-permute-start(bf16[64,128]{1,0:T(8,128)(2,1)S(1)} %get-tuple-element.37), channel_id=1, source_target_pairs={{0,6},{2,12},{4,2},{6,8},{8,14},{10,4},{12,10},{14,0},{16,22},{18,... | collective-permute-start | bytes 49160 | tf_op jit(solution)/shard_map/ppermute | solution.py:233
  9.4 0.5 %collective-permute-start.6 = (bf16[64,128]{1,0:T(8,128)(2,1)S(1)}, bf16[64,128]{1,0:T(8,128)(2,1)S(1)}, u32[]{:S(2)}, u32[]{:S(2)}) collective-permute-start(bf16[64,128]{1,0:T(8,128)(2,1)S(1)} %get-tuple-element.38), channel_id=1, source_target_pairs={{0,2},{2,8},{4,6},{6,12},{8,10},{10,0},{12,14},{14,4},{16,18},{18,... | collective-permute-start | bytes 49160 | tf_op jit(solution)/shard_map/ppermute | solution.py:233
  9.9 1.1 %rows.1 = (bf16[256,512]{1,0:T(8,128)(2,1)S(1)}, bf16[256,512]{1,0:T(8,128)(2,1)S(1)}, f32[128,256]{1,0:T(8,128)S(1)}) custom-call(s32[1,8,8]{2,1,0:T(8,128)S(1)} %copy-done.4, bf16[2048,128]{1,0:T(8,128)(2,1)S(1)} %bitcast.9, bf16[2048,128]{1,0:T(8,128)(2,1)S(1)} %collective-permute-done.3.mate, f32[256,128]{1,0:T(8,128)S(1)} %bitcast.13), custom_call_target="tpu_custom_call" | custom-call | tf_op jit(solution)/shard_map/rows/pallas_call | solution.py:202
  11.0 2.3 %collective-permute-done.4.refs_1_ = bf16[64,128]{1,0:T(8,128)(2,1)S(1)} collective-permute-done((bf16[64,128]{1,0:T(8,128)(2,1)S(1)}, bf16[64,128]{1,0:T(8,128)(2,1)S(1)}, u32[]{:S(2)}, u32[]{:S(2)}) %collective-permute-start.4) | collective-permute-done | bytes 16416 | tf_op jit(solution)/shard_map/ppermute | solution.py:233
  13.3 0.3 %image.1 = (f32[2,128,256]{2,1,0:T(8,128)S(1)}, bf16[2,128,256]{2,1,0:T(8,128)(2,1)S(1)}) custom-call(bf16[64,128]{1,0:T(8,128)(2,1)S(1)} %collective-permute-done.2.refs_0_, bf16[64,128]{1,0:T(8,128)(2,1)S(1)} %collective-permute-done.4.refs_1_, bf16[64,128]{1,0:T(8,128)(2,1)S(1)} %collective-permute-done.5.refs_2_, ...), custom_call_target="tpu_custom_call" | custom-call | flops 67108864 | bytes 1114112 | tf_op jit(solution)/shard_map/image/pallas_call | solution.py:202
  13.6 0.2 collective-permute-start.7
  13.8 1.6 %collective-permute-start.9 = (f32[256,128]{1,0:T(8,128)S(1)}, f32[256,128]{1,0:T(8,128)S(1)}, u32[]{:S(2)}, u32[]{:S(2)}) collective-permute-start(f32[256,128]{1,0:T(8,128)S(1)} %collective-permute-done.start), channel_id=1, source_target_pairs={{0,3},{1,2},{2,1},{3,0},{4,7},{5,6},{6,5},{7,4},{8,11},{9,10},{10,... | collective-permute-start | bytes 393224 | tf_op jit(solution)/shard_map/ppermute | solution.py:221
  15.3 0.3 %back.1 = (bf16[64,128]{1,0:T(8,128)(2,1)S(1)}, bf16[64,128]{1,0:T(8,128)(2,1)S(1)}, bf16[64,128]{1,0:T(8,128)(2,1)S(1)}, bf16[64,128]{1,0:T(8,128)(2,1)S(1)}) custom-call(f32[2,128,256]{2,1,0:T(8,128)S(1)} %get-tuple-element.39.here, bf16[2,128,256]{2,1,0:T(8,128)(2,1)S(1)} %collective-permute-done.7.there, ...), custom_call_target="tpu_custom_call" | custom-call | flops 67108864 | bytes 983040 | tf_op jit(solution)/shard_map/back/pallas_call | solution.py:202
  15.7 2.4 %collective-permute-start.8 = (bf16[64,128]{1,0:T(8,128)(2,1)S(1)}, bf16[64,128]{1,0:T(8,128)(2,1)S(1)}, u32[]{:S(2)}, u32[]{:S(2)}) collective-permute-start(bf16[64,128]{1,0:T(8,128)(2,1)S(1)} %get-tuple-element.41), channel_id=1, source_target_pairs={{0,30},{2,24},{4,26},{6,28},{8,22},{10,16},{12,18},{14,20},{16,14}... | collective-permute-start | bytes 49160 | tf_op jit(solution)/shard_map/ppermute | solution.py:233
  18.1 0.6 %collective-permute-start.10 = (bf16[64,128]{1,0:T(8,128)(2,1)S(1)}, bf16[64,128]{1,0:T(8,128)(2,1)S(1)}, u32[]{:S(2)}, u32[]{:S(2)}) collective-permute-start(bf16[64,128]{1,0:T(8,128)(2,1)S(1)} %get-tuple-element.45), channel_id=1, source_target_pairs={{0,22},{2,16},{4,18},{6,20},{8,30},{10,24},{12,26},{14,28},{16,6},... | collective-permute-start | bytes 49160 | tf_op jit(solution)/shard_map/ppermute | solution.py:233
  18.7 1.8 %collective-permute-start.11 = (bf16[64,128]{1,0:T(8,128)(2,1)S(1)}, bf16[64,128]{1,0:T(8,128)(2,1)S(1)}, u32[]{:S(2)}, u32[]{:S(2)}) collective-permute-start(bf16[64,128]{1,0:T(8,128)(2,1)S(1)} %get-tuple-element.46), channel_id=1, source_target_pairs={{0,14},{2,4},{4,10},{6,0},{8,6},{10,12},{12,2},{14,8},{16,30},{18,... | collective-permute-start | bytes 49160 | tf_op jit(solution)/shard_map/ppermute | solution.py:233
  20.4 0.6 %collective-permute-start.12 = (bf16[64,128]{1,0:T(8,128)(2,1)S(1)}, bf16[64,128]{1,0:T(8,128)(2,1)S(1)}, u32[]{:S(2)}, u32[]{:S(2)}) collective-permute-start(bf16[64,128]{1,0:T(8,128)(2,1)S(1)} %get-tuple-element.47), channel_id=1, source_target_pairs={{0,10},{2,0},{4,14},{6,4},{8,2},{10,8},{12,6},{14,12},{16,26},{18,... | collective-permute-start | bytes 49160 | tf_op jit(solution)/shard_map/ppermute | solution.py:233
  21.0 0.3 columns.2.factors
  21.3 0.8 %collective-permute-done.10.refs_1_ = bf16[64,128]{1,0:T(8,128)(2,1)S(1)} collective-permute-done((bf16[64,128]{1,0:T(8,128)(2,1)S(1)}, bf16[64,128]{1,0:T(8,128)(2,1)S(1)}, u32[]{:S(2)}, u32[]{:S(2)}) %collective-permute-start.10) | collective-permute-done | bytes 16416 | tf_op jit(solution)/shard_map/ppermute | solution.py:233
  22.1 0.3 %collective-permute-done.12.refs_3_ = bf16[64,128]{1,0:T(8,128)(2,1)S(1)} collective-permute-done((bf16[64,128]{1,0:T(8,128)(2,1)S(1)}, bf16[64,128]{1,0:T(8,128)(2,1)S(1)}, u32[]{:S(2)}, u32[]{:S(2)}) %collective-permute-start.12) | collective-permute-done | bytes 16416 | tf_op jit(solution)/shard_map/ppermute | solution.py:233
  22.5 0.3 collective-permute-start.13
  22.7 1.0 %collective-permute-done.13.mate = bf16[4,64,128]{2,1,0:T(8,128)(2,1)S(1)} collective-permute-done((bf16[4,64,128]{2,1,0:T(8,128)(2,1)S(1)}, bf16[4,64,128]{2,1,0:T(8,128)(2,1)S(1)}, u32[]{:S(2)}, u32[]{:S(2)}) %collective-permute-start.13) | collective-permute-done | bytes 65568 | tf_op jit(solution)/shard_map/ppermute | solution.py:215
  23.7 0.4 %gradient.1 = (bf16[256,128]{1,0:T(8,128)(2,1)S(1)}, bf16[128,1024]{1,0:T(8,128)(2,1)S(1)}) custom-call(bf16[4,64,128]{2,1,0:T(8,128)(2,1)S(1)} %pack.1.own, bf16[4,64,128]{2,1,0:T(8,128)(2,1)S(1)} %collective-permute-done.13.mate, bf16[256,1024]{1,0:T(8,128)(2,1)S(1)} %columns.2.factors), custom_call_target="tpu_custom_call" | custom-call | flops 67108864 | bytes 983040 | tf_op jit(solution)/shard_map/gradient/pallas_call | solution.py:202
  24.1 1.3 %collective-permute-start.14 = (bf16[256,128]{1,0:T(8,128)(2,1)S(1)}, bf16[256,128]{1,0:T(8,128)(2,1)S(1)}, u32[]{:S(2)}, u32[]{:S(2)}) collective-permute-start(bf16[256,128]{1,0:T(8,128)(2,1)S(1)} %get-tuple-element.48), channel_id=1, source_target_pairs={{0,3},{1,2},{2,1},{3,0},{4,7},{5,6},{6,5},{7,4},{8,11},{9,10},{10,... | collective-permute-start | bytes 196616 | tf_op jit(solution)/shard_map/ppermute | solution.py:221
  25.4 0.3 columns.3.factors
  25.7 0.3 %pair.1 = (f32[256,128]{1,0:T(8,128)S(1)}, f32[256,128]{1,0:T(8,128)S(1)}) custom-call(bf16[256,1024]{1,0:T(8,128)(2,1)S(1)} %columns.3.factors, bf16[128,1024]{1,0:T(8,128)(2,1)S(1)} %get-tuple-element.50.left, f32[256,128]{1,0:T(8,128)S(1)} %bitcast.12, f32[256,128]{1,0:T(8,128)S(1)} %collective-permute-done.9.there), custom_call_target="tpu_custom_call" | custom-call | flops 67108864 | bytes 1310720 | tf_op jit(solution)/shard_map/pair/pallas_call | solution.py:202
  26.0 2.2 %collective-permute-done.14.gradient = bf16[256,128]{1,0:T(8,128)(2,1)S(1)} collective-permute-done((bf16[256,128]{1,0:T(8,128)(2,1)S(1)}, bf16[256,128]{1,0:T(8,128)(2,1)S(1)}, u32[]{:S(2)}, u32[]{:S(2)}) %collective-permute-start.14) | collective-permute-done | bytes 65568 | tf_op jit(solution)/shard_map/ppermute | solution.py:221
  28.2 0.7 %shrink.1 = f32[256,128]{1,0:T(8,128)} custom-call(f32[256,128]{1,0:T(8,128)S(1)} %get-tuple-element.51.total, f32[256,128]{1,0:T(8,128)S(1)} %get-tuple-element.52.difference, bf16[256,128]{1,0:T(8,128)(2,1)S(1)} %collective-permute-done.14.gradient), custom_call_target="tpu_custom_call" | custom-call | tf_op jit(solution)/shard_map/shrink/pallas_call | solution.py:202
  (19 shorter events, 0.1 us)
Async XLA Ops:
  0.0 2.4 %collective-permute-start.1 = (bf16[2048,128]{1,0:T(8,128)(2,1)}, bf16[2048,128]{1,0:T(8,128)(2,1)S(1)}, u32[]{:S(2)}, u32[]{:S(2)}) collective-permute-start(bf16[2048,128]{1,0:T(8,128)(2,1)} %bitcast.5), channel_id=1, source_target_pairs={{0,2},{2,0},{4,6},{6,4},{8,10},{10,8},{12,14},{14,12},{16,18},{18,... | collective-permute-start | bytes 1572872 | tf_op jit(solution)/shard_map/ppermute | solution.py:215
  0.5 1.9 %collective-permute-start = (f32[256,128]{1,0:T(8,128)}, f32[256,128]{1,0:T(8,128)S(1)}, u32[]{:S(2)}, u32[]{:S(2)}) collective-permute-start(f32[256,128]{1,0:T(8,128)} %bitcast.10), channel_id=1, source_target_pairs={{0,2},{2,0},{4,6},{6,4},{8,10},{10,8},{12,14},{14,12},{16,18},{18,... | collective-permute-start | bytes 393224 | tf_op jit(solution)/shard_map/ppermute | solution.py:215
  2.1 1.0 %copy-start.1 = (bf16[1,256,8,128]{3,2,1,0:T(8,128)(2,1)S(1)}, bf16[1,256,8,128]{3,2,1,0:T(8,128)(2,1)}, u32[]{:S(2)}) copy-start(bf16[1,256,8,128]{3,2,1,0:T(8,128)(2,1)} %param.5) | copy-start | bytes 1572868
  2.1 7.8 %copy-start.3 = (f32[1,256,128]{2,1,0:T(8,128)S(1)}, f32[1,256,128]{2,1,0:T(8,128)}, u32[]{:S(2)}) copy-start(f32[1,256,128]{2,1,0:T(8,128)} %param.8) | copy-start | bytes 393220
  3.1 6.8 %copy-start.4 = (s32[1,8,8]{2,1,0:T(8,128)S(1)}, s32[1,8,8]{2,1,0:T(8,128)}, u32[]{:S(2)}) copy-start(s32[1,8,8]{2,1,0:T(8,128)} %ranks.1) | copy-start | bytes 772
  3.1 6.8 %collective-permute-start.3 = (bf16[2048,128]{1,0:T(8,128)(2,1)S(1)}, bf16[2048,128]{1,0:T(8,128)(2,1)S(1)}, u32[]{:S(2)}, u32[]{:S(2)}) collective-permute-start(bf16[2048,128]{1,0:T(8,128)(2,1)S(1)} %bitcast.8), channel_id=1, source_target_pairs={{0,2},{2,0},{4,6},{6,4},{8,10},{10,8},{12,14},{14,12},{16,18},{18,... | collective-permute-start | bytes 1572872 | tf_op jit(solution)/shard_map/ppermute | solution.py:215
  3.6 7.4 %collective-permute-start.2 = (bf16[64,128]{1,0:T(8,128)(2,1)S(1)}, bf16[64,128]{1,0:T(8,128)(2,1)S(1)}, u32[]{:S(2)}, u32[]{:S(2)}) collective-permute-start(bf16[64,128]{1,0:T(8,128)(2,1)S(1)} %get-tuple-element.29), channel_id=1, source_target_pairs={{0,26},{2,28},{4,30},{6,24},{8,18},{10,20},{12,22},{14,16},{16,10}... | collective-permute-start | bytes 49160 | tf_op jit(solution)/shard_map/ppermute | solution.py:233
  8.3 5.0 %collective-permute-start.4 = (bf16[64,128]{1,0:T(8,128)(2,1)S(1)}, bf16[64,128]{1,0:T(8,128)(2,1)S(1)}, u32[]{:S(2)}, u32[]{:S(2)}) collective-permute-start(bf16[64,128]{1,0:T(8,128)(2,1)S(1)} %get-tuple-element.36), channel_id=1, source_target_pairs={{0,18},{2,20},{4,22},{6,16},{8,26},{10,28},{12,30},{14,24},{16,2},... | collective-permute-start | bytes 49160 | tf_op jit(solution)/shard_map/ppermute | solution.py:233
  8.3 5.0 %collective-permute-start.5 = (bf16[64,128]{1,0:T(8,128)(2,1)S(1)}, bf16[64,128]{1,0:T(8,128)(2,1)S(1)}, u32[]{:S(2)}, u32[]{:S(2)}) collective-permute-start(bf16[64,128]{1,0:T(8,128)(2,1)S(1)} %get-tuple-element.37), channel_id=1, source_target_pairs={{0,6},{2,12},{4,2},{6,8},{8,14},{10,4},{12,10},{14,0},{16,22},{18,... | collective-permute-start | bytes 49160 | tf_op jit(solution)/shard_map/ppermute | solution.py:233
  9.4 3.9 %collective-permute-start.6 = (bf16[64,128]{1,0:T(8,128)(2,1)S(1)}, bf16[64,128]{1,0:T(8,128)(2,1)S(1)}, u32[]{:S(2)}, u32[]{:S(2)}) collective-permute-start(bf16[64,128]{1,0:T(8,128)(2,1)S(1)} %get-tuple-element.38), channel_id=1, source_target_pairs={{0,2},{2,8},{4,6},{6,12},{8,10},{10,0},{12,14},{14,4},{16,18},{18,... | collective-permute-start | bytes 49160 | tf_op jit(solution)/shard_map/ppermute | solution.py:233
  13.6 1.7 %collective-permute-start.7 = (bf16[2,128,256]{2,1,0:T(8,128)(2,1)S(1)}, bf16[2,128,256]{2,1,0:T(8,128)(2,1)S(1)}, u32[]{:S(2)}, u32[]{:S(2)}) collective-permute-start(bf16[2,128,256]{2,1,0:T(8,128)(2,1)S(1)} %get-tuple-element.40), channel_id=1, source_target_pairs={{0,2},{2,0},{4,6},{6,4},{8,10},{10,8},{12,14},{14,12},{16,18},{18,... | collective-permute-start | bytes 393224 | tf_op jit(solution)/shard_map/ppermute | solution.py:215
  13.8 7.5 %collective-permute-start.9 = (f32[256,128]{1,0:T(8,128)S(1)}, f32[256,128]{1,0:T(8,128)S(1)}, u32[]{:S(2)}, u32[]{:S(2)}) collective-permute-start(f32[256,128]{1,0:T(8,128)S(1)} %collective-permute-done.start), channel_id=1, source_target_pairs={{0,3},{1,2},{2,1},{3,0},{4,7},{5,6},{6,5},{7,4},{8,11},{9,10},{10,... | collective-permute-start | bytes 393224 | tf_op jit(solution)/shard_map/ppermute | solution.py:221
  15.7 5.6 %collective-permute-start.8 = (bf16[64,128]{1,0:T(8,128)(2,1)S(1)}, bf16[64,128]{1,0:T(8,128)(2,1)S(1)}, u32[]{:S(2)}, u32[]{:S(2)}) collective-permute-start(bf16[64,128]{1,0:T(8,128)(2,1)S(1)} %get-tuple-element.41), channel_id=1, source_target_pairs={{0,30},{2,24},{4,26},{6,28},{8,22},{10,16},{12,18},{14,20},{16,14}... | collective-permute-start | bytes 49160 | tf_op jit(solution)/shard_map/ppermute | solution.py:233
  18.1 4.1 %collective-permute-start.10 = (bf16[64,128]{1,0:T(8,128)(2,1)S(1)}, bf16[64,128]{1,0:T(8,128)(2,1)S(1)}, u32[]{:S(2)}, u32[]{:S(2)}) collective-permute-start(bf16[64,128]{1,0:T(8,128)(2,1)S(1)} %get-tuple-element.45), channel_id=1, source_target_pairs={{0,22},{2,16},{4,18},{6,20},{8,30},{10,24},{12,26},{14,28},{16,6},... | collective-permute-start | bytes 49160 | tf_op jit(solution)/shard_map/ppermute | solution.py:233
  18.7 3.5 %collective-permute-start.11 = (bf16[64,128]{1,0:T(8,128)(2,1)S(1)}, bf16[64,128]{1,0:T(8,128)(2,1)S(1)}, u32[]{:S(2)}, u32[]{:S(2)}) collective-permute-start(bf16[64,128]{1,0:T(8,128)(2,1)S(1)} %get-tuple-element.46), channel_id=1, source_target_pairs={{0,14},{2,4},{4,10},{6,0},{8,6},{10,12},{12,2},{14,8},{16,30},{18,... | collective-permute-start | bytes 49160 | tf_op jit(solution)/shard_map/ppermute | solution.py:233
  20.4 2.0 %collective-permute-start.12 = (bf16[64,128]{1,0:T(8,128)(2,1)S(1)}, bf16[64,128]{1,0:T(8,128)(2,1)S(1)}, u32[]{:S(2)}, u32[]{:S(2)}) collective-permute-start(bf16[64,128]{1,0:T(8,128)(2,1)S(1)} %get-tuple-element.47), channel_id=1, source_target_pairs={{0,10},{2,0},{4,14},{6,4},{8,2},{10,8},{12,6},{14,12},{16,26},{18,... | collective-permute-start | bytes 49160 | tf_op jit(solution)/shard_map/ppermute | solution.py:233
  21.3 4.1 %copy-start = (bf16[1,256,8,128]{3,2,1,0:T(8,128)(2,1)S(1)}, bf16[1,256,8,128]{3,2,1,0:T(8,128)(2,1)}, u32[]{:S(2)}) copy-start(bf16[1,256,8,128]{3,2,1,0:T(8,128)(2,1)} %param.6) | copy-start | bytes 1572868
  22.5 1.3 %collective-permute-start.13 = (bf16[4,64,128]{2,1,0:T(8,128)(2,1)S(1)}, bf16[4,64,128]{2,1,0:T(8,128)(2,1)S(1)}, u32[]{:S(2)}, u32[]{:S(2)}) collective-permute-start(bf16[4,64,128]{2,1,0:T(8,128)(2,1)S(1)} %pack.1.own), channel_id=1, source_target_pairs={{0,2},{2,0},{4,6},{6,4},{8,10},{10,8},{12,14},{14,12},{16,18},{18,... | collective-permute-start | bytes 196616 | tf_op jit(solution)/shard_map/ppermute | solution.py:215
  24.1 1.6 %copy-start.2 = (f32[1,256,128]{2,1,0:T(8,128)S(1)}, f32[1,256,128]{2,1,0:T(8,128)}, u32[]{:S(2)}) copy-start(f32[1,256,128]{2,1,0:T(8,128)} %param.9) | copy-start | bytes 393220
  24.1 4.1 %collective-permute-start.14 = (bf16[256,128]{1,0:T(8,128)(2,1)S(1)}, bf16[256,128]{1,0:T(8,128)(2,1)S(1)}, u32[]{:S(2)}, u32[]{:S(2)}) collective-permute-start(bf16[256,128]{1,0:T(8,128)(2,1)S(1)} %get-tuple-element.48), channel_id=1, source_target_pairs={{0,3},{1,2},{2,1},{3,0},{4,7},{5,6},{6,5},{7,4},{8,11},{9,10},{10,... | collective-permute-start | bytes 196616 | tf_op jit(solution)/shard_map/ppermute | solution.py:221

commit v13 on v10

--- a/solution.py
+++ b/solution.py
@@ -14,6 +14,7 @@
 VMEM_LIMIT = 32 * 1024 * 1024
 FIRST_LIMIT = 55050 * 1024
 PIECES = 4
+HIDE = 256
 F32 = jnp.float32
 BF16 = jnp.bfloat16
 
@@ -150,13 +151,17 @@
     gradient[...] = times_transposed(factors[...], left[...]).astype(BF16)
 
 
+def step_kernel(factors, left, start, estimate):
+    estimate[...] = start[...] - STEP_SIZE * times_transposed(factors[...], left[...])
+
+
 def thin_out(values):
     return values - jnp.clip(values, -LEVEL, LEVEL)
 
 
-def pair_kernel(here, there, gradient, total, difference):
+def pair_kernel(factors, left, here, there, total, difference):
     scale = 1.0 / math.sqrt(2)
-    estimate = here[...] - STEP_SIZE * gradient[...].astype(F32)
+    estimate = here[...] - STEP_SIZE * times_transposed(factors[...], left[...])
     total[...] = (estimate + there[...]) * scale
     difference[...] = (estimate - there[...]) * scale
 
@@ -168,12 +173,10 @@
 
 
 def shrink_kernel(band, *refs):
-    tables, starts, gradients, out = refs[: -2 * band - 1], refs[-2 * band - 1 : -band - 1], refs[-band - 1 : -1], refs[-1]
-    estimates = [
-        start[...] - STEP_SIZE * gradient[...].astype(F32) for start, gradient in zip(starts, gradients)
-    ]
+    tables, own, starts, gradients, out = refs[0], refs[1], refs[2 : band + 1], refs[band + 1 : -1], refs[-1]
+    others = [start[...] - STEP_SIZE * gradient[...].astype(F32) for start, gradient in zip(starts, gradients)]
+    estimates = [own[...], *others]
     scale = 1.0 / math.sqrt(band)
-    (tables,) = tables
     half = out.shape[1] // 2
     lane = lax.broadcasted_iota(jnp.int32, (1, out.shape[1]), 1)
     turn = jnp.where(lane < half, -1.0, 1.0).astype(F32)
@@ -190,7 +193,7 @@
 
 def call(kernel, name, outs, inputs, scratch=(), flops=0, spaces=(), limit=VMEM_LIMIT):
     spaces = (*spaces, *[pltpu.VMEM] * (len(inputs) - len(spaces)))
-    moved = sum(x.size * x.dtype.itemsize for x in [*inputs, *outs])
+    moved = sum(x.size * x.dtype.itemsize for x in [*inputs, *outs]) if flops else 0
     return pl.pallas_call(
         kernel,
         out_shape=outs,
@@ -207,6 +210,12 @@
     return lax.ppermute(value, "tile", [(i, i ^ 1) for i in range(lax.axis_size("tile"))])
 
 
+def across(value, shift):
+    count, band = lax.axis_size("tile"), lax.axis_size("freq")
+    pairs = [(i * band + f, (i ^ 1) * band + (f - shift) % band) for i in range(count) for f in range(band)]
+    return lax.ppermute(value, ("tile", "freq"), pairs)
+
+
 def after(value, *others):
     return lax.optimization_barrier((value, *others))[0]
 
@@ -239,7 +248,7 @@
     block = shape(sources // 2, width)
     blocks = shape(members, sources // 2, width)
     chosen = shape(rows, members * width)
-    spread = pltpu.VMEM((sources, columns), BF16)
+    factor = shape(rows, columns)
     flops = 2 * rows * columns * sources
 
     keep, give = call(
@@ -259,19 +268,16 @@
         [pltpu.HBM] * 2,
         FIRST_LIMIT,
     )
-    sends = call(add_kernel, "add", [block] * members, [keep, to_mate(give)])
-    left_rows = after(left_rows, sends[0])
+    sends = call(add_kernel, "add", [block] * members, [keep, to_mate(give)], flops=HIDE * flops)
+    mate_left = to_mate(after(left_rows, give))
     own_left, mate_left, turned, start = call(
         functools.partial(rows_kernel, shifts),
         "rows",
         [chosen, chosen, shape(sources, rows, dtype=F32), shape(rows, sources, dtype=F32)],
-        [ranks, left_rows, to_mate(left_rows), after(observed, give), after(start, give)],
+        [ranks, after(left_rows, give), mate_left, after(observed, give), after(start, give)],
         [wide],
         spaces=[pltpu.SMEM],
     )
-    starts = [start]
-    for shift in range(1, band):
-        starts.append(lax.ppermute(start, "freq", [(f, (f - shift) % band) for f in range(band)]))
     (misfit,) = call(
         image_kernel,
         "image",
@@ -280,38 +286,47 @@
         [pltpu.VMEM((sources, members * width), BF16)],
         flops,
     )
+    starts = [start]
+    for shift in range(1, band):
+        starts.append(lax.ppermute(start, "freq", [(f, (f - shift) % band) for f in range(band)]))
+    mate_right = to_mate(after(right_rows, misfit))
+    (mate_right,) = call(columns_kernel, "columns", [factor], [mate_right], [wide])
     sends = call(
         back_kernel,
         "back",
         [block] * members,
         [misfit, to_mate(misfit), own_left, mate_left],
         [pltpu.VMEM((2, sources, members * width), F32)],
-        flops,
-    )
-    (right,) = call(columns_kernel, "columns", [shape(rows, columns)], [after(right_rows, sends[0])], [wide])
-    (own,) = call(pack_kernel, "pack", [blocks], exchange(sends, shifts[::-1], [right, *starts[1:]]))
-    (gradient,) = call(
+        HIDE * flops,
+    )
+    (own,) = call(pack_kernel, "pack", [blocks], exchange(sends, shifts[::-1], [mate_right, *starts[1:]]))
+    gradient, left = call(
         functools.partial(gradient_kernel, shifts),
         "gradient",
-        [shape(rows, sources)],
-        [own, to_mate(own), right],
-        [spread],
-        flops,
-    )
-    gradients = [gradient]
+        [shape(rows, sources), shape(sources, columns)],
+        [own, to_mate(own), mate_right],
+        flops=flops,
+    )
+    (right,) = call(columns_kernel, "columns", [factor], [after(right_rows, gradient)], [wide])
+    gradients = []
     for shift in range(1, band):
-        gradients.append(lax.ppermute(gradient, "freq", [(f, (f - shift) % band) for f in range(band)]))
+        gradients.append(across(gradient, shift))
     result = shape(rows, sources, dtype=F32)
     if band == 2:
-        halves = call(pair_kernel, "pair", [result] * 2, [*starts, gradient])
-        (estimate,) = call(shrink_pair_kernel, "shrink", [result], [*halves, gradients[1]])
+        halves = call(pair_kernel, "pair", [result] * 2, [right, left, *starts], flops=flops)
+        (estimate,) = call(shrink_pair_kernel, "shrink", [result], [*halves, *gradients])
         return estimate[None]
     bands = jnp.arange(band, dtype=jnp.int32)
     phases = (bands[:, None] + lax.axis_index("freq")) * bands[None, :] % band
     phases = (2.0 * math.pi / band) * phases.astype(F32)
     tables = jnp.stack([jnp.cos(phases), jnp.sin(phases)])
+    (estimate,) = call(step_kernel, "step", [result], [right, left, start], flops=flops)
     (estimate,) = call(
-        functools.partial(shrink_kernel, band), "shrink", [result], [tables, *starts, *gradients], spaces=[pltpu.SMEM]
+        functools.partial(shrink_kernel, band),
+        "shrink",
+        [result],
+        [tables, estimate, *starts[1:], *gradients],
+        spaces=[pltpu.SMEM],
     )
     return estimate[None]
 

time: 29.6 us -> 29.3 us (0.990)
  waiting for transfers between devices: 8.09 us -> 7.36 us
  Pallas kernels: 4.91 us -> 5.46 us
    ppermute x1, waiting for transfers between devices: 2.89 us -> 2.32 us  [across(): return lax.ppermute(value, ('tile', 'freq'), pairs)]
    pallas_call x10 -> x11, Pallas kernels: 4.91 us -> 5.46 us  [call(): pl.pallas_call(kernel, out_shape=outs, in_specs=[pl.BlockSpec(memory_spac...]
    ppermute x1, starting transfers between devices: 1.5 us -> 1.09 us  [across(): return lax.ppermute(value, ('tile', 'freq'), pairs)]
    ppermute x4 -> x5, starting transfers between devices: 1.63 us -> 1.84 us  [to_mate(): lax.ppermute(value, 'tile', [(i, i ^ 1) for i in range(lax.axis_size('til...]
    ppermute x4 -> x5, waiting for transfers between devices: 1.81 us -> 1.72 us  [to_mate(): lax.ppermute(value, 'tile', [(i, i ^ 1) for i in range(lax.axis_size('til...]
  transfers between devices with their start and end apart: 14 -> 15, of which waited for: 6 -> 6; matrix products, arithmetic and copies ran while one was open for 0% -> 0% of each run, Pallas kernels for 6% -> 8%
where the time goes in v13:
time: 29.3 us; the launch traced here: 29.2 us
  starting transfers between devices  16.2 us (55%)
  waiting for transfers between devices  7.36 us (25%)
  Pallas kernels  5.46 us (19%)
    ppermute x8, starting transfers between devices, exchange(): arrived.append(lax.ppermute(send, 'tile', pairs))  11.8 us
    pallas_call x11, Pallas kernels, call(): pl.pallas_call(kernel, out_shape=outs, in_specs=[pl.BlockSpec(memory_spac...  5.46 us
    ppermute x8, waiting for transfers between devices, exchange(): arrived.append(lax.ppermute(send, 'tile', pairs))  3.32 us
    ppermute x1, waiting for transfers between devices, across(): return lax.ppermute(value, ('tile', 'freq'), pairs)  2.32 us
    ppermute x5, starting transfers between devices, to_mate(): lax.ppermute(value, 'tile', [(i, i ^ 1) for i in range(lax.axis_size('til...  1.84 us
    ppermute x5, waiting for transfers between devices, to_mate(): lax.ppermute(value, 'tile', [(i, i ^ 1) for i in range(lax.axis_size('til...  1.72 us
    ppermute x1, starting transfers between devices, body(): lax.ppermute(start, 'freq', [(f, (f - shift) % band) for f in range(band)])  1.52 us
    ppermute x1, starting transfers between devices, across(): return lax.ppermute(value, ('tile', 'freq'), pairs)  1.09 us
  transfers between devices with their start and end apart: 15, of which 6 were waited for; matrix products, arithmetic and copies ran while one was open for 0% of the time, Pallas kernels for 8%

profile of v13, /device:TPU:0, one launch (start us, length us, event | category | flops | bytes accessed | tf_op | source)
XLA Modules:
  0.0 29.2 jit_solution(11975857454958568765)
XLA Ops:
  0.0 1.7 %forward.1 = (bf16[4,64,128]{2,1,0:T(8,128)(2,1)S(1)}, bf16[4,64,128]{2,1,0:T(8,128)(2,1)S(1)}) custom-call(f32[256,128]{1,0:T(8,128)} %bitcast.8, bf16[2048,128]{1,0:T(8,128)(2,1)} %bitcast.5), custom_call_target="tpu_custom_call" | custom-call | flops 67108864 | bytes 786432 | tf_op jit(solution)/shard_map/forward/pallas_call | solution.py:197
  1.7 0.5 %collective-permute-start = (bf16[4,64,128]{2,1,0:T(8,128)(2,1)S(1)}, bf16[4,64,128]{2,1,0:T(8,128)(2,1)S(1)}, u32[]{:S(2)}, u32[]{:S(2)}) collective-permute-start(bf16[4,64,128]{2,1,0:T(8,128)(2,1)S(1)} %get-tuple-element.31), channel_id=1, source_target_pairs={{0,2},{2,0},{4,6},{6,4},{8,10},{10,8},{12,14},{14,12},{16,18},{18,... | collective-permute-start | bytes 196616 | tf_op jit(solution)/shard_map/ppermute | solution.py:210
  2.3 0.1 collective-permute-start.2
  2.4 0.8 %collective-permute-done.arrived = bf16[4,64,128]{2,1,0:T(8,128)(2,1)S(1)} collective-permute-done((bf16[4,64,128]{2,1,0:T(8,128)(2,1)S(1)}, bf16[4,64,128]{2,1,0:T(8,128)(2,1)S(1)}, u32[]{:S(2)}, u32[]{:S(2)}) %collective-permute-start) | collective-permute-done | bytes 65568 | tf_op jit(solution)/shard_map/ppermute | solution.py:210
  3.2 0.0 copy-start.4
  3.2 4.8 %collective-permute-start.1 = (bf16[64,128]{1,0:T(8,128)(2,1)S(1)}, bf16[64,128]{1,0:T(8,128)(2,1)S(1)}, u32[]{:S(2)}, u32[]{:S(2)}) collective-permute-start(bf16[64,128]{1,0:T(8,128)(2,1)S(1)} %get-tuple-element.32), channel_id=1, source_target_pairs={{0,26},{2,28},{4,30},{6,24},{8,18},{10,20},{12,22},{14,16},{16,10}... | collective-permute-start | bytes 49160 | tf_op jit(solution)/shard_map/ppermute | solution.py:228
  8.0 0.3 %collective-permute-start.3 = (bf16[64,128]{1,0:T(8,128)(2,1)S(1)}, bf16[64,128]{1,0:T(8,128)(2,1)S(1)}, u32[]{:S(2)}, u32[]{:S(2)}) collective-permute-start(bf16[64,128]{1,0:T(8,128)(2,1)S(1)} %get-tuple-element.40), channel_id=1, source_target_pairs={{0,18},{2,20},{4,22},{6,16},{8,26},{10,28},{12,30},{14,24},{16,2},... | collective-permute-start | bytes 49160 | tf_op jit(solution)/shard_map/ppermute | solution.py:228
  8.3 1.1 %collective-permute-start.4 = (bf16[64,128]{1,0:T(8,128)(2,1)S(1)}, bf16[64,128]{1,0:T(8,128)(2,1)S(1)}, u32[]{:S(2)}, u32[]{:S(2)}) collective-permute-start(bf16[64,128]{1,0:T(8,128)(2,1)S(1)} %get-tuple-element.41), channel_id=1, source_target_pairs={{0,6},{2,12},{4,2},{6,8},{8,14},{10,4},{12,10},{14,0},{16,22},{18,... | collective-permute-start | bytes 49160 | tf_op jit(solution)/shard_map/ppermute | solution.py:228
  9.4 0.2 collective-permute-start.5
  9.7 1.1 %rows.1 = (bf16[256,512]{1,0:T(8,128)(2,1)S(1)}, bf16[256,512]{1,0:T(8,128)(2,1)S(1)}, f32[128,256]{1,0:T(8,128)S(1)}, f32[256,128]{1,0:T(8,128)S(1)}) custom-call(s32[1,8,8]{2,1,0:T(8,128)S(1)} %copy-done.4, bf16[2048,128]{1,0:T(8,128)(2,1)S(1)} %bitcast.11, bf16[2048,128]{1,0:T(8,128)(2,1)S(1)} %collective-permute-done.2.mate, f32[256,128]{1,0:T(8,128)S(1)} %bitcast.12, ...), custom_call_target="tpu_custom_call" | custom-call | tf_op jit(solution)/shard_map/rows/pallas_call | solution.py:197
  10.7 0.0 copy-start
  10.8 2.2 %collective-permute-done.3.refs_1_ = bf16[64,128]{1,0:T(8,128)(2,1)S(1)} collective-permute-done((bf16[64,128]{1,0:T(8,128)(2,1)S(1)}, bf16[64,128]{1,0:T(8,128)(2,1)S(1)}, u32[]{:S(2)}, u32[]{:S(2)}) %collective-permute-start.3) | collective-permute-done | bytes 16416 | tf_op jit(solution)/shard_map/ppermute | solution.py:228
  12.9 0.0 collective-permute-done.4.refs_2_
  12.9 0.3 %image.1.here = f32[2,128,256]{2,1,0:T(8,128)S(1)} custom-call(bf16[64,128]{1,0:T(8,128)(2,1)S(1)} %collective-permute-done.1.refs_0_, bf16[64,128]{1,0:T(8,128)(2,1)S(1)} %collective-permute-done.3.refs_1_, bf16[64,128]{1,0:T(8,128)(2,1)S(1)} %collective-permute-done.4.refs_2_, bf16[64,128]{1,0:T(8,128)(2,1)S(1)} %collective-permute-done.5.refs_3_, ...), custom_call_target="tpu_custom_call" | custom-call | flops 67108864 | bytes 983040 | tf_op jit(solution)/shard_map/image/pallas_call | solution.py:197
  13.3 0.4 %collective-permute-start.6 = (f32[2,128,256]{2,1,0:T(8,128)S(1)}, f32[2,128,256]{2,1,0:T(8,128)S(1)}, u32[]{:S(2)}, u32[]{:S(2)}) collective-permute-start(f32[2,128,256]{2,1,0:T(8,128)S(1)} %image.1.here), channel_id=1, source_target_pairs={{0,2},{2,0},{4,6},{6,4},{8,10},{10,8},{12,14},{14,12},{16,18},{18,... | collective-permute-start | bytes 786440 | tf_op jit(solution)/shard_map/ppermute | solution.py:210
  13.7 1.5 %collective-permute-start.9 = (f32[256,128]{1,0:T(8,128)S(1)}, f32[256,128]{1,0:T(8,128)S(1)}, u32[]{:S(2)}, u32[]{:S(2)}) collective-permute-start(f32[256,128]{1,0:T(8,128)S(1)} %get-tuple-element.45.here), channel_id=1, source_target_pairs={{0,1},{1,0},{2,3},{3,2},{4,5},{5,4},{6,7},{7,6},{8,9},{9,8},{10,11... | collective-permute-start | bytes 393224 | tf_op jit(solution)/shard_map/ppermute | solution.py:291
  15.2 0.3 %back.1 = (bf16[64,128]{1,0:T(8,128)(2,1)S(1)}, bf16[64,128]{1,0:T(8,128)(2,1)S(1)}, bf16[64,128]{1,0:T(8,128)(2,1)S(1)}, bf16[64,128]{1,0:T(8,128)(2,1)S(1)}) custom-call(f32[2,128,256]{2,1,0:T(8,128)S(1)} %image.1.here, f32[2,128,256]{2,1,0:T(8,128)S(1)} %collective-permute-done.6.there, bf16[256,512]{1,0:T(8,128)(2,1)S(1)} %get-tuple-element.36.refs_4_.own, ...), custom_call_target="tpu_custom_call" | custom-call | flops 17179869184 | bytes 1114112 | tf_op jit(solution)/shard_map/back/pallas_call | solution.py:197
  15.6 2.6 %collective-permute-start.7 = (bf16[64,128]{1,0:T(8,128)(2,1)S(1)}, bf16[64,128]{1,0:T(8,128)(2,1)S(1)}, u32[]{:S(2)}, u32[]{:S(2)}) collective-permute-start(bf16[64,128]{1,0:T(8,128)(2,1)S(1)} %get-tuple-element.43), channel_id=1, source_target_pairs={{0,30},{2,24},{4,26},{6,28},{8,22},{10,16},{12,18},{14,20},{16,14}... | collective-permute-start | bytes 49160 | tf_op jit(solution)/shard_map/ppermute | solution.py:228
  18.2 0.6 %collective-permute-start.10 = (bf16[64,128]{1,0:T(8,128)(2,1)S(1)}, bf16[64,128]{1,0:T(8,128)(2,1)S(1)}, u32[]{:S(2)}, u32[]{:S(2)}) collective-permute-start(bf16[64,128]{1,0:T(8,128)(2,1)S(1)} %get-tuple-element.47), channel_id=1, source_target_pairs={{0,22},{2,16},{4,18},{6,20},{8,30},{10,24},{12,26},{14,28},{16,6},... | collective-permute-start | bytes 49160 | tf_op jit(solution)/shard_map/ppermute | solution.py:228
  18.7 2.0 %collective-permute-start.11 = (bf16[64,128]{1,0:T(8,128)(2,1)S(1)}, bf16[64,128]{1,0:T(8,128)(2,1)S(1)}, u32[]{:S(2)}, u32[]{:S(2)}) collective-permute-start(bf16[64,128]{1,0:T(8,128)(2,1)S(1)} %get-tuple-element.48), channel_id=1, source_target_pairs={{0,14},{2,4},{4,10},{6,0},{8,6},{10,12},{12,2},{14,8},{16,30},{18,... | collective-permute-start | bytes 49160 | tf_op jit(solution)/shard_map/ppermute | solution.py:228
  20.8 0.2 collective-permute-start.12
  20.9 0.3 columns.2.factors
  21.2 1.0 %collective-permute-done.10.refs_1_ = bf16[64,128]{1,0:T(8,128)(2,1)S(1)} collective-permute-done((bf16[64,128]{1,0:T(8,128)(2,1)S(1)}, bf16[64,128]{1,0:T(8,128)(2,1)S(1)}, u32[]{:S(2)}, u32[]{:S(2)}) %collective-permute-start.10) | collective-permute-done | bytes 16416 | tf_op jit(solution)/shard_map/ppermute | solution.py:228
  22.3 0.1 collective-permute-done.12.refs_3_
  22.4 0.8 %collective-permute-start.13 = (bf16[4,64,128]{2,1,0:T(8,128)(2,1)S(1)}, bf16[4,64,128]{2,1,0:T(8,128)(2,1)S(1)}, u32[]{:S(2)}, u32[]{:S(2)}) collective-permute-start(bf16[4,64,128]{2,1,0:T(8,128)(2,1)S(1)} %pack.1.own), channel_id=1, source_target_pairs={{0,2},{2,0},{4,6},{6,4},{8,10},{10,8},{12,14},{14,12},{16,18},{18,... | collective-permute-start | bytes 196616 | tf_op jit(solution)/shard_map/ppermute | solution.py:210
  23.2 0.9 %collective-permute-done.13.mate = bf16[4,64,128]{2,1,0:T(8,128)(2,1)S(1)} collective-permute-done((bf16[4,64,128]{2,1,0:T(8,128)(2,1)S(1)}, bf16[4,64,128]{2,1,0:T(8,128)(2,1)S(1)}, u32[]{:S(2)}, u32[]{:S(2)}) %collective-permute-start.13) | collective-permute-done | bytes 65568 | tf_op jit(solution)/shard_map/ppermute | solution.py:210
  24.1 0.4 %gradient.1 = (bf16[256,128]{1,0:T(8,128)(2,1)S(1)}, bf16[128,1024]{1,0:T(8,128)(2,1)S(1)}) custom-call(bf16[4,64,128]{2,1,0:T(8,128)(2,1)S(1)} %pack.1.own, bf16[4,64,128]{2,1,0:T(8,128)(2,1)S(1)} %collective-permute-done.13.mate, bf16[256,1024]{1,0:T(8,128)(2,1)S(1)} %columns.2.factors), custom_call_target="tpu_custom_call" | custom-call | flops 67108864 | bytes 983040 | tf_op jit(solution)/shard_map/gradient/pallas_call | solution.py:197
  24.5 1.1 %collective-permute-start.14 = (bf16[256,128]{1,0:T(8,128)(2,1)S(1)}, bf16[256,128]{1,0:T(8,128)(2,1)S(1)}, u32[]{:S(2)}, u32[]{:S(2)}) collective-permute-start(bf16[256,128]{1,0:T(8,128)(2,1)S(1)} %get-tuple-element.50), channel_id=1, source_target_pairs={{0,3},{1,2},{2,1},{3,0},{4,7},{5,6},{6,5},{7,4},{8,11},{9,10},{10,... | collective-permute-start | bytes 196616 | tf_op jit(solution)/shard_map/ppermute | solution.py:216
  25.6 0.3 columns.3.factors
  25.9 0.3 %pair.1 = (f32[256,128]{1,0:T(8,128)S(1)}, f32[256,128]{1,0:T(8,128)S(1)}) custom-call(bf16[256,1024]{1,0:T(8,128)(2,1)S(1)} %columns.3.factors, bf16[128,1024]{1,0:T(8,128)(2,1)S(1)} %get-tuple-element.52.left, f32[256,128]{1,0:T(8,128)S(1)} %get-tuple-element.45.here, f32[256,128]{1,0:T(8,128)S(1)} %collective-permute-done.9.there), custom_call_target="tpu_custom_call" | custom-call | flops 67108864 | bytes 1310720 | tf_op jit(solution)/shard_map/pair/pallas_call | solution.py:197
  26.2 2.3 %collective-permute-done.14.gradient = bf16[256,128]{1,0:T(8,128)(2,1)S(1)} collective-permute-done((bf16[256,128]{1,0:T(8,128)(2,1)S(1)}, bf16[256,128]{1,0:T(8,128)(2,1)S(1)}, u32[]{:S(2)}, u32[]{:S(2)}) %collective-permute-start.14) | collective-permute-done | bytes 65568 | tf_op jit(solution)/shard_map/ppermute | solution.py:216
  28.5 0.7 %shrink.1 = f32[256,128]{1,0:T(8,128)} custom-call(f32[256,128]{1,0:T(8,128)S(1)} %get-tuple-element.53.total, f32[256,128]{1,0:T(8,128)S(1)} %get-tuple-element.54.difference, bf16[256,128]{1,0:T(8,128)(2,1)S(1)} %collective-permute-done.14.gradient), custom_call_target="tpu_custom_call" | custom-call | tf_op jit(solution)/shard_map/shrink/pallas_call | solution.py:197
  (19 shorter events, 0.1 us)
Async XLA Ops:
  0.0 2.3 %copy-start.2 = (bf16[1,256,8,128]{3,2,1,0:T(8,128)(2,1)S(1)}, bf16[1,256,8,128]{3,2,1,0:T(8,128)(2,1)}, u32[]{:S(2)}) copy-start(bf16[1,256,8,128]{3,2,1,0:T(8,128)(2,1)} %param.5) | copy-start | bytes 1572868
  1.7 1.4 %collective-permute-start = (bf16[4,64,128]{2,1,0:T(8,128)(2,1)S(1)}, bf16[4,64,128]{2,1,0:T(8,128)(2,1)S(1)}, u32[]{:S(2)}, u32[]{:S(2)}) collective-permute-start(bf16[4,64,128]{2,1,0:T(8,128)(2,1)S(1)} %get-tuple-element.31), channel_id=1, source_target_pairs={{0,2},{2,0},{4,6},{6,4},{8,10},{10,8},{12,14},{14,12},{16,18},{18,... | collective-permute-start | bytes 196616 | tf_op jit(solution)/shard_map/ppermute | solution.py:210
  2.3 7.4 %collective-permute-start.2 = (bf16[2048,128]{1,0:T(8,128)(2,1)S(1)}, bf16[2048,128]{1,0:T(8,128)(2,1)S(1)}, u32[]{:S(2)}, u32[]{:S(2)}) collective-permute-start(bf16[2048,128]{1,0:T(8,128)(2,1)S(1)} %bitcast.10), channel_id=1, source_target_pairs={{0,2},{2,0},{4,6},{6,4},{8,10},{10,8},{12,14},{14,12},{16,18},{18,... | collective-permute-start | bytes 1572872 | tf_op jit(solution)/shard_map/ppermute | solution.py:210
  3.2 6.5 %copy-start.1 = (f32[1,256,128]{2,1,0:T(8,128)S(1)}, f32[1,256,128]{2,1,0:T(8,128)}, u32[]{:S(2)}) copy-start(f32[1,256,128]{2,1,0:T(8,128)} %param.9) | copy-start | bytes 393220
  3.2 6.5 %copy-start.3 = (f32[1,256,128]{2,1,0:T(8,128)S(1)}, f32[1,256,128]{2,1,0:T(8,128)}, u32[]{:S(2)}) copy-start(f32[1,256,128]{2,1,0:T(8,128)} %param.8) | copy-start | bytes 393220
  3.2 6.5 %copy-start.4 = (s32[1,8,8]{2,1,0:T(8,128)S(1)}, s32[1,8,8]{2,1,0:T(8,128)}, u32[]{:S(2)}) copy-start(s32[1,8,8]{2,1,0:T(8,128)} %ranks.1) | copy-start | bytes 772
  3.2 7.6 %collective-permute-start.1 = (bf16[64,128]{1,0:T(8,128)(2,1)S(1)}, bf16[64,128]{1,0:T(8,128)(2,1)S(1)}, u32[]{:S(2)}, u32[]{:S(2)}) collective-permute-start(bf16[64,128]{1,0:T(8,128)(2,1)S(1)} %get-tuple-element.32), channel_id=1, source_target_pairs={{0,26},{2,28},{4,30},{6,24},{8,18},{10,20},{12,22},{14,16},{16,10}... | collective-permute-start | bytes 49160 | tf_op jit(solution)/shard_map/ppermute | solution.py:228
  8.0 5.0 %collective-permute-start.3 = (bf16[64,128]{1,0:T(8,128)(2,1)S(1)}, bf16[64,128]{1,0:T(8,128)(2,1)S(1)}, u32[]{:S(2)}, u32[]{:S(2)}) collective-permute-start(bf16[64,128]{1,0:T(8,128)(2,1)S(1)} %get-tuple-element.40), channel_id=1, source_target_pairs={{0,18},{2,20},{4,22},{6,16},{8,26},{10,28},{12,30},{14,24},{16,2},... | collective-permute-start | bytes 49160 | tf_op jit(solution)/shard_map/ppermute | solution.py:228
  8.3 4.6 %collective-permute-start.4 = (bf16[64,128]{1,0:T(8,128)(2,1)S(1)}, bf16[64,128]{1,0:T(8,128)(2,1)S(1)}, u32[]{:S(2)}, u32[]{:S(2)}) collective-permute-start(bf16[64,128]{1,0:T(8,128)(2,1)S(1)} %get-tuple-element.41), channel_id=1, source_target_pairs={{0,6},{2,12},{4,2},{6,8},{8,14},{10,4},{12,10},{14,0},{16,22},{18,... | collective-permute-start | bytes 49160 | tf_op jit(solution)/shard_map/ppermute | solution.py:228
  9.4 3.5 %collective-permute-start.5 = (bf16[64,128]{1,0:T(8,128)(2,1)S(1)}, bf16[64,128]{1,0:T(8,128)(2,1)S(1)}, u32[]{:S(2)}, u32[]{:S(2)}) collective-permute-start(bf16[64,128]{1,0:T(8,128)(2,1)S(1)} %get-tuple-element.42), channel_id=1, source_target_pairs={{0,2},{2,8},{4,6},{6,12},{8,10},{10,0},{12,14},{14,4},{16,18},{18,... | collective-permute-start | bytes 49160 | tf_op jit(solution)/shard_map/ppermute | solution.py:228
  10.7 4.5 %copy-start = (bf16[1,256,8,128]{3,2,1,0:T(8,128)(2,1)S(1)}, bf16[1,256,8,128]{3,2,1,0:T(8,128)(2,1)}, u32[]{:S(2)}) copy-start(bf16[1,256,8,128]{3,2,1,0:T(8,128)(2,1)} %param.6) | copy-start | bytes 1572868
  13.3 2.0 %collective-permute-start.6 = (f32[2,128,256]{2,1,0:T(8,128)S(1)}, f32[2,128,256]{2,1,0:T(8,128)S(1)}, u32[]{:S(2)}, u32[]{:S(2)}) collective-permute-start(f32[2,128,256]{2,1,0:T(8,128)S(1)} %image.1.here), channel_id=1, source_target_pairs={{0,2},{2,0},{4,6},{6,4},{8,10},{10,8},{12,14},{14,12},{16,18},{18,... | collective-permute-start | bytes 786440 | tf_op jit(solution)/shard_map/ppermute | solution.py:210
  13.7 7.5 %collective-permute-start.9 = (f32[256,128]{1,0:T(8,128)S(1)}, f32[256,128]{1,0:T(8,128)S(1)}, u32[]{:S(2)}, u32[]{:S(2)}) collective-permute-start(f32[256,128]{1,0:T(8,128)S(1)} %get-tuple-element.45.here), channel_id=1, source_target_pairs={{0,1},{1,0},{2,3},{3,2},{4,5},{5,4},{6,7},{7,6},{8,9},{9,8},{10,11... | collective-permute-start | bytes 393224 | tf_op jit(solution)/shard_map/ppermute | solution.py:291
  15.2 5.5 %collective-permute-start.8 = (bf16[2048,128]{1,0:T(8,128)(2,1)S(1)}, bf16[2048,128]{1,0:T(8,128)(2,1)S(1)}, u32[]{:S(2)}, u32[]{:S(2)}) collective-permute-start(bf16[2048,128]{1,0:T(8,128)(2,1)S(1)} %bitcast.6), channel_id=1, source_target_pairs={{0,2},{2,0},{4,6},{6,4},{8,10},{10,8},{12,14},{14,12},{16,18},{18,... | collective-permute-start | bytes 1572872 | tf_op jit(solution)/shard_map/ppermute | solution.py:210
  15.6 5.6 %collective-permute-start.7 = (bf16[64,128]{1,0:T(8,128)(2,1)S(1)}, bf16[64,128]{1,0:T(8,128)(2,1)S(1)}, u32[]{:S(2)}, u32[]{:S(2)}) collective-permute-start(bf16[64,128]{1,0:T(8,128)(2,1)S(1)} %get-tuple-element.43), channel_id=1, source_target_pairs={{0,30},{2,24},{4,26},{6,28},{8,22},{10,16},{12,18},{14,20},{16,14}... | collective-permute-start | bytes 49160 | tf_op jit(solution)/shard_map/ppermute | solution.py:228
  18.2 4.1 %collective-permute-start.10 = (bf16[64,128]{1,0:T(8,128)(2,1)S(1)}, bf16[64,128]{1,0:T(8,128)(2,1)S(1)}, u32[]{:S(2)}, u32[]{:S(2)}) collective-permute-start(bf16[64,128]{1,0:T(8,128)(2,1)S(1)} %get-tuple-element.47), channel_id=1, source_target_pairs={{0,22},{2,16},{4,18},{6,20},{8,30},{10,24},{12,26},{14,28},{16,6},... | collective-permute-start | bytes 49160 | tf_op jit(solution)/shard_map/ppermute | solution.py:228
  18.7 3.5 %collective-permute-start.11 = (bf16[64,128]{1,0:T(8,128)(2,1)S(1)}, bf16[64,128]{1,0:T(8,128)(2,1)S(1)}, u32[]{:S(2)}, u32[]{:S(2)}) collective-permute-start(bf16[64,128]{1,0:T(8,128)(2,1)S(1)} %get-tuple-element.48), channel_id=1, source_target_pairs={{0,14},{2,4},{4,10},{6,0},{8,6},{10,12},{12,2},{14,8},{16,30},{18,... | collective-permute-start | bytes 49160 | tf_op jit(solution)/shard_map/ppermute | solution.py:228
  20.8 1.6 %collective-permute-start.12 = (bf16[64,128]{1,0:T(8,128)(2,1)S(1)}, bf16[64,128]{1,0:T(8,128)(2,1)S(1)}, u32[]{:S(2)}, u32[]{:S(2)}) collective-permute-start(bf16[64,128]{1,0:T(8,128)(2,1)S(1)} %get-tuple-element.49), channel_id=1, source_target_pairs={{0,10},{2,0},{4,14},{6,4},{8,2},{10,8},{12,6},{14,12},{16,26},{18,... | collective-permute-start | bytes 49160 | tf_op jit(solution)/shard_map/ppermute | solution.py:228
  22.4 1.7 %collective-permute-start.13 = (bf16[4,64,128]{2,1,0:T(8,128)(2,1)S(1)}, bf16[4,64,128]{2,1,0:T(8,128)(2,1)S(1)}, u32[]{:S(2)}, u32[]{:S(2)}) collective-permute-start(bf16[4,64,128]{2,1,0:T(8,128)(2,1)S(1)} %pack.1.own), channel_id=1, source_target_pairs={{0,2},{2,0},{4,6},{6,4},{8,10},{10,8},{12,14},{14,12},{16,18},{18,... | collective-permute-start | bytes 196616 | tf_op jit(solution)/shard_map/ppermute | solution.py:210
  24.5 4.0 %collective-permute-start.14 = (bf16[256,128]{1,0:T(8,128)(2,1)S(1)}, bf16[256,128]{1,0:T(8,128)(2,1)S(1)}, u32[]{:S(2)}, u32[]{:S(2)}) collective-permute-start(bf16[256,128]{1,0:T(8,128)(2,1)S(1)} %get-tuple-element.50), channel_id=1, source_target_pairs={{0,3},{1,2},{2,1},{3,0},{4,7},{5,6},{6,5},{7,4},{8,11},{9,10},{10,... | collective-permute-start | bytes 196616 | tf_op jit(solution)/shard_map/ppermute | solution.py:216

commit v14 on v13

--- a/solution.py
+++ b/solution.py
@@ -48,15 +48,19 @@
     return jnp.where(lane < LANES // 2, 1.0, -1.0).astype(F32)
 
 
-def separate(source, wide, target, chosen, masks=None):
+def pick(wide, target, chosen, masks=None):
     rows = target.shape[0]
-    tiles = source.shape[0] // rows
-    wide[...] = source[...].astype(F32)
+    tiles = wide.shape[0] // rows
     for index, tile in enumerate(chosen):
         part = wide[pl.ds(tile, rows, stride=tiles), :]
         if masks is not None:
             part = jnp.where(masks[index], part, 0.0)
         target[:, index * LANES : (index + 1) * LANES] = part.astype(BF16)
+
+
+def separate(source, wide, target, chosen, masks=None):
+    wide[...] = source[...].astype(F32)
+    pick(wide, target, chosen, masks)
 
 
 def adjoint_block(product, tile):
@@ -106,37 +110,48 @@
         out[...] = (keep[index].astype(F32) + arrived[index].astype(F32)).astype(BF16)
 
 
-def rows_kernel(shifts, ranks, own, mate, observed, start, own_out, mate_out, turned, start_out, wide):
+def rows_kernel(shifts, ranks, own, mate, observed, start, both, turned, start_out, wide):
     chip, _ = place()
     _, chosen = both_shifts(shifts)
+    rows = both.shape[0] // 2
     lane = lax.broadcasted_iota(jnp.int32, (1, LANES), 1) % (LANES // 2)
     masks = [lane < ranks[0, chip, tile] for tile in chosen]
-    separate(own, wide, own_out, chosen, masks)
-    separate(mate, wide, mate_out, chosen, masks)
+    separate(own, wide, both.at[:rows], chosen, masks)
+    separate(mate, wide, both.at[rows:], chosen, masks)
     turned[...] = observed[...].T
     start_out[...] = start[...]
 
 
-def columns_kernel(factors, separated, wide):
-    separate(factors, wide, separated, range(separated.shape[1] // LANES))
+def columns_kernel(shifts, factors, own, other, wide):
+    chosen, rest = both_shifts(shifts)
+    separate(factors, wide, own, chosen)
+    pick(wide, other, rest)
+
+
+def early_kernel(first, second, factors, observed, misfit, left):
+    for index, block in enumerate((first, second)):
+        spread_block(block[...], left, index)
+    rows = observed.shape[1]
+    image = times_transposed(left[...], factors[:, : left.shape[1]])
+    misfit[:, :rows] = image[:, :rows] - observed[...]
+    misfit[:, rows:] = image[:, rows:]
 
 
 def image_kernel(*refs):
-    arrived, (own, mate, observed, misfit, left) = refs[:-5], refs[-5:]
-    for index, block in enumerate(arrived):
+    blocks, (early, factors, misfit, left) = refs[:-4], refs[-4:]
+    for index, block in enumerate(blocks):
         spread_block(block[...], left, index)
-    misfit[0] = times_transposed(left[...], own[...]) - observed[...]
-    misfit[1] = times_transposed(left[...], mate[...])
-
-
-def back_kernel(here, there, own, mate, *refs):
-    outs, products = refs[:-1], refs[-1]
-    for rows, factors in ((0, own), (1, mate)):
-        misfit = (here[rows] + there[1 - rows]).astype(BF16)
-        products[rows] = jnp.dot(misfit, factors[...], preferred_element_type=F32)
+    misfit[...] = early[...] + times_transposed(left[...], factors[:, -left.shape[1] :])
+
+
+def back_kernel(here, there, factors, *refs):
+    outs, (misfit, product) = refs[:-2], refs[-2:]
+    rows = here.shape[1] // 2
+    misfit[:, :rows] = (here[:, :rows] + there[:, rows:]).astype(BF16)
+    misfit[:, rows:] = (here[:, rows:] + there[:, :rows]).astype(BF16)
+    product[...] = jnp.dot(misfit[...], factors[...], preferred_element_type=F32)
     for index, out in enumerate(outs):
-        parts = [adjoint_block(products.at[rows], index).astype(F32) for rows in range(2)]
-        out[...] = (parts[0] + parts[1]).astype(BF16)
+        out[...] = adjoint_block(product, index)
 
 
 def pack_kernel(*refs):
@@ -144,26 +159,33 @@
         refs[-1][index] = block[...]
 
 
-def gradient_kernel(shifts, own, mate, factors, gradient, left):
-    for blocks, chosen in zip((own, mate), both_shifts(shifts)):
-        for index, tile in enumerate(chosen):
-            spread_block(blocks[index], left, tile)
-    gradient[...] = times_transposed(factors[...], left[...]).astype(BF16)
-
-
-def step_kernel(factors, left, start, estimate):
-    estimate[...] = start[...] - STEP_SIZE * times_transposed(factors[...], left[...])
+def part_kernel(blocks, factors, part, left):
+    for index in range(blocks.shape[0]):
+        spread_block(blocks[index], left, index)
+    part[...] = times_transposed(factors[...], left[...])
+
+
+def gradient_kernel(part, blocks, factors, gradient, left):
+    for index in range(blocks.shape[0]):
+        spread_block(blocks[index], left, index)
+    gradient[...] = (part[...] + times_transposed(factors[...], left[...])).astype(BF16)
+
+
+def step_kernel(own, other, own_left, other_left, start, estimate):
+    gradient = times_transposed(own[...], own_left[...]) + times_transposed(other[...], other_left[...])
+    estimate[...] = start[...] - STEP_SIZE * gradient
+
+
+def pair_kernel(own, other, own_left, other_left, here, there, total, difference):
+    scale = 1.0 / math.sqrt(2)
+    gradient = times_transposed(own[...], own_left[...]) + times_transposed(other[...], other_left[...])
+    estimate = here[...] - STEP_SIZE * gradient
+    total[...] = (estimate + there[...]) * scale
+    difference[...] = (estimate - there[...]) * scale
 
 
 def thin_out(values):
     return values - jnp.clip(values, -LEVEL, LEVEL)
-
-
-def pair_kernel(factors, left, here, there, total, difference):
-    scale = 1.0 / math.sqrt(2)
-    estimate = here[...] - STEP_SIZE * times_transposed(factors[...], left[...])
-    total[...] = (estimate + there[...]) * scale
-    difference[...] = (estimate - there[...]) * scale
 
 
 def shrink_pair_kernel(total, difference, gradient, out):
@@ -247,8 +269,7 @@
     wide = pltpu.VMEM((rows * tiles, width), F32)
     block = shape(sources // 2, width)
     blocks = shape(members, sources // 2, width)
-    chosen = shape(rows, members * width)
-    factor = shape(rows, columns)
+    factor = shape(rows, members * width)
     flops = 2 * rows * columns * sources
 
     keep, give = call(
@@ -270,57 +291,73 @@
     )
     sends = call(add_kernel, "add", [block] * members, [keep, to_mate(give)], flops=HIDE * flops)
     mate_left = to_mate(after(left_rows, give))
-    own_left, mate_left, turned, start = call(
+    both_left, turned, start = call(
         functools.partial(rows_kernel, shifts),
         "rows",
-        [chosen, chosen, shape(sources, rows, dtype=F32), shape(rows, sources, dtype=F32)],
+        [shape(2 * rows, members * width), shape(sources, rows, dtype=F32), shape(rows, sources, dtype=F32)],
         [ranks, after(left_rows, give), mate_left, after(observed, give), after(start, give)],
         [wide],
         spaces=[pltpu.SMEM],
     )
+    starts = [start]
+    for shift in range(1, band):
+        starts.append(lax.ppermute(start, "freq", [(f, (f - shift) % band) for f in range(band)]))
+    arrived = exchange(sends, shifts, [both_left, turned])
+    misfit = shape(sources, 2 * rows, dtype=F32)
+    (misfit_early,) = call(
+        early_kernel,
+        "early",
+        [misfit],
+        [*arrived[:2], both_left, turned],
+        [pltpu.VMEM((sources, 2 * width), BF16)],
+        flops // 2,
+    )
     (misfit,) = call(
         image_kernel,
         "image",
-        [shape(2, sources, rows, dtype=F32)],
-        [*exchange(sends, shifts, [own_left, mate_left, turned]), own_left, mate_left, turned],
-        [pltpu.VMEM((sources, members * width), BF16)],
-        flops,
-    )
-    starts = [start]
-    for shift in range(1, band):
-        starts.append(lax.ppermute(start, "freq", [(f, (f - shift) % band) for f in range(band)]))
+        [misfit],
+        [*arrived[2:], misfit_early, both_left],
+        [pltpu.VMEM((sources, (members - 2) * width), BF16)],
+        flops // 2,
+    )
     mate_right = to_mate(after(right_rows, misfit))
-    (mate_right,) = call(columns_kernel, "columns", [factor], [mate_right], [wide])
+    mate_right = call(functools.partial(columns_kernel, shifts), "columns", [factor] * 2, [mate_right], [wide])
     sends = call(
         back_kernel,
         "back",
         [block] * members,
-        [misfit, to_mate(misfit), own_left, mate_left],
-        [pltpu.VMEM((2, sources, members * width), F32)],
+        [misfit, to_mate(misfit), both_left],
+        [pltpu.VMEM((sources, 2 * rows), BF16), pltpu.VMEM((sources, members * width), F32)],
         HIDE * flops,
     )
-    (own,) = call(pack_kernel, "pack", [blocks], exchange(sends, shifts[::-1], [mate_right, *starts[1:]]))
-    gradient, left = call(
-        functools.partial(gradient_kernel, shifts),
+    (own,) = call(pack_kernel, "pack", [blocks], exchange(sends, shifts[::-1], [*mate_right, *starts[1:]]))
+    spread = shape(sources, members * width)
+    part, own_left = call(
+        part_kernel, "part", [shape(rows, sources, dtype=F32), spread], [own, mate_right[0]], flops=flops // 2
+    )
+    gradient, other_left = call(
+        gradient_kernel,
         "gradient",
-        [shape(rows, sources), shape(sources, columns)],
-        [own, to_mate(own), mate_right],
-        flops=flops,
-    )
-    (right,) = call(columns_kernel, "columns", [factor], [after(right_rows, gradient)], [wide])
+        [shape(rows, sources), spread],
+        [part, to_mate(own), mate_right[1]],
+        flops=flops // 2,
+    )
+    right = call(
+        functools.partial(columns_kernel, shifts), "columns", [factor] * 2, [after(right_rows, gradient)], [wide]
+    )
     gradients = []
     for shift in range(1, band):
         gradients.append(across(gradient, shift))
     result = shape(rows, sources, dtype=F32)
     if band == 2:
-        halves = call(pair_kernel, "pair", [result] * 2, [right, left, *starts], flops=flops)
+        halves = call(pair_kernel, "pair", [result] * 2, [*right, own_left, other_left, *starts], flops=flops)
         (estimate,) = call(shrink_pair_kernel, "shrink", [result], [*halves, *gradients])
         return estimate[None]
     bands = jnp.arange(band, dtype=jnp.int32)
     phases = (bands[:, None] + lax.axis_index("freq")) * bands[None, :] % band
     phases = (2.0 * math.pi / band) * phases.astype(F32)
     tables = jnp.stack([jnp.cos(phases), jnp.sin(phases)])
-    (estimate,) = call(step_kernel, "step", [result], [right, left, start], flops=flops)
+    (estimate,) = call(step_kernel, "step", [result], [*right, own_left, other_left, start], flops=flops)
     (estimate,) = call(
         functools.partial(shrink_kernel, band),
         "shrink",

time: 29.3 us -> 29.1 us (level)
  Pallas kernels: 5.46 us -> 5.91 us
  waiting for transfers between devices: 7.36 us -> 6.96 us
    pallas_call x11 -> x13, Pallas kernels: 5.46 us -> 5.91 us  [call(): pl.pallas_call(kernel, out_shape=outs, in_specs=[pl.BlockSpec(memory_spac...]
    ppermute x5, waiting for transfers between devices: 1.72 us -> 1.43 us  [to_mate(): lax.ppermute(value, 'tile', [(i, i ^ 1) for i in range(lax.axis_size('til...]
  transfers between devices with their start and end apart: 15 -> 15, of which waited for: 6 -> 6; matrix products, arithmetic and copies ran while one was open for 0% -> 0% of each run, Pallas kernels for 8% -> 10%
where the time goes in v14:
time: 29.1 us; the launch traced here: 29 us
  starting transfers between devices  16 us (55%)
  waiting for transfers between devices  6.96 us (24%)
  Pallas kernels  5.91 us (20%)
    ppermute x8, starting transfers between devices, exchange(): arrived.append(lax.ppermute(send, 'tile', pairs))  11.8 us
    pallas_call x13, Pallas kernels, call(): pl.pallas_call(kernel, out_shape=outs, in_specs=[pl.BlockSpec(memory_spac...  5.91 us
    ppermute x8, waiting for transfers between devices, exchange(): arrived.append(lax.ppermute(send, 'tile', pairs))  3.26 us
    ppermute x1, waiting for transfers between devices, across(): return lax.ppermute(value, ('tile', 'freq'), pairs)  2.27 us
    ppermute x5, starting transfers between devices, to_mate(): lax.ppermute(value, 'tile', [(i, i ^ 1) for i in range(lax.axis_size('til...  1.58 us
    ppermute x1, starting transfers between devices, body(): lax.ppermute(start, 'freq', [(f, (f - shift) % band) for f in range(band)])  1.52 us
    ppermute x5, waiting for transfers between devices, to_mate(): lax.ppermute(value, 'tile', [(i, i ^ 1) for i in range(lax.axis_size('til...  1.43 us
    ppermute x1, starting transfers between devices, across(): return lax.ppermute(value, ('tile', 'freq'), pairs)  1.09 us
  transfers between devices with their start and end apart: 15, of which 6 were waited for; matrix products, arithmetic and copies ran while one was open for 0% of the time, Pallas kernels for 10%

profile of v14, /device:TPU:0, one launch (start us, length us, event | category | flops | bytes accessed | tf_op | source)
XLA Modules:
  0.0 29.0 jit_solution(17408974001238077923)
XLA Ops:
  0.0 1.7 %forward.1 = (bf16[4,64,128]{2,1,0:T(8,128)(2,1)S(1)}, bf16[4,64,128]{2,1,0:T(8,128)(2,1)S(1)}) custom-call(f32[256,128]{1,0:T(8,128)} %bitcast.8, bf16[2048,128]{1,0:T(8,128)(2,1)} %bitcast.5), custom_call_target="tpu_custom_call" | custom-call | flops 67108864 | bytes 786432 | tf_op jit(solution)/shard_map/forward/pallas_call | solution.py:219
  1.7 0.5 %collective-permute-start = (bf16[4,64,128]{2,1,0:T(8,128)(2,1)S(1)}, bf16[4,64,128]{2,1,0:T(8,128)(2,1)S(1)}, u32[]{:S(2)}, u32[]{:S(2)}) collective-permute-start(bf16[4,64,128]{2,1,0:T(8,128)(2,1)S(1)} %get-tuple-element.36), channel_id=1, source_target_pairs={{0,2},{2,0},{4,6},{6,4},{8,10},{10,8},{12,14},{14,12},{16,18},{18,... | collective-permute-start | bytes 196616 | tf_op jit(solution)/shard_map/ppermute | solution.py:232
  2.3 0.1 collective-permute-start.4
  2.4 0.8 %collective-permute-done.arrived = bf16[4,64,128]{2,1,0:T(8,128)(2,1)S(1)} collective-permute-done((bf16[4,64,128]{2,1,0:T(8,128)(2,1)S(1)}, bf16[4,64,128]{2,1,0:T(8,128)(2,1)S(1)}, u32[]{:S(2)}, u32[]{:S(2)}) %collective-permute-start) | collective-permute-done | bytes 65568 | tf_op jit(solution)/shard_map/ppermute | solution.py:232
  3.2 0.0 copy-start.4
  3.2 4.8 %collective-permute-start.3 = (bf16[64,128]{1,0:T(8,128)(2,1)S(1)}, bf16[64,128]{1,0:T(8,128)(2,1)S(1)}, u32[]{:S(2)}, u32[]{:S(2)}) collective-permute-start(bf16[64,128]{1,0:T(8,128)(2,1)S(1)} %get-tuple-element.39), channel_id=1, source_target_pairs={{0,26},{2,28},{4,30},{6,24},{8,18},{10,20},{12,22},{14,16},{16,10}... | collective-permute-start | bytes 49160 | tf_op jit(solution)/shard_map/ppermute | solution.py:250
  8.0 0.3 %collective-permute-start.5 = (bf16[64,128]{1,0:T(8,128)(2,1)S(1)}, bf16[64,128]{1,0:T(8,128)(2,1)S(1)}, u32[]{:S(2)}, u32[]{:S(2)}) collective-permute-start(bf16[64,128]{1,0:T(8,128)(2,1)S(1)} %get-tuple-element.46), channel_id=1, source_target_pairs={{0,18},{2,20},{4,22},{6,16},{8,26},{10,28},{12,30},{14,24},{16,2},... | collective-permute-start | bytes 49160 | tf_op jit(solution)/shard_map/ppermute | solution.py:250
  8.3 1.1 %collective-permute-start.1 = (bf16[64,128]{1,0:T(8,128)(2,1)S(1)}, bf16[64,128]{1,0:T(8,128)(2,1)S(1)}, u32[]{:S(2)}, u32[]{:S(2)}) collective-permute-start(bf16[64,128]{1,0:T(8,128)(2,1)S(1)} %get-tuple-element.37), channel_id=1, source_target_pairs={{0,6},{2,12},{4,2},{6,8},{8,14},{10,4},{12,10},{14,0},{16,22},{18,... | collective-permute-start | bytes 49160 | tf_op jit(solution)/shard_map/ppermute | solution.py:250
  9.4 0.2 collective-permute-start.2
  9.7 1.1 %rows.1 = (bf16[512,512]{1,0:T(8,128)(2,1)S(1)}, f32[128,256]{1,0:T(8,128)S(1)}, f32[256,128]{1,0:T(8,128)S(1)}) custom-call(s32[1,8,8]{2,1,0:T(8,128)S(1)} %copy-done.4, bf16[2048,128]{1,0:T(8,128)(2,1)S(1)} %bitcast.11, bf16[2048,128]{1,0:T(8,128)(2,1)S(1)} %collective-permute-done.4.mate, f32[256,128]{1,0:T(8,128)S(1)} %bitcast.12, f32[256,128]{1,0:T(8,128)S(1)} %bitcast.9), custom_call_target="tpu_custom_call" | custom-call | tf_op jit(solution)/shard_map/rows/pallas_call | solution.py:219
  10.8 2.2 %collective-permute-done.5.second = bf16[64,128]{1,0:T(8,128)(2,1)S(1)} collective-permute-done((bf16[64,128]{1,0:T(8,128)(2,1)S(1)}, bf16[64,128]{1,0:T(8,128)(2,1)S(1)}, u32[]{:S(2)}, u32[]{:S(2)}) %collective-permute-start.5) | collective-permute-done | bytes 16416 | tf_op jit(solution)/shard_map/ppermute | solution.py:250
  12.9 0.2 early.1.refs_2_
  13.2 0.2 image.1.here
  13.4 0.4 %collective-permute-start.6 = (f32[128,512]{1,0:T(8,128)S(1)}, f32[128,512]{1,0:T(8,128)S(1)}, u32[]{:S(2)}, u32[]{:S(2)}) collective-permute-start(f32[128,512]{1,0:T(8,128)S(1)} %image.1.here), channel_id=1, source_target_pairs={{0,2},{2,0},{4,6},{6,4},{8,10},{10,8},{12,14},{14,12},{16,18},{18,... | collective-permute-start | bytes 786440 | tf_op jit(solution)/shard_map/ppermute | solution.py:232
  13.9 1.5 %collective-permute-start.9 = (f32[256,128]{1,0:T(8,128)S(1)}, f32[256,128]{1,0:T(8,128)S(1)}, u32[]{:S(2)}, u32[]{:S(2)}) collective-permute-start(f32[256,128]{1,0:T(8,128)S(1)} %get-tuple-element.51.here), channel_id=1, source_target_pairs={{0,1},{1,0},{2,3},{3,2},{4,5},{5,4},{6,7},{7,6},{8,9},{9,8},{10,11... | collective-permute-start | bytes 393224 | tf_op jit(solution)/shard_map/ppermute | solution.py:304
  15.4 0.3 %back.1 = (bf16[64,128]{1,0:T(8,128)(2,1)S(1)}, bf16[64,128]{1,0:T(8,128)(2,1)S(1)}, bf16[64,128]{1,0:T(8,128)(2,1)S(1)}, bf16[64,128]{1,0:T(8,128)(2,1)S(1)}) custom-call(f32[128,512]{1,0:T(8,128)S(1)} %image.1.here, f32[128,512]{1,0:T(8,128)S(1)} %collective-permute-done.6.there, bf16[512,512]{1,0:T(8,128)(2,1)S(1)} %get-tuple-element.43.factors.refs_3_), custom_call_target="tpu_custom_call" | custom-call | flops 17179869184 | bytes 1114112 | tf_op jit(solution)/shard_map/back/pallas_call | solution.py:219
  15.8 2.6 %collective-permute-start.7 = (bf16[64,128]{1,0:T(8,128)(2,1)S(1)}, bf16[64,128]{1,0:T(8,128)(2,1)S(1)}, u32[]{:S(2)}, u32[]{:S(2)}) collective-permute-start(bf16[64,128]{1,0:T(8,128)(2,1)S(1)} %get-tuple-element.47), channel_id=1, source_target_pairs={{0,30},{2,24},{4,26},{6,28},{8,22},{10,16},{12,18},{14,20},{16,14}... | collective-permute-start | bytes 49160 | tf_op jit(solution)/shard_map/ppermute | solution.py:250
  18.3 0.3 %collective-permute-start.10 = (bf16[64,128]{1,0:T(8,128)(2,1)S(1)}, bf16[64,128]{1,0:T(8,128)(2,1)S(1)}, u32[]{:S(2)}, u32[]{:S(2)}) collective-permute-start(bf16[64,128]{1,0:T(8,128)(2,1)S(1)} %get-tuple-element.53), channel_id=1, source_target_pairs={{0,22},{2,16},{4,18},{6,20},{8,30},{10,24},{12,26},{14,28},{16,6},... | collective-permute-start | bytes 49160 | tf_op jit(solution)/shard_map/ppermute | solution.py:250
  18.6 2.3 %collective-permute-start.11 = (bf16[64,128]{1,0:T(8,128)(2,1)S(1)}, bf16[64,128]{1,0:T(8,128)(2,1)S(1)}, u32[]{:S(2)}, u32[]{:S(2)}) collective-permute-start(bf16[64,128]{1,0:T(8,128)(2,1)S(1)} %get-tuple-element.54), channel_id=1, source_target_pairs={{0,14},{2,4},{4,10},{6,0},{8,6},{10,12},{12,2},{14,8},{16,30},{18,... | collective-permute-start | bytes 49160 | tf_op jit(solution)/shard_map/ppermute | solution.py:250
  20.9 0.2 collective-permute-start.12
  21.1 0.3 %columns.2 = (bf16[256,512]{1,0:T(8,128)(2,1)S(1)}, bf16[256,512]{1,0:T(8,128)(2,1)S(1)}) custom-call(bf16[2048,128]{1,0:T(8,128)(2,1)S(1)} %collective-permute-done.8.factors), custom_call_target="tpu_custom_call" | custom-call | tf_op jit(solution)/shard_map/columns/pallas_call | solution.py:219
  21.5 0.9 %collective-permute-done.10.refs_1_ = bf16[64,128]{1,0:T(8,128)(2,1)S(1)} collective-permute-done((bf16[64,128]{1,0:T(8,128)(2,1)S(1)}, bf16[64,128]{1,0:T(8,128)(2,1)S(1)}, u32[]{:S(2)}, u32[]{:S(2)}) %collective-permute-start.10) | collective-permute-done | bytes 16416 | tf_op jit(solution)/shard_map/ppermute | solution.py:250
  22.4 0.2 collective-permute-done.12.refs_3_
  22.6 0.5 %collective-permute-start.13 = (bf16[4,64,128]{2,1,0:T(8,128)(2,1)S(1)}, bf16[4,64,128]{2,1,0:T(8,128)(2,1)S(1)}, u32[]{:S(2)}, u32[]{:S(2)}) collective-permute-start(bf16[4,64,128]{2,1,0:T(8,128)(2,1)S(1)} %pack.1.blocks), channel_id=1, source_target_pairs={{0,2},{2,0},{4,6},{6,4},{8,10},{10,8},{12,14},{14,12},{16,18},{18,... | collective-permute-start | bytes 196616 | tf_op jit(solution)/shard_map/ppermute | solution.py:232
  23.1 0.3 part.1
  23.4 0.6 %collective-permute-done.13.blocks = bf16[4,64,128]{2,1,0:T(8,128)(2,1)S(1)} collective-permute-done((bf16[4,64,128]{2,1,0:T(8,128)(2,1)S(1)}, bf16[4,64,128]{2,1,0:T(8,128)(2,1)S(1)}, u32[]{:S(2)}, u32[]{:S(2)}) %collective-permute-start.13) | collective-permute-done | bytes 65568 | tf_op jit(solution)/shard_map/ppermute | solution.py:232
  24.0 0.3 %gradient.1 = (bf16[256,128]{1,0:T(8,128)(2,1)S(1)}, bf16[128,512]{1,0:T(8,128)(2,1)S(1)}) custom-call(f32[256,128]{1,0:T(8,128)S(1)} %get-tuple-element.56.part, bf16[4,64,128]{2,1,0:T(8,128)(2,1)S(1)} %collective-permute-done.13.blocks, bf16[256,512]{1,0:T(8,128)(2,1)S(1)} %get-tuple-element.50.factors), custom_call_target="tpu_custom_call" | custom-call | flops 33554432 | bytes 655360 | tf_op jit(solution)/shard_map/gradient/pallas_call | solution.py:219
  24.3 1.1 %collective-permute-start.14 = (bf16[256,128]{1,0:T(8,128)(2,1)S(1)}, bf16[256,128]{1,0:T(8,128)(2,1)S(1)}, u32[]{:S(2)}, u32[]{:S(2)}) collective-permute-start(bf16[256,128]{1,0:T(8,128)(2,1)S(1)} %get-tuple-element.57), channel_id=1, source_target_pairs={{0,3},{1,2},{2,1},{3,0},{4,7},{5,6},{6,5},{7,4},{8,11},{9,10},{10,... | collective-permute-start | bytes 196616 | tf_op jit(solution)/shard_map/ppermute | solution.py:238
  25.4 0.3 %columns.3 = (bf16[256,512]{1,0:T(8,128)(2,1)S(1)}, bf16[256,512]{1,0:T(8,128)(2,1)S(1)}) custom-call(bf16[2048,128]{1,0:T(8,128)(2,1)S(1)} %bitcast.7), custom_call_target="tpu_custom_call" | custom-call | tf_op jit(solution)/shard_map/columns/pallas_call | solution.py:219
  25.7 0.3 %pair.1 = (f32[256,128]{1,0:T(8,128)S(1)}, f32[256,128]{1,0:T(8,128)S(1)}) custom-call(bf16[256,512]{1,0:T(8,128)(2,1)S(1)} %get-tuple-element.59.own, bf16[256,512]{1,0:T(8,128)(2,1)S(1)} %get-tuple-element.60.other, bf16[128,512]{1,0:T(8,128)(2,1)S(1)} %get-tuple-element.61.own_left, bf16[128,512]{1,0:T(8,128)(2,1)S(1)} %get-tuple-element.62.other_left, ...), custom_call_target="tpu_custom_call" | custom-call | flops 67108864 | bytes 1310720 | tf_op jit(solution)/shard_map/pair/pallas_call | solution.py:219
  26.0 2.3 %collective-permute-done.14.gradient = bf16[256,128]{1,0:T(8,128)(2,1)S(1)} collective-permute-done((bf16[256,128]{1,0:T(8,128)(2,1)S(1)}, bf16[256,128]{1,0:T(8,128)(2,1)S(1)}, u32[]{:S(2)}, u32[]{:S(2)}) %collective-permute-start.14) | collective-permute-done | bytes 65568 | tf_op jit(solution)/shard_map/ppermute | solution.py:238
  28.3 0.7 %shrink.1 = f32[256,128]{1,0:T(8,128)} custom-call(f32[256,128]{1,0:T(8,128)S(1)} %get-tuple-element.63.total, f32[256,128]{1,0:T(8,128)S(1)} %get-tuple-element.64.difference, bf16[256,128]{1,0:T(8,128)(2,1)S(1)} %collective-permute-done.14.gradient), custom_call_target="tpu_custom_call" | custom-call | tf_op jit(solution)/shard_map/shrink/pallas_call | solution.py:219
  (21 shorter events, 0.1 us)
Async XLA Ops:
  0.0 2.3 %copy-start.2 = (bf16[1,256,8,128]{3,2,1,0:T(8,128)(2,1)S(1)}, bf16[1,256,8,128]{3,2,1,0:T(8,128)(2,1)}, u32[]{:S(2)}) copy-start(bf16[1,256,8,128]{3,2,1,0:T(8,128)(2,1)} %param.5) | copy-start | bytes 1572868
  1.7 1.4 %collective-permute-start = (bf16[4,64,128]{2,1,0:T(8,128)(2,1)S(1)}, bf16[4,64,128]{2,1,0:T(8,128)(2,1)S(1)}, u32[]{:S(2)}, u32[]{:S(2)}) collective-permute-start(bf16[4,64,128]{2,1,0:T(8,128)(2,1)S(1)} %get-tuple-element.36), channel_id=1, source_target_pairs={{0,2},{2,0},{4,6},{6,4},{8,10},{10,8},{12,14},{14,12},{16,18},{18,... | collective-permute-start | bytes 196616 | tf_op jit(solution)/shard_map/ppermute | solution.py:232
  2.3 7.4 %collective-permute-start.4 = (bf16[2048,128]{1,0:T(8,128)(2,1)S(1)}, bf16[2048,128]{1,0:T(8,128)(2,1)S(1)}, u32[]{:S(2)}, u32[]{:S(2)}) collective-permute-start(bf16[2048,128]{1,0:T(8,128)(2,1)S(1)} %bitcast.10), channel_id=1, source_target_pairs={{0,2},{2,0},{4,6},{6,4},{8,10},{10,8},{12,14},{14,12},{16,18},{18,... | collective-permute-start | bytes 1572872 | tf_op jit(solution)/shard_map/ppermute | solution.py:232
  3.2 6.5 %copy-start.1 = (f32[1,256,128]{2,1,0:T(8,128)S(1)}, f32[1,256,128]{2,1,0:T(8,128)}, u32[]{:S(2)}) copy-start(f32[1,256,128]{2,1,0:T(8,128)} %param.9) | copy-start | bytes 393220
  3.2 6.5 %copy-start.3 = (f32[1,256,128]{2,1,0:T(8,128)S(1)}, f32[1,256,128]{2,1,0:T(8,128)}, u32[]{:S(2)}) copy-start(f32[1,256,128]{2,1,0:T(8,128)} %param.8) | copy-start | bytes 393220
  3.2 6.5 %copy-start.4 = (s32[1,8,8]{2,1,0:T(8,128)S(1)}, s32[1,8,8]{2,1,0:T(8,128)}, u32[]{:S(2)}) copy-start(s32[1,8,8]{2,1,0:T(8,128)} %ranks.1) | copy-start | bytes 772
  3.2 7.5 %collective-permute-start.3 = (bf16[64,128]{1,0:T(8,128)(2,1)S(1)}, bf16[64,128]{1,0:T(8,128)(2,1)S(1)}, u32[]{:S(2)}, u32[]{:S(2)}) collective-permute-start(bf16[64,128]{1,0:T(8,128)(2,1)S(1)} %get-tuple-element.39), channel_id=1, source_target_pairs={{0,26},{2,28},{4,30},{6,24},{8,18},{10,20},{12,22},{14,16},{16,10}... | collective-permute-start | bytes 49160 | tf_op jit(solution)/shard_map/ppermute | solution.py:250
  8.0 5.0 %collective-permute-start.5 = (bf16[64,128]{1,0:T(8,128)(2,1)S(1)}, bf16[64,128]{1,0:T(8,128)(2,1)S(1)}, u32[]{:S(2)}, u32[]{:S(2)}) collective-permute-start(bf16[64,128]{1,0:T(8,128)(2,1)S(1)} %get-tuple-element.46), channel_id=1, source_target_pairs={{0,18},{2,20},{4,22},{6,16},{8,26},{10,28},{12,30},{14,24},{16,2},... | collective-permute-start | bytes 49160 | tf_op jit(solution)/shard_map/ppermute | solution.py:250
  8.3 4.9 %collective-permute-start.1 = (bf16[64,128]{1,0:T(8,128)(2,1)S(1)}, bf16[64,128]{1,0:T(8,128)(2,1)S(1)}, u32[]{:S(2)}, u32[]{:S(2)}) collective-permute-start(bf16[64,128]{1,0:T(8,128)(2,1)S(1)} %get-tuple-element.37), channel_id=1, source_target_pairs={{0,6},{2,12},{4,2},{6,8},{8,14},{10,4},{12,10},{14,0},{16,22},{18,... | collective-permute-start | bytes 49160 | tf_op jit(solution)/shard_map/ppermute | solution.py:250
  9.4 3.8 %collective-permute-start.2 = (bf16[64,128]{1,0:T(8,128)(2,1)S(1)}, bf16[64,128]{1,0:T(8,128)(2,1)S(1)}, u32[]{:S(2)}, u32[]{:S(2)}) collective-permute-start(bf16[64,128]{1,0:T(8,128)(2,1)S(1)} %get-tuple-element.38), channel_id=1, source_target_pairs={{0,2},{2,8},{4,6},{6,12},{8,10},{10,0},{12,14},{14,4},{16,18},{18,... | collective-permute-start | bytes 49160 | tf_op jit(solution)/shard_map/ppermute | solution.py:250
  13.2 2.2 %copy-start = (bf16[1,256,8,128]{3,2,1,0:T(8,128)(2,1)S(1)}, bf16[1,256,8,128]{3,2,1,0:T(8,128)(2,1)}, u32[]{:S(2)}) copy-start(bf16[1,256,8,128]{3,2,1,0:T(8,128)(2,1)} %param.6) | copy-start | bytes 1572868
  13.4 2.0 %collective-permute-start.6 = (f32[128,512]{1,0:T(8,128)S(1)}, f32[128,512]{1,0:T(8,128)S(1)}, u32[]{:S(2)}, u32[]{:S(2)}) collective-permute-start(f32[128,512]{1,0:T(8,128)S(1)} %image.1.here), channel_id=1, source_target_pairs={{0,2},{2,0},{4,6},{6,4},{8,10},{10,8},{12,14},{14,12},{16,18},{18,... | collective-permute-start | bytes 786440 | tf_op jit(solution)/shard_map/ppermute | solution.py:232
  13.9 7.6 %collective-permute-start.9 = (f32[256,128]{1,0:T(8,128)S(1)}, f32[256,128]{1,0:T(8,128)S(1)}, u32[]{:S(2)}, u32[]{:S(2)}) collective-permute-start(f32[256,128]{1,0:T(8,128)S(1)} %get-tuple-element.51.here), channel_id=1, source_target_pairs={{0,1},{1,0},{2,3},{3,2},{4,5},{5,4},{6,7},{7,6},{8,9},{9,8},{10,11... | collective-permute-start | bytes 393224 | tf_op jit(solution)/shard_map/ppermute | solution.py:304
  15.4 5.5 %collective-permute-start.8 = (bf16[2048,128]{1,0:T(8,128)(2,1)S(1)}, bf16[2048,128]{1,0:T(8,128)(2,1)S(1)}, u32[]{:S(2)}, u32[]{:S(2)}) collective-permute-start(bf16[2048,128]{1,0:T(8,128)(2,1)S(1)} %bitcast.6), channel_id=1, source_target_pairs={{0,2},{2,0},{4,6},{6,4},{8,10},{10,8},{12,14},{14,12},{16,18},{18,... | collective-permute-start | bytes 1572872 | tf_op jit(solution)/shard_map/ppermute | solution.py:232
  15.8 5.7 %collective-permute-start.7 = (bf16[64,128]{1,0:T(8,128)(2,1)S(1)}, bf16[64,128]{1,0:T(8,128)(2,1)S(1)}, u32[]{:S(2)}, u32[]{:S(2)}) collective-permute-start(bf16[64,128]{1,0:T(8,128)(2,1)S(1)} %get-tuple-element.47), channel_id=1, source_target_pairs={{0,30},{2,24},{4,26},{6,28},{8,22},{10,16},{12,18},{14,20},{16,14}... | collective-permute-start | bytes 49160 | tf_op jit(solution)/shard_map/ppermute | solution.py:250
  18.3 4.1 %collective-permute-start.10 = (bf16[64,128]{1,0:T(8,128)(2,1)S(1)}, bf16[64,128]{1,0:T(8,128)(2,1)S(1)}, u32[]{:S(2)}, u32[]{:S(2)}) collective-permute-start(bf16[64,128]{1,0:T(8,128)(2,1)S(1)} %get-tuple-element.53), channel_id=1, source_target_pairs={{0,22},{2,16},{4,18},{6,20},{8,30},{10,24},{12,26},{14,28},{16,6},... | collective-permute-start | bytes 49160 | tf_op jit(solution)/shard_map/ppermute | solution.py:250
  18.6 3.7 %collective-permute-start.11 = (bf16[64,128]{1,0:T(8,128)(2,1)S(1)}, bf16[64,128]{1,0:T(8,128)(2,1)S(1)}, u32[]{:S(2)}, u32[]{:S(2)}) collective-permute-start(bf16[64,128]{1,0:T(8,128)(2,1)S(1)} %get-tuple-element.54), channel_id=1, source_target_pairs={{0,14},{2,4},{4,10},{6,0},{8,6},{10,12},{12,2},{14,8},{16,30},{18,... | collective-permute-start | bytes 49160 | tf_op jit(solution)/shard_map/ppermute | solution.py:250
  20.9 1.6 %collective-permute-start.12 = (bf16[64,128]{1,0:T(8,128)(2,1)S(1)}, bf16[64,128]{1,0:T(8,128)(2,1)S(1)}, u32[]{:S(2)}, u32[]{:S(2)}) collective-permute-start(bf16[64,128]{1,0:T(8,128)(2,1)S(1)} %get-tuple-element.55), channel_id=1, source_target_pairs={{0,10},{2,0},{4,14},{6,4},{8,2},{10,8},{12,6},{14,12},{16,26},{18,... | collective-permute-start | bytes 49160 | tf_op jit(solution)/shard_map/ppermute | solution.py:250
  22.6 1.4 %collective-permute-start.13 = (bf16[4,64,128]{2,1,0:T(8,128)(2,1)S(1)}, bf16[4,64,128]{2,1,0:T(8,128)(2,1)S(1)}, u32[]{:S(2)}, u32[]{:S(2)}) collective-permute-start(bf16[4,64,128]{2,1,0:T(8,128)(2,1)S(1)} %pack.1.blocks), channel_id=1, source_target_pairs={{0,2},{2,0},{4,6},{6,4},{8,10},{10,8},{12,14},{14,12},{16,18},{18,... | collective-permute-start | bytes 196616 | tf_op jit(solution)/shard_map/ppermute | solution.py:232
  24.3 4.0 %collective-permute-start.14 = (bf16[256,128]{1,0:T(8,128)(2,1)S(1)}, bf16[256,128]{1,0:T(8,128)(2,1)S(1)}, u32[]{:S(2)}, u32[]{:S(2)}) collective-permute-start(bf16[256,128]{1,0:T(8,128)(2,1)S(1)} %get-tuple-element.57), channel_id=1, source_target_pairs={{0,3},{1,2},{2,1},{3,0},{4,7},{5,6},{6,5},{7,4},{8,11},{9,10},{10,... | collective-permute-start | bytes 196616 | tf_op jit(solution)/shard_map/ppermute | solution.py:238

commit v15 on v14

--- a/solution.py
+++ b/solution.py
@@ -13,8 +13,8 @@
 LANES = 128
 VMEM_LIMIT = 32 * 1024 * 1024
 FIRST_LIMIT = 55050 * 1024
-PIECES = 4
-HIDE = 256
+PIECES = 8
+HIDE = 128
 F32 = jnp.float32
 BF16 = jnp.bfloat16
 
@@ -145,13 +145,15 @@
 
 
 def back_kernel(here, there, factors, *refs):
-    outs, (misfit, product) = refs[:-2], refs[-2:]
+    outs, products = refs[:-1], refs[-1]
     rows = here.shape[1] // 2
-    misfit[:, :rows] = (here[:, :rows] + there[:, rows:]).astype(BF16)
-    misfit[:, rows:] = (here[:, rows:] + there[:, :rows]).astype(BF16)
-    product[...] = jnp.dot(misfit[...], factors[...], preferred_element_type=F32)
+    for side in range(2):
+        at, other = pl.ds(side * rows, rows), pl.ds((1 - side) * rows, rows)
+        misfit = (here[:, at] + there[:, other]).astype(BF16)
+        products[side] = jnp.dot(misfit, factors[at, :], preferred_element_type=F32)
     for index, out in enumerate(outs):
-        out[...] = adjoint_block(product, index)
+        parts = [adjoint_block(products.at[side], index).astype(F32) for side in range(2)]
+        out[...] = (parts[0] + parts[1]).astype(BF16)
 
 
 def pack_kernel(*refs):
@@ -318,17 +320,17 @@
         [misfit],
         [*arrived[2:], misfit_early, both_left],
         [pltpu.VMEM((sources, (members - 2) * width), BF16)],
-        flops // 2,
-    )
-    mate_right = to_mate(after(right_rows, misfit))
+        HIDE * flops,
+    )
+    mate_right = to_mate(after(right_rows, both_left))
     mate_right = call(functools.partial(columns_kernel, shifts), "columns", [factor] * 2, [mate_right], [wide])
     sends = call(
         back_kernel,
         "back",
         [block] * members,
         [misfit, to_mate(misfit), both_left],
-        [pltpu.VMEM((sources, 2 * rows), BF16), pltpu.VMEM((sources, members * width), F32)],
-        HIDE * flops,
+        [pltpu.VMEM((2, sources, members * width), F32)],
+        flops,
     )
     (own,) = call(pack_kernel, "pack", [blocks], exchange(sends, shifts[::-1], [*mate_right, *starts[1:]]))
     spread = shape(sources, members * width)

time: 29.1 us -> 29.1 us (level)
  waiting for transfers between devices: 6.96 us -> 6.42 us
  starting transfers between devices: 16 us -> 16.4 us
    ppermute x8, waiting for transfers between devices: 3.26 us -> 2.69 us  [exchange(): arrived.append(lax.ppermute(send, 'tile', pairs))]
  transfers between devices with their start and end apart: 15 -> 15, of which waited for: 6 -> 6; matrix products, arithmetic and copies ran while one was open for 0% -> 0% of each run, Pallas kernels for 10% -> 11%
where the time goes in v15:
time: 29.1 us; the launch traced here: 29 us
  starting transfers between devices  16.4 us (56%)
  waiting for transfers between devices  6.42 us (22%)
  Pallas kernels  5.98 us (21%)
    ppermute x8, starting transfers between devices, exchange(): arrived.append(lax.ppermute(send, 'tile', pairs))  11.8 us
    pallas_call x13, Pallas kernels, call(): pl.pallas_call(kernel, out_shape=outs, in_specs=[pl.BlockSpec(memory_spac...  5.98 us
    ppermute x8, waiting for transfers between devices, exchange(): arrived.append(lax.ppermute(send, 'tile', pairs))  2.69 us
    ppermute x1, waiting for transfers between devices, across(): return lax.ppermute(value, ('tile', 'freq'), pairs)  2.16 us
    ppermute x5, starting transfers between devices, to_mate(): lax.ppermute(value, 'tile', [(i, i ^ 1) for i in range(lax.axis_size('til...  1.83 us
    ppermute x5, waiting for transfers between devices, to_mate(): lax.ppermute(value, 'tile', [(i, i ^ 1) for i in range(lax.axis_size('til...  1.56 us
    ppermute x1, starting transfers between devices, body(): lax.ppermute(start, 'freq', [(f, (f - shift) % band) for f in range(band)])  1.52 us
    ppermute x1, starting transfers between devices, across(): return lax.ppermute(value, ('tile', 'freq'), pairs)  1.32 us
  transfers between devices with their start and end apart: 15, of which 6 were waited for; matrix products, arithmetic and copies ran while one was open for 0% of the time, Pallas kernels for 11%

profile of v15, /device:TPU:0, one launch (start us, length us, event | category | flops | bytes accessed | tf_op | source)
XLA Modules:
  0.0 29.0 jit_solution(1297170625236928070)
XLA Ops:
  0.0 1.8 %forward.1 = (bf16[4,64,128]{2,1,0:T(8,128)(2,1)S(1)}, bf16[4,64,128]{2,1,0:T(8,128)(2,1)S(1)}) custom-call(f32[256,128]{1,0:T(8,128)} %bitcast.8, bf16[2048,128]{1,0:T(8,128)(2,1)} %bitcast.5), custom_call_target="tpu_custom_call" | custom-call | flops 67108864 | bytes 786432 | tf_op jit(solution)/shard_map/forward/pallas_call | solution.py:221
  1.8 0.5 %collective-permute-start = (bf16[4,64,128]{2,1,0:T(8,128)(2,1)S(1)}, bf16[4,64,128]{2,1,0:T(8,128)(2,1)S(1)}, u32[]{:S(2)}, u32[]{:S(2)}) collective-permute-start(bf16[4,64,128]{2,1,0:T(8,128)(2,1)S(1)} %get-tuple-element.36), channel_id=1, source_target_pairs={{0,2},{2,0},{4,6},{6,4},{8,10},{10,8},{12,14},{14,12},{16,18},{18,... | collective-permute-start | bytes 196616 | tf_op jit(solution)/shard_map/ppermute | solution.py:234
  2.3 0.1 collective-permute-start.4
  2.4 0.8 %collective-permute-done.arrived = bf16[4,64,128]{2,1,0:T(8,128)(2,1)S(1)} collective-permute-done((bf16[4,64,128]{2,1,0:T(8,128)(2,1)S(1)}, bf16[4,64,128]{2,1,0:T(8,128)(2,1)S(1)}, u32[]{:S(2)}, u32[]{:S(2)}) %collective-permute-start) | collective-permute-done | bytes 65568 | tf_op jit(solution)/shard_map/ppermute | solution.py:234
  3.3 4.8 %collective-permute-start.3 = (bf16[64,128]{1,0:T(8,128)(2,1)S(1)}, bf16[64,128]{1,0:T(8,128)(2,1)S(1)}, u32[]{:S(2)}, u32[]{:S(2)}) collective-permute-start(bf16[64,128]{1,0:T(8,128)(2,1)S(1)} %get-tuple-element.39), channel_id=1, source_target_pairs={{0,26},{2,28},{4,30},{6,24},{8,18},{10,20},{12,22},{14,16},{16,10}... | collective-permute-start | bytes 49160 | tf_op jit(solution)/shard_map/ppermute | solution.py:252
  8.0 0.3 %collective-permute-start.5 = (bf16[64,128]{1,0:T(8,128)(2,1)S(1)}, bf16[64,128]{1,0:T(8,128)(2,1)S(1)}, u32[]{:S(2)}, u32[]{:S(2)}) collective-permute-start(bf16[64,128]{1,0:T(8,128)(2,1)S(1)} %get-tuple-element.46), channel_id=1, source_target_pairs={{0,18},{2,20},{4,22},{6,16},{8,26},{10,28},{12,30},{14,24},{16,2},... | collective-permute-start | bytes 49160 | tf_op jit(solution)/shard_map/ppermute | solution.py:252
  8.4 1.1 %collective-permute-start.1 = (bf16[64,128]{1,0:T(8,128)(2,1)S(1)}, bf16[64,128]{1,0:T(8,128)(2,1)S(1)}, u32[]{:S(2)}, u32[]{:S(2)}) collective-permute-start(bf16[64,128]{1,0:T(8,128)(2,1)S(1)} %get-tuple-element.37), channel_id=1, source_target_pairs={{0,6},{2,12},{4,2},{6,8},{8,14},{10,4},{12,10},{14,0},{16,22},{18,... | collective-permute-start | bytes 49160 | tf_op jit(solution)/shard_map/ppermute | solution.py:252
  9.5 0.2 collective-permute-start.2
  9.7 1.1 %rows.1 = (bf16[512,512]{1,0:T(8,128)(2,1)S(1)}, f32[128,256]{1,0:T(8,128)S(1)}, f32[256,128]{1,0:T(8,128)S(1)}) custom-call(s32[1,8,8]{2,1,0:T(8,128)S(1)} %copy-done.4, bf16[2048,128]{1,0:T(8,128)(2,1)S(1)} %bitcast.11, bf16[2048,128]{1,0:T(8,128)(2,1)S(1)} %collective-permute-done.4.mate, f32[256,128]{1,0:T(8,128)S(1)} %bitcast.12, f32[256,128]{1,0:T(8,128)S(1)} %bitcast.9), custom_call_target="tpu_custom_call" | custom-call | tf_op jit(solution)/shard_map/rows/pallas_call | solution.py:221
  10.8 0.6 %collective-permute-start.8 = (bf16[2048,128]{1,0:T(8,128)(2,1)S(1)}, bf16[2048,128]{1,0:T(8,128)(2,1)S(1)}, u32[]{:S(2)}, u32[]{:S(2)}) collective-permute-start(bf16[2048,128]{1,0:T(8,128)(2,1)S(1)} %bitcast.6), channel_id=1, source_target_pairs={{0,2},{2,0},{4,6},{6,4},{8,10},{10,8},{12,14},{14,12},{16,18},{18,... | collective-permute-start | bytes 1572872 | tf_op jit(solution)/shard_map/ppermute | solution.py:234
  11.4 1.6 %collective-permute-done.5.second = bf16[64,128]{1,0:T(8,128)(2,1)S(1)} collective-permute-done((bf16[64,128]{1,0:T(8,128)(2,1)S(1)}, bf16[64,128]{1,0:T(8,128)(2,1)S(1)}, u32[]{:S(2)}, u32[]{:S(2)}) %collective-permute-start.5) | collective-permute-done | bytes 16416 | tf_op jit(solution)/shard_map/ppermute | solution.py:252
  13.0 0.2 early.1.refs_2_
  13.3 0.2 image.1.here
  13.5 0.4 %collective-permute-start.6 = (f32[128,512]{1,0:T(8,128)S(1)}, f32[128,512]{1,0:T(8,128)S(1)}, u32[]{:S(2)}, u32[]{:S(2)}) collective-permute-start(f32[128,512]{1,0:T(8,128)S(1)} %image.1.here), channel_id=1, source_target_pairs={{0,2},{2,0},{4,6},{6,4},{8,10},{10,8},{12,14},{14,12},{16,18},{18,... | collective-permute-start | bytes 786440 | tf_op jit(solution)/shard_map/ppermute | solution.py:234
  13.9 1.5 %collective-permute-start.9 = (f32[256,128]{1,0:T(8,128)S(1)}, f32[256,128]{1,0:T(8,128)S(1)}, u32[]{:S(2)}, u32[]{:S(2)}) collective-permute-start(f32[256,128]{1,0:T(8,128)S(1)} %get-tuple-element.51.here), channel_id=1, source_target_pairs={{0,1},{1,0},{2,3},{3,2},{4,5},{5,4},{6,7},{7,6},{8,9},{9,8},{10,11... | collective-permute-start | bytes 393224 | tf_op jit(solution)/shard_map/ppermute | solution.py:306
  15.5 0.3 %back.1 = (bf16[64,128]{1,0:T(8,128)(2,1)S(1)}, bf16[64,128]{1,0:T(8,128)(2,1)S(1)}, bf16[64,128]{1,0:T(8,128)(2,1)S(1)}, bf16[64,128]{1,0:T(8,128)(2,1)S(1)}) custom-call(f32[128,512]{1,0:T(8,128)S(1)} %image.1.here, f32[128,512]{1,0:T(8,128)S(1)} %collective-permute-done.6.there, bf16[512,512]{1,0:T(8,128)(2,1)S(1)} %get-tuple-element.43.factors.refs_3_), custom_call_target="tpu_custom_call" | custom-call | flops 67108864 | bytes 1114112 | tf_op jit(solution)/shard_map/back/pallas_call | solution.py:221
  15.8 2.4 %collective-permute-start.7 = (bf16[64,128]{1,0:T(8,128)(2,1)S(1)}, bf16[64,128]{1,0:T(8,128)(2,1)S(1)}, u32[]{:S(2)}, u32[]{:S(2)}) collective-permute-start(bf16[64,128]{1,0:T(8,128)(2,1)S(1)} %get-tuple-element.47), channel_id=1, source_target_pairs={{0,30},{2,24},{4,26},{6,28},{8,22},{10,16},{12,18},{14,20},{16,14}... | collective-permute-start | bytes 49160 | tf_op jit(solution)/shard_map/ppermute | solution.py:252
  18.2 0.2 collective-permute-start.10
  18.4 2.1 %collective-permute-start.11 = (bf16[64,128]{1,0:T(8,128)(2,1)S(1)}, bf16[64,128]{1,0:T(8,128)(2,1)S(1)}, u32[]{:S(2)}, u32[]{:S(2)}) collective-permute-start(bf16[64,128]{1,0:T(8,128)(2,1)S(1)} %get-tuple-element.54), channel_id=1, source_target_pairs={{0,14},{2,4},{4,10},{6,0},{8,6},{10,12},{12,2},{14,8},{16,30},{18,... | collective-permute-start | bytes 49160 | tf_op jit(solution)/shard_map/ppermute | solution.py:252
  20.5 0.7 %collective-permute-start.12 = (bf16[64,128]{1,0:T(8,128)(2,1)S(1)}, bf16[64,128]{1,0:T(8,128)(2,1)S(1)}, u32[]{:S(2)}, u32[]{:S(2)}) collective-permute-start(bf16[64,128]{1,0:T(8,128)(2,1)S(1)} %get-tuple-element.55), channel_id=1, source_target_pairs={{0,10},{2,0},{4,14},{6,4},{8,2},{10,8},{12,6},{14,12},{16,26},{18,... | collective-permute-start | bytes 49160 | tf_op jit(solution)/shard_map/ppermute | solution.py:252
  21.2 0.3 %columns.2 = (bf16[256,512]{1,0:T(8,128)(2,1)S(1)}, bf16[256,512]{1,0:T(8,128)(2,1)S(1)}) custom-call(bf16[2048,128]{1,0:T(8,128)(2,1)S(1)} %collective-permute-done.8.factors), custom_call_target="tpu_custom_call" | custom-call | tf_op jit(solution)/shard_map/columns/pallas_call | solution.py:221
  21.5 0.7 %collective-permute-done.10.refs_1_ = bf16[64,128]{1,0:T(8,128)(2,1)S(1)} collective-permute-done((bf16[64,128]{1,0:T(8,128)(2,1)S(1)}, bf16[64,128]{1,0:T(8,128)(2,1)S(1)}, u32[]{:S(2)}, u32[]{:S(2)}) %collective-permute-start.10) | collective-permute-done | bytes 16416 | tf_op jit(solution)/shard_map/ppermute | solution.py:252
  22.2 0.4 %collective-permute-done.12.refs_3_ = bf16[64,128]{1,0:T(8,128)(2,1)S(1)} collective-permute-done((bf16[64,128]{1,0:T(8,128)(2,1)S(1)}, bf16[64,128]{1,0:T(8,128)(2,1)S(1)}, u32[]{:S(2)}, u32[]{:S(2)}) %collective-permute-start.12) | collective-permute-done | bytes 16416 | tf_op jit(solution)/shard_map/ppermute | solution.py:252
  22.6 0.2 collective-permute-start.13
  22.8 0.3 %part.1 = (f32[256,128]{1,0:T(8,128)S(1)}, bf16[128,512]{1,0:T(8,128)(2,1)S(1)}) custom-call(bf16[4,64,128]{2,1,0:T(8,128)(2,1)S(1)} %pack.1.blocks, bf16[256,512]{1,0:T(8,128)(2,1)S(1)} %get-tuple-element.49.factors), custom_call_target="tpu_custom_call" | custom-call | flops 33554432 | bytes 589824 | tf_op jit(solution)/shard_map/part/pallas_call | solution.py:221
  23.1 0.7 %collective-permute-done.13.blocks = bf16[4,64,128]{2,1,0:T(8,128)(2,1)S(1)} collective-permute-done((bf16[4,64,128]{2,1,0:T(8,128)(2,1)S(1)}, bf16[4,64,128]{2,1,0:T(8,128)(2,1)S(1)}, u32[]{:S(2)}, u32[]{:S(2)}) %collective-permute-start.13) | collective-permute-done | bytes 65568 | tf_op jit(solution)/shard_map/ppermute | solution.py:234
  23.9 0.3 %gradient.1 = (bf16[256,128]{1,0:T(8,128)(2,1)S(1)}, bf16[128,512]{1,0:T(8,128)(2,1)S(1)}) custom-call(f32[256,128]{1,0:T(8,128)S(1)} %get-tuple-element.56.part, bf16[4,64,128]{2,1,0:T(8,128)(2,1)S(1)} %collective-permute-done.13.blocks, bf16[256,512]{1,0:T(8,128)(2,1)S(1)} %get-tuple-element.50.factors), custom_call_target="tpu_custom_call" | custom-call | flops 33554432 | bytes 655360 | tf_op jit(solution)/shard_map/gradient/pallas_call | solution.py:221
  24.2 1.3 %collective-permute-start.14 = (bf16[256,128]{1,0:T(8,128)(2,1)S(1)}, bf16[256,128]{1,0:T(8,128)(2,1)S(1)}, u32[]{:S(2)}, u32[]{:S(2)}) collective-permute-start(bf16[256,128]{1,0:T(8,128)(2,1)S(1)} %get-tuple-element.57), channel_id=1, source_target_pairs={{0,3},{1,2},{2,1},{3,0},{4,7},{5,6},{6,5},{7,4},{8,11},{9,10},{10,... | collective-permute-start | bytes 196616 | tf_op jit(solution)/shard_map/ppermute | solution.py:240
  25.5 0.3 %columns.3 = (bf16[256,512]{1,0:T(8,128)(2,1)S(1)}, bf16[256,512]{1,0:T(8,128)(2,1)S(1)}) custom-call(bf16[2048,128]{1,0:T(8,128)(2,1)S(1)} %bitcast.7), custom_call_target="tpu_custom_call" | custom-call | tf_op jit(solution)/shard_map/columns/pallas_call | solution.py:221
  25.8 0.3 %pair.1 = (f32[256,128]{1,0:T(8,128)S(1)}, f32[256,128]{1,0:T(8,128)S(1)}) custom-call(bf16[256,512]{1,0:T(8,128)(2,1)S(1)} %get-tuple-element.59.own, bf16[256,512]{1,0:T(8,128)(2,1)S(1)} %get-tuple-element.60.other, bf16[128,512]{1,0:T(8,128)(2,1)S(1)} %get-tuple-element.61.own_left, bf16[128,512]{1,0:T(8,128)(2,1)S(1)} %get-tuple-element.62.other_left, ...), custom_call_target="tpu_custom_call" | custom-call | flops 67108864 | bytes 1310720 | tf_op jit(solution)/shard_map/pair/pallas_call | solution.py:221
  26.1 2.2 %collective-permute-done.14.gradient = bf16[256,128]{1,0:T(8,128)(2,1)S(1)} collective-permute-done((bf16[256,128]{1,0:T(8,128)(2,1)S(1)}, bf16[256,128]{1,0:T(8,128)(2,1)S(1)}, u32[]{:S(2)}, u32[]{:S(2)}) %collective-permute-start.14) | collective-permute-done | bytes 65568 | tf_op jit(solution)/shard_map/ppermute | solution.py:240
  28.3 0.7 %shrink.1 = f32[256,128]{1,0:T(8,128)} custom-call(f32[256,128]{1,0:T(8,128)S(1)} %get-tuple-element.63.total, f32[256,128]{1,0:T(8,128)S(1)} %get-tuple-element.64.difference, bf16[256,128]{1,0:T(8,128)(2,1)S(1)} %collective-permute-done.14.gradient), custom_call_target="tpu_custom_call" | custom-call | tf_op jit(solution)/shard_map/shrink/pallas_call | solution.py:221
  (21 shorter events, 0.1 us)
Async XLA Ops:
  0.0 2.3 %copy-start.2 = (bf16[1,256,8,128]{3,2,1,0:T(8,128)(2,1)S(1)}, bf16[1,256,8,128]{3,2,1,0:T(8,128)(2,1)}, u32[]{:S(2)}) copy-start(bf16[1,256,8,128]{3,2,1,0:T(8,128)(2,1)} %param.5) | copy-start | bytes 1572868
  1.8 1.4 %collective-permute-start = (bf16[4,64,128]{2,1,0:T(8,128)(2,1)S(1)}, bf16[4,64,128]{2,1,0:T(8,128)(2,1)S(1)}, u32[]{:S(2)}, u32[]{:S(2)}) collective-permute-start(bf16[4,64,128]{2,1,0:T(8,128)(2,1)S(1)} %get-tuple-element.36), channel_id=1, source_target_pairs={{0,2},{2,0},{4,6},{6,4},{8,10},{10,8},{12,14},{14,12},{16,18},{18,... | collective-permute-start | bytes 196616 | tf_op jit(solution)/shard_map/ppermute | solution.py:234
  2.3 7.4 %collective-permute-start.4 = (bf16[2048,128]{1,0:T(8,128)(2,1)S(1)}, bf16[2048,128]{1,0:T(8,128)(2,1)S(1)}, u32[]{:S(2)}, u32[]{:S(2)}) collective-permute-start(bf16[2048,128]{1,0:T(8,128)(2,1)S(1)} %bitcast.10), channel_id=1, source_target_pairs={{0,2},{2,0},{4,6},{6,4},{8,10},{10,8},{12,14},{14,12},{16,18},{18,... | collective-permute-start | bytes 1572872 | tf_op jit(solution)/shard_map/ppermute | solution.py:234
  3.2 6.5 %copy-start.1 = (f32[1,256,128]{2,1,0:T(8,128)S(1)}, f32[1,256,128]{2,1,0:T(8,128)}, u32[]{:S(2)}) copy-start(f32[1,256,128]{2,1,0:T(8,128)} %param.9) | copy-start | bytes 393220
  3.2 6.5 %copy-start.3 = (f32[1,256,128]{2,1,0:T(8,128)S(1)}, f32[1,256,128]{2,1,0:T(8,128)}, u32[]{:S(2)}) copy-start(f32[1,256,128]{2,1,0:T(8,128)} %param.8) | copy-start | bytes 393220
  3.3 6.5 %copy-start.4 = (s32[1,8,8]{2,1,0:T(8,128)S(1)}, s32[1,8,8]{2,1,0:T(8,128)}, u32[]{:S(2)}) copy-start(s32[1,8,8]{2,1,0:T(8,128)} %ranks.1) | copy-start | bytes 772
  3.3 7.5 %collective-permute-start.3 = (bf16[64,128]{1,0:T(8,128)(2,1)S(1)}, bf16[64,128]{1,0:T(8,128)(2,1)S(1)}, u32[]{:S(2)}, u32[]{:S(2)}) collective-permute-start(bf16[64,128]{1,0:T(8,128)(2,1)S(1)} %get-tuple-element.39), channel_id=1, source_target_pairs={{0,26},{2,28},{4,30},{6,24},{8,18},{10,20},{12,22},{14,16},{16,10}... | collective-permute-start | bytes 49160 | tf_op jit(solution)/shard_map/ppermute | solution.py:252
  8.0 5.0 %collective-permute-start.5 = (bf16[64,128]{1,0:T(8,128)(2,1)S(1)}, bf16[64,128]{1,0:T(8,128)(2,1)S(1)}, u32[]{:S(2)}, u32[]{:S(2)}) collective-permute-start(bf16[64,128]{1,0:T(8,128)(2,1)S(1)} %get-tuple-element.46), channel_id=1, source_target_pairs={{0,18},{2,20},{4,22},{6,16},{8,26},{10,28},{12,30},{14,24},{16,2},... | collective-permute-start | bytes 49160 | tf_op jit(solution)/shard_map/ppermute | solution.py:252
  8.4 4.9 %collective-permute-start.1 = (bf16[64,128]{1,0:T(8,128)(2,1)S(1)}, bf16[64,128]{1,0:T(8,128)(2,1)S(1)}, u32[]{:S(2)}, u32[]{:S(2)}) collective-permute-start(bf16[64,128]{1,0:T(8,128)(2,1)S(1)} %get-tuple-element.37), channel_id=1, source_target_pairs={{0,6},{2,12},{4,2},{6,8},{8,14},{10,4},{12,10},{14,0},{16,22},{18,... | collective-permute-start | bytes 49160 | tf_op jit(solution)/shard_map/ppermute | solution.py:252
  9.5 3.8 %collective-permute-start.2 = (bf16[64,128]{1,0:T(8,128)(2,1)S(1)}, bf16[64,128]{1,0:T(8,128)(2,1)S(1)}, u32[]{:S(2)}, u32[]{:S(2)}) collective-permute-start(bf16[64,128]{1,0:T(8,128)(2,1)S(1)} %get-tuple-element.38), channel_id=1, source_target_pairs={{0,2},{2,8},{4,6},{6,12},{8,10},{10,0},{12,14},{14,4},{16,18},{18,... | collective-permute-start | bytes 49160 | tf_op jit(solution)/shard_map/ppermute | solution.py:252
  9.7 1.1 %copy-start = (bf16[1,256,8,128]{3,2,1,0:T(8,128)(2,1)S(1)}, bf16[1,256,8,128]{3,2,1,0:T(8,128)(2,1)}, u32[]{:S(2)}) copy-start(bf16[1,256,8,128]{3,2,1,0:T(8,128)(2,1)} %param.6) | copy-start | bytes 1572868
  10.8 9.7 %collective-permute-start.8 = (bf16[2048,128]{1,0:T(8,128)(2,1)S(1)}, bf16[2048,128]{1,0:T(8,128)(2,1)S(1)}, u32[]{:S(2)}, u32[]{:S(2)}) collective-permute-start(bf16[2048,128]{1,0:T(8,128)(2,1)S(1)} %bitcast.6), channel_id=1, source_target_pairs={{0,2},{2,0},{4,6},{6,4},{8,10},{10,8},{12,14},{14,12},{16,18},{18,... | collective-permute-start | bytes 1572872 | tf_op jit(solution)/shard_map/ppermute | solution.py:234
  13.5 2.0 %collective-permute-start.6 = (f32[128,512]{1,0:T(8,128)S(1)}, f32[128,512]{1,0:T(8,128)S(1)}, u32[]{:S(2)}, u32[]{:S(2)}) collective-permute-start(f32[128,512]{1,0:T(8,128)S(1)} %image.1.here), channel_id=1, source_target_pairs={{0,2},{2,0},{4,6},{6,4},{8,10},{10,8},{12,14},{14,12},{16,18},{18,... | collective-permute-start | bytes 786440 | tf_op jit(solution)/shard_map/ppermute | solution.py:234
  13.9 7.6 %collective-permute-start.9 = (f32[256,128]{1,0:T(8,128)S(1)}, f32[256,128]{1,0:T(8,128)S(1)}, u32[]{:S(2)}, u32[]{:S(2)}) collective-permute-start(f32[256,128]{1,0:T(8,128)S(1)} %get-tuple-element.51.here), channel_id=1, source_target_pairs={{0,1},{1,0},{2,3},{3,2},{4,5},{5,4},{6,7},{7,6},{8,9},{9,8},{10,11... | collective-permute-start | bytes 393224 | tf_op jit(solution)/shard_map/ppermute | solution.py:306
  15.8 5.7 %collective-permute-start.7 = (bf16[64,128]{1,0:T(8,128)(2,1)S(1)}, bf16[64,128]{1,0:T(8,128)(2,1)S(1)}, u32[]{:S(2)}, u32[]{:S(2)}) collective-permute-start(bf16[64,128]{1,0:T(8,128)(2,1)S(1)} %get-tuple-element.47), channel_id=1, source_target_pairs={{0,30},{2,24},{4,26},{6,28},{8,22},{10,16},{12,18},{14,20},{16,14}... | collective-permute-start | bytes 49160 | tf_op jit(solution)/shard_map/ppermute | solution.py:252
  18.2 4.1 %collective-permute-start.10 = (bf16[64,128]{1,0:T(8,128)(2,1)S(1)}, bf16[64,128]{1,0:T(8,128)(2,1)S(1)}, u32[]{:S(2)}, u32[]{:S(2)}) collective-permute-start(bf16[64,128]{1,0:T(8,128)(2,1)S(1)} %get-tuple-element.53), channel_id=1, source_target_pairs={{0,22},{2,16},{4,18},{6,20},{8,30},{10,24},{12,26},{14,28},{16,6},... | collective-permute-start | bytes 49160 | tf_op jit(solution)/shard_map/ppermute | solution.py:252
  18.4 3.9 %collective-permute-start.11 = (bf16[64,128]{1,0:T(8,128)(2,1)S(1)}, bf16[64,128]{1,0:T(8,128)(2,1)S(1)}, u32[]{:S(2)}, u32[]{:S(2)}) collective-permute-start(bf16[64,128]{1,0:T(8,128)(2,1)S(1)} %get-tuple-element.54), channel_id=1, source_target_pairs={{0,14},{2,4},{4,10},{6,0},{8,6},{10,12},{12,2},{14,8},{16,30},{18,... | collective-permute-start | bytes 49160 | tf_op jit(solution)/shard_map/ppermute | solution.py:252
  20.5 2.1 %collective-permute-start.12 = (bf16[64,128]{1,0:T(8,128)(2,1)S(1)}, bf16[64,128]{1,0:T(8,128)(2,1)S(1)}, u32[]{:S(2)}, u32[]{:S(2)}) collective-permute-start(bf16[64,128]{1,0:T(8,128)(2,1)S(1)} %get-tuple-element.55), channel_id=1, source_target_pairs={{0,10},{2,0},{4,14},{6,4},{8,2},{10,8},{12,6},{14,12},{16,26},{18,... | collective-permute-start | bytes 49160 | tf_op jit(solution)/shard_map/ppermute | solution.py:252
  22.6 1.3 %collective-permute-start.13 = (bf16[4,64,128]{2,1,0:T(8,128)(2,1)S(1)}, bf16[4,64,128]{2,1,0:T(8,128)(2,1)S(1)}, u32[]{:S(2)}, u32[]{:S(2)}) collective-permute-start(bf16[4,64,128]{2,1,0:T(8,128)(2,1)S(1)} %pack.1.blocks), channel_id=1, source_target_pairs={{0,2},{2,0},{4,6},{6,4},{8,10},{10,8},{12,14},{14,12},{16,18},{18,... | collective-permute-start | bytes 196616 | tf_op jit(solution)/shard_map/ppermute | solution.py:234
  24.2 4.1 %collective-permute-start.14 = (bf16[256,128]{1,0:T(8,128)(2,1)S(1)}, bf16[256,128]{1,0:T(8,128)(2,1)S(1)}, u32[]{:S(2)}, u32[]{:S(2)}) collective-permute-start(bf16[256,128]{1,0:T(8,128)(2,1)S(1)} %get-tuple-element.57), channel_id=1, source_target_pairs={{0,3},{1,2},{2,1},{3,0},{4,7},{5,6},{6,5},{7,4},{8,11},{9,10},{10,... | collective-permute-start | bytes 196616 | tf_op jit(solution)/shard_map/ppermute | solution.py:240

commit v16 on v15

--- a/solution.py
+++ b/solution.py
@@ -13,7 +13,7 @@
 LANES = 128
 VMEM_LIMIT = 32 * 1024 * 1024
 FIRST_LIMIT = 55050 * 1024
-PIECES = 8
+PIECES = 4
 HIDE = 128
 F32 = jnp.float32
 BF16 = jnp.bfloat16
@@ -63,10 +63,16 @@
     pick(wide, target, chosen, masks)
 
 
-def adjoint_block(product, tile):
-    half = product.shape[0] // 2
-    real, imaginary = product[:half, columns_of(tile)], product[half:, columns_of(tile)]
-    return (real * signs(half) + pltpu.roll(imaginary, LANES // 2, 1)).astype(BF16)
+def adjoint_blocks(values, factors):
+    half = values.shape[0] // 2
+    pair = 2 * LANES
+    blocks = []
+    for at in range(0, factors.shape[1], pair):
+        product = jnp.dot(values, factors[:, at : at + pair], preferred_element_type=F32)
+        for lanes in (slice(0, LANES), slice(LANES, pair)):
+            real, imaginary = product[:half, lanes], product[half:, lanes]
+            blocks.append((real * signs(half) + pltpu.roll(imaginary, LANES // 2, 1)).astype(BF16))
+    return blocks
 
 
 def spread_block(block, left, tile):
@@ -80,7 +86,7 @@
     return lax.dot_general(left, right, (((1,), (1,)), ((), ())), preferred_element_type=F32)
 
 
-def forward_kernel(shifts, start, factors, keep, give, start_here, factors_here, wide, separated, product, sems):
+def forward_kernel(shifts, start, factors, keep, give, start_here, factors_here, wide, separated, blocks, sems):
     pieces = sems.shape[0] - 1
     rows, columns = separated.shape
     tiles = columns // LANES
@@ -99,10 +105,11 @@
         separate(
             factors_here.at[at], wide.at[at], separated.at[pl.ds(piece * (rows // pieces), rows // pieces)], range(tiles)
         )
-    product[...] = jnp.dot(values, separated[...], preferred_element_type=F32)
+    for tile, block in enumerate(adjoint_blocks(values, separated)):
+        blocks[tile] = block
     for out, chosen in zip((keep, give), both_shifts(shifts)):
         for index, tile in enumerate(chosen):
-            out[index] = adjoint_block(product, tile)
+            out[index] = blocks[tile]
 
 
 def add_kernel(keep, arrived, *outs):
@@ -144,16 +151,15 @@
     misfit[...] = early[...] + times_transposed(left[...], factors[:, -left.shape[1] :])
 
 
-def back_kernel(here, there, factors, *refs):
-    outs, products = refs[:-1], refs[-1]
+def back_kernel(here, there, factors, *outs):
     rows = here.shape[1] // 2
+    parts = []
     for side in range(2):
         at, other = pl.ds(side * rows, rows), pl.ds((1 - side) * rows, rows)
         misfit = (here[:, at] + there[:, other]).astype(BF16)
-        products[side] = jnp.dot(misfit, factors[at, :], preferred_element_type=F32)
-    for index, out in enumerate(outs):
-        parts = [adjoint_block(products.at[side], index).astype(F32) for side in range(2)]
-        out[...] = (parts[0] + parts[1]).astype(BF16)
+        parts.append(adjoint_blocks(misfit, factors.at[at]))
+    for out, first, second in zip(outs, *parts):
+        out[...] = (first.astype(F32) + second.astype(F32)).astype(BF16)
 
 
 def pack_kernel(*refs):
@@ -284,7 +290,7 @@
             pltpu.VMEM(right_rows.shape, BF16),
             wide,
             pltpu.VMEM((rows, columns), BF16),
-            pltpu.VMEM((sources, columns), F32),
+            pltpu.VMEM((tiles, sources // 2, width), BF16),
             pltpu.SemaphoreType.DMA((PIECES + 1,)),
         ],
         flops,
@@ -329,8 +335,7 @@
         "back",
         [block] * members,
         [misfit, to_mate(misfit), both_left],
-        [pltpu.VMEM((2, sources, members * width), F32)],
-        flops,
+        flops=flops,
     )
     (own,) = call(pack_kernel, "pack", [blocks], exchange(sends, shifts[::-1], [*mate_right, *starts[1:]]))
     spread = shape(sources, members * width)

time: 29.1 us -> 29 us (level)
  no operation moved by 1% of the time
where the time goes in v16:
time: 29 us; the launch traced here: 28.9 us
  starting transfers between devices  16.5 us (57%)
  waiting for transfers between devices  6.41 us (22%)
  Pallas kernels  5.87 us (20%)
    ppermute x8, starting transfers between devices, exchange(): arrived.append(lax.ppermute(send, 'tile', pairs))  11.8 us
    pallas_call x13, Pallas kernels, call(): pl.pallas_call(kernel, out_shape=outs, in_specs=[pl.BlockSpec(memory_spac...  5.87 us
    ppermute x8, waiting for transfers between devices, exchange(): arrived.append(lax.ppermute(send, 'tile', pairs))  2.69 us
    ppermute x1, waiting for transfers between devices, across(): return lax.ppermute(value, ('tile', 'freq'), pairs)  2.15 us
    ppermute x5, starting transfers between devices, to_mate(): lax.ppermute(value, 'tile', [(i, i ^ 1) for i in range(lax.axis_size('til...  1.83 us
    ppermute x5, waiting for transfers between devices, to_mate(): lax.ppermute(value, 'tile', [(i, i ^ 1) for i in range(lax.axis_size('til...  1.56 us
    ppermute x1, starting transfers between devices, body(): lax.ppermute(start, 'freq', [(f, (f - shift) % band) for f in range(band)])  1.52 us
    ppermute x1, starting transfers between devices, across(): return lax.ppermute(value, ('tile', 'freq'), pairs)  1.33 us
  transfers between devices with their start and end apart: 15, of which 6 were waited for; matrix products, arithmetic and copies ran while one was open for 0% of the time, Pallas kernels for 11%

profile of v16, /device:TPU:0, one launch (start us, length us, event | category | flops | bytes accessed | tf_op | source)
XLA Modules:
  0.0 28.9 jit_solution(10256789023373510083)
XLA Ops:
  0.0 1.7 %forward.1 = (bf16[4,64,128]{2,1,0:T(8,128)(2,1)S(1)}, bf16[4,64,128]{2,1,0:T(8,128)(2,1)S(1)}) custom-call(f32[256,128]{1,0:T(8,128)} %bitcast.8, bf16[2048,128]{1,0:T(8,128)(2,1)} %bitcast.5), custom_call_target="tpu_custom_call" | custom-call | flops 67108864 | bytes 786432 | tf_op jit(solution)/shard_map/forward/pallas_call | solution.py:227
  1.7 0.5 %collective-permute-start = (bf16[4,64,128]{2,1,0:T(8,128)(2,1)S(1)}, bf16[4,64,128]{2,1,0:T(8,128)(2,1)S(1)}, u32[]{:S(2)}, u32[]{:S(2)}) collective-permute-start(bf16[4,64,128]{2,1,0:T(8,128)(2,1)S(1)} %get-tuple-element.36), channel_id=1, source_target_pairs={{0,2},{2,0},{4,6},{6,4},{8,10},{10,8},{12,14},{14,12},{16,18},{18,... | collective-permute-start | bytes 196616 | tf_op jit(solution)/shard_map/ppermute | solution.py:240
  2.2 0.1 collective-permute-start.4
  2.3 0.8 %collective-permute-done.arrived = bf16[4,64,128]{2,1,0:T(8,128)(2,1)S(1)} collective-permute-done((bf16[4,64,128]{2,1,0:T(8,128)(2,1)S(1)}, bf16[4,64,128]{2,1,0:T(8,128)(2,1)S(1)}, u32[]{:S(2)}, u32[]{:S(2)}) %collective-permute-start) | collective-permute-done | bytes 65568 | tf_op jit(solution)/shard_map/ppermute | solution.py:240
  3.2 4.8 %collective-permute-start.3 = (bf16[64,128]{1,0:T(8,128)(2,1)S(1)}, bf16[64,128]{1,0:T(8,128)(2,1)S(1)}, u32[]{:S(2)}, u32[]{:S(2)}) collective-permute-start(bf16[64,128]{1,0:T(8,128)(2,1)S(1)} %get-tuple-element.39), channel_id=1, source_target_pairs={{0,26},{2,28},{4,30},{6,24},{8,18},{10,20},{12,22},{14,16},{16,10}... | collective-permute-start | bytes 49160 | tf_op jit(solution)/shard_map/ppermute | solution.py:258
  7.9 0.3 %collective-permute-start.5 = (bf16[64,128]{1,0:T(8,128)(2,1)S(1)}, bf16[64,128]{1,0:T(8,128)(2,1)S(1)}, u32[]{:S(2)}, u32[]{:S(2)}) collective-permute-start(bf16[64,128]{1,0:T(8,128)(2,1)S(1)} %get-tuple-element.46), channel_id=1, source_target_pairs={{0,18},{2,20},{4,22},{6,16},{8,26},{10,28},{12,30},{14,24},{16,2},... | collective-permute-start | bytes 49160 | tf_op jit(solution)/shard_map/ppermute | solution.py:258
  8.3 1.1 %collective-permute-start.1 = (bf16[64,128]{1,0:T(8,128)(2,1)S(1)}, bf16[64,128]{1,0:T(8,128)(2,1)S(1)}, u32[]{:S(2)}, u32[]{:S(2)}) collective-permute-start(bf16[64,128]{1,0:T(8,128)(2,1)S(1)} %get-tuple-element.37), channel_id=1, source_target_pairs={{0,6},{2,12},{4,2},{6,8},{8,14},{10,4},{12,10},{14,0},{16,22},{18,... | collective-permute-start | bytes 49160 | tf_op jit(solution)/shard_map/ppermute | solution.py:258
  9.4 0.2 collective-permute-start.2
  9.6 1.1 %rows.1 = (bf16[512,512]{1,0:T(8,128)(2,1)S(1)}, f32[128,256]{1,0:T(8,128)S(1)}, f32[256,128]{1,0:T(8,128)S(1)}) custom-call(s32[1,8,8]{2,1,0:T(8,128)S(1)} %copy-done.4, bf16[2048,128]{1,0:T(8,128)(2,1)S(1)} %bitcast.11, bf16[2048,128]{1,0:T(8,128)(2,1)S(1)} %collective-permute-done.4.mate, f32[256,128]{1,0:T(8,128)S(1)} %bitcast.12, f32[256,128]{1,0:T(8,128)S(1)} %bitcast.9), custom_call_target="tpu_custom_call" | custom-call | tf_op jit(solution)/shard_map/rows/pallas_call | solution.py:227
  10.7 0.6 %collective-permute-start.8 = (bf16[2048,128]{1,0:T(8,128)(2,1)S(1)}, bf16[2048,128]{1,0:T(8,128)(2,1)S(1)}, u32[]{:S(2)}, u32[]{:S(2)}) collective-permute-start(bf16[2048,128]{1,0:T(8,128)(2,1)S(1)} %bitcast.6), channel_id=1, source_target_pairs={{0,2},{2,0},{4,6},{6,4},{8,10},{10,8},{12,14},{14,12},{16,18},{18,... | collective-permute-start | bytes 1572872 | tf_op jit(solution)/shard_map/ppermute | solution.py:240
  11.3 1.6 %collective-permute-done.5.second = bf16[64,128]{1,0:T(8,128)(2,1)S(1)} collective-permute-done((bf16[64,128]{1,0:T(8,128)(2,1)S(1)}, bf16[64,128]{1,0:T(8,128)(2,1)S(1)}, u32[]{:S(2)}, u32[]{:S(2)}) %collective-permute-start.5) | collective-permute-done | bytes 16416 | tf_op jit(solution)/shard_map/ppermute | solution.py:258
  12.9 0.2 early.1.refs_2_
  13.1 0.2 image.1.here
  13.4 0.4 %collective-permute-start.6 = (f32[128,512]{1,0:T(8,128)S(1)}, f32[128,512]{1,0:T(8,128)S(1)}, u32[]{:S(2)}, u32[]{:S(2)}) collective-permute-start(f32[128,512]{1,0:T(8,128)S(1)} %image.1.here), channel_id=1, source_target_pairs={{0,2},{2,0},{4,6},{6,4},{8,10},{10,8},{12,14},{14,12},{16,18},{18,... | collective-permute-start | bytes 786440 | tf_op jit(solution)/shard_map/ppermute | solution.py:240
  13.8 1.5 %collective-permute-start.9 = (f32[256,128]{1,0:T(8,128)S(1)}, f32[256,128]{1,0:T(8,128)S(1)}, u32[]{:S(2)}, u32[]{:S(2)}) collective-permute-start(f32[256,128]{1,0:T(8,128)S(1)} %get-tuple-element.51.here), channel_id=1, source_target_pairs={{0,1},{1,0},{2,3},{3,2},{4,5},{5,4},{6,7},{7,6},{8,9},{9,8},{10,11... | collective-permute-start | bytes 393224 | tf_op jit(solution)/shard_map/ppermute | solution.py:312
  15.4 0.3 %back.1 = (bf16[64,128]{1,0:T(8,128)(2,1)S(1)}, bf16[64,128]{1,0:T(8,128)(2,1)S(1)}, bf16[64,128]{1,0:T(8,128)(2,1)S(1)}, bf16[64,128]{1,0:T(8,128)(2,1)S(1)}) custom-call(f32[128,512]{1,0:T(8,128)S(1)} %image.1.here, f32[128,512]{1,0:T(8,128)S(1)} %collective-permute-done.6.there, bf16[512,512]{1,0:T(8,128)(2,1)S(1)} %get-tuple-element.43.factors.refs_3_), custom_call_target="tpu_custom_call" | custom-call | flops 67108864 | bytes 1114112 | tf_op jit(solution)/shard_map/back/pallas_call | solution.py:227
  15.7 2.3 %collective-permute-start.7 = (bf16[64,128]{1,0:T(8,128)(2,1)S(1)}, bf16[64,128]{1,0:T(8,128)(2,1)S(1)}, u32[]{:S(2)}, u32[]{:S(2)}) collective-permute-start(bf16[64,128]{1,0:T(8,128)(2,1)S(1)} %get-tuple-element.47), channel_id=1, source_target_pairs={{0,30},{2,24},{4,26},{6,28},{8,22},{10,16},{12,18},{14,20},{16,14}... | collective-permute-start | bytes 49160 | tf_op jit(solution)/shard_map/ppermute | solution.py:258
  18.0 0.2 collective-permute-start.10
  18.3 2.1 %collective-permute-start.11 = (bf16[64,128]{1,0:T(8,128)(2,1)S(1)}, bf16[64,128]{1,0:T(8,128)(2,1)S(1)}, u32[]{:S(2)}, u32[]{:S(2)}) collective-permute-start(bf16[64,128]{1,0:T(8,128)(2,1)S(1)} %get-tuple-element.54), channel_id=1, source_target_pairs={{0,14},{2,4},{4,10},{6,0},{8,6},{10,12},{12,2},{14,8},{16,30},{18,... | collective-permute-start | bytes 49160 | tf_op jit(solution)/shard_map/ppermute | solution.py:258
  20.4 0.7 %collective-permute-start.12 = (bf16[64,128]{1,0:T(8,128)(2,1)S(1)}, bf16[64,128]{1,0:T(8,128)(2,1)S(1)}, u32[]{:S(2)}, u32[]{:S(2)}) collective-permute-start(bf16[64,128]{1,0:T(8,128)(2,1)S(1)} %get-tuple-element.55), channel_id=1, source_target_pairs={{0,10},{2,0},{4,14},{6,4},{8,2},{10,8},{12,6},{14,12},{16,26},{18,... | collective-permute-start | bytes 49160 | tf_op jit(solution)/shard_map/ppermute | solution.py:258
  21.0 0.3 %columns.2 = (bf16[256,512]{1,0:T(8,128)(2,1)S(1)}, bf16[256,512]{1,0:T(8,128)(2,1)S(1)}) custom-call(bf16[2048,128]{1,0:T(8,128)(2,1)S(1)} %collective-permute-done.8.factors), custom_call_target="tpu_custom_call" | custom-call | tf_op jit(solution)/shard_map/columns/pallas_call | solution.py:227
  21.4 0.7 %collective-permute-done.10.refs_1_ = bf16[64,128]{1,0:T(8,128)(2,1)S(1)} collective-permute-done((bf16[64,128]{1,0:T(8,128)(2,1)S(1)}, bf16[64,128]{1,0:T(8,128)(2,1)S(1)}, u32[]{:S(2)}, u32[]{:S(2)}) %collective-permute-start.10) | collective-permute-done | bytes 16416 | tf_op jit(solution)/shard_map/ppermute | solution.py:258
  22.1 0.4 %collective-permute-done.12.refs_3_ = bf16[64,128]{1,0:T(8,128)(2,1)S(1)} collective-permute-done((bf16[64,128]{1,0:T(8,128)(2,1)S(1)}, bf16[64,128]{1,0:T(8,128)(2,1)S(1)}, u32[]{:S(2)}, u32[]{:S(2)}) %collective-permute-start.12) | collective-permute-done | bytes 16416 | tf_op jit(solution)/shard_map/ppermute | solution.py:258
  22.5 0.2 collective-permute-start.13
  22.7 0.3 %part.1 = (f32[256,128]{1,0:T(8,128)S(1)}, bf16[128,512]{1,0:T(8,128)(2,1)S(1)}) custom-call(bf16[4,64,128]{2,1,0:T(8,128)(2,1)S(1)} %pack.1.blocks, bf16[256,512]{1,0:T(8,128)(2,1)S(1)} %get-tuple-element.49.factors), custom_call_target="tpu_custom_call" | custom-call | flops 33554432 | bytes 589824 | tf_op jit(solution)/shard_map/part/pallas_call | solution.py:227
  23.0 0.7 %collective-permute-done.13.blocks = bf16[4,64,128]{2,1,0:T(8,128)(2,1)S(1)} collective-permute-done((bf16[4,64,128]{2,1,0:T(8,128)(2,1)S(1)}, bf16[4,64,128]{2,1,0:T(8,128)(2,1)S(1)}, u32[]{:S(2)}, u32[]{:S(2)}) %collective-permute-start.13) | collective-permute-done | bytes 65568 | tf_op jit(solution)/shard_map/ppermute | solution.py:240
  23.8 0.3 gradient.1
  24.0 1.3 %collective-permute-start.14 = (bf16[256,128]{1,0:T(8,128)(2,1)S(1)}, bf16[256,128]{1,0:T(8,128)(2,1)S(1)}, u32[]{:S(2)}, u32[]{:S(2)}) collective-permute-start(bf16[256,128]{1,0:T(8,128)(2,1)S(1)} %get-tuple-element.57), channel_id=1, source_target_pairs={{0,3},{1,2},{2,1},{3,0},{4,7},{5,6},{6,5},{7,4},{8,11},{9,10},{10,... | collective-permute-start | bytes 196616 | tf_op jit(solution)/shard_map/ppermute | solution.py:246
  25.4 0.3 %columns.3 = (bf16[256,512]{1,0:T(8,128)(2,1)S(1)}, bf16[256,512]{1,0:T(8,128)(2,1)S(1)}) custom-call(bf16[2048,128]{1,0:T(8,128)(2,1)S(1)} %bitcast.7), custom_call_target="tpu_custom_call" | custom-call | tf_op jit(solution)/shard_map/columns/pallas_call | solution.py:227
  25.7 0.3 %pair.1 = (f32[256,128]{1,0:T(8,128)S(1)}, f32[256,128]{1,0:T(8,128)S(1)}) custom-call(bf16[256,512]{1,0:T(8,128)(2,1)S(1)} %get-tuple-element.59.own, bf16[256,512]{1,0:T(8,128)(2,1)S(1)} %get-tuple-element.60.other, bf16[128,512]{1,0:T(8,128)(2,1)S(1)} %get-tuple-element.61.own_left, bf16[128,512]{1,0:T(8,128)(2,1)S(1)} %get-tuple-element.62.other_left, ...), custom_call_target="tpu_custom_call" | custom-call | flops 67108864 | bytes 1310720 | tf_op jit(solution)/shard_map/pair/pallas_call | solution.py:227
  26.0 2.2 %collective-permute-done.14.gradient = bf16[256,128]{1,0:T(8,128)(2,1)S(1)} collective-permute-done((bf16[256,128]{1,0:T(8,128)(2,1)S(1)}, bf16[256,128]{1,0:T(8,128)(2,1)S(1)}, u32[]{:S(2)}, u32[]{:S(2)}) %collective-permute-start.14) | collective-permute-done | bytes 65568 | tf_op jit(solution)/shard_map/ppermute | solution.py:246
  28.2 0.7 %shrink.1 = f32[256,128]{1,0:T(8,128)} custom-call(f32[256,128]{1,0:T(8,128)S(1)} %get-tuple-element.63.total, f32[256,128]{1,0:T(8,128)S(1)} %get-tuple-element.64.difference, bf16[256,128]{1,0:T(8,128)(2,1)S(1)} %collective-permute-done.14.gradient), custom_call_target="tpu_custom_call" | custom-call | tf_op jit(solution)/shard_map/shrink/pallas_call | solution.py:227
  (21 shorter events, 0.1 us)
Async XLA Ops:
  0.0 2.2 %copy-start.2 = (bf16[1,256,8,128]{3,2,1,0:T(8,128)(2,1)S(1)}, bf16[1,256,8,128]{3,2,1,0:T(8,128)(2,1)}, u32[]{:S(2)}) copy-start(bf16[1,256,8,128]{3,2,1,0:T(8,128)(2,1)} %param.5) | copy-start | bytes 1572868
  1.7 1.4 %collective-permute-start = (bf16[4,64,128]{2,1,0:T(8,128)(2,1)S(1)}, bf16[4,64,128]{2,1,0:T(8,128)(2,1)S(1)}, u32[]{:S(2)}, u32[]{:S(2)}) collective-permute-start(bf16[4,64,128]{2,1,0:T(8,128)(2,1)S(1)} %get-tuple-element.36), channel_id=1, source_target_pairs={{0,2},{2,0},{4,6},{6,4},{8,10},{10,8},{12,14},{14,12},{16,18},{18,... | collective-permute-start | bytes 196616 | tf_op jit(solution)/shard_map/ppermute | solution.py:240
  2.2 7.4 %collective-permute-start.4 = (bf16[2048,128]{1,0:T(8,128)(2,1)S(1)}, bf16[2048,128]{1,0:T(8,128)(2,1)S(1)}, u32[]{:S(2)}, u32[]{:S(2)}) collective-permute-start(bf16[2048,128]{1,0:T(8,128)(2,1)S(1)} %bitcast.10), channel_id=1, source_target_pairs={{0,2},{2,0},{4,6},{6,4},{8,10},{10,8},{12,14},{14,12},{16,18},{18,... | collective-permute-start | bytes 1572872 | tf_op jit(solution)/shard_map/ppermute | solution.py:240
  3.1 6.5 %copy-start.1 = (f32[1,256,128]{2,1,0:T(8,128)S(1)}, f32[1,256,128]{2,1,0:T(8,128)}, u32[]{:S(2)}) copy-start(f32[1,256,128]{2,1,0:T(8,128)} %param.9) | copy-start | bytes 393220
  3.1 6.5 %copy-start.3 = (f32[1,256,128]{2,1,0:T(8,128)S(1)}, f32[1,256,128]{2,1,0:T(8,128)}, u32[]{:S(2)}) copy-start(f32[1,256,128]{2,1,0:T(8,128)} %param.8) | copy-start | bytes 393220
  3.2 6.5 %copy-start.4 = (s32[1,8,8]{2,1,0:T(8,128)S(1)}, s32[1,8,8]{2,1,0:T(8,128)}, u32[]{:S(2)}) copy-start(s32[1,8,8]{2,1,0:T(8,128)} %ranks.1) | copy-start | bytes 772
  3.2 7.5 %collective-permute-start.3 = (bf16[64,128]{1,0:T(8,128)(2,1)S(1)}, bf16[64,128]{1,0:T(8,128)(2,1)S(1)}, u32[]{:S(2)}, u32[]{:S(2)}) collective-permute-start(bf16[64,128]{1,0:T(8,128)(2,1)S(1)} %get-tuple-element.39), channel_id=1, source_target_pairs={{0,26},{2,28},{4,30},{6,24},{8,18},{10,20},{12,22},{14,16},{16,10}... | collective-permute-start | bytes 49160 | tf_op jit(solution)/shard_map/ppermute | solution.py:258
  7.9 5.0 %collective-permute-start.5 = (bf16[64,128]{1,0:T(8,128)(2,1)S(1)}, bf16[64,128]{1,0:T(8,128)(2,1)S(1)}, u32[]{:S(2)}, u32[]{:S(2)}) collective-permute-start(bf16[64,128]{1,0:T(8,128)(2,1)S(1)} %get-tuple-element.46), channel_id=1, source_target_pairs={{0,18},{2,20},{4,22},{6,16},{8,26},{10,28},{12,30},{14,24},{16,2},... | collective-permute-start | bytes 49160 | tf_op jit(solution)/shard_map/ppermute | solution.py:258
  8.3 4.9 %collective-permute-start.1 = (bf16[64,128]{1,0:T(8,128)(2,1)S(1)}, bf16[64,128]{1,0:T(8,128)(2,1)S(1)}, u32[]{:S(2)}, u32[]{:S(2)}) collective-permute-start(bf16[64,128]{1,0:T(8,128)(2,1)S(1)} %get-tuple-element.37), channel_id=1, source_target_pairs={{0,6},{2,12},{4,2},{6,8},{8,14},{10,4},{12,10},{14,0},{16,22},{18,... | collective-permute-start | bytes 49160 | tf_op jit(solution)/shard_map/ppermute | solution.py:258
  9.4 3.8 %collective-permute-start.2 = (bf16[64,128]{1,0:T(8,128)(2,1)S(1)}, bf16[64,128]{1,0:T(8,128)(2,1)S(1)}, u32[]{:S(2)}, u32[]{:S(2)}) collective-permute-start(bf16[64,128]{1,0:T(8,128)(2,1)S(1)} %get-tuple-element.38), channel_id=1, source_target_pairs={{0,2},{2,8},{4,6},{6,12},{8,10},{10,0},{12,14},{14,4},{16,18},{18,... | collective-permute-start | bytes 49160 | tf_op jit(solution)/shard_map/ppermute | solution.py:258
  9.6 1.1 %copy-start = (bf16[1,256,8,128]{3,2,1,0:T(8,128)(2,1)S(1)}, bf16[1,256,8,128]{3,2,1,0:T(8,128)(2,1)}, u32[]{:S(2)}) copy-start(bf16[1,256,8,128]{3,2,1,0:T(8,128)(2,1)} %param.6) | copy-start | bytes 1572868
  10.7 9.6 %collective-permute-start.8 = (bf16[2048,128]{1,0:T(8,128)(2,1)S(1)}, bf16[2048,128]{1,0:T(8,128)(2,1)S(1)}, u32[]{:S(2)}, u32[]{:S(2)}) collective-permute-start(bf16[2048,128]{1,0:T(8,128)(2,1)S(1)} %bitcast.6), channel_id=1, source_target_pairs={{0,2},{2,0},{4,6},{6,4},{8,10},{10,8},{12,14},{14,12},{16,18},{18,... | collective-permute-start | bytes 1572872 | tf_op jit(solution)/shard_map/ppermute | solution.py:240
  13.4 2.0 %collective-permute-start.6 = (f32[128,512]{1,0:T(8,128)S(1)}, f32[128,512]{1,0:T(8,128)S(1)}, u32[]{:S(2)}, u32[]{:S(2)}) collective-permute-start(f32[128,512]{1,0:T(8,128)S(1)} %image.1.here), channel_id=1, source_target_pairs={{0,2},{2,0},{4,6},{6,4},{8,10},{10,8},{12,14},{14,12},{16,18},{18,... | collective-permute-start | bytes 786440 | tf_op jit(solution)/shard_map/ppermute | solution.py:240
  13.8 7.6 %collective-permute-start.9 = (f32[256,128]{1,0:T(8,128)S(1)}, f32[256,128]{1,0:T(8,128)S(1)}, u32[]{:S(2)}, u32[]{:S(2)}) collective-permute-start(f32[256,128]{1,0:T(8,128)S(1)} %get-tuple-element.51.here), channel_id=1, source_target_pairs={{0,1},{1,0},{2,3},{3,2},{4,5},{5,4},{6,7},{7,6},{8,9},{9,8},{10,11... | collective-permute-start | bytes 393224 | tf_op jit(solution)/shard_map/ppermute | solution.py:312
  15.7 5.7 %collective-permute-start.7 = (bf16[64,128]{1,0:T(8,128)(2,1)S(1)}, bf16[64,128]{1,0:T(8,128)(2,1)S(1)}, u32[]{:S(2)}, u32[]{:S(2)}) collective-permute-start(bf16[64,128]{1,0:T(8,128)(2,1)S(1)} %get-tuple-element.47), channel_id=1, source_target_pairs={{0,30},{2,24},{4,26},{6,28},{8,22},{10,16},{12,18},{14,20},{16,14}... | collective-permute-start | bytes 49160 | tf_op jit(solution)/shard_map/ppermute | solution.py:258
  18.0 4.1 %collective-permute-start.10 = (bf16[64,128]{1,0:T(8,128)(2,1)S(1)}, bf16[64,128]{1,0:T(8,128)(2,1)S(1)}, u32[]{:S(2)}, u32[]{:S(2)}) collective-permute-start(bf16[64,128]{1,0:T(8,128)(2,1)S(1)} %get-tuple-element.53), channel_id=1, source_target_pairs={{0,22},{2,16},{4,18},{6,20},{8,30},{10,24},{12,26},{14,28},{16,6},... | collective-permute-start | bytes 49160 | tf_op jit(solution)/shard_map/ppermute | solution.py:258
  18.3 3.9 %collective-permute-start.11 = (bf16[64,128]{1,0:T(8,128)(2,1)S(1)}, bf16[64,128]{1,0:T(8,128)(2,1)S(1)}, u32[]{:S(2)}, u32[]{:S(2)}) collective-permute-start(bf16[64,128]{1,0:T(8,128)(2,1)S(1)} %get-tuple-element.54), channel_id=1, source_target_pairs={{0,14},{2,4},{4,10},{6,0},{8,6},{10,12},{12,2},{14,8},{16,30},{18,... | collective-permute-start | bytes 49160 | tf_op jit(solution)/shard_map/ppermute | solution.py:258
  20.4 2.1 %collective-permute-start.12 = (bf16[64,128]{1,0:T(8,128)(2,1)S(1)}, bf16[64,128]{1,0:T(8,128)(2,1)S(1)}, u32[]{:S(2)}, u32[]{:S(2)}) collective-permute-start(bf16[64,128]{1,0:T(8,128)(2,1)S(1)} %get-tuple-element.55), channel_id=1, source_target_pairs={{0,10},{2,0},{4,14},{6,4},{8,2},{10,8},{12,6},{14,12},{16,26},{18,... | collective-permute-start | bytes 49160 | tf_op jit(solution)/shard_map/ppermute | solution.py:258
  22.5 1.3 %collective-permute-start.13 = (bf16[4,64,128]{2,1,0:T(8,128)(2,1)S(1)}, bf16[4,64,128]{2,1,0:T(8,128)(2,1)S(1)}, u32[]{:S(2)}, u32[]{:S(2)}) collective-permute-start(bf16[4,64,128]{2,1,0:T(8,128)(2,1)S(1)} %pack.1.blocks), channel_id=1, source_target_pairs={{0,2},{2,0},{4,6},{6,4},{8,10},{10,8},{12,14},{14,12},{16,18},{18,... | collective-permute-start | bytes 196616 | tf_op jit(solution)/shard_map/ppermute | solution.py:240
  24.0 4.1 %collective-permute-start.14 = (bf16[256,128]{1,0:T(8,128)(2,1)S(1)}, bf16[256,128]{1,0:T(8,128)(2,1)S(1)}, u32[]{:S(2)}, u32[]{:S(2)}) collective-permute-start(bf16[256,128]{1,0:T(8,128)(2,1)S(1)} %get-tuple-element.57), channel_id=1, source_target_pairs={{0,3},{1,2},{2,1},{3,0},{4,7},{5,6},{6,5},{7,4},{8,11},{9,10},{10,... | collective-permute-start | bytes 196616 | tf_op jit(solution)/shard_map/ppermute | solution.py:246

commit v17 on v16

--- a/solution.py
+++ b/solution.py
@@ -20,10 +20,8 @@
 
 
 def shifts_of(chips):
-    even = list(range(chips - 2, -1, -2))
-    odd = [shift + 1 for shift in even]
-    even[-2], odd[-1] = odd[-1], even[-2]
-    return [even, odd]
+    far = range(chips - 1, 3, -1)
+    return [[*[shift for shift in far if shift % 2], 1, 0], [*[shift for shift in far if shift % 2 == 0], 3, 2]]
 
 
 def place():

time: 29 us -> 28.9 us (level)
  waiting for transfers between devices: 6.41 us -> 6.07 us
  transfers between devices with their start and end apart: 15 -> 15, of which waited for: 6 -> 7; matrix products, arithmetic and copies ran while one was open for 0% -> 0% of each run, Pallas kernels for 11% -> 11%
where the time goes in v17:
time: 28.9 us; the launch traced here: 28.7 us
  starting transfers between devices  16.6 us (57%)
  waiting for transfers between devices  6.07 us (21%)
  Pallas kernels  5.87 us (20%)
    ppermute x8, starting transfers between devices, exchange(): arrived.append(lax.ppermute(send, 'tile', pairs))  11.7 us
    pallas_call x13, Pallas kernels, call(): pl.pallas_call(kernel, out_shape=outs, in_specs=[pl.BlockSpec(memory_spac...  5.87 us
    ppermute x8, waiting for transfers between devices, exchange(): arrived.append(lax.ppermute(send, 'tile', pairs))  2.7 us
    ppermute x5, starting transfers between devices, to_mate(): lax.ppermute(value, 'tile', [(i, i ^ 1) for i in range(lax.axis_size('til...  1.97 us
    ppermute x1, waiting for transfers between devices, across(): return lax.ppermute(value, ('tile', 'freq'), pairs)  1.94 us
    ppermute x1, starting transfers between devices, body(): lax.ppermute(start, 'freq', [(f, (f - shift) % band) for f in range(band)])  1.52 us
    ppermute x5, waiting for transfers between devices, to_mate(): lax.ppermute(value, 'tile', [(i, i ^ 1) for i in range(lax.axis_size('til...  1.42 us
    ppermute x1, starting transfers between devices, across(): return lax.ppermute(value, ('tile', 'freq'), pairs)  1.4 us
  transfers between devices with their start and end apart: 15, of which 7 were waited for; matrix products, arithmetic and copies ran while one was open for 0% of the time, Pallas kernels for 11%

profile of v17, /device:TPU:0, one launch (start us, length us, event | category | flops | bytes accessed | tf_op | source)
XLA Modules:
  0.0 28.7 jit_solution(4828550540027930777)
XLA Ops:
  0.0 1.7 %forward.1 = (bf16[4,64,128]{2,1,0:T(8,128)(2,1)S(1)}, bf16[4,64,128]{2,1,0:T(8,128)(2,1)S(1)}) custom-call(f32[256,128]{1,0:T(8,128)} %bitcast.8, bf16[2048,128]{1,0:T(8,128)(2,1)} %bitcast.5), custom_call_target="tpu_custom_call" | custom-call | flops 67108864 | bytes 786432 | tf_op jit(solution)/shard_map/forward/pallas_call | solution.py:225
  1.7 0.5 %collective-permute-start = (bf16[4,64,128]{2,1,0:T(8,128)(2,1)S(1)}, bf16[4,64,128]{2,1,0:T(8,128)(2,1)S(1)}, u32[]{:S(2)}, u32[]{:S(2)}) collective-permute-start(bf16[4,64,128]{2,1,0:T(8,128)(2,1)S(1)} %get-tuple-element.36), channel_id=1, source_target_pairs={{0,2},{2,0},{4,6},{6,4},{8,10},{10,8},{12,14},{14,12},{16,18},{18,... | collective-permute-start | bytes 196616 | tf_op jit(solution)/shard_map/ppermute | solution.py:238
  2.2 0.1 collective-permute-start.4
  2.3 0.8 %collective-permute-done.arrived = bf16[4,64,128]{2,1,0:T(8,128)(2,1)S(1)} collective-permute-done((bf16[4,64,128]{2,1,0:T(8,128)(2,1)S(1)}, bf16[4,64,128]{2,1,0:T(8,128)(2,1)S(1)}, u32[]{:S(2)}, u32[]{:S(2)}) %collective-permute-start) | collective-permute-done | bytes 65568 | tf_op jit(solution)/shard_map/ppermute | solution.py:238
  3.2 5.7 %collective-permute-start.3 = (bf16[64,128]{1,0:T(8,128)(2,1)S(1)}, bf16[64,128]{1,0:T(8,128)(2,1)S(1)}, u32[]{:S(2)}, u32[]{:S(2)}) collective-permute-start(bf16[64,128]{1,0:T(8,128)(2,1)S(1)} %get-tuple-element.39), channel_id=1, source_target_pairs={{0,30},{2,24},{4,26},{6,28},{8,22},{10,16},{12,18},{14,20},{16,14}... | collective-permute-start | bytes 49160 | tf_op jit(solution)/shard_map/ppermute | solution.py:256
  8.9 0.5 %collective-permute-start.1 = (bf16[64,128]{1,0:T(8,128)(2,1)S(1)}, bf16[64,128]{1,0:T(8,128)(2,1)S(1)}, u32[]{:S(2)}, u32[]{:S(2)}) collective-permute-start(bf16[64,128]{1,0:T(8,128)(2,1)S(1)} %get-tuple-element.37), channel_id=1, source_target_pairs={{0,6},{2,12},{4,2},{6,8},{8,14},{10,4},{12,10},{14,0},{16,22},{18,... | collective-permute-start | bytes 49160 | tf_op jit(solution)/shard_map/ppermute | solution.py:256
  9.4 0.2 collective-permute-start.2
  9.6 1.1 %rows.1 = (bf16[512,512]{1,0:T(8,128)(2,1)S(1)}, f32[128,256]{1,0:T(8,128)S(1)}, f32[256,128]{1,0:T(8,128)S(1)}) custom-call(s32[1,8,8]{2,1,0:T(8,128)S(1)} %copy-done.4, bf16[2048,128]{1,0:T(8,128)(2,1)S(1)} %bitcast.11, bf16[2048,128]{1,0:T(8,128)(2,1)S(1)} %collective-permute-done.4.mate, f32[256,128]{1,0:T(8,128)S(1)} %bitcast.12, f32[256,128]{1,0:T(8,128)S(1)} %bitcast.9), custom_call_target="tpu_custom_call" | custom-call | tf_op jit(solution)/shard_map/rows/pallas_call | solution.py:225
  10.7 0.6 %collective-permute-start.8 = (bf16[2048,128]{1,0:T(8,128)(2,1)S(1)}, bf16[2048,128]{1,0:T(8,128)(2,1)S(1)}, u32[]{:S(2)}, u32[]{:S(2)}) collective-permute-start(bf16[2048,128]{1,0:T(8,128)(2,1)S(1)} %bitcast.6), channel_id=1, source_target_pairs={{0,2},{2,0},{4,6},{6,4},{8,10},{10,8},{12,14},{14,12},{16,18},{18,... | collective-permute-start | bytes 1572872 | tf_op jit(solution)/shard_map/ppermute | solution.py:238
  11.3 1.6 %collective-permute-done.5.second = bf16[64,128]{1,0:T(8,128)(2,1)S(1)} collective-permute-done((bf16[64,128]{1,0:T(8,128)(2,1)S(1)}, bf16[64,128]{1,0:T(8,128)(2,1)S(1)}, u32[]{:S(2)}, u32[]{:S(2)}) %collective-permute-start.5) | collective-permute-done | bytes 16416 | tf_op jit(solution)/shard_map/ppermute | solution.py:256
  12.9 0.2 early.1.refs_2_
  13.2 0.2 image.1.here
  13.4 0.4 %collective-permute-start.6 = (f32[128,512]{1,0:T(8,128)S(1)}, f32[128,512]{1,0:T(8,128)S(1)}, u32[]{:S(2)}, u32[]{:S(2)}) collective-permute-start(f32[128,512]{1,0:T(8,128)S(1)} %image.1.here), channel_id=1, source_target_pairs={{0,2},{2,0},{4,6},{6,4},{8,10},{10,8},{12,14},{14,12},{16,18},{18,... | collective-permute-start | bytes 786440 | tf_op jit(solution)/shard_map/ppermute | solution.py:238
  13.8 1.5 %collective-permute-start.9 = (f32[256,128]{1,0:T(8,128)S(1)}, f32[256,128]{1,0:T(8,128)S(1)}, u32[]{:S(2)}, u32[]{:S(2)}) collective-permute-start(f32[256,128]{1,0:T(8,128)S(1)} %get-tuple-element.51.here), channel_id=1, source_target_pairs={{0,1},{1,0},{2,3},{3,2},{4,5},{5,4},{6,7},{7,6},{8,9},{9,8},{10,11... | collective-permute-start | bytes 393224 | tf_op jit(solution)/shard_map/ppermute | solution.py:310
  15.3 0.3 %back.1 = (bf16[64,128]{1,0:T(8,128)(2,1)S(1)}, bf16[64,128]{1,0:T(8,128)(2,1)S(1)}, bf16[64,128]{1,0:T(8,128)(2,1)S(1)}, bf16[64,128]{1,0:T(8,128)(2,1)S(1)}) custom-call(f32[128,512]{1,0:T(8,128)S(1)} %image.1.here, f32[128,512]{1,0:T(8,128)S(1)} %collective-permute-done.6.there, bf16[512,512]{1,0:T(8,128)(2,1)S(1)} %get-tuple-element.43.factors.refs_3_), custom_call_target="tpu_custom_call" | custom-call | flops 67108864 | bytes 1114112 | tf_op jit(solution)/shard_map/back/pallas_call | solution.py:225
  15.7 1.5 %collective-permute-start.7 = (bf16[64,128]{1,0:T(8,128)(2,1)S(1)}, bf16[64,128]{1,0:T(8,128)(2,1)S(1)}, u32[]{:S(2)}, u32[]{:S(2)}) collective-permute-start(bf16[64,128]{1,0:T(8,128)(2,1)S(1)} %get-tuple-element.47), channel_id=1, source_target_pairs={{0,26},{2,28},{4,30},{6,24},{8,18},{10,20},{12,22},{14,16},{16,10}... | collective-permute-start | bytes 49160 | tf_op jit(solution)/shard_map/ppermute | solution.py:256
  17.1 0.8 %collective-permute-start.10 = (bf16[64,128]{1,0:T(8,128)(2,1)S(1)}, bf16[64,128]{1,0:T(8,128)(2,1)S(1)}, u32[]{:S(2)}, u32[]{:S(2)}) collective-permute-start(bf16[64,128]{1,0:T(8,128)(2,1)S(1)} %get-tuple-element.53), channel_id=1, source_target_pairs={{0,18},{2,20},{4,22},{6,16},{8,26},{10,28},{12,30},{14,24},{16,2},... | collective-permute-start | bytes 49160 | tf_op jit(solution)/shard_map/ppermute | solution.py:256
  17.9 2.4 %collective-permute-start.11 = (bf16[64,128]{1,0:T(8,128)(2,1)S(1)}, bf16[64,128]{1,0:T(8,128)(2,1)S(1)}, u32[]{:S(2)}, u32[]{:S(2)}) collective-permute-start(bf16[64,128]{1,0:T(8,128)(2,1)S(1)} %get-tuple-element.54), channel_id=1, source_target_pairs={{0,14},{2,4},{4,10},{6,0},{8,6},{10,12},{12,2},{14,8},{16,30},{18,... | collective-permute-start | bytes 49160 | tf_op jit(solution)/shard_map/ppermute | solution.py:256
  20.3 0.7 %collective-permute-start.12 = (bf16[64,128]{1,0:T(8,128)(2,1)S(1)}, bf16[64,128]{1,0:T(8,128)(2,1)S(1)}, u32[]{:S(2)}, u32[]{:S(2)}) collective-permute-start(bf16[64,128]{1,0:T(8,128)(2,1)S(1)} %get-tuple-element.55), channel_id=1, source_target_pairs={{0,10},{2,0},{4,14},{6,4},{8,2},{10,8},{12,6},{14,12},{16,26},{18,... | collective-permute-start | bytes 49160 | tf_op jit(solution)/shard_map/ppermute | solution.py:256
  21.0 0.3 %columns.2 = (bf16[256,512]{1,0:T(8,128)(2,1)S(1)}, bf16[256,512]{1,0:T(8,128)(2,1)S(1)}) custom-call(bf16[2048,128]{1,0:T(8,128)(2,1)S(1)} %collective-permute-done.8.factors), custom_call_target="tpu_custom_call" | custom-call | tf_op jit(solution)/shard_map/columns/pallas_call | solution.py:225
  21.4 0.2 collective-permute-done.7.refs_0_
  21.6 0.5 %collective-permute-done.10.refs_1_ = bf16[64,128]{1,0:T(8,128)(2,1)S(1)} collective-permute-done((bf16[64,128]{1,0:T(8,128)(2,1)S(1)}, bf16[64,128]{1,0:T(8,128)(2,1)S(1)}, u32[]{:S(2)}, u32[]{:S(2)}) %collective-permute-start.10) | collective-permute-done | bytes 16416 | tf_op jit(solution)/shard_map/ppermute | solution.py:256
  22.1 0.4 %collective-permute-done.12.refs_3_ = bf16[64,128]{1,0:T(8,128)(2,1)S(1)} collective-permute-done((bf16[64,128]{1,0:T(8,128)(2,1)S(1)}, bf16[64,128]{1,0:T(8,128)(2,1)S(1)}, u32[]{:S(2)}, u32[]{:S(2)}) %collective-permute-start.12) | collective-permute-done | bytes 16416 | tf_op jit(solution)/shard_map/ppermute | solution.py:256
  22.5 0.4 %collective-permute-start.13 = (bf16[4,64,128]{2,1,0:T(8,128)(2,1)S(1)}, bf16[4,64,128]{2,1,0:T(8,128)(2,1)S(1)}, u32[]{:S(2)}, u32[]{:S(2)}) collective-permute-start(bf16[4,64,128]{2,1,0:T(8,128)(2,1)S(1)} %pack.1.blocks), channel_id=1, source_target_pairs={{0,2},{2,0},{4,6},{6,4},{8,10},{10,8},{12,14},{14,12},{16,18},{18,... | collective-permute-start | bytes 196616 | tf_op jit(solution)/shard_map/ppermute | solution.py:238
  22.8 0.3 %part.1 = (f32[256,128]{1,0:T(8,128)S(1)}, bf16[128,512]{1,0:T(8,128)(2,1)S(1)}) custom-call(bf16[4,64,128]{2,1,0:T(8,128)(2,1)S(1)} %pack.1.blocks, bf16[256,512]{1,0:T(8,128)(2,1)S(1)} %get-tuple-element.49.factors), custom_call_target="tpu_custom_call" | custom-call | flops 33554432 | bytes 589824 | tf_op jit(solution)/shard_map/part/pallas_call | solution.py:225
  23.1 0.6 %collective-permute-done.13.blocks = bf16[4,64,128]{2,1,0:T(8,128)(2,1)S(1)} collective-permute-done((bf16[4,64,128]{2,1,0:T(8,128)(2,1)S(1)}, bf16[4,64,128]{2,1,0:T(8,128)(2,1)S(1)}, u32[]{:S(2)}, u32[]{:S(2)}) %collective-permute-start.13) | collective-permute-done | bytes 65568 | tf_op jit(solution)/shard_map/ppermute | solution.py:238
  23.7 0.3 %gradient.1 = (bf16[256,128]{1,0:T(8,128)(2,1)S(1)}, bf16[128,512]{1,0:T(8,128)(2,1)S(1)}) custom-call(f32[256,128]{1,0:T(8,128)S(1)} %get-tuple-element.56.part, bf16[4,64,128]{2,1,0:T(8,128)(2,1)S(1)} %collective-permute-done.13.blocks, bf16[256,512]{1,0:T(8,128)(2,1)S(1)} %get-tuple-element.50.factors), custom_call_target="tpu_custom_call" | custom-call | flops 33554432 | bytes 655360 | tf_op jit(solution)/shard_map/gradient/pallas_call | solution.py:225
  24.0 1.4 %collective-permute-start.14 = (bf16[256,128]{1,0:T(8,128)(2,1)S(1)}, bf16[256,128]{1,0:T(8,128)(2,1)S(1)}, u32[]{:S(2)}, u32[]{:S(2)}) collective-permute-start(bf16[256,128]{1,0:T(8,128)(2,1)S(1)} %get-tuple-element.57), channel_id=1, source_target_pairs={{0,3},{1,2},{2,1},{3,0},{4,7},{5,6},{6,5},{7,4},{8,11},{9,10},{10,... | collective-permute-start | bytes 196616 | tf_op jit(solution)/shard_map/ppermute | solution.py:244
  25.4 0.3 %columns.3 = (bf16[256,512]{1,0:T(8,128)(2,1)S(1)}, bf16[256,512]{1,0:T(8,128)(2,1)S(1)}) custom-call(bf16[2048,128]{1,0:T(8,128)(2,1)S(1)} %bitcast.7), custom_call_target="tpu_custom_call" | custom-call | tf_op jit(solution)/shard_map/columns/pallas_call | solution.py:225
  25.8 0.3 %pair.1 = (f32[256,128]{1,0:T(8,128)S(1)}, f32[256,128]{1,0:T(8,128)S(1)}) custom-call(bf16[256,512]{1,0:T(8,128)(2,1)S(1)} %get-tuple-element.59.own, bf16[256,512]{1,0:T(8,128)(2,1)S(1)} %get-tuple-element.60.other, bf16[128,512]{1,0:T(8,128)(2,1)S(1)} %get-tuple-element.61.own_left, bf16[128,512]{1,0:T(8,128)(2,1)S(1)} %get-tuple-element.62.other_left, ...), custom_call_target="tpu_custom_call" | custom-call | flops 67108864 | bytes 1310720 | tf_op jit(solution)/shard_map/pair/pallas_call | solution.py:225
  26.1 1.9 %collective-permute-done.14.gradient = bf16[256,128]{1,0:T(8,128)(2,1)S(1)} collective-permute-done((bf16[256,128]{1,0:T(8,128)(2,1)S(1)}, bf16[256,128]{1,0:T(8,128)(2,1)S(1)}, u32[]{:S(2)}, u32[]{:S(2)}) %collective-permute-start.14) | collective-permute-done | bytes 65568 | tf_op jit(solution)/shard_map/ppermute | solution.py:244
  28.0 0.7 %shrink.1 = f32[256,128]{1,0:T(8,128)} custom-call(f32[256,128]{1,0:T(8,128)S(1)} %get-tuple-element.63.total, f32[256,128]{1,0:T(8,128)S(1)} %get-tuple-element.64.difference, bf16[256,128]{1,0:T(8,128)(2,1)S(1)} %collective-permute-done.14.gradient), custom_call_target="tpu_custom_call" | custom-call | tf_op jit(solution)/shard_map/shrink/pallas_call | solution.py:225
  (21 shorter events, 0.1 us)
Async XLA Ops:
  0.0 2.2 %copy-start.2 = (bf16[1,256,8,128]{3,2,1,0:T(8,128)(2,1)S(1)}, bf16[1,256,8,128]{3,2,1,0:T(8,128)(2,1)}, u32[]{:S(2)}) copy-start(bf16[1,256,8,128]{3,2,1,0:T(8,128)(2,1)} %param.5) | copy-start | bytes 1572868
  1.7 1.4 %collective-permute-start = (bf16[4,64,128]{2,1,0:T(8,128)(2,1)S(1)}, bf16[4,64,128]{2,1,0:T(8,128)(2,1)S(1)}, u32[]{:S(2)}, u32[]{:S(2)}) collective-permute-start(bf16[4,64,128]{2,1,0:T(8,128)(2,1)S(1)} %get-tuple-element.36), channel_id=1, source_target_pairs={{0,2},{2,0},{4,6},{6,4},{8,10},{10,8},{12,14},{14,12},{16,18},{18,... | collective-permute-start | bytes 196616 | tf_op jit(solution)/shard_map/ppermute | solution.py:238
  2.2 7.3 %collective-permute-start.4 = (bf16[2048,128]{1,0:T(8,128)(2,1)S(1)}, bf16[2048,128]{1,0:T(8,128)(2,1)S(1)}, u32[]{:S(2)}, u32[]{:S(2)}) collective-permute-start(bf16[2048,128]{1,0:T(8,128)(2,1)S(1)} %bitcast.10), channel_id=1, source_target_pairs={{0,2},{2,0},{4,6},{6,4},{8,10},{10,8},{12,14},{14,12},{16,18},{18,... | collective-permute-start | bytes 1572872 | tf_op jit(solution)/shard_map/ppermute | solution.py:238
  3.1 6.5 %copy-start.1 = (f32[1,256,128]{2,1,0:T(8,128)S(1)}, f32[1,256,128]{2,1,0:T(8,128)}, u32[]{:S(2)}) copy-start(f32[1,256,128]{2,1,0:T(8,128)} %param.9) | copy-start | bytes 393220
  3.1 6.5 %copy-start.3 = (f32[1,256,128]{2,1,0:T(8,128)S(1)}, f32[1,256,128]{2,1,0:T(8,128)}, u32[]{:S(2)}) copy-start(f32[1,256,128]{2,1,0:T(8,128)} %param.8) | copy-start | bytes 393220
  3.2 6.4 %copy-start.4 = (s32[1,8,8]{2,1,0:T(8,128)S(1)}, s32[1,8,8]{2,1,0:T(8,128)}, u32[]{:S(2)}) copy-start(s32[1,8,8]{2,1,0:T(8,128)} %ranks.1) | copy-start | bytes 772
  3.2 7.5 %collective-permute-start.3 = (bf16[64,128]{1,0:T(8,128)(2,1)S(1)}, bf16[64,128]{1,0:T(8,128)(2,1)S(1)}, u32[]{:S(2)}, u32[]{:S(2)}) collective-permute-start(bf16[64,128]{1,0:T(8,128)(2,1)S(1)} %get-tuple-element.39), channel_id=1, source_target_pairs={{0,30},{2,24},{4,26},{6,28},{8,22},{10,16},{12,18},{14,20},{16,14}... | collective-permute-start | bytes 49160 | tf_op jit(solution)/shard_map/ppermute | solution.py:256
  8.9 4.1 %collective-permute-start.5 = (bf16[64,128]{1,0:T(8,128)(2,1)S(1)}, bf16[64,128]{1,0:T(8,128)(2,1)S(1)}, u32[]{:S(2)}, u32[]{:S(2)}) collective-permute-start(bf16[64,128]{1,0:T(8,128)(2,1)S(1)} %get-tuple-element.46), channel_id=1, source_target_pairs={{0,22},{2,16},{4,18},{6,20},{8,30},{10,24},{12,26},{14,28},{16,6},... | collective-permute-start | bytes 49160 | tf_op jit(solution)/shard_map/ppermute | solution.py:256
  8.9 4.3 %collective-permute-start.1 = (bf16[64,128]{1,0:T(8,128)(2,1)S(1)}, bf16[64,128]{1,0:T(8,128)(2,1)S(1)}, u32[]{:S(2)}, u32[]{:S(2)}) collective-permute-start(bf16[64,128]{1,0:T(8,128)(2,1)S(1)} %get-tuple-element.37), channel_id=1, source_target_pairs={{0,6},{2,12},{4,2},{6,8},{8,14},{10,4},{12,10},{14,0},{16,22},{18,... | collective-permute-start | bytes 49160 | tf_op jit(solution)/shard_map/ppermute | solution.py:256
  9.4 3.8 %collective-permute-start.2 = (bf16[64,128]{1,0:T(8,128)(2,1)S(1)}, bf16[64,128]{1,0:T(8,128)(2,1)S(1)}, u32[]{:S(2)}, u32[]{:S(2)}) collective-permute-start(bf16[64,128]{1,0:T(8,128)(2,1)S(1)} %get-tuple-element.38), channel_id=1, source_target_pairs={{0,2},{2,8},{4,6},{6,12},{8,10},{10,0},{12,14},{14,4},{16,18},{18,... | collective-permute-start | bytes 49160 | tf_op jit(solution)/shard_map/ppermute | solution.py:256
  9.6 1.1 %copy-start = (bf16[1,256,8,128]{3,2,1,0:T(8,128)(2,1)S(1)}, bf16[1,256,8,128]{3,2,1,0:T(8,128)(2,1)}, u32[]{:S(2)}) copy-start(bf16[1,256,8,128]{3,2,1,0:T(8,128)(2,1)} %param.6) | copy-start | bytes 1572868
  10.7 9.6 %collective-permute-start.8 = (bf16[2048,128]{1,0:T(8,128)(2,1)S(1)}, bf16[2048,128]{1,0:T(8,128)(2,1)S(1)}, u32[]{:S(2)}, u32[]{:S(2)}) collective-permute-start(bf16[2048,128]{1,0:T(8,128)(2,1)S(1)} %bitcast.6), channel_id=1, source_target_pairs={{0,2},{2,0},{4,6},{6,4},{8,10},{10,8},{12,14},{14,12},{16,18},{18,... | collective-permute-start | bytes 1572872 | tf_op jit(solution)/shard_map/ppermute | solution.py:238
  13.4 1.9 %collective-permute-start.6 = (f32[128,512]{1,0:T(8,128)S(1)}, f32[128,512]{1,0:T(8,128)S(1)}, u32[]{:S(2)}, u32[]{:S(2)}) collective-permute-start(f32[128,512]{1,0:T(8,128)S(1)} %image.1.here), channel_id=1, source_target_pairs={{0,2},{2,0},{4,6},{6,4},{8,10},{10,8},{12,14},{14,12},{16,18},{18,... | collective-permute-start | bytes 786440 | tf_op jit(solution)/shard_map/ppermute | solution.py:238
  13.8 7.6 %collective-permute-start.9 = (f32[256,128]{1,0:T(8,128)S(1)}, f32[256,128]{1,0:T(8,128)S(1)}, u32[]{:S(2)}, u32[]{:S(2)}) collective-permute-start(f32[256,128]{1,0:T(8,128)S(1)} %get-tuple-element.51.here), channel_id=1, source_target_pairs={{0,1},{1,0},{2,3},{3,2},{4,5},{5,4},{6,7},{7,6},{8,9},{9,8},{10,11... | collective-permute-start | bytes 393224 | tf_op jit(solution)/shard_map/ppermute | solution.py:310
  15.7 5.9 %collective-permute-start.7 = (bf16[64,128]{1,0:T(8,128)(2,1)S(1)}, bf16[64,128]{1,0:T(8,128)(2,1)S(1)}, u32[]{:S(2)}, u32[]{:S(2)}) collective-permute-start(bf16[64,128]{1,0:T(8,128)(2,1)S(1)} %get-tuple-element.47), channel_id=1, source_target_pairs={{0,26},{2,28},{4,30},{6,24},{8,18},{10,20},{12,22},{14,16},{16,10}... | collective-permute-start | bytes 49160 | tf_op jit(solution)/shard_map/ppermute | solution.py:256
  17.1 5.0 %collective-permute-start.10 = (bf16[64,128]{1,0:T(8,128)(2,1)S(1)}, bf16[64,128]{1,0:T(8,128)(2,1)S(1)}, u32[]{:S(2)}, u32[]{:S(2)}) collective-permute-start(bf16[64,128]{1,0:T(8,128)(2,1)S(1)} %get-tuple-element.53), channel_id=1, source_target_pairs={{0,18},{2,20},{4,22},{6,16},{8,26},{10,28},{12,30},{14,24},{16,2},... | collective-permute-start | bytes 49160 | tf_op jit(solution)/shard_map/ppermute | solution.py:256
  17.9 4.1 %collective-permute-start.11 = (bf16[64,128]{1,0:T(8,128)(2,1)S(1)}, bf16[64,128]{1,0:T(8,128)(2,1)S(1)}, u32[]{:S(2)}, u32[]{:S(2)}) collective-permute-start(bf16[64,128]{1,0:T(8,128)(2,1)S(1)} %get-tuple-element.54), channel_id=1, source_target_pairs={{0,14},{2,4},{4,10},{6,0},{8,6},{10,12},{12,2},{14,8},{16,30},{18,... | collective-permute-start | bytes 49160 | tf_op jit(solution)/shard_map/ppermute | solution.py:256
  20.3 2.1 %collective-permute-start.12 = (bf16[64,128]{1,0:T(8,128)(2,1)S(1)}, bf16[64,128]{1,0:T(8,128)(2,1)S(1)}, u32[]{:S(2)}, u32[]{:S(2)}) collective-permute-start(bf16[64,128]{1,0:T(8,128)(2,1)S(1)} %get-tuple-element.55), channel_id=1, source_target_pairs={{0,10},{2,0},{4,14},{6,4},{8,2},{10,8},{12,6},{14,12},{16,26},{18,... | collective-permute-start | bytes 49160 | tf_op jit(solution)/shard_map/ppermute | solution.py:256
  22.5 1.3 %collective-permute-start.13 = (bf16[4,64,128]{2,1,0:T(8,128)(2,1)S(1)}, bf16[4,64,128]{2,1,0:T(8,128)(2,1)S(1)}, u32[]{:S(2)}, u32[]{:S(2)}) collective-permute-start(bf16[4,64,128]{2,1,0:T(8,128)(2,1)S(1)} %pack.1.blocks), channel_id=1, source_target_pairs={{0,2},{2,0},{4,6},{6,4},{8,10},{10,8},{12,14},{14,12},{16,18},{18,... | collective-permute-start | bytes 196616 | tf_op jit(solution)/shard_map/ppermute | solution.py:238
  24.0 4.0 %collective-permute-start.14 = (bf16[256,128]{1,0:T(8,128)(2,1)S(1)}, bf16[256,128]{1,0:T(8,128)(2,1)S(1)}, u32[]{:S(2)}, u32[]{:S(2)}) collective-permute-start(bf16[256,128]{1,0:T(8,128)(2,1)S(1)} %get-tuple-element.57), channel_id=1, source_target_pairs={{0,3},{1,2},{2,1},{3,0},{4,7},{5,6},{6,5},{7,4},{8,11},{9,10},{10,... | collective-permute-start | bytes 196616 | tf_op jit(solution)/shard_map/ppermute | solution.py:244

commit v18 on v17

--- a/solution.py
+++ b/solution.py
@@ -19,9 +19,31 @@
 BF16 = jnp.bfloat16
 
 
-def shifts_of(chips):
-    far = range(chips - 1, 3, -1)
-    return [[*[shift for shift in far if shift % 2], 1, 0], [*[shift for shift in far if shift % 2 == 0], 3, 2]]
+MEETINGS = {
+    8: [
+        [(0o77666677, 0o55555555), (0o11777711, 0o34444443), (0o66001166, 0o43333334), (0o00110000, 0o22222222)],
+        [(0o22555533, 0o77060677), (0o55223355, 0o16777761), (0o44444444, 0o61606016), (0o33332222, 0o00111100)],
+    ]
+}
+
+
+def routes_of(chips):
+    if chips in MEETINGS:
+        shifts = [
+            [[[packed >> 3 * chip & 7 for chip in range(chips)] for packed in pair] for pair in way]
+            for way in MEETINGS[chips]
+        ]
+    else:
+        far = range(chips - 1, 3, -1)
+        first = [*[shift for shift in far if shift % 2], 1, 0]
+        second = [*[shift for shift in far if shift % 2 == 0], 3, 2]
+        out = [[[shift] * chips for shift in pair] for pair in zip(first, second)]
+        shifts = [out, [pair[::-1] for pair in out]]
+    return [[[[chip ^ shift for chip, shift in enumerate(core)] for core in pair] for pair in way] for way in shifts]
+
+
+def arrivals_of(routes):
+    return [[[pair[1 - core].index(chip) for chip in range(len(pair[core]))] for core in range(2)] for pair in routes]
 
 
 def place():
@@ -33,12 +55,19 @@
     return pl.ds(pl.multiple_of(tile * LANES, LANES), LANES)
 
 
-def both_shifts(shifts):
+def entry(first, second):
     chip, core = place()
-    pairs = list(zip(*shifts))
-    own = [chip ^ jnp.where(core == 0, first, second) for first, second in pairs]
-    mate = [chip ^ jnp.where(core == 0, second, first) for first, second in pairs]
-    return own, mate
+    if len(set(first)) == 1 and len(set(second)) == 1:
+        return jnp.where(core == 0, first[0], second[0])
+    bits = max(*first, *second).bit_length()
+    first, second = [sum(value << bits * at for at, value in enumerate(values)) for values in (first, second)]
+    return jnp.where(core == 0, first, second) >> bits * chip & (1 << bits) - 1
+
+
+def both_tiles(routes):
+    chip, _ = place()
+    shifts = [[[at ^ other for at, other in enumerate(core)] for core in pair] for pair in routes]
+    return [chip ^ entry(*pair) for pair in shifts], [chip ^ entry(*pair[::-1]) for pair in shifts]
 
 
 def signs(rows):
@@ -84,7 +113,7 @@
     return lax.dot_general(left, right, (((1,), (1,)), ((), ())), preferred_element_type=F32)
 
 
-def forward_kernel(shifts, start, factors, keep, give, start_here, factors_here, wide, separated, blocks, sems):
+def forward_kernel(routes, start, factors, keep, give, start_here, factors_here, wide, separated, blocks, sems):
     pieces = sems.shape[0] - 1
     rows, columns = separated.shape
     tiles = columns // LANES
@@ -105,7 +134,7 @@
         )
     for tile, block in enumerate(adjoint_blocks(values, separated)):
         blocks[tile] = block
-    for out, chosen in zip((keep, give), both_shifts(shifts)):
+    for out, chosen in zip((keep, give), both_tiles(routes)):
         for index, tile in enumerate(chosen):
             out[index] = blocks[tile]
 
@@ -115,9 +144,9 @@
         out[...] = (keep[index].astype(F32) + arrived[index].astype(F32)).astype(BF16)
 
 
-def rows_kernel(shifts, ranks, own, mate, observed, start, both, turned, start_out, wide):
+def rows_kernel(arrivals, ranks, own, mate, observed, start, both, turned, start_out, wide):
     chip, _ = place()
-    _, chosen = both_shifts(shifts)
+    chosen, _ = both_tiles(arrivals)
     rows = both.shape[0] // 2
     lane = lax.broadcasted_iota(jnp.int32, (1, LANES), 1) % (LANES // 2)
     masks = [lane < ranks[0, chip, tile] for tile in chosen]
@@ -127,8 +156,8 @@
     start_out[...] = start[...]
 
 
-def columns_kernel(shifts, factors, own, other, wide):
-    chosen, rest = both_shifts(shifts)
+def columns_kernel(arrivals, factors, own, other, wide):
+    chosen, rest = both_tiles(arrivals)
     separate(factors, wide, own, chosen)
     pick(wide, other, rest)
 
@@ -149,15 +178,18 @@
     misfit[...] = early[...] + times_transposed(left[...], factors[:, -left.shape[1] :])
 
 
-def back_kernel(here, there, factors, *outs):
+def back_kernel(places, here, there, factors, *refs):
+    outs, blocks = refs[:-1], refs[-1]
     rows = here.shape[1] // 2
     parts = []
     for side in range(2):
         at, other = pl.ds(side * rows, rows), pl.ds((1 - side) * rows, rows)
         misfit = (here[:, at] + there[:, other]).astype(BF16)
         parts.append(adjoint_blocks(misfit, factors.at[at]))
-    for out, first, second in zip(outs, *parts):
-        out[...] = (first.astype(F32) + second.astype(F32)).astype(BF16)
+    for index, (first, second) in enumerate(zip(*parts)):
+        blocks[index] = (first.astype(F32) + second.astype(F32)).astype(BF16)
+    for out, pair in zip(outs, places):
+        out[...] = blocks[entry(*pair)]
 
 
 def pack_kernel(*refs):
@@ -248,12 +280,11 @@
     return lax.optimization_barrier((value, *others))[0]
 
 
-def exchange(sends, shifts, beside):
-    count = lax.axis_size("tile")
+def exchange(sends, routes, beside):
     arrived = []
-    for index, send in enumerate(sends):
-        pairs = [(i, i ^ 2 * shifts[i % 2][index] ^ 1) for i in range(count)]
-        arrived.append(lax.ppermute(send, "tile", pairs))
+    for send, pair in zip(sends, routes):
+        pairs = [(2 * at + core, 2 * to + 1 - core) for core in range(2) for at, to in enumerate(pair[core])]
+        arrived.append(lax.ppermute(send, "tile", sorted(pairs)))
     return [after(arrived[0], *beside), *arrived[1:]]
 
 
@@ -266,7 +297,15 @@
     right_rows = v_factors.reshape(rows * tiles, width)
     observed = observed.reshape(rows, sources)
     start = start.reshape(rows, sources)
-    shifts = shifts_of(tiles)
+    routes, back_routes = routes_of(tiles)
+    arrivals, back_arrivals = arrivals_of(routes), arrivals_of(back_routes)
+    places = [
+        [
+            [[came[core][chip] for came in arrivals].index(to) for chip, to in enumerate(pair[core])]
+            for core in range(2)
+        ]
+        for pair in back_routes
+    ]
 
     def shape(*dims, dtype=BF16):
         return jax.ShapeDtypeStruct(dims, dtype)
@@ -279,7 +318,7 @@
     flops = 2 * rows * columns * sources
 
     keep, give = call(
-        functools.partial(forward_kernel, shifts),
+        functools.partial(forward_kernel, routes),
         "forward",
         [blocks, blocks],
         [start, right_rows],
@@ -298,7 +337,7 @@
     sends = call(add_kernel, "add", [block] * members, [keep, to_mate(give)], flops=HIDE * flops)
     mate_left = to_mate(after(left_rows, give))
     both_left, turned, start = call(
-        functools.partial(rows_kernel, shifts),
+        functools.partial(rows_kernel, arrivals),
         "rows",
         [shape(2 * rows, members * width), shape(sources, rows, dtype=F32), shape(rows, sources, dtype=F32)],
         [ranks, after(left_rows, give), mate_left, after(observed, give), after(start, give)],
@@ -308,7 +347,7 @@
     starts = [start]
     for shift in range(1, band):
         starts.append(lax.ppermute(start, "freq", [(f, (f - shift) % band) for f in range(band)]))
-    arrived = exchange(sends, shifts, [both_left, turned])
+    arrived = exchange(sends, routes, [both_left, turned])
     misfit = shape(sources, 2 * rows, dtype=F32)
     (misfit_early,) = call(
         early_kernel,
@@ -327,15 +366,16 @@
         HIDE * flops,
     )
     mate_right = to_mate(after(right_rows, both_left))
-    mate_right = call(functools.partial(columns_kernel, shifts), "columns", [factor] * 2, [mate_right], [wide])
+    mate_right = call(functools.partial(columns_kernel, back_arrivals), "columns", [factor] * 2, [mate_right], [wide])
     sends = call(
-        back_kernel,
+        functools.partial(back_kernel, places),
         "back",
         [block] * members,
         [misfit, to_mate(misfit), both_left],
-        flops=flops,
-    )
-    (own,) = call(pack_kernel, "pack", [blocks], exchange(sends, shifts[::-1], [*mate_right, *starts[1:]]))
+        [pltpu.VMEM((members, sources // 2, width), BF16)],
+        flops,
+    )
+    (own,) = call(pack_kernel, "pack", [blocks], exchange(sends, back_routes, [*mate_right, *starts[1:]]))
     spread = shape(sources, members * width)
     part, own_left = call(
         part_kernel, "part", [shape(rows, sources, dtype=F32), spread], [own, mate_right[0]], flops=flops // 2
@@ -348,7 +388,7 @@
         flops=flops // 2,
     )
     right = call(
-        functools.partial(columns_kernel, shifts), "columns", [factor] * 2, [after(right_rows, gradient)], [wide]
+        functools.partial(columns_kernel, back_arrivals), "columns", [factor] * 2, [after(right_rows, gradient)], [wide]
     )
     gradients = []
     for shift in range(1, band):

time: 28.9 us -> 28.2 us (0.976)
  waiting for transfers between devices: 6.07 us -> 5.16 us
    ppermute x8, waiting for transfers between devices: 2.7 us -> 1.88 us  [exchange(): arrived.append(lax.ppermute(send, 'tile', sorted(pairs)))]
    ppermute x8, starting transfers between devices: 11.7 us -> 12.4 us  [exchange(): arrived.append(lax.ppermute(send, 'tile', sorted(pairs)))]
    ppermute x5, starting transfers between devices: 1.97 us -> 1.41 us  [to_mate(): lax.ppermute(value, 'tile', [(i, i ^ 1) for i in range(lax.axis_size('til...]
  transfers between devices with their start and end apart: 15 -> 15, of which waited for: 7 -> 6; matrix products, arithmetic and copies ran while one was open for 0% -> 0% of each run, Pallas kernels for 11% -> 11%
where the time goes in v18:
time: 28.2 us; the launch traced here: 28 us
  starting transfers between devices  16.8 us (60%)
  Pallas kernels  5.87 us (21%)
  waiting for transfers between devices  5.16 us (18%)
    ppermute x8, starting transfers between devices, exchange(): arrived.append(lax.ppermute(send, 'tile', sorted(pairs)))  12.4 us
    pallas_call x13, Pallas kernels, call(): pl.pallas_call(kernel, out_shape=outs, in_specs=[pl.BlockSpec(memory_spac...  5.87 us
    ppermute x8, waiting for transfers between devices, exchange(): arrived.append(lax.ppermute(send, 'tile', sorted(pairs)))  1.88 us
    ppermute x1, waiting for transfers between devices, across(): return lax.ppermute(value, ('tile', 'freq'), pairs)  1.85 us
    ppermute x1, starting transfers between devices, body(): lax.ppermute(start, 'freq', [(f, (f - shift) % band) for f in range(band)])  1.52 us
    ppermute x1, starting transfers between devices, across(): return lax.ppermute(value, ('tile', 'freq'), pairs)  1.48 us
    ppermute x5, waiting for transfers between devices, to_mate(): lax.ppermute(value, 'tile', [(i, i ^ 1) for i in range(lax.axis_size('til...  1.43 us
    ppermute x5, starting transfers between devices, to_mate(): lax.ppermute(value, 'tile', [(i, i ^ 1) for i in range(lax.axis_size('til...  1.41 us
  transfers between devices with their start and end apart: 15, of which 6 were waited for; matrix products, arithmetic and copies ran while one was open for 0% of the time, Pallas kernels for 11%

profile of v18, /device:TPU:0, one launch (start us, length us, event | category | flops | bytes accessed | tf_op | source)
XLA Modules:
  0.0 28.0 jit_solution(3199519943074411603)
XLA Ops:
  0.0 1.7 %forward.1 = (bf16[4,64,128]{2,1,0:T(8,128)(2,1)S(1)}, bf16[4,64,128]{2,1,0:T(8,128)(2,1)S(1)}) custom-call(f32[256,128]{1,0:T(8,128)} %bitcast.8, bf16[2048,128]{1,0:T(8,128)(2,1)} %bitcast.5), custom_call_target="tpu_custom_call" | custom-call | flops 67108864 | bytes 786432 | tf_op jit(solution)/shard_map/forward/pallas_call | solution.py:257
  1.7 0.5 %collective-permute-start = (bf16[4,64,128]{2,1,0:T(8,128)(2,1)S(1)}, bf16[4,64,128]{2,1,0:T(8,128)(2,1)S(1)}, u32[]{:S(2)}, u32[]{:S(2)}) collective-permute-start(bf16[4,64,128]{2,1,0:T(8,128)(2,1)S(1)} %get-tuple-element.36), channel_id=1, source_target_pairs={{0,2},{2,0},{4,6},{6,4},{8,10},{10,8},{12,14},{14,12},{16,18},{18,... | collective-permute-start | bytes 196616 | tf_op jit(solution)/shard_map/ppermute | solution.py:270
  2.2 0.1 collective-permute-start.4
  2.3 0.8 %collective-permute-done.arrived = bf16[4,64,128]{2,1,0:T(8,128)(2,1)S(1)} collective-permute-done((bf16[4,64,128]{2,1,0:T(8,128)(2,1)S(1)}, bf16[4,64,128]{2,1,0:T(8,128)(2,1)S(1)}, u32[]{:S(2)}, u32[]{:S(2)}) %collective-permute-start) | collective-permute-done | bytes 65568 | tf_op jit(solution)/shard_map/ppermute | solution.py:270
  3.2 0.0 copy-start.4
  3.2 5.7 %collective-permute-start.3 = (bf16[64,128]{1,0:T(8,128)(2,1)S(1)}, bf16[64,128]{1,0:T(8,128)(2,1)S(1)}, u32[]{:S(2)}, u32[]{:S(2)}) collective-permute-start(bf16[64,128]{1,0:T(8,128)(2,1)S(1)} %get-tuple-element.39), channel_id=1, source_target_pairs={{0,30},{2,20},{4,26},{6,16},{8,18},{10,28},{12,22},{14,24},{16,10}... | collective-permute-start | bytes 49160 | tf_op jit(solution)/shard_map/ppermute | solution.py:287
  8.9 0.7 %collective-permute-start.1 = (bf16[64,128]{1,0:T(8,128)(2,1)S(1)}, bf16[64,128]{1,0:T(8,128)(2,1)S(1)}, u32[]{:S(2)}, u32[]{:S(2)}) collective-permute-start(bf16[64,128]{1,0:T(8,128)(2,1)S(1)} %get-tuple-element.37), channel_id=1, source_target_pairs={{0,26},{2,16},{4,30},{6,8},{8,14},{10,4},{12,10},{14,0},{16,18},{1... | collective-permute-start | bytes 49160 | tf_op jit(solution)/shard_map/ppermute | solution.py:287
  9.6 1.4 %collective-permute-start.2 = (bf16[64,128]{1,0:T(8,128)(2,1)S(1)}, bf16[64,128]{1,0:T(8,128)(2,1)S(1)}, u32[]{:S(2)}, u32[]{:S(2)}) collective-permute-start(bf16[64,128]{1,0:T(8,128)(2,1)S(1)} %get-tuple-element.38), channel_id=1, source_target_pairs={{0,2},{2,8},{4,6},{6,12},{8,10},{10,0},{12,14},{14,4},{16,22},{18,... | collective-permute-start | bytes 49160 | tf_op jit(solution)/shard_map/ppermute | solution.py:287
  11.0 1.1 %rows.1 = (bf16[512,512]{1,0:T(8,128)(2,1)S(1)}, f32[128,256]{1,0:T(8,128)S(1)}, f32[256,128]{1,0:T(8,128)S(1)}) custom-call(s32[1,8,8]{2,1,0:T(8,128)S(1)} %copy-done.4, bf16[2048,128]{1,0:T(8,128)(2,1)S(1)} %bitcast.11, bf16[2048,128]{1,0:T(8,128)(2,1)S(1)} %collective-permute-done.4.mate, f32[256,128]{1,0:T(8,128)S(1)} %bitcast.12, f32[256,128]{1,0:T(8,128)S(1)} %bitcast.9), custom_call_target="tpu_custom_call" | custom-call | tf_op jit(solution)/shard_map/rows/pallas_call | solution.py:257
  12.1 0.1 collective-permute-start.8
  12.1 0.8 %collective-permute-done.5.second = bf16[64,128]{1,0:T(8,128)(2,1)S(1)} collective-permute-done((bf16[64,128]{1,0:T(8,128)(2,1)S(1)}, bf16[64,128]{1,0:T(8,128)(2,1)S(1)}, u32[]{:S(2)}, u32[]{:S(2)}) %collective-permute-start.5) | collective-permute-done | bytes 16416 | tf_op jit(solution)/shard_map/ppermute | solution.py:287
  12.9 0.2 early.1.refs_2_
  13.2 0.2 image.1.here
  13.4 0.4 %collective-permute-start.6 = (f32[128,512]{1,0:T(8,128)S(1)}, f32[128,512]{1,0:T(8,128)S(1)}, u32[]{:S(2)}, u32[]{:S(2)}) collective-permute-start(f32[128,512]{1,0:T(8,128)S(1)} %image.1.here), channel_id=1, source_target_pairs={{0,2},{2,0},{4,6},{6,4},{8,10},{10,8},{12,14},{14,12},{16,18},{18,... | collective-permute-start | bytes 786440 | tf_op jit(solution)/shard_map/ppermute | solution.py:270
  13.8 1.5 %collective-permute-start.9 = (f32[256,128]{1,0:T(8,128)S(1)}, f32[256,128]{1,0:T(8,128)S(1)}, u32[]{:S(2)}, u32[]{:S(2)}) collective-permute-start(f32[256,128]{1,0:T(8,128)S(1)} %get-tuple-element.51.here), channel_id=1, source_target_pairs={{0,1},{1,0},{2,3},{3,2},{4,5},{5,4},{6,7},{7,6},{8,9},{9,8},{10,11... | collective-permute-start | bytes 393224 | tf_op jit(solution)/shard_map/ppermute | solution.py:349
  15.3 0.3 %back.1 = (bf16[64,128]{1,0:T(8,128)(2,1)S(1)}, bf16[64,128]{1,0:T(8,128)(2,1)S(1)}, bf16[64,128]{1,0:T(8,128)(2,1)S(1)}, bf16[64,128]{1,0:T(8,128)(2,1)S(1)}) custom-call(f32[128,512]{1,0:T(8,128)S(1)} %image.1.here, f32[128,512]{1,0:T(8,128)S(1)} %collective-permute-done.6.there, bf16[512,512]{1,0:T(8,128)(2,1)S(1)} %get-tuple-element.43.factors.refs_3_), custom_call_target="tpu_custom_call" | custom-call | flops 67108864 | bytes 1114112 | tf_op jit(solution)/shard_map/back/pallas_call | solution.py:257
  15.7 0.4 %collective-permute-start.7 = (bf16[64,128]{1,0:T(8,128)(2,1)S(1)}, bf16[64,128]{1,0:T(8,128)(2,1)S(1)}, u32[]{:S(2)}, u32[]{:S(2)}) collective-permute-start(bf16[64,128]{1,0:T(8,128)(2,1)S(1)} %get-tuple-element.47), channel_id=1, source_target_pairs={{0,14},{2,28},{4,10},{6,24},{8,30},{10,16},{12,26},{14,12},{16,6},... | collective-permute-start | bytes 49160 | tf_op jit(solution)/shard_map/ppermute | solution.py:287
  16.1 2.1 %collective-permute-start.10 = (bf16[64,128]{1,0:T(8,128)(2,1)S(1)}, bf16[64,128]{1,0:T(8,128)(2,1)S(1)}, u32[]{:S(2)}, u32[]{:S(2)}) collective-permute-start(bf16[64,128]{1,0:T(8,128)(2,1)S(1)} %get-tuple-element.53), channel_id=1, source_target_pairs={{0,22},{2,4},{4,18},{6,28},{8,6},{10,20},{12,2},{14,16},{16,26},{1... | collective-permute-start | bytes 49160 | tf_op jit(solution)/shard_map/ppermute | solution.py:287
  18.2 1.8 %collective-permute-start.11 = (bf16[64,128]{1,0:T(8,128)(2,1)S(1)}, bf16[64,128]{1,0:T(8,128)(2,1)S(1)}, u32[]{:S(2)}, u32[]{:S(2)}) collective-permute-start(bf16[64,128]{1,0:T(8,128)(2,1)S(1)} %get-tuple-element.54), channel_id=1, source_target_pairs={{0,18},{2,24},{4,22},{6,0},{8,26},{10,8},{12,30},{14,20},{16,2},{1... | collective-permute-start | bytes 49160 | tf_op jit(solution)/shard_map/ppermute | solution.py:287
  20.0 0.3 %collective-permute-start.12 = (bf16[64,128]{1,0:T(8,128)(2,1)S(1)}, bf16[64,128]{1,0:T(8,128)(2,1)S(1)}, u32[]{:S(2)}, u32[]{:S(2)}) collective-permute-start(bf16[64,128]{1,0:T(8,128)(2,1)S(1)} %get-tuple-element.55), channel_id=1, source_target_pairs={{0,10},{2,0},{4,14},{6,4},{8,2},{10,12},{12,6},{14,8},{16,30},{18,... | collective-permute-start | bytes 49160 | tf_op jit(solution)/shard_map/ppermute | solution.py:287
  20.3 0.3 %columns.2 = (bf16[256,512]{1,0:T(8,128)(2,1)S(1)}, bf16[256,512]{1,0:T(8,128)(2,1)S(1)}) custom-call(bf16[2048,128]{1,0:T(8,128)(2,1)S(1)} %collective-permute-done.8.factors), custom_call_target="tpu_custom_call" | custom-call | tf_op jit(solution)/shard_map/columns/pallas_call | solution.py:257
  20.7 0.9 %collective-permute-done.7.refs_0_ = bf16[64,128]{1,0:T(8,128)(2,1)S(1)} collective-permute-done((bf16[64,128]{1,0:T(8,128)(2,1)S(1)}, bf16[64,128]{1,0:T(8,128)(2,1)S(1)}, u32[]{:S(2)}, u32[]{:S(2)}) %collective-permute-start.7) | collective-permute-done | bytes 16416 | tf_op jit(solution)/shard_map/ppermute | solution.py:287
  21.6 0.2 collective-permute-done.12.refs_3_
  21.8 0.4 %collective-permute-start.13 = (bf16[4,64,128]{2,1,0:T(8,128)(2,1)S(1)}, bf16[4,64,128]{2,1,0:T(8,128)(2,1)S(1)}, u32[]{:S(2)}, u32[]{:S(2)}) collective-permute-start(bf16[4,64,128]{2,1,0:T(8,128)(2,1)S(1)} %pack.1.blocks), channel_id=1, source_target_pairs={{0,2},{2,0},{4,6},{6,4},{8,10},{10,8},{12,14},{14,12},{16,18},{18,... | collective-permute-start | bytes 196616 | tf_op jit(solution)/shard_map/ppermute | solution.py:270
  22.1 0.3 %part.1 = (f32[256,128]{1,0:T(8,128)S(1)}, bf16[128,512]{1,0:T(8,128)(2,1)S(1)}) custom-call(bf16[4,64,128]{2,1,0:T(8,128)(2,1)S(1)} %pack.1.blocks, bf16[256,512]{1,0:T(8,128)(2,1)S(1)} %get-tuple-element.49.factors), custom_call_target="tpu_custom_call" | custom-call | flops 33554432 | bytes 589824 | tf_op jit(solution)/shard_map/part/pallas_call | solution.py:257
  22.4 0.6 %collective-permute-done.13.blocks = bf16[4,64,128]{2,1,0:T(8,128)(2,1)S(1)} collective-permute-done((bf16[4,64,128]{2,1,0:T(8,128)(2,1)S(1)}, bf16[4,64,128]{2,1,0:T(8,128)(2,1)S(1)}, u32[]{:S(2)}, u32[]{:S(2)}) %collective-permute-start.13) | collective-permute-done | bytes 65568 | tf_op jit(solution)/shard_map/ppermute | solution.py:270
  23.0 0.3 %gradient.1 = (bf16[256,128]{1,0:T(8,128)(2,1)S(1)}, bf16[128,512]{1,0:T(8,128)(2,1)S(1)}) custom-call(f32[256,128]{1,0:T(8,128)S(1)} %get-tuple-element.56.part, bf16[4,64,128]{2,1,0:T(8,128)(2,1)S(1)} %collective-permute-done.13.blocks, bf16[256,512]{1,0:T(8,128)(2,1)S(1)} %get-tuple-element.50.factors), custom_call_target="tpu_custom_call" | custom-call | flops 33554432 | bytes 655360 | tf_op jit(solution)/shard_map/gradient/pallas_call | solution.py:257
  23.3 1.5 %collective-permute-start.14 = (bf16[256,128]{1,0:T(8,128)(2,1)S(1)}, bf16[256,128]{1,0:T(8,128)(2,1)S(1)}, u32[]{:S(2)}, u32[]{:S(2)}) collective-permute-start(bf16[256,128]{1,0:T(8,128)(2,1)S(1)} %get-tuple-element.57), channel_id=1, source_target_pairs={{0,3},{1,2},{2,1},{3,0},{4,7},{5,6},{6,5},{7,4},{8,11},{9,10},{10,... | collective-permute-start | bytes 196616 | tf_op jit(solution)/shard_map/ppermute | solution.py:276
  24.8 0.3 %columns.3 = (bf16[256,512]{1,0:T(8,128)(2,1)S(1)}, bf16[256,512]{1,0:T(8,128)(2,1)S(1)}) custom-call(bf16[2048,128]{1,0:T(8,128)(2,1)S(1)} %bitcast.7), custom_call_target="tpu_custom_call" | custom-call | tf_op jit(solution)/shard_map/columns/pallas_call | solution.py:257
  25.2 0.3 %pair.1 = (f32[256,128]{1,0:T(8,128)S(1)}, f32[256,128]{1,0:T(8,128)S(1)}) custom-call(bf16[256,512]{1,0:T(8,128)(2,1)S(1)} %get-tuple-element.59.own, bf16[256,512]{1,0:T(8,128)(2,1)S(1)} %get-tuple-element.60.other, bf16[128,512]{1,0:T(8,128)(2,1)S(1)} %get-tuple-element.61.own_left, bf16[128,512]{1,0:T(8,128)(2,1)S(1)} %get-tuple-element.62.other_left, ...), custom_call_target="tpu_custom_call" | custom-call | flops 67108864 | bytes 1310720 | tf_op jit(solution)/shard_map/pair/pallas_call | solution.py:257
  25.5 1.9 %collective-permute-done.14.gradient = bf16[256,128]{1,0:T(8,128)(2,1)S(1)} collective-permute-done((bf16[256,128]{1,0:T(8,128)(2,1)S(1)}, bf16[256,128]{1,0:T(8,128)(2,1)S(1)}, u32[]{:S(2)}, u32[]{:S(2)}) %collective-permute-start.14) | collective-permute-done | bytes 65568 | tf_op jit(solution)/shard_map/ppermute | solution.py:276
  27.3 0.7 %shrink.1 = f32[256,128]{1,0:T(8,128)} custom-call(f32[256,128]{1,0:T(8,128)S(1)} %get-tuple-element.63.total, f32[256,128]{1,0:T(8,128)S(1)} %get-tuple-element.64.difference, bf16[256,128]{1,0:T(8,128)(2,1)S(1)} %collective-permute-done.14.gradient), custom_call_target="tpu_custom_call" | custom-call | tf_op jit(solution)/shard_map/shrink/pallas_call | solution.py:257
  (21 shorter events, 0.1 us)
Async XLA Ops:
  0.0 2.2 %copy-start.2 = (bf16[1,256,8,128]{3,2,1,0:T(8,128)(2,1)S(1)}, bf16[1,256,8,128]{3,2,1,0:T(8,128)(2,1)}, u32[]{:S(2)}) copy-start(bf16[1,256,8,128]{3,2,1,0:T(8,128)(2,1)} %param.5) | copy-start | bytes 1572868
  1.7 1.4 %collective-permute-start = (bf16[4,64,128]{2,1,0:T(8,128)(2,1)S(1)}, bf16[4,64,128]{2,1,0:T(8,128)(2,1)S(1)}, u32[]{:S(2)}, u32[]{:S(2)}) collective-permute-start(bf16[4,64,128]{2,1,0:T(8,128)(2,1)S(1)} %get-tuple-element.36), channel_id=1, source_target_pairs={{0,2},{2,0},{4,6},{6,4},{8,10},{10,8},{12,14},{14,12},{16,18},{18,... | collective-permute-start | bytes 196616 | tf_op jit(solution)/shard_map/ppermute | solution.py:270
  2.2 8.7 %collective-permute-start.4 = (bf16[2048,128]{1,0:T(8,128)(2,1)S(1)}, bf16[2048,128]{1,0:T(8,128)(2,1)S(1)}, u32[]{:S(2)}, u32[]{:S(2)}) collective-permute-start(bf16[2048,128]{1,0:T(8,128)(2,1)S(1)} %bitcast.10), channel_id=1, source_target_pairs={{0,2},{2,0},{4,6},{6,4},{8,10},{10,8},{12,14},{14,12},{16,18},{18,... | collective-permute-start | bytes 1572872 | tf_op jit(solution)/shard_map/ppermute | solution.py:270
  3.1 7.8 %copy-start.1 = (f32[1,256,128]{2,1,0:T(8,128)S(1)}, f32[1,256,128]{2,1,0:T(8,128)}, u32[]{:S(2)}) copy-start(f32[1,256,128]{2,1,0:T(8,128)} %param.9) | copy-start | bytes 393220
  3.1 7.8 %copy-start.3 = (f32[1,256,128]{2,1,0:T(8,128)S(1)}, f32[1,256,128]{2,1,0:T(8,128)}, u32[]{:S(2)}) copy-start(f32[1,256,128]{2,1,0:T(8,128)} %param.8) | copy-start | bytes 393220
  3.2 7.8 %copy-start.4 = (s32[1,8,8]{2,1,0:T(8,128)S(1)}, s32[1,8,8]{2,1,0:T(8,128)}, u32[]{:S(2)}) copy-start(s32[1,8,8]{2,1,0:T(8,128)} %ranks.1) | copy-start | bytes 772
  3.2 8.9 %collective-permute-start.3 = (bf16[64,128]{1,0:T(8,128)(2,1)S(1)}, bf16[64,128]{1,0:T(8,128)(2,1)S(1)}, u32[]{:S(2)}, u32[]{:S(2)}) collective-permute-start(bf16[64,128]{1,0:T(8,128)(2,1)S(1)} %get-tuple-element.39), channel_id=1, source_target_pairs={{0,30},{2,20},{4,26},{6,16},{8,18},{10,28},{12,22},{14,24},{16,10}... | collective-permute-start | bytes 49160 | tf_op jit(solution)/shard_map/ppermute | solution.py:287
  8.9 4.1 %collective-permute-start.5 = (bf16[64,128]{1,0:T(8,128)(2,1)S(1)}, bf16[64,128]{1,0:T(8,128)(2,1)S(1)}, u32[]{:S(2)}, u32[]{:S(2)}) collective-permute-start(bf16[64,128]{1,0:T(8,128)(2,1)S(1)} %get-tuple-element.46), channel_id=1, source_target_pairs={{0,6},{2,12},{4,2},{6,20},{8,22},{10,24},{12,18},{14,28},{16,14},{... | collective-permute-start | bytes 49160 | tf_op jit(solution)/shard_map/ppermute | solution.py:287
  8.9 4.3 %collective-permute-start.1 = (bf16[64,128]{1,0:T(8,128)(2,1)S(1)}, bf16[64,128]{1,0:T(8,128)(2,1)S(1)}, u32[]{:S(2)}, u32[]{:S(2)}) collective-permute-start(bf16[64,128]{1,0:T(8,128)(2,1)S(1)} %get-tuple-element.37), channel_id=1, source_target_pairs={{0,26},{2,16},{4,30},{6,8},{8,14},{10,4},{12,10},{14,0},{16,18},{1... | collective-permute-start | bytes 49160 | tf_op jit(solution)/shard_map/ppermute | solution.py:287
  9.6 3.6 %collective-permute-start.2 = (bf16[64,128]{1,0:T(8,128)(2,1)S(1)}, bf16[64,128]{1,0:T(8,128)(2,1)S(1)}, u32[]{:S(2)}, u32[]{:S(2)}) collective-permute-start(bf16[64,128]{1,0:T(8,128)(2,1)S(1)} %get-tuple-element.38), channel_id=1, source_target_pairs={{0,2},{2,8},{4,6},{6,12},{8,10},{10,0},{12,14},{14,4},{16,22},{18,... | collective-permute-start | bytes 49160 | tf_op jit(solution)/shard_map/ppermute | solution.py:287
  10.9 1.1 %copy-start = (bf16[1,256,8,128]{3,2,1,0:T(8,128)(2,1)S(1)}, bf16[1,256,8,128]{3,2,1,0:T(8,128)(2,1)}, u32[]{:S(2)}) copy-start(bf16[1,256,8,128]{3,2,1,0:T(8,128)(2,1)} %param.6) | copy-start | bytes 1572868
  12.1 7.9 %collective-permute-start.8 = (bf16[2048,128]{1,0:T(8,128)(2,1)S(1)}, bf16[2048,128]{1,0:T(8,128)(2,1)S(1)}, u32[]{:S(2)}, u32[]{:S(2)}) collective-permute-start(bf16[2048,128]{1,0:T(8,128)(2,1)S(1)} %bitcast.6), channel_id=1, source_target_pairs={{0,2},{2,0},{4,6},{6,4},{8,10},{10,8},{12,14},{14,12},{16,18},{18,... | collective-permute-start | bytes 1572872 | tf_op jit(solution)/shard_map/ppermute | solution.py:270
  13.4 1.9 %collective-permute-start.6 = (f32[128,512]{1,0:T(8,128)S(1)}, f32[128,512]{1,0:T(8,128)S(1)}, u32[]{:S(2)}, u32[]{:S(2)}) collective-permute-start(f32[128,512]{1,0:T(8,128)S(1)} %image.1.here), channel_id=1, source_target_pairs={{0,2},{2,0},{4,6},{6,4},{8,10},{10,8},{12,14},{14,12},{16,18},{18,... | collective-permute-start | bytes 786440 | tf_op jit(solution)/shard_map/ppermute | solution.py:270
  13.8 6.9 %collective-permute-start.9 = (f32[256,128]{1,0:T(8,128)S(1)}, f32[256,128]{1,0:T(8,128)S(1)}, u32[]{:S(2)}, u32[]{:S(2)}) collective-permute-start(f32[256,128]{1,0:T(8,128)S(1)} %get-tuple-element.51.here), channel_id=1, source_target_pairs={{0,1},{1,0},{2,3},{3,2},{4,5},{5,4},{6,7},{7,6},{8,9},{9,8},{10,11... | collective-permute-start | bytes 393224 | tf_op jit(solution)/shard_map/ppermute | solution.py:349
  15.7 5.9 %collective-permute-start.7 = (bf16[64,128]{1,0:T(8,128)(2,1)S(1)}, bf16[64,128]{1,0:T(8,128)(2,1)S(1)}, u32[]{:S(2)}, u32[]{:S(2)}) collective-permute-start(bf16[64,128]{1,0:T(8,128)(2,1)S(1)} %get-tuple-element.47), channel_id=1, source_target_pairs={{0,14},{2,28},{4,10},{6,24},{8,30},{10,16},{12,26},{14,12},{16,6},... | collective-permute-start | bytes 49160 | tf_op jit(solution)/shard_map/ppermute | solution.py:287
  16.1 5.5 %collective-permute-start.10 = (bf16[64,128]{1,0:T(8,128)(2,1)S(1)}, bf16[64,128]{1,0:T(8,128)(2,1)S(1)}, u32[]{:S(2)}, u32[]{:S(2)}) collective-permute-start(bf16[64,128]{1,0:T(8,128)(2,1)S(1)} %get-tuple-element.53), channel_id=1, source_target_pairs={{0,22},{2,4},{4,18},{6,28},{8,6},{10,20},{12,2},{14,16},{16,26},{1... | collective-permute-start | bytes 49160 | tf_op jit(solution)/shard_map/ppermute | solution.py:287
  18.2 3.4 %collective-permute-start.11 = (bf16[64,128]{1,0:T(8,128)(2,1)S(1)}, bf16[64,128]{1,0:T(8,128)(2,1)S(1)}, u32[]{:S(2)}, u32[]{:S(2)}) collective-permute-start(bf16[64,128]{1,0:T(8,128)(2,1)S(1)} %get-tuple-element.54), channel_id=1, source_target_pairs={{0,18},{2,24},{4,22},{6,0},{8,26},{10,8},{12,30},{14,20},{16,2},{1... | collective-permute-start | bytes 49160 | tf_op jit(solution)/shard_map/ppermute | solution.py:287
  20.0 1.8 %collective-permute-start.12 = (bf16[64,128]{1,0:T(8,128)(2,1)S(1)}, bf16[64,128]{1,0:T(8,128)(2,1)S(1)}, u32[]{:S(2)}, u32[]{:S(2)}) collective-permute-start(bf16[64,128]{1,0:T(8,128)(2,1)S(1)} %get-tuple-element.55), channel_id=1, source_target_pairs={{0,10},{2,0},{4,14},{6,4},{8,2},{10,12},{12,6},{14,8},{16,30},{18,... | collective-permute-start | bytes 49160 | tf_op jit(solution)/shard_map/ppermute | solution.py:287
  21.8 1.3 %collective-permute-start.13 = (bf16[4,64,128]{2,1,0:T(8,128)(2,1)S(1)}, bf16[4,64,128]{2,1,0:T(8,128)(2,1)S(1)}, u32[]{:S(2)}, u32[]{:S(2)}) collective-permute-start(bf16[4,64,128]{2,1,0:T(8,128)(2,1)S(1)} %pack.1.blocks), channel_id=1, source_target_pairs={{0,2},{2,0},{4,6},{6,4},{8,10},{10,8},{12,14},{14,12},{16,18},{18,... | collective-permute-start | bytes 196616 | tf_op jit(solution)/shard_map/ppermute | solution.py:270
  23.3 4.0 %collective-permute-start.14 = (bf16[256,128]{1,0:T(8,128)(2,1)S(1)}, bf16[256,128]{1,0:T(8,128)(2,1)S(1)}, u32[]{:S(2)}, u32[]{:S(2)}) collective-permute-start(bf16[256,128]{1,0:T(8,128)(2,1)S(1)} %get-tuple-element.57), channel_id=1, source_target_pairs={{0,3},{1,2},{2,1},{3,0},{4,7},{5,6},{6,5},{7,4},{8,11},{9,10},{10,... | collective-permute-start | bytes 196616 | tf_op jit(solution)/shard_map/ppermute | solution.py:276

commit v19 on v18

--- a/solution.py
+++ b/solution.py
@@ -21,8 +21,8 @@
 
 MEETINGS = {
     8: [
-        [(0o77666677, 0o55555555), (0o11777711, 0o34444443), (0o66001166, 0o43333334), (0o00110000, 0o22222222)],
-        [(0o22555533, 0o77060677), (0o55223355, 0o16777761), (0o44444444, 0o61606016), (0o33332222, 0o00111100)],
+        [(0o77037433, 0o16666551), (0o33473077, 0o52555165), (0o44344344, 0o65211616), (0o00700700, 0o21122222)],
+        [(0o11551155, 0o70074334), (0o66166526, 0o47703777), (0o55215611, 0o04447443), (0o22622262, 0o33330000)],
     ]
 }
 

time: 28.2 us -> 28.4 us (level)
  waiting for transfers between devices: 5.16 us -> 5.52 us
    ppermute x8, starting transfers between devices: 12.4 us -> 11.6 us  [exchange(): arrived.append(lax.ppermute(send, 'tile', sorted(pairs)))]
    ppermute x5, starting transfers between devices: 1.41 us -> 2.18 us  [to_mate(): lax.ppermute(value, 'tile', [(i, i ^ 1) for i in range(lax.axis_size('til...]
    ppermute x1, waiting for transfers between devices: 1.85 us -> 2.24 us  [across(): return lax.ppermute(value, ('tile', 'freq'), pairs)]
  transfers between devices with their start and end apart: 15 -> 15, of which waited for: 6 -> 8; matrix products, arithmetic and copies ran while one was open for 0% -> 0% of each run, Pallas kernels for 11% -> 11%
where the time goes in v19:
time: 28.4 us; the launch traced here: 28.2 us
  starting transfers between devices  16.7 us (59%)
  Pallas kernels  5.87 us (21%)
  waiting for transfers between devices  5.52 us (19%)
    ppermute x8, starting transfers between devices, exchange(): arrived.append(lax.ppermute(send, 'tile', sorted(pairs)))  11.6 us
    pallas_call x13, Pallas kernels, call(): pl.pallas_call(kernel, out_shape=outs, in_specs=[pl.BlockSpec(memory_spac...  5.87 us
    ppermute x1, waiting for transfers between devices, across(): return lax.ppermute(value, ('tile', 'freq'), pairs)  2.24 us
    ppermute x5, starting transfers between devices, to_mate(): lax.ppermute(value, 'tile', [(i, i ^ 1) for i in range(lax.axis_size('til...  2.18 us
    ppermute x8, waiting for transfers between devices, exchange(): arrived.append(lax.ppermute(send, 'tile', sorted(pairs)))  1.69 us
    ppermute x1, starting transfers between devices, body(): lax.ppermute(start, 'freq', [(f, (f - shift) % band) for f in range(band)])  1.59 us
    ppermute x5, waiting for transfers between devices, to_mate(): lax.ppermute(value, 'tile', [(i, i ^ 1) for i in range(lax.axis_size('til...  1.59 us
    ppermute x1, starting transfers between devices, across(): return lax.ppermute(value, ('tile', 'freq'), pairs)  1.28 us
  transfers between devices with their start and end apart: 15, of which 8 were waited for; matrix products, arithmetic and copies ran while one was open for 0% of the time, Pallas kernels for 11%

profile of v19, /device:TPU:0, one launch (start us, length us, event | category | flops | bytes accessed | tf_op | source)
XLA Modules:
  0.0 28.2 jit_solution(18181161659683297340)
XLA Ops:
  0.0 1.7 %forward.1 = (bf16[4,64,128]{2,1,0:T(8,128)(2,1)S(1)}, bf16[4,64,128]{2,1,0:T(8,128)(2,1)S(1)}) custom-call(f32[256,128]{1,0:T(8,128)} %bitcast.8, bf16[2048,128]{1,0:T(8,128)(2,1)} %bitcast.5), custom_call_target="tpu_custom_call" | custom-call | flops 67108864 | bytes 786432 | tf_op jit(solution)/shard_map/forward/pallas_call | solution.py:257
  1.7 0.5 %collective-permute-start = (bf16[4,64,128]{2,1,0:T(8,128)(2,1)S(1)}, bf16[4,64,128]{2,1,0:T(8,128)(2,1)S(1)}, u32[]{:S(2)}, u32[]{:S(2)}) collective-permute-start(bf16[4,64,128]{2,1,0:T(8,128)(2,1)S(1)} %get-tuple-element.36), channel_id=1, source_target_pairs={{0,2},{2,0},{4,6},{6,4},{8,10},{10,8},{12,14},{14,12},{16,18},{18,... | collective-permute-start | bytes 196616 | tf_op jit(solution)/shard_map/ppermute | solution.py:270
  2.2 0.1 collective-permute-start.4
  2.3 0.8 %collective-permute-done.arrived = bf16[4,64,128]{2,1,0:T(8,128)(2,1)S(1)} collective-permute-done((bf16[4,64,128]{2,1,0:T(8,128)(2,1)S(1)}, bf16[4,64,128]{2,1,0:T(8,128)(2,1)S(1)}, u32[]{:S(2)}, u32[]{:S(2)}) %collective-permute-start) | collective-permute-done | bytes 65568 | tf_op jit(solution)/shard_map/ppermute | solution.py:270
  3.2 3.7 %collective-permute-start.3 = (bf16[64,128]{1,0:T(8,128)(2,1)S(1)}, bf16[64,128]{1,0:T(8,128)(2,1)S(1)}, u32[]{:S(2)}, u32[]{:S(2)}) collective-permute-start(bf16[64,128]{1,0:T(8,128)(2,1)S(1)} %get-tuple-element.39), channel_id=1, source_target_pairs={{0,14},{2,4},{4,10},{6,16},{8,26},{10,28},{12,18},{14,20},{16,30},... | collective-permute-start | bytes 49160 | tf_op jit(solution)/shard_map/ppermute | solution.py:287
  6.8 2.5 %collective-permute-start.5 = (bf16[64,128]{1,0:T(8,128)(2,1)S(1)}, bf16[64,128]{1,0:T(8,128)(2,1)S(1)}, u32[]{:S(2)}, u32[]{:S(2)}) collective-permute-start(bf16[64,128]{1,0:T(8,128)(2,1)S(1)} %get-tuple-element.46), channel_id=1, source_target_pairs={{0,30},{2,20},{4,26},{6,28},{8,10},{10,12},{12,2},{14,24},{16,14},... | collective-permute-start | bytes 49160 | tf_op jit(solution)/shard_map/ppermute | solution.py:287
  9.3 0.1 collective-permute-start.1
  9.4 0.4 %collective-permute-start.2 = (bf16[64,128]{1,0:T(8,128)(2,1)S(1)}, bf16[64,128]{1,0:T(8,128)(2,1)S(1)}, u32[]{:S(2)}, u32[]{:S(2)}) collective-permute-start(bf16[64,128]{1,0:T(8,128)(2,1)S(1)} %get-tuple-element.38), channel_id=1, source_target_pairs={{0,2},{2,8},{4,6},{6,12},{8,22},{10,0},{12,14},{14,4},{16,18},{18,... | collective-permute-start | bytes 49160 | tf_op jit(solution)/shard_map/ppermute | solution.py:287
  9.9 1.1 %rows.1 = (bf16[512,512]{1,0:T(8,128)(2,1)S(1)}, f32[128,256]{1,0:T(8,128)S(1)}, f32[256,128]{1,0:T(8,128)S(1)}) custom-call(s32[1,8,8]{2,1,0:T(8,128)S(1)} %copy-done.4, bf16[2048,128]{1,0:T(8,128)(2,1)S(1)} %bitcast.11, bf16[2048,128]{1,0:T(8,128)(2,1)S(1)} %collective-permute-done.4.mate, f32[256,128]{1,0:T(8,128)S(1)} %bitcast.12, f32[256,128]{1,0:T(8,128)S(1)} %bitcast.9), custom_call_target="tpu_custom_call" | custom-call | tf_op jit(solution)/shard_map/rows/pallas_call | solution.py:257
  11.0 1.3 %collective-permute-start.8 = (bf16[2048,128]{1,0:T(8,128)(2,1)S(1)}, bf16[2048,128]{1,0:T(8,128)(2,1)S(1)}, u32[]{:S(2)}, u32[]{:S(2)}) collective-permute-start(bf16[2048,128]{1,0:T(8,128)(2,1)S(1)} %bitcast.6), channel_id=1, source_target_pairs={{0,2},{2,0},{4,6},{6,4},{8,10},{10,8},{12,14},{14,12},{16,18},{18,... | collective-permute-start | bytes 1572872 | tf_op jit(solution)/shard_map/ppermute | solution.py:270
  12.2 0.2 early.1.refs_2_
  12.5 0.4 %collective-permute-done.2.refs_1_ = bf16[64,128]{1,0:T(8,128)(2,1)S(1)} collective-permute-done((bf16[64,128]{1,0:T(8,128)(2,1)S(1)}, bf16[64,128]{1,0:T(8,128)(2,1)S(1)}, u32[]{:S(2)}, u32[]{:S(2)}) %collective-permute-start.2) | collective-permute-done | bytes 16416 | tf_op jit(solution)/shard_map/ppermute | solution.py:287
  12.9 0.2 image.1.here
  13.3 1.6 %collective-permute-start.9 = (f32[256,128]{1,0:T(8,128)S(1)}, f32[256,128]{1,0:T(8,128)S(1)}, u32[]{:S(2)}, u32[]{:S(2)}) collective-permute-start(f32[256,128]{1,0:T(8,128)S(1)} %get-tuple-element.51.here), channel_id=1, source_target_pairs={{0,1},{1,0},{2,3},{3,2},{4,5},{5,4},{6,7},{7,6},{8,9},{9,8},{10,11... | collective-permute-start | bytes 393224 | tf_op jit(solution)/shard_map/ppermute | solution.py:349
  14.9 0.3 %back.1 = (bf16[64,128]{1,0:T(8,128)(2,1)S(1)}, bf16[64,128]{1,0:T(8,128)(2,1)S(1)}, bf16[64,128]{1,0:T(8,128)(2,1)S(1)}, bf16[64,128]{1,0:T(8,128)(2,1)S(1)}) custom-call(f32[128,512]{1,0:T(8,128)S(1)} %image.1.here, f32[128,512]{1,0:T(8,128)S(1)} %collective-permute-done.6.there, bf16[512,512]{1,0:T(8,128)(2,1)S(1)} %get-tuple-element.43.factors.refs_3_), custom_call_target="tpu_custom_call" | custom-call | flops 67108864 | bytes 1114112 | tf_op jit(solution)/shard_map/back/pallas_call | solution.py:257
  15.2 2.1 %collective-permute-start.7 = (bf16[64,128]{1,0:T(8,128)(2,1)S(1)}, bf16[64,128]{1,0:T(8,128)(2,1)S(1)}, u32[]{:S(2)}, u32[]{:S(2)}) collective-permute-start(bf16[64,128]{1,0:T(8,128)(2,1)S(1)} %get-tuple-element.47), channel_id=1, source_target_pairs={{0,22},{2,16},{4,18},{6,8},{8,14},{10,4},{12,10},{14,28},{16,6},{1... | collective-permute-start | bytes 49160 | tf_op jit(solution)/shard_map/ppermute | solution.py:287
  17.3 0.2 collective-permute-start.10
  17.5 2.3 %collective-permute-start.11 = (bf16[64,128]{1,0:T(8,128)(2,1)S(1)}, bf16[64,128]{1,0:T(8,128)(2,1)S(1)}, u32[]{:S(2)}, u32[]{:S(2)}) collective-permute-start(bf16[64,128]{1,0:T(8,128)(2,1)S(1)} %get-tuple-element.54), channel_id=1, source_target_pairs={{0,6},{2,12},{4,2},{6,20},{8,18},{10,24},{12,26},{14,16},{16,22},{... | collective-permute-start | bytes 49160 | tf_op jit(solution)/shard_map/ppermute | solution.py:287
  19.8 0.4 %collective-permute-start.12 = (bf16[64,128]{1,0:T(8,128)(2,1)S(1)}, bf16[64,128]{1,0:T(8,128)(2,1)S(1)}, u32[]{:S(2)}, u32[]{:S(2)}) collective-permute-start(bf16[64,128]{1,0:T(8,128)(2,1)S(1)} %get-tuple-element.55), channel_id=1, source_target_pairs={{0,10},{2,0},{4,30},{6,4},{8,2},{10,8},{12,6},{14,12},{16,26},{18,... | collective-permute-start | bytes 49160 | tf_op jit(solution)/shard_map/ppermute | solution.py:287
  20.2 0.3 %columns.2 = (bf16[256,512]{1,0:T(8,128)(2,1)S(1)}, bf16[256,512]{1,0:T(8,128)(2,1)S(1)}) custom-call(bf16[2048,128]{1,0:T(8,128)(2,1)S(1)} %collective-permute-done.8.factors), custom_call_target="tpu_custom_call" | custom-call | tf_op jit(solution)/shard_map/columns/pallas_call | solution.py:257
  20.5 0.6 %collective-permute-done.7.refs_0_ = bf16[64,128]{1,0:T(8,128)(2,1)S(1)} collective-permute-done((bf16[64,128]{1,0:T(8,128)(2,1)S(1)}, bf16[64,128]{1,0:T(8,128)(2,1)S(1)}, u32[]{:S(2)}, u32[]{:S(2)}) %collective-permute-start.7) | collective-permute-done | bytes 16416 | tf_op jit(solution)/shard_map/ppermute | solution.py:287
  21.1 0.3 collective-permute-done.10.refs_1_
  21.4 0.4 %collective-permute-done.11.refs_2_ = bf16[64,128]{1,0:T(8,128)(2,1)S(1)} collective-permute-done((bf16[64,128]{1,0:T(8,128)(2,1)S(1)}, bf16[64,128]{1,0:T(8,128)(2,1)S(1)}, u32[]{:S(2)}, u32[]{:S(2)}) %collective-permute-start.11) | collective-permute-done | bytes 16416 | tf_op jit(solution)/shard_map/ppermute | solution.py:287
  21.7 0.3 collective-permute-start.13
  22.0 0.3 %part.1 = (f32[256,128]{1,0:T(8,128)S(1)}, bf16[128,512]{1,0:T(8,128)(2,1)S(1)}) custom-call(bf16[4,64,128]{2,1,0:T(8,128)(2,1)S(1)} %pack.1.blocks, bf16[256,512]{1,0:T(8,128)(2,1)S(1)} %get-tuple-element.49.factors), custom_call_target="tpu_custom_call" | custom-call | flops 33554432 | bytes 589824 | tf_op jit(solution)/shard_map/part/pallas_call | solution.py:257
  22.3 0.8 %collective-permute-done.13.blocks = bf16[4,64,128]{2,1,0:T(8,128)(2,1)S(1)} collective-permute-done((bf16[4,64,128]{2,1,0:T(8,128)(2,1)S(1)}, bf16[4,64,128]{2,1,0:T(8,128)(2,1)S(1)}, u32[]{:S(2)}, u32[]{:S(2)}) %collective-permute-start.13) | collective-permute-done | bytes 65568 | tf_op jit(solution)/shard_map/ppermute | solution.py:270
  23.1 0.3 %gradient.1 = (bf16[256,128]{1,0:T(8,128)(2,1)S(1)}, bf16[128,512]{1,0:T(8,128)(2,1)S(1)}) custom-call(f32[256,128]{1,0:T(8,128)S(1)} %get-tuple-element.56.part, bf16[4,64,128]{2,1,0:T(8,128)(2,1)S(1)} %collective-permute-done.13.blocks, bf16[256,512]{1,0:T(8,128)(2,1)S(1)} %get-tuple-element.50.factors), custom_call_target="tpu_custom_call" | custom-call | flops 33554432 | bytes 655360 | tf_op jit(solution)/shard_map/gradient/pallas_call | solution.py:257
  23.3 1.3 %collective-permute-start.14 = (bf16[256,128]{1,0:T(8,128)(2,1)S(1)}, bf16[256,128]{1,0:T(8,128)(2,1)S(1)}, u32[]{:S(2)}, u32[]{:S(2)}) collective-permute-start(bf16[256,128]{1,0:T(8,128)(2,1)S(1)} %get-tuple-element.57), channel_id=1, source_target_pairs={{0,3},{1,2},{2,1},{3,0},{4,7},{5,6},{6,5},{7,4},{8,11},{9,10},{10,... | collective-permute-start | bytes 196616 | tf_op jit(solution)/shard_map/ppermute | solution.py:276
  24.6 0.3 %columns.3 = (bf16[256,512]{1,0:T(8,128)(2,1)S(1)}, bf16[256,512]{1,0:T(8,128)(2,1)S(1)}) custom-call(bf16[2048,128]{1,0:T(8,128)(2,1)S(1)} %bitcast.7), custom_call_target="tpu_custom_call" | custom-call | tf_op jit(solution)/shard_map/columns/pallas_call | solution.py:257
  25.0 0.3 %pair.1 = (f32[256,128]{1,0:T(8,128)S(1)}, f32[256,128]{1,0:T(8,128)S(1)}) custom-call(bf16[256,512]{1,0:T(8,128)(2,1)S(1)} %get-tuple-element.59.own, bf16[256,512]{1,0:T(8,128)(2,1)S(1)} %get-tuple-element.60.other, bf16[128,512]{1,0:T(8,128)(2,1)S(1)} %get-tuple-element.61.own_left, bf16[128,512]{1,0:T(8,128)(2,1)S(1)} %get-tuple-element.62.other_left, ...), custom_call_target="tpu_custom_call" | custom-call | flops 67108864 | bytes 1310720 | tf_op jit(solution)/shard_map/pair/pallas_call | solution.py:257
  25.3 2.2 %collective-permute-done.14.gradient = bf16[256,128]{1,0:T(8,128)(2,1)S(1)} collective-permute-done((bf16[256,128]{1,0:T(8,128)(2,1)S(1)}, bf16[256,128]{1,0:T(8,128)(2,1)S(1)}, u32[]{:S(2)}, u32[]{:S(2)}) %collective-permute-start.14) | collective-permute-done | bytes 65568 | tf_op jit(solution)/shard_map/ppermute | solution.py:276
  27.5 0.7 %shrink.1 = f32[256,128]{1,0:T(8,128)} custom-call(f32[256,128]{1,0:T(8,128)S(1)} %get-tuple-element.63.total, f32[256,128]{1,0:T(8,128)S(1)} %get-tuple-element.64.difference, bf16[256,128]{1,0:T(8,128)(2,1)S(1)} %collective-permute-done.14.gradient), custom_call_target="tpu_custom_call" | custom-call | tf_op jit(solution)/shard_map/shrink/pallas_call | solution.py:257
  (21 shorter events, 0.2 us)
Async XLA Ops:
  0.0 2.2 %copy-start.2 = (bf16[1,256,8,128]{3,2,1,0:T(8,128)(2,1)S(1)}, bf16[1,256,8,128]{3,2,1,0:T(8,128)(2,1)}, u32[]{:S(2)}) copy-start(bf16[1,256,8,128]{3,2,1,0:T(8,128)(2,1)} %param.5) | copy-start | bytes 1572868
  1.7 1.4 %collective-permute-start = (bf16[4,64,128]{2,1,0:T(8,128)(2,1)S(1)}, bf16[4,64,128]{2,1,0:T(8,128)(2,1)S(1)}, u32[]{:S(2)}, u32[]{:S(2)}) collective-permute-start(bf16[4,64,128]{2,1,0:T(8,128)(2,1)S(1)} %get-tuple-element.36), channel_id=1, source_target_pairs={{0,2},{2,0},{4,6},{6,4},{8,10},{10,8},{12,14},{14,12},{16,18},{18,... | collective-permute-start | bytes 196616 | tf_op jit(solution)/shard_map/ppermute | solution.py:270
  2.2 7.6 %collective-permute-start.4 = (bf16[2048,128]{1,0:T(8,128)(2,1)S(1)}, bf16[2048,128]{1,0:T(8,128)(2,1)S(1)}, u32[]{:S(2)}, u32[]{:S(2)}) collective-permute-start(bf16[2048,128]{1,0:T(8,128)(2,1)S(1)} %bitcast.10), channel_id=1, source_target_pairs={{0,2},{2,0},{4,6},{6,4},{8,10},{10,8},{12,14},{14,12},{16,18},{18,... | collective-permute-start | bytes 1572872 | tf_op jit(solution)/shard_map/ppermute | solution.py:270
  3.1 6.7 %copy-start.1 = (f32[1,256,128]{2,1,0:T(8,128)S(1)}, f32[1,256,128]{2,1,0:T(8,128)}, u32[]{:S(2)}) copy-start(f32[1,256,128]{2,1,0:T(8,128)} %param.9) | copy-start | bytes 393220
  3.1 6.7 %copy-start.3 = (f32[1,256,128]{2,1,0:T(8,128)S(1)}, f32[1,256,128]{2,1,0:T(8,128)}, u32[]{:S(2)}) copy-start(f32[1,256,128]{2,1,0:T(8,128)} %param.8) | copy-start | bytes 393220
  3.2 6.7 %copy-start.4 = (s32[1,8,8]{2,1,0:T(8,128)S(1)}, s32[1,8,8]{2,1,0:T(8,128)}, u32[]{:S(2)}) copy-start(s32[1,8,8]{2,1,0:T(8,128)} %ranks.1) | copy-start | bytes 772
  3.2 7.8 %collective-permute-start.3 = (bf16[64,128]{1,0:T(8,128)(2,1)S(1)}, bf16[64,128]{1,0:T(8,128)(2,1)S(1)}, u32[]{:S(2)}, u32[]{:S(2)}) collective-permute-start(bf16[64,128]{1,0:T(8,128)(2,1)S(1)} %get-tuple-element.39), channel_id=1, source_target_pairs={{0,14},{2,4},{4,10},{6,16},{8,26},{10,28},{12,18},{14,20},{16,30},... | collective-permute-start | bytes 49160 | tf_op jit(solution)/shard_map/ppermute | solution.py:287
  6.8 5.4 %collective-permute-start.5 = (bf16[64,128]{1,0:T(8,128)(2,1)S(1)}, bf16[64,128]{1,0:T(8,128)(2,1)S(1)}, u32[]{:S(2)}, u32[]{:S(2)}) collective-permute-start(bf16[64,128]{1,0:T(8,128)(2,1)S(1)} %get-tuple-element.46), channel_id=1, source_target_pairs={{0,30},{2,20},{4,26},{6,28},{8,10},{10,12},{12,2},{14,24},{16,14},... | collective-permute-start | bytes 49160 | tf_op jit(solution)/shard_map/ppermute | solution.py:287
  9.3 3.2 %collective-permute-start.1 = (bf16[64,128]{1,0:T(8,128)(2,1)S(1)}, bf16[64,128]{1,0:T(8,128)(2,1)S(1)}, u32[]{:S(2)}, u32[]{:S(2)}) collective-permute-start(bf16[64,128]{1,0:T(8,128)(2,1)S(1)} %get-tuple-element.37), channel_id=1, source_target_pairs={{0,18},{2,24},{4,22},{6,0},{8,6},{10,16},{12,30},{14,8},{16,2},{18... | collective-permute-start | bytes 49160 | tf_op jit(solution)/shard_map/ppermute | solution.py:287
  9.4 3.5 %collective-permute-start.2 = (bf16[64,128]{1,0:T(8,128)(2,1)S(1)}, bf16[64,128]{1,0:T(8,128)(2,1)S(1)}, u32[]{:S(2)}, u32[]{:S(2)}) collective-permute-start(bf16[64,128]{1,0:T(8,128)(2,1)S(1)} %get-tuple-element.38), channel_id=1, source_target_pairs={{0,2},{2,8},{4,6},{6,12},{8,22},{10,0},{12,14},{14,4},{16,18},{18,... | collective-permute-start | bytes 49160 | tf_op jit(solution)/shard_map/ppermute | solution.py:287
  9.8 1.1 %copy-start = (bf16[1,256,8,128]{3,2,1,0:T(8,128)(2,1)S(1)}, bf16[1,256,8,128]{3,2,1,0:T(8,128)(2,1)}, u32[]{:S(2)}) copy-start(bf16[1,256,8,128]{3,2,1,0:T(8,128)(2,1)} %param.6) | copy-start | bytes 1572868
  11.0 8.8 %collective-permute-start.8 = (bf16[2048,128]{1,0:T(8,128)(2,1)S(1)}, bf16[2048,128]{1,0:T(8,128)(2,1)S(1)}, u32[]{:S(2)}, u32[]{:S(2)}) collective-permute-start(bf16[2048,128]{1,0:T(8,128)(2,1)S(1)} %bitcast.6), channel_id=1, source_target_pairs={{0,2},{2,0},{4,6},{6,4},{8,10},{10,8},{12,14},{14,12},{16,18},{18,... | collective-permute-start | bytes 1572872 | tf_op jit(solution)/shard_map/ppermute | solution.py:270
  13.2 1.7 %collective-permute-start.6 = (f32[128,512]{1,0:T(8,128)S(1)}, f32[128,512]{1,0:T(8,128)S(1)}, u32[]{:S(2)}, u32[]{:S(2)}) collective-permute-start(f32[128,512]{1,0:T(8,128)S(1)} %image.1.here), channel_id=1, source_target_pairs={{0,2},{2,0},{4,6},{6,4},{8,10},{10,8},{12,14},{14,12},{16,18},{18,... | collective-permute-start | bytes 786440 | tf_op jit(solution)/shard_map/ppermute | solution.py:270
  13.3 7.3 %collective-permute-start.9 = (f32[256,128]{1,0:T(8,128)S(1)}, f32[256,128]{1,0:T(8,128)S(1)}, u32[]{:S(2)}, u32[]{:S(2)}) collective-permute-start(f32[256,128]{1,0:T(8,128)S(1)} %get-tuple-element.51.here), channel_id=1, source_target_pairs={{0,1},{1,0},{2,3},{3,2},{4,5},{5,4},{6,7},{7,6},{8,9},{9,8},{10,11... | collective-permute-start | bytes 393224 | tf_op jit(solution)/shard_map/ppermute | solution.py:349
  15.2 5.9 %collective-permute-start.7 = (bf16[64,128]{1,0:T(8,128)(2,1)S(1)}, bf16[64,128]{1,0:T(8,128)(2,1)S(1)}, u32[]{:S(2)}, u32[]{:S(2)}) collective-permute-start(bf16[64,128]{1,0:T(8,128)(2,1)S(1)} %get-tuple-element.47), channel_id=1, source_target_pairs={{0,22},{2,16},{4,18},{6,8},{8,14},{10,4},{12,10},{14,28},{16,6},{1... | collective-permute-start | bytes 49160 | tf_op jit(solution)/shard_map/ppermute | solution.py:287
  17.3 4.1 %collective-permute-start.10 = (bf16[64,128]{1,0:T(8,128)(2,1)S(1)}, bf16[64,128]{1,0:T(8,128)(2,1)S(1)}, u32[]{:S(2)}, u32[]{:S(2)}) collective-permute-start(bf16[64,128]{1,0:T(8,128)(2,1)S(1)} %get-tuple-element.53), channel_id=1, source_target_pairs={{0,26},{2,28},{4,14},{6,24},{8,30},{10,20},{12,22},{14,0},{16,10},... | collective-permute-start | bytes 49160 | tf_op jit(solution)/shard_map/ppermute | solution.py:287
  17.5 4.2 %collective-permute-start.11 = (bf16[64,128]{1,0:T(8,128)(2,1)S(1)}, bf16[64,128]{1,0:T(8,128)(2,1)S(1)}, u32[]{:S(2)}, u32[]{:S(2)}) collective-permute-start(bf16[64,128]{1,0:T(8,128)(2,1)S(1)} %get-tuple-element.54), channel_id=1, source_target_pairs={{0,6},{2,12},{4,2},{6,20},{8,18},{10,24},{12,26},{14,16},{16,22},{... | collective-permute-start | bytes 49160 | tf_op jit(solution)/shard_map/ppermute | solution.py:287
  19.8 1.9 %collective-permute-start.12 = (bf16[64,128]{1,0:T(8,128)(2,1)S(1)}, bf16[64,128]{1,0:T(8,128)(2,1)S(1)}, u32[]{:S(2)}, u32[]{:S(2)}) collective-permute-start(bf16[64,128]{1,0:T(8,128)(2,1)S(1)} %get-tuple-element.55), channel_id=1, source_target_pairs={{0,10},{2,0},{4,30},{6,4},{8,2},{10,8},{12,6},{14,12},{16,26},{18,... | collective-permute-start | bytes 49160 | tf_op jit(solution)/shard_map/ppermute | solution.py:287
  21.7 1.3 %collective-permute-start.13 = (bf16[4,64,128]{2,1,0:T(8,128)(2,1)S(1)}, bf16[4,64,128]{2,1,0:T(8,128)(2,1)S(1)}, u32[]{:S(2)}, u32[]{:S(2)}) collective-permute-start(bf16[4,64,128]{2,1,0:T(8,128)(2,1)S(1)} %pack.1.blocks), channel_id=1, source_target_pairs={{0,2},{2,0},{4,6},{6,4},{8,10},{10,8},{12,14},{14,12},{16,18},{18,... | collective-permute-start | bytes 196616 | tf_op jit(solution)/shard_map/ppermute | solution.py:270
  23.3 4.2 %collective-permute-start.14 = (bf16[256,128]{1,0:T(8,128)(2,1)S(1)}, bf16[256,128]{1,0:T(8,128)(2,1)S(1)}, u32[]{:S(2)}, u32[]{:S(2)}) collective-permute-start(bf16[256,128]{1,0:T(8,128)(2,1)S(1)} %get-tuple-element.57), channel_id=1, source_target_pairs={{0,3},{1,2},{2,1},{3,0},{4,7},{5,6},{6,5},{7,4},{8,11},{9,10},{10,... | collective-permute-start | bytes 196616 | tf_op jit(solution)/shard_map/ppermute | solution.py:276

commit v20 on v18

--- a/solution.py
+++ b/solution.py
@@ -104,9 +104,8 @@
 
 def spread_block(block, left, tile):
     half = block.shape[0]
-    block = block.astype(F32)
-    left[:half, columns_of(tile)] = (block * signs(half)).astype(BF16)
-    left[half:, columns_of(tile)] = pltpu.roll(block, LANES // 2, 1).astype(BF16)
+    left[:half, columns_of(tile)] = block * signs(half).astype(BF16)
+    left[half:, columns_of(tile)] = pltpu.roll(block, LANES // 2, 1)
 
 
 def times_transposed(left, right):

time: 28.2 us -> 28.2 us (level)
  no operation moved by 1% of the time
where the time goes in v20:
time: 28.2 us; the launch traced here: 28 us
  starting transfers between devices  16.8 us (60%)
  Pallas kernels  5.86 us (21%)
  waiting for transfers between devices  5.17 us (18%)
    ppermute x8, starting transfers between devices, exchange(): arrived.append(lax.ppermute(send, 'tile', sorted(pairs)))  12.4 us
    pallas_call x13, Pallas kernels, call(): pl.pallas_call(kernel, out_shape=outs, in_specs=[pl.BlockSpec(memory_spac...  5.86 us
    ppermute x8, waiting for transfers between devices, exchange(): arrived.append(lax.ppermute(send, 'tile', sorted(pairs)))  1.88 us
    ppermute x1, waiting for transfers between devices, across(): return lax.ppermute(value, ('tile', 'freq'), pairs)  1.86 us
    ppermute x1, starting transfers between devices, body(): lax.ppermute(start, 'freq', [(f, (f - shift) % band) for f in range(band)])  1.52 us
    ppermute x1, starting transfers between devices, across(): return lax.ppermute(value, ('tile', 'freq'), pairs)  1.47 us
    ppermute x5, waiting for transfers between devices, to_mate(): lax.ppermute(value, 'tile', [(i, i ^ 1) for i in range(lax.axis_size('til...  1.43 us
    ppermute x5, starting transfers between devices, to_mate(): lax.ppermute(value, 'tile', [(i, i ^ 1) for i in range(lax.axis_size('til...  1.41 us
  transfers between devices with their start and end apart: 15, of which 6 were waited for; matrix products, arithmetic and copies ran while one was open for 0% of the time, Pallas kernels for 11%

profile of v20, /device:TPU:0, one launch (start us, length us, event | category | flops | bytes accessed | tf_op | source)
XLA Modules:
  0.0 28.0 jit_solution(8627056581458233326)
XLA Ops:
  0.0 1.7 %forward.1 = (bf16[4,64,128]{2,1,0:T(8,128)(2,1)S(1)}, bf16[4,64,128]{2,1,0:T(8,128)(2,1)S(1)}) custom-call(f32[256,128]{1,0:T(8,128)} %bitcast.8, bf16[2048,128]{1,0:T(8,128)(2,1)} %bitcast.5), custom_call_target="tpu_custom_call" | custom-call | flops 67108864 | bytes 786432 | tf_op jit(solution)/shard_map/forward/pallas_call | solution.py:256
  1.7 0.5 %collective-permute-start = (bf16[4,64,128]{2,1,0:T(8,128)(2,1)S(1)}, bf16[4,64,128]{2,1,0:T(8,128)(2,1)S(1)}, u32[]{:S(2)}, u32[]{:S(2)}) collective-permute-start(bf16[4,64,128]{2,1,0:T(8,128)(2,1)S(1)} %get-tuple-element.36), channel_id=1, source_target_pairs={{0,2},{2,0},{4,6},{6,4},{8,10},{10,8},{12,14},{14,12},{16,18},{18,... | collective-permute-start | bytes 196616 | tf_op jit(solution)/shard_map/ppermute | solution.py:269
  2.2 0.1 collective-permute-start.4
  2.3 0.8 %collective-permute-done.arrived = bf16[4,64,128]{2,1,0:T(8,128)(2,1)S(1)} collective-permute-done((bf16[4,64,128]{2,1,0:T(8,128)(2,1)S(1)}, bf16[4,64,128]{2,1,0:T(8,128)(2,1)S(1)}, u32[]{:S(2)}, u32[]{:S(2)}) %collective-permute-start) | collective-permute-done | bytes 65568 | tf_op jit(solution)/shard_map/ppermute | solution.py:269
  3.2 0.0 copy-start.4
  3.2 5.7 %collective-permute-start.3 = (bf16[64,128]{1,0:T(8,128)(2,1)S(1)}, bf16[64,128]{1,0:T(8,128)(2,1)S(1)}, u32[]{:S(2)}, u32[]{:S(2)}) collective-permute-start(bf16[64,128]{1,0:T(8,128)(2,1)S(1)} %get-tuple-element.39), channel_id=1, source_target_pairs={{0,30},{2,20},{4,26},{6,16},{8,18},{10,28},{12,22},{14,24},{16,10}... | collective-permute-start | bytes 49160 | tf_op jit(solution)/shard_map/ppermute | solution.py:286
  8.9 0.7 %collective-permute-start.1 = (bf16[64,128]{1,0:T(8,128)(2,1)S(1)}, bf16[64,128]{1,0:T(8,128)(2,1)S(1)}, u32[]{:S(2)}, u32[]{:S(2)}) collective-permute-start(bf16[64,128]{1,0:T(8,128)(2,1)S(1)} %get-tuple-element.37), channel_id=1, source_target_pairs={{0,26},{2,16},{4,30},{6,8},{8,14},{10,4},{12,10},{14,0},{16,18},{1... | collective-permute-start | bytes 49160 | tf_op jit(solution)/shard_map/ppermute | solution.py:286
  9.6 1.4 %collective-permute-start.2 = (bf16[64,128]{1,0:T(8,128)(2,1)S(1)}, bf16[64,128]{1,0:T(8,128)(2,1)S(1)}, u32[]{:S(2)}, u32[]{:S(2)}) collective-permute-start(bf16[64,128]{1,0:T(8,128)(2,1)S(1)} %get-tuple-element.38), channel_id=1, source_target_pairs={{0,2},{2,8},{4,6},{6,12},{8,10},{10,0},{12,14},{14,4},{16,22},{18,... | collective-permute-start | bytes 49160 | tf_op jit(solution)/shard_map/ppermute | solution.py:286
  11.0 1.1 %rows.1 = (bf16[512,512]{1,0:T(8,128)(2,1)S(1)}, f32[128,256]{1,0:T(8,128)S(1)}, f32[256,128]{1,0:T(8,128)S(1)}) custom-call(s32[1,8,8]{2,1,0:T(8,128)S(1)} %copy-done.4, bf16[2048,128]{1,0:T(8,128)(2,1)S(1)} %bitcast.11, bf16[2048,128]{1,0:T(8,128)(2,1)S(1)} %collective-permute-done.4.mate, f32[256,128]{1,0:T(8,128)S(1)} %bitcast.12, f32[256,128]{1,0:T(8,128)S(1)} %bitcast.9), custom_call_target="tpu_custom_call" | custom-call | tf_op jit(solution)/shard_map/rows/pallas_call | solution.py:256
  12.1 0.1 collective-permute-start.8
  12.1 0.8 %collective-permute-done.5.second = bf16[64,128]{1,0:T(8,128)(2,1)S(1)} collective-permute-done((bf16[64,128]{1,0:T(8,128)(2,1)S(1)}, bf16[64,128]{1,0:T(8,128)(2,1)S(1)}, u32[]{:S(2)}, u32[]{:S(2)}) %collective-permute-start.5) | collective-permute-done | bytes 16416 | tf_op jit(solution)/shard_map/ppermute | solution.py:286
  12.9 0.2 early.1.refs_2_
  13.2 0.2 image.1.here
  13.4 0.4 %collective-permute-start.6 = (f32[128,512]{1,0:T(8,128)S(1)}, f32[128,512]{1,0:T(8,128)S(1)}, u32[]{:S(2)}, u32[]{:S(2)}) collective-permute-start(f32[128,512]{1,0:T(8,128)S(1)} %image.1.here), channel_id=1, source_target_pairs={{0,2},{2,0},{4,6},{6,4},{8,10},{10,8},{12,14},{14,12},{16,18},{18,... | collective-permute-start | bytes 786440 | tf_op jit(solution)/shard_map/ppermute | solution.py:269
  13.8 1.5 %collective-permute-start.9 = (f32[256,128]{1,0:T(8,128)S(1)}, f32[256,128]{1,0:T(8,128)S(1)}, u32[]{:S(2)}, u32[]{:S(2)}) collective-permute-start(f32[256,128]{1,0:T(8,128)S(1)} %get-tuple-element.51.here), channel_id=1, source_target_pairs={{0,1},{1,0},{2,3},{3,2},{4,5},{5,4},{6,7},{7,6},{8,9},{9,8},{10,11... | collective-permute-start | bytes 393224 | tf_op jit(solution)/shard_map/ppermute | solution.py:348
  15.3 0.3 %back.1 = (bf16[64,128]{1,0:T(8,128)(2,1)S(1)}, bf16[64,128]{1,0:T(8,128)(2,1)S(1)}, bf16[64,128]{1,0:T(8,128)(2,1)S(1)}, bf16[64,128]{1,0:T(8,128)(2,1)S(1)}) custom-call(f32[128,512]{1,0:T(8,128)S(1)} %image.1.here, f32[128,512]{1,0:T(8,128)S(1)} %collective-permute-done.6.there, bf16[512,512]{1,0:T(8,128)(2,1)S(1)} %get-tuple-element.43.factors.refs_3_), custom_call_target="tpu_custom_call" | custom-call | flops 67108864 | bytes 1114112 | tf_op jit(solution)/shard_map/back/pallas_call | solution.py:256
  15.7 0.4 %collective-permute-start.7 = (bf16[64,128]{1,0:T(8,128)(2,1)S(1)}, bf16[64,128]{1,0:T(8,128)(2,1)S(1)}, u32[]{:S(2)}, u32[]{:S(2)}) collective-permute-start(bf16[64,128]{1,0:T(8,128)(2,1)S(1)} %get-tuple-element.47), channel_id=1, source_target_pairs={{0,14},{2,28},{4,10},{6,24},{8,30},{10,16},{12,26},{14,12},{16,6},... | collective-permute-start | bytes 49160 | tf_op jit(solution)/shard_map/ppermute | solution.py:286
  16.1 2.1 %collective-permute-start.10 = (bf16[64,128]{1,0:T(8,128)(2,1)S(1)}, bf16[64,128]{1,0:T(8,128)(2,1)S(1)}, u32[]{:S(2)}, u32[]{:S(2)}) collective-permute-start(bf16[64,128]{1,0:T(8,128)(2,1)S(1)} %get-tuple-element.53), channel_id=1, source_target_pairs={{0,22},{2,4},{4,18},{6,28},{8,6},{10,20},{12,2},{14,16},{16,26},{1... | collective-permute-start | bytes 49160 | tf_op jit(solution)/shard_map/ppermute | solution.py:286
  18.2 1.8 %collective-permute-start.11 = (bf16[64,128]{1,0:T(8,128)(2,1)S(1)}, bf16[64,128]{1,0:T(8,128)(2,1)S(1)}, u32[]{:S(2)}, u32[]{:S(2)}) collective-permute-start(bf16[64,128]{1,0:T(8,128)(2,1)S(1)} %get-tuple-element.54), channel_id=1, source_target_pairs={{0,18},{2,24},{4,22},{6,0},{8,26},{10,8},{12,30},{14,20},{16,2},{1... | collective-permute-start | bytes 49160 | tf_op jit(solution)/shard_map/ppermute | solution.py:286
  20.0 0.3 %collective-permute-start.12 = (bf16[64,128]{1,0:T(8,128)(2,1)S(1)}, bf16[64,128]{1,0:T(8,128)(2,1)S(1)}, u32[]{:S(2)}, u32[]{:S(2)}) collective-permute-start(bf16[64,128]{1,0:T(8,128)(2,1)S(1)} %get-tuple-element.55), channel_id=1, source_target_pairs={{0,10},{2,0},{4,14},{6,4},{8,2},{10,12},{12,6},{14,8},{16,30},{18,... | collective-permute-start | bytes 49160 | tf_op jit(solution)/shard_map/ppermute | solution.py:286
  20.3 0.3 %columns.2 = (bf16[256,512]{1,0:T(8,128)(2,1)S(1)}, bf16[256,512]{1,0:T(8,128)(2,1)S(1)}) custom-call(bf16[2048,128]{1,0:T(8,128)(2,1)S(1)} %collective-permute-done.8.factors), custom_call_target="tpu_custom_call" | custom-call | tf_op jit(solution)/shard_map/columns/pallas_call | solution.py:256
  20.7 0.9 %collective-permute-done.7.refs_0_ = bf16[64,128]{1,0:T(8,128)(2,1)S(1)} collective-permute-done((bf16[64,128]{1,0:T(8,128)(2,1)S(1)}, bf16[64,128]{1,0:T(8,128)(2,1)S(1)}, u32[]{:S(2)}, u32[]{:S(2)}) %collective-permute-start.7) | collective-permute-done | bytes 16416 | tf_op jit(solution)/shard_map/ppermute | solution.py:286
  21.6 0.2 collective-permute-done.12.refs_3_
  21.8 0.3 %collective-permute-start.13 = (bf16[4,64,128]{2,1,0:T(8,128)(2,1)S(1)}, bf16[4,64,128]{2,1,0:T(8,128)(2,1)S(1)}, u32[]{:S(2)}, u32[]{:S(2)}) collective-permute-start(bf16[4,64,128]{2,1,0:T(8,128)(2,1)S(1)} %pack.1.blocks), channel_id=1, source_target_pairs={{0,2},{2,0},{4,6},{6,4},{8,10},{10,8},{12,14},{14,12},{16,18},{18,... | collective-permute-start | bytes 196616 | tf_op jit(solution)/shard_map/ppermute | solution.py:269
  22.1 0.3 %part.1 = (f32[256,128]{1,0:T(8,128)S(1)}, bf16[128,512]{1,0:T(8,128)(2,1)S(1)}) custom-call(bf16[4,64,128]{2,1,0:T(8,128)(2,1)S(1)} %pack.1.blocks, bf16[256,512]{1,0:T(8,128)(2,1)S(1)} %get-tuple-element.49.factors), custom_call_target="tpu_custom_call" | custom-call | flops 33554432 | bytes 589824 | tf_op jit(solution)/shard_map/part/pallas_call | solution.py:256
  22.4 0.6 %collective-permute-done.13.blocks = bf16[4,64,128]{2,1,0:T(8,128)(2,1)S(1)} collective-permute-done((bf16[4,64,128]{2,1,0:T(8,128)(2,1)S(1)}, bf16[4,64,128]{2,1,0:T(8,128)(2,1)S(1)}, u32[]{:S(2)}, u32[]{:S(2)}) %collective-permute-start.13) | collective-permute-done | bytes 65568 | tf_op jit(solution)/shard_map/ppermute | solution.py:269
  23.0 0.3 %gradient.1 = (bf16[256,128]{1,0:T(8,128)(2,1)S(1)}, bf16[128,512]{1,0:T(8,128)(2,1)S(1)}) custom-call(f32[256,128]{1,0:T(8,128)S(1)} %get-tuple-element.56.part, bf16[4,64,128]{2,1,0:T(8,128)(2,1)S(1)} %collective-permute-done.13.blocks, bf16[256,512]{1,0:T(8,128)(2,1)S(1)} %get-tuple-element.50.factors), custom_call_target="tpu_custom_call" | custom-call | flops 33554432 | bytes 655360 | tf_op jit(solution)/shard_map/gradient/pallas_call | solution.py:256
  23.3 1.5 %collective-permute-start.14 = (bf16[256,128]{1,0:T(8,128)(2,1)S(1)}, bf16[256,128]{1,0:T(8,128)(2,1)S(1)}, u32[]{:S(2)}, u32[]{:S(2)}) collective-permute-start(bf16[256,128]{1,0:T(8,128)(2,1)S(1)} %get-tuple-element.57), channel_id=1, source_target_pairs={{0,3},{1,2},{2,1},{3,0},{4,7},{5,6},{6,5},{7,4},{8,11},{9,10},{10,... | collective-permute-start | bytes 196616 | tf_op jit(solution)/shard_map/ppermute | solution.py:275
  24.8 0.3 %columns.3 = (bf16[256,512]{1,0:T(8,128)(2,1)S(1)}, bf16[256,512]{1,0:T(8,128)(2,1)S(1)}) custom-call(bf16[2048,128]{1,0:T(8,128)(2,1)S(1)} %bitcast.7), custom_call_target="tpu_custom_call" | custom-call | tf_op jit(solution)/shard_map/columns/pallas_call | solution.py:256
  25.2 0.3 %pair.1 = (f32[256,128]{1,0:T(8,128)S(1)}, f32[256,128]{1,0:T(8,128)S(1)}) custom-call(bf16[256,512]{1,0:T(8,128)(2,1)S(1)} %get-tuple-element.59.own, bf16[256,512]{1,0:T(8,128)(2,1)S(1)} %get-tuple-element.60.other, bf16[128,512]{1,0:T(8,128)(2,1)S(1)} %get-tuple-element.61.own_left, bf16[128,512]{1,0:T(8,128)(2,1)S(1)} %get-tuple-element.62.other_left, ...), custom_call_target="tpu_custom_call" | custom-call | flops 67108864 | bytes 1310720 | tf_op jit(solution)/shard_map/pair/pallas_call | solution.py:256
  25.5 1.9 %collective-permute-done.14.gradient = bf16[256,128]{1,0:T(8,128)(2,1)S(1)} collective-permute-done((bf16[256,128]{1,0:T(8,128)(2,1)S(1)}, bf16[256,128]{1,0:T(8,128)(2,1)S(1)}, u32[]{:S(2)}, u32[]{:S(2)}) %collective-permute-start.14) | collective-permute-done | bytes 65568 | tf_op jit(solution)/shard_map/ppermute | solution.py:275
  27.3 0.7 %shrink.1 = f32[256,128]{1,0:T(8,128)} custom-call(f32[256,128]{1,0:T(8,128)S(1)} %get-tuple-element.63.total, f32[256,128]{1,0:T(8,128)S(1)} %get-tuple-element.64.difference, bf16[256,128]{1,0:T(8,128)(2,1)S(1)} %collective-permute-done.14.gradient), custom_call_target="tpu_custom_call" | custom-call | tf_op jit(solution)/shard_map/shrink/pallas_call | solution.py:256
  (21 shorter events, 0.1 us)
Async XLA Ops:
  0.0 2.2 %copy-start.2 = (bf16[1,256,8,128]{3,2,1,0:T(8,128)(2,1)S(1)}, bf16[1,256,8,128]{3,2,1,0:T(8,128)(2,1)}, u32[]{:S(2)}) copy-start(bf16[1,256,8,128]{3,2,1,0:T(8,128)(2,1)} %param.5) | copy-start | bytes 1572868
  1.7 1.4 %collective-permute-start = (bf16[4,64,128]{2,1,0:T(8,128)(2,1)S(1)}, bf16[4,64,128]{2,1,0:T(8,128)(2,1)S(1)}, u32[]{:S(2)}, u32[]{:S(2)}) collective-permute-start(bf16[4,64,128]{2,1,0:T(8,128)(2,1)S(1)} %get-tuple-element.36), channel_id=1, source_target_pairs={{0,2},{2,0},{4,6},{6,4},{8,10},{10,8},{12,14},{14,12},{16,18},{18,... | collective-permute-start | bytes 196616 | tf_op jit(solution)/shard_map/ppermute | solution.py:269
  2.2 8.7 %collective-permute-start.4 = (bf16[2048,128]{1,0:T(8,128)(2,1)S(1)}, bf16[2048,128]{1,0:T(8,128)(2,1)S(1)}, u32[]{:S(2)}, u32[]{:S(2)}) collective-permute-start(bf16[2048,128]{1,0:T(8,128)(2,1)S(1)} %bitcast.10), channel_id=1, source_target_pairs={{0,2},{2,0},{4,6},{6,4},{8,10},{10,8},{12,14},{14,12},{16,18},{18,... | collective-permute-start | bytes 1572872 | tf_op jit(solution)/shard_map/ppermute | solution.py:269
  3.1 7.8 %copy-start.1 = (f32[1,256,128]{2,1,0:T(8,128)S(1)}, f32[1,256,128]{2,1,0:T(8,128)}, u32[]{:S(2)}) copy-start(f32[1,256,128]{2,1,0:T(8,128)} %param.9) | copy-start | bytes 393220
  3.1 7.8 %copy-start.3 = (f32[1,256,128]{2,1,0:T(8,128)S(1)}, f32[1,256,128]{2,1,0:T(8,128)}, u32[]{:S(2)}) copy-start(f32[1,256,128]{2,1,0:T(8,128)} %param.8) | copy-start | bytes 393220
  3.2 7.8 %copy-start.4 = (s32[1,8,8]{2,1,0:T(8,128)S(1)}, s32[1,8,8]{2,1,0:T(8,128)}, u32[]{:S(2)}) copy-start(s32[1,8,8]{2,1,0:T(8,128)} %ranks.1) | copy-start | bytes 772
  3.2 8.9 %collective-permute-start.3 = (bf16[64,128]{1,0:T(8,128)(2,1)S(1)}, bf16[64,128]{1,0:T(8,128)(2,1)S(1)}, u32[]{:S(2)}, u32[]{:S(2)}) collective-permute-start(bf16[64,128]{1,0:T(8,128)(2,1)S(1)} %get-tuple-element.39), channel_id=1, source_target_pairs={{0,30},{2,20},{4,26},{6,16},{8,18},{10,28},{12,22},{14,24},{16,10}... | collective-permute-start | bytes 49160 | tf_op jit(solution)/shard_map/ppermute | solution.py:286
  8.9 4.1 %collective-permute-start.5 = (bf16[64,128]{1,0:T(8,128)(2,1)S(1)}, bf16[64,128]{1,0:T(8,128)(2,1)S(1)}, u32[]{:S(2)}, u32[]{:S(2)}) collective-permute-start(bf16[64,128]{1,0:T(8,128)(2,1)S(1)} %get-tuple-element.46), channel_id=1, source_target_pairs={{0,6},{2,12},{4,2},{6,20},{8,22},{10,24},{12,18},{14,28},{16,14},{... | collective-permute-start | bytes 49160 | tf_op jit(solution)/shard_map/ppermute | solution.py:286
  8.9 4.3 %collective-permute-start.1 = (bf16[64,128]{1,0:T(8,128)(2,1)S(1)}, bf16[64,128]{1,0:T(8,128)(2,1)S(1)}, u32[]{:S(2)}, u32[]{:S(2)}) collective-permute-start(bf16[64,128]{1,0:T(8,128)(2,1)S(1)} %get-tuple-element.37), channel_id=1, source_target_pairs={{0,26},{2,16},{4,30},{6,8},{8,14},{10,4},{12,10},{14,0},{16,18},{1... | collective-permute-start | bytes 49160 | tf_op jit(solution)/shard_map/ppermute | solution.py:286
  9.6 3.6 %collective-permute-start.2 = (bf16[64,128]{1,0:T(8,128)(2,1)S(1)}, bf16[64,128]{1,0:T(8,128)(2,1)S(1)}, u32[]{:S(2)}, u32[]{:S(2)}) collective-permute-start(bf16[64,128]{1,0:T(8,128)(2,1)S(1)} %get-tuple-element.38), channel_id=1, source_target_pairs={{0,2},{2,8},{4,6},{6,12},{8,10},{10,0},{12,14},{14,4},{16,22},{18,... | collective-permute-start | bytes 49160 | tf_op jit(solution)/shard_map/ppermute | solution.py:286
  10.9 1.1 %copy-start = (bf16[1,256,8,128]{3,2,1,0:T(8,128)(2,1)S(1)}, bf16[1,256,8,128]{3,2,1,0:T(8,128)(2,1)}, u32[]{:S(2)}) copy-start(bf16[1,256,8,128]{3,2,1,0:T(8,128)(2,1)} %param.6) | copy-start | bytes 1572868
  12.1 7.9 %collective-permute-start.8 = (bf16[2048,128]{1,0:T(8,128)(2,1)S(1)}, bf16[2048,128]{1,0:T(8,128)(2,1)S(1)}, u32[]{:S(2)}, u32[]{:S(2)}) collective-permute-start(bf16[2048,128]{1,0:T(8,128)(2,1)S(1)} %bitcast.6), channel_id=1, source_target_pairs={{0,2},{2,0},{4,6},{6,4},{8,10},{10,8},{12,14},{14,12},{16,18},{18,... | collective-permute-start | bytes 1572872 | tf_op jit(solution)/shard_map/ppermute | solution.py:269
  13.4 1.9 %collective-permute-start.6 = (f32[128,512]{1,0:T(8,128)S(1)}, f32[128,512]{1,0:T(8,128)S(1)}, u32[]{:S(2)}, u32[]{:S(2)}) collective-permute-start(f32[128,512]{1,0:T(8,128)S(1)} %image.1.here), channel_id=1, source_target_pairs={{0,2},{2,0},{4,6},{6,4},{8,10},{10,8},{12,14},{14,12},{16,18},{18,... | collective-permute-start | bytes 786440 | tf_op jit(solution)/shard_map/ppermute | solution.py:269
  13.8 6.9 %collective-permute-start.9 = (f32[256,128]{1,0:T(8,128)S(1)}, f32[256,128]{1,0:T(8,128)S(1)}, u32[]{:S(2)}, u32[]{:S(2)}) collective-permute-start(f32[256,128]{1,0:T(8,128)S(1)} %get-tuple-element.51.here), channel_id=1, source_target_pairs={{0,1},{1,0},{2,3},{3,2},{4,5},{5,4},{6,7},{7,6},{8,9},{9,8},{10,11... | collective-permute-start | bytes 393224 | tf_op jit(solution)/shard_map/ppermute | solution.py:348
  15.7 5.9 %collective-permute-start.7 = (bf16[64,128]{1,0:T(8,128)(2,1)S(1)}, bf16[64,128]{1,0:T(8,128)(2,1)S(1)}, u32[]{:S(2)}, u32[]{:S(2)}) collective-permute-start(bf16[64,128]{1,0:T(8,128)(2,1)S(1)} %get-tuple-element.47), channel_id=1, source_target_pairs={{0,14},{2,28},{4,10},{6,24},{8,30},{10,16},{12,26},{14,12},{16,6},... | collective-permute-start | bytes 49160 | tf_op jit(solution)/shard_map/ppermute | solution.py:286
  16.1 5.5 %collective-permute-start.10 = (bf16[64,128]{1,0:T(8,128)(2,1)S(1)}, bf16[64,128]{1,0:T(8,128)(2,1)S(1)}, u32[]{:S(2)}, u32[]{:S(2)}) collective-permute-start(bf16[64,128]{1,0:T(8,128)(2,1)S(1)} %get-tuple-element.53), channel_id=1, source_target_pairs={{0,22},{2,4},{4,18},{6,28},{8,6},{10,20},{12,2},{14,16},{16,26},{1... | collective-permute-start | bytes 49160 | tf_op jit(solution)/shard_map/ppermute | solution.py:286
  18.2 3.4 %collective-permute-start.11 = (bf16[64,128]{1,0:T(8,128)(2,1)S(1)}, bf16[64,128]{1,0:T(8,128)(2,1)S(1)}, u32[]{:S(2)}, u32[]{:S(2)}) collective-permute-start(bf16[64,128]{1,0:T(8,128)(2,1)S(1)} %get-tuple-element.54), channel_id=1, source_target_pairs={{0,18},{2,24},{4,22},{6,0},{8,26},{10,8},{12,30},{14,20},{16,2},{1... | collective-permute-start | bytes 49160 | tf_op jit(solution)/shard_map/ppermute | solution.py:286
  20.0 1.8 %collective-permute-start.12 = (bf16[64,128]{1,0:T(8,128)(2,1)S(1)}, bf16[64,128]{1,0:T(8,128)(2,1)S(1)}, u32[]{:S(2)}, u32[]{:S(2)}) collective-permute-start(bf16[64,128]{1,0:T(8,128)(2,1)S(1)} %get-tuple-element.55), channel_id=1, source_target_pairs={{0,10},{2,0},{4,14},{6,4},{8,2},{10,12},{12,6},{14,8},{16,30},{18,... | collective-permute-start | bytes 49160 | tf_op jit(solution)/shard_map/ppermute | solution.py:286
  21.8 1.3 %collective-permute-start.13 = (bf16[4,64,128]{2,1,0:T(8,128)(2,1)S(1)}, bf16[4,64,128]{2,1,0:T(8,128)(2,1)S(1)}, u32[]{:S(2)}, u32[]{:S(2)}) collective-permute-start(bf16[4,64,128]{2,1,0:T(8,128)(2,1)S(1)} %pack.1.blocks), channel_id=1, source_target_pairs={{0,2},{2,0},{4,6},{6,4},{8,10},{10,8},{12,14},{14,12},{16,18},{18,... | collective-permute-start | bytes 196616 | tf_op jit(solution)/shard_map/ppermute | solution.py:269
  23.3 4.0 %collective-permute-start.14 = (bf16[256,128]{1,0:T(8,128)(2,1)S(1)}, bf16[256,128]{1,0:T(8,128)(2,1)S(1)}, u32[]{:S(2)}, u32[]{:S(2)}) collective-permute-start(bf16[256,128]{1,0:T(8,128)(2,1)S(1)} %get-tuple-element.57), channel_id=1, source_target_pairs={{0,3},{1,2},{2,1},{3,0},{4,7},{5,6},{6,5},{7,4},{8,11},{9,10},{10,... | collective-permute-start | bytes 196616 | tf_op jit(solution)/shard_map/ppermute | solution.py:275

commit v21 on v20

--- a/solution.py
+++ b/solution.py
@@ -143,7 +143,7 @@
         out[...] = (keep[index].astype(F32) + arrived[index].astype(F32)).astype(BF16)
 
 
-def rows_kernel(arrivals, ranks, own, mate, observed, start, both, turned, start_out, wide):
+def rows_kernel(arrivals, ranks, own, mate, observed, start, both, turned_both, turned, start_out, wide):
     chip, _ = place()
     chosen, _ = both_tiles(arrivals)
     rows = both.shape[0] // 2
@@ -151,6 +151,9 @@
     masks = [lane < ranks[0, chip, tile] for tile in chosen]
     separate(own, wide, both.at[:rows], chosen, masks)
     separate(mate, wide, both.at[rows:], chosen, masks)
+    for index in range(len(chosen)):
+        columns = slice(index * LANES, (index + 1) * LANES)
+        turned_both[columns, :] = both[:, columns].T
     turned[...] = observed[...].T
     start_out[...] = start[...]
 
@@ -165,7 +168,7 @@
     for index, block in enumerate((first, second)):
         spread_block(block[...], left, index)
     rows = observed.shape[1]
-    image = times_transposed(left[...], factors[:, : left.shape[1]])
+    image = jnp.dot(left[...], factors[: left.shape[1], :], preferred_element_type=F32)
     misfit[:, :rows] = image[:, :rows] - observed[...]
     misfit[:, rows:] = image[:, rows:]
 
@@ -174,7 +177,7 @@
     blocks, (early, factors, misfit, left) = refs[:-4], refs[-4:]
     for index, block in enumerate(blocks):
         spread_block(block[...], left, index)
-    misfit[...] = early[...] + times_transposed(left[...], factors[:, -left.shape[1] :])
+    misfit[...] = early[...] + jnp.dot(left[...], factors[-left.shape[1] :, :], preferred_element_type=F32)
 
 
 def back_kernel(places, here, there, factors, *refs):
@@ -335,10 +338,15 @@
     )
     sends = call(add_kernel, "add", [block] * members, [keep, to_mate(give)], flops=HIDE * flops)
     mate_left = to_mate(after(left_rows, give))
-    both_left, turned, start = call(
+    both_left, turned_left, turned, start = call(
         functools.partial(rows_kernel, arrivals),
         "rows",
-        [shape(2 * rows, members * width), shape(sources, rows, dtype=F32), shape(rows, sources, dtype=F32)],
+        [
+            shape(2 * rows, members * width),
+            shape(members * width, 2 * rows),
+            shape(sources, rows, dtype=F32),
+            shape(rows, sources, dtype=F32),
+        ],
         [ranks, after(left_rows, give), mate_left, after(observed, give), after(start, give)],
         [wide],
         spaces=[pltpu.SMEM],
@@ -346,13 +354,13 @@
     starts = [start]
     for shift in range(1, band):
         starts.append(lax.ppermute(start, "freq", [(f, (f - shift) % band) for f in range(band)]))
-    arrived = exchange(sends, routes, [both_left, turned])
+    arrived = exchange(sends, routes, [turned_left, turned])
     misfit = shape(sources, 2 * rows, dtype=F32)
     (misfit_early,) = call(
         early_kernel,
         "early",
         [misfit],
-        [*arrived[:2], both_left, turned],
+        [*arrived[:2], turned_left, turned],
         [pltpu.VMEM((sources, 2 * width), BF16)],
         flops // 2,
     )
@@ -360,7 +368,7 @@
         image_kernel,
         "image",
         [misfit],
-        [*arrived[2:], misfit_early, both_left],
+        [*arrived[2:], misfit_early, turned_left],
         [pltpu.VMEM((sources, (members - 2) * width), BF16)],
         HIDE * flops,
     )

time: 28.2 us -> 28.3 us (level)
  transfers between devices with their start and end apart: 15 -> 15, of which waited for: 6 -> 6; matrix products, arithmetic and copies ran while one was open for 0% -> 0% of each run, Pallas kernels for 11% -> 12%
where the time goes in v21:
time: 28.3 us; the launch traced here: 28.1 us
  starting transfers between devices  16.8 us (59%)
  Pallas kernels  5.98 us (21%)
  waiting for transfers between devices  5.17 us (18%)
    ppermute x8, starting transfers between devices, exchange(): arrived.append(lax.ppermute(send, 'tile', sorted(pairs)))  12.5 us
    pallas_call x13, Pallas kernels, call(): pl.pallas_call(kernel, out_shape=outs, in_specs=[pl.BlockSpec(memory_spac...  5.98 us
    ppermute x1, waiting for transfers between devices, across(): return lax.ppermute(value, ('tile', 'freq'), pairs)  1.99 us
    ppermute x8, waiting for transfers between devices, exchange(): arrived.append(lax.ppermute(send, 'tile', sorted(pairs)))  1.73 us
    ppermute x1, starting transfers between devices, body(): lax.ppermute(start, 'freq', [(f, (f - shift) % band) for f in range(band)])  1.52 us
    ppermute x5, waiting for transfers between devices, to_mate(): lax.ppermute(value, 'tile', [(i, i ^ 1) for i in range(lax.axis_size('til...  1.46 us
    ppermute x5, starting transfers between devices, to_mate(): lax.ppermute(value, 'tile', [(i, i ^ 1) for i in range(lax.axis_size('til...  1.39 us
    ppermute x1, starting transfers between devices, across(): return lax.ppermute(value, ('tile', 'freq'), pairs)  1.39 us
  transfers between devices with their start and end apart: 15, of which 6 were waited for; matrix products, arithmetic and copies ran while one was open for 0% of the time, Pallas kernels for 12%

profile of v21, /device:TPU:0, one launch (start us, length us, event | category | flops | bytes accessed | tf_op | source)
XLA Modules:
  0.0 28.1 jit_solution(11756974415778623764)
XLA Ops:
  0.0 1.7 %forward.1 = (bf16[4,64,128]{2,1,0:T(8,128)(2,1)S(1)}, bf16[4,64,128]{2,1,0:T(8,128)(2,1)S(1)}) custom-call(f32[256,128]{1,0:T(8,128)} %bitcast.8, bf16[2048,128]{1,0:T(8,128)(2,1)} %bitcast.5), custom_call_target="tpu_custom_call" | custom-call | flops 67108864 | bytes 786432 | tf_op jit(solution)/shard_map/forward/pallas_call | solution.py:259
  1.7 0.5 %collective-permute-start = (bf16[4,64,128]{2,1,0:T(8,128)(2,1)S(1)}, bf16[4,64,128]{2,1,0:T(8,128)(2,1)S(1)}, u32[]{:S(2)}, u32[]{:S(2)}) collective-permute-start(bf16[4,64,128]{2,1,0:T(8,128)(2,1)S(1)} %get-tuple-element.37), channel_id=1, source_target_pairs={{0,2},{2,0},{4,6},{6,4},{8,10},{10,8},{12,14},{14,12},{16,18},{18,... | collective-permute-start | bytes 196616 | tf_op jit(solution)/shard_map/ppermute | solution.py:272
  2.2 0.1 collective-permute-start.4
  2.3 0.8 %collective-permute-done.arrived = bf16[4,64,128]{2,1,0:T(8,128)(2,1)S(1)} collective-permute-done((bf16[4,64,128]{2,1,0:T(8,128)(2,1)S(1)}, bf16[4,64,128]{2,1,0:T(8,128)(2,1)S(1)}, u32[]{:S(2)}, u32[]{:S(2)}) %collective-permute-start) | collective-permute-done | bytes 65568 | tf_op jit(solution)/shard_map/ppermute | solution.py:272
  3.2 0.0 copy-start.4
  3.2 5.7 %collective-permute-start.3 = (bf16[64,128]{1,0:T(8,128)(2,1)S(1)}, bf16[64,128]{1,0:T(8,128)(2,1)S(1)}, u32[]{:S(2)}, u32[]{:S(2)}) collective-permute-start(bf16[64,128]{1,0:T(8,128)(2,1)S(1)} %get-tuple-element.40), channel_id=1, source_target_pairs={{0,30},{2,20},{4,26},{6,16},{8,18},{10,28},{12,22},{14,24},{16,10}... | collective-permute-start | bytes 49160 | tf_op jit(solution)/shard_map/ppermute | solution.py:289
  8.9 0.7 %collective-permute-start.1 = (bf16[64,128]{1,0:T(8,128)(2,1)S(1)}, bf16[64,128]{1,0:T(8,128)(2,1)S(1)}, u32[]{:S(2)}, u32[]{:S(2)}) collective-permute-start(bf16[64,128]{1,0:T(8,128)(2,1)S(1)} %get-tuple-element.38), channel_id=1, source_target_pairs={{0,26},{2,16},{4,30},{6,8},{8,14},{10,4},{12,10},{14,0},{16,18},{1... | collective-permute-start | bytes 49160 | tf_op jit(solution)/shard_map/ppermute | solution.py:289
  9.6 1.4 %collective-permute-start.2 = (bf16[64,128]{1,0:T(8,128)(2,1)S(1)}, bf16[64,128]{1,0:T(8,128)(2,1)S(1)}, u32[]{:S(2)}, u32[]{:S(2)}) collective-permute-start(bf16[64,128]{1,0:T(8,128)(2,1)S(1)} %get-tuple-element.39), channel_id=1, source_target_pairs={{0,2},{2,8},{4,6},{6,12},{8,10},{10,0},{12,14},{14,4},{16,22},{18,... | collective-permute-start | bytes 49160 | tf_op jit(solution)/shard_map/ppermute | solution.py:289
  11.0 1.2 %rows.1 = (bf16[512,512]{1,0:T(8,128)(2,1)S(1)}, bf16[512,512]{1,0:T(8,128)(2,1)S(1)}, f32[128,256]{1,0:T(8,128)S(1)}, f32[256,128]{1,0:T(8,128)S(1)}) custom-call(s32[1,8,8]{2,1,0:T(8,128)S(1)} %copy-done.4, bf16[2048,128]{1,0:T(8,128)(2,1)S(1)} %bitcast.11, bf16[2048,128]{1,0:T(8,128)(2,1)S(1)} %collective-permute-done.4.mate, f32[256,128]{1,0:T(8,128)S(1)} %bitcast.12, ...), custom_call_target="tpu_custom_call" | custom-call | tf_op jit(solution)/shard_map/rows/pallas_call | solution.py:259
  12.2 0.1 collective-permute-start.8
  12.3 0.6 %collective-permute-done.5.second = bf16[64,128]{1,0:T(8,128)(2,1)S(1)} collective-permute-done((bf16[64,128]{1,0:T(8,128)(2,1)S(1)}, bf16[64,128]{1,0:T(8,128)(2,1)S(1)}, u32[]{:S(2)}, u32[]{:S(2)}) %collective-permute-start.5) | collective-permute-done | bytes 16416 | tf_op jit(solution)/shard_map/ppermute | solution.py:289
  12.9 0.2 early.1.refs_2_
  13.2 0.2 image.1.here
  13.4 0.4 %collective-permute-start.6 = (f32[128,512]{1,0:T(8,128)S(1)}, f32[128,512]{1,0:T(8,128)S(1)}, u32[]{:S(2)}, u32[]{:S(2)}) collective-permute-start(f32[128,512]{1,0:T(8,128)S(1)} %image.1.here), channel_id=1, source_target_pairs={{0,2},{2,0},{4,6},{6,4},{8,10},{10,8},{12,14},{14,12},{16,18},{18,... | collective-permute-start | bytes 786440 | tf_op jit(solution)/shard_map/ppermute | solution.py:272
  13.8 1.5 %collective-permute-start.9 = (f32[256,128]{1,0:T(8,128)S(1)}, f32[256,128]{1,0:T(8,128)S(1)}, u32[]{:S(2)}, u32[]{:S(2)}) collective-permute-start(f32[256,128]{1,0:T(8,128)S(1)} %get-tuple-element.53.here), channel_id=1, source_target_pairs={{0,1},{1,0},{2,3},{3,2},{4,5},{5,4},{6,7},{7,6},{8,9},{9,8},{10,11... | collective-permute-start | bytes 393224 | tf_op jit(solution)/shard_map/ppermute | solution.py:356
  15.3 0.3 %back.1 = (bf16[64,128]{1,0:T(8,128)(2,1)S(1)}, bf16[64,128]{1,0:T(8,128)(2,1)S(1)}, bf16[64,128]{1,0:T(8,128)(2,1)S(1)}, bf16[64,128]{1,0:T(8,128)(2,1)S(1)}) custom-call(f32[128,512]{1,0:T(8,128)S(1)} %image.1.here, f32[128,512]{1,0:T(8,128)S(1)} %collective-permute-done.6.there, bf16[512,512]{1,0:T(8,128)(2,1)S(1)} %get-tuple-element.48.factors), custom_call_target="tpu_custom_call" | custom-call | flops 67108864 | bytes 1114112 | tf_op jit(solution)/shard_map/back/pallas_call | solution.py:259
  15.6 0.4 %collective-permute-start.7 = (bf16[64,128]{1,0:T(8,128)(2,1)S(1)}, bf16[64,128]{1,0:T(8,128)(2,1)S(1)}, u32[]{:S(2)}, u32[]{:S(2)}) collective-permute-start(bf16[64,128]{1,0:T(8,128)(2,1)S(1)} %get-tuple-element.49), channel_id=1, source_target_pairs={{0,14},{2,28},{4,10},{6,24},{8,30},{10,16},{12,26},{14,12},{16,6},... | collective-permute-start | bytes 49160 | tf_op jit(solution)/shard_map/ppermute | solution.py:289
  16.1 2.1 %collective-permute-start.10 = (bf16[64,128]{1,0:T(8,128)(2,1)S(1)}, bf16[64,128]{1,0:T(8,128)(2,1)S(1)}, u32[]{:S(2)}, u32[]{:S(2)}) collective-permute-start(bf16[64,128]{1,0:T(8,128)(2,1)S(1)} %get-tuple-element.55), channel_id=1, source_target_pairs={{0,22},{2,4},{4,18},{6,28},{8,6},{10,20},{12,2},{14,16},{16,26},{1... | collective-permute-start | bytes 49160 | tf_op jit(solution)/shard_map/ppermute | solution.py:289
  18.2 1.8 %collective-permute-start.11 = (bf16[64,128]{1,0:T(8,128)(2,1)S(1)}, bf16[64,128]{1,0:T(8,128)(2,1)S(1)}, u32[]{:S(2)}, u32[]{:S(2)}) collective-permute-start(bf16[64,128]{1,0:T(8,128)(2,1)S(1)} %get-tuple-element.56), channel_id=1, source_target_pairs={{0,18},{2,24},{4,22},{6,0},{8,26},{10,8},{12,30},{14,20},{16,2},{1... | collective-permute-start | bytes 49160 | tf_op jit(solution)/shard_map/ppermute | solution.py:289
  20.0 0.4 %collective-permute-start.12 = (bf16[64,128]{1,0:T(8,128)(2,1)S(1)}, bf16[64,128]{1,0:T(8,128)(2,1)S(1)}, u32[]{:S(2)}, u32[]{:S(2)}) collective-permute-start(bf16[64,128]{1,0:T(8,128)(2,1)S(1)} %get-tuple-element.57), channel_id=1, source_target_pairs={{0,10},{2,0},{4,14},{6,4},{8,2},{10,12},{12,6},{14,8},{16,30},{18,... | collective-permute-start | bytes 49160 | tf_op jit(solution)/shard_map/ppermute | solution.py:289
  20.4 0.3 %columns.2 = (bf16[256,512]{1,0:T(8,128)(2,1)S(1)}, bf16[256,512]{1,0:T(8,128)(2,1)S(1)}) custom-call(bf16[2048,128]{1,0:T(8,128)(2,1)S(1)} %collective-permute-done.8.factors), custom_call_target="tpu_custom_call" | custom-call | tf_op jit(solution)/shard_map/columns/pallas_call | solution.py:259
  20.8 0.8 %collective-permute-done.7.refs_0_ = bf16[64,128]{1,0:T(8,128)(2,1)S(1)} collective-permute-done((bf16[64,128]{1,0:T(8,128)(2,1)S(1)}, bf16[64,128]{1,0:T(8,128)(2,1)S(1)}, u32[]{:S(2)}, u32[]{:S(2)}) %collective-permute-start.7) | collective-permute-done | bytes 16416 | tf_op jit(solution)/shard_map/ppermute | solution.py:289
  21.6 0.3 collective-permute-done.12.refs_3_
  21.8 0.3 %collective-permute-start.13 = (bf16[4,64,128]{2,1,0:T(8,128)(2,1)S(1)}, bf16[4,64,128]{2,1,0:T(8,128)(2,1)S(1)}, u32[]{:S(2)}, u32[]{:S(2)}) collective-permute-start(bf16[4,64,128]{2,1,0:T(8,128)(2,1)S(1)} %pack.1.blocks), channel_id=1, source_target_pairs={{0,2},{2,0},{4,6},{6,4},{8,10},{10,8},{12,14},{14,12},{16,18},{18,... | collective-permute-start | bytes 196616 | tf_op jit(solution)/shard_map/ppermute | solution.py:272
  22.2 0.3 %part.1 = (f32[256,128]{1,0:T(8,128)S(1)}, bf16[128,512]{1,0:T(8,128)(2,1)S(1)}) custom-call(bf16[4,64,128]{2,1,0:T(8,128)(2,1)S(1)} %pack.1.blocks, bf16[256,512]{1,0:T(8,128)(2,1)S(1)} %get-tuple-element.51.factors), custom_call_target="tpu_custom_call" | custom-call | flops 33554432 | bytes 589824 | tf_op jit(solution)/shard_map/part/pallas_call | solution.py:259
  22.5 0.6 %collective-permute-done.13.blocks = bf16[4,64,128]{2,1,0:T(8,128)(2,1)S(1)} collective-permute-done((bf16[4,64,128]{2,1,0:T(8,128)(2,1)S(1)}, bf16[4,64,128]{2,1,0:T(8,128)(2,1)S(1)}, u32[]{:S(2)}, u32[]{:S(2)}) %collective-permute-start.13) | collective-permute-done | bytes 65568 | tf_op jit(solution)/shard_map/ppermute | solution.py:272
  23.1 0.3 %gradient.1 = (bf16[256,128]{1,0:T(8,128)(2,1)S(1)}, bf16[128,512]{1,0:T(8,128)(2,1)S(1)}) custom-call(f32[256,128]{1,0:T(8,128)S(1)} %get-tuple-element.58.part, bf16[4,64,128]{2,1,0:T(8,128)(2,1)S(1)} %collective-permute-done.13.blocks, bf16[256,512]{1,0:T(8,128)(2,1)S(1)} %get-tuple-element.52.factors), custom_call_target="tpu_custom_call" | custom-call | flops 33554432 | bytes 655360 | tf_op jit(solution)/shard_map/gradient/pallas_call | solution.py:259
  23.4 1.4 %collective-permute-start.14 = (bf16[256,128]{1,0:T(8,128)(2,1)S(1)}, bf16[256,128]{1,0:T(8,128)(2,1)S(1)}, u32[]{:S(2)}, u32[]{:S(2)}) collective-permute-start(bf16[256,128]{1,0:T(8,128)(2,1)S(1)} %get-tuple-element.59), channel_id=1, source_target_pairs={{0,3},{1,2},{2,1},{3,0},{4,7},{5,6},{6,5},{7,4},{8,11},{9,10},{10,... | collective-permute-start | bytes 196616 | tf_op jit(solution)/shard_map/ppermute | solution.py:278
  24.8 0.3 %columns.3 = (bf16[256,512]{1,0:T(8,128)(2,1)S(1)}, bf16[256,512]{1,0:T(8,128)(2,1)S(1)}) custom-call(bf16[2048,128]{1,0:T(8,128)(2,1)S(1)} %bitcast.7), custom_call_target="tpu_custom_call" | custom-call | tf_op jit(solution)/shard_map/columns/pallas_call | solution.py:259
  25.1 0.3 %pair.1 = (f32[256,128]{1,0:T(8,128)S(1)}, f32[256,128]{1,0:T(8,128)S(1)}) custom-call(bf16[256,512]{1,0:T(8,128)(2,1)S(1)} %get-tuple-element.61.own, bf16[256,512]{1,0:T(8,128)(2,1)S(1)} %get-tuple-element.62.other, bf16[128,512]{1,0:T(8,128)(2,1)S(1)} %get-tuple-element.63.own_left, bf16[128,512]{1,0:T(8,128)(2,1)S(1)} %get-tuple-element.64.other_left, ...), custom_call_target="tpu_custom_call" | custom-call | flops 67108864 | bytes 1310720 | tf_op jit(solution)/shard_map/pair/pallas_call | solution.py:259
  25.4 2.0 %collective-permute-done.14.gradient = bf16[256,128]{1,0:T(8,128)(2,1)S(1)} collective-permute-done((bf16[256,128]{1,0:T(8,128)(2,1)S(1)}, bf16[256,128]{1,0:T(8,128)(2,1)S(1)}, u32[]{:S(2)}, u32[]{:S(2)}) %collective-permute-start.14) | collective-permute-done | bytes 65568 | tf_op jit(solution)/shard_map/ppermute | solution.py:278
  27.4 0.7 %shrink.1 = f32[256,128]{1,0:T(8,128)} custom-call(f32[256,128]{1,0:T(8,128)S(1)} %get-tuple-element.65.total, f32[256,128]{1,0:T(8,128)S(1)} %get-tuple-element.66.difference, bf16[256,128]{1,0:T(8,128)(2,1)S(1)} %collective-permute-done.14.gradient), custom_call_target="tpu_custom_call" | custom-call | tf_op jit(solution)/shard_map/shrink/pallas_call | solution.py:259
  (21 shorter events, 0.1 us)
Async XLA Ops:
  0.0 2.2 %copy-start.2 = (bf16[1,256,8,128]{3,2,1,0:T(8,128)(2,1)S(1)}, bf16[1,256,8,128]{3,2,1,0:T(8,128)(2,1)}, u32[]{:S(2)}) copy-start(bf16[1,256,8,128]{3,2,1,0:T(8,128)(2,1)} %param.5) | copy-start | bytes 1572868
  1.7 1.4 %collective-permute-start = (bf16[4,64,128]{2,1,0:T(8,128)(2,1)S(1)}, bf16[4,64,128]{2,1,0:T(8,128)(2,1)S(1)}, u32[]{:S(2)}, u32[]{:S(2)}) collective-permute-start(bf16[4,64,128]{2,1,0:T(8,128)(2,1)S(1)} %get-tuple-element.37), channel_id=1, source_target_pairs={{0,2},{2,0},{4,6},{6,4},{8,10},{10,8},{12,14},{14,12},{16,18},{18,... | collective-permute-start | bytes 196616 | tf_op jit(solution)/shard_map/ppermute | solution.py:272
  2.2 8.7 %collective-permute-start.4 = (bf16[2048,128]{1,0:T(8,128)(2,1)S(1)}, bf16[2048,128]{1,0:T(8,128)(2,1)S(1)}, u32[]{:S(2)}, u32[]{:S(2)}) collective-permute-start(bf16[2048,128]{1,0:T(8,128)(2,1)S(1)} %bitcast.10), channel_id=1, source_target_pairs={{0,2},{2,0},{4,6},{6,4},{8,10},{10,8},{12,14},{14,12},{16,18},{18,... | collective-permute-start | bytes 1572872 | tf_op jit(solution)/shard_map/ppermute | solution.py:272
  3.1 7.8 %copy-start.1 = (f32[1,256,128]{2,1,0:T(8,128)S(1)}, f32[1,256,128]{2,1,0:T(8,128)}, u32[]{:S(2)}) copy-start(f32[1,256,128]{2,1,0:T(8,128)} %param.9) | copy-start | bytes 393220
  3.1 7.8 %copy-start.3 = (f32[1,256,128]{2,1,0:T(8,128)S(1)}, f32[1,256,128]{2,1,0:T(8,128)}, u32[]{:S(2)}) copy-start(f32[1,256,128]{2,1,0:T(8,128)} %param.8) | copy-start | bytes 393220
  3.2 7.8 %copy-start.4 = (s32[1,8,8]{2,1,0:T(8,128)S(1)}, s32[1,8,8]{2,1,0:T(8,128)}, u32[]{:S(2)}) copy-start(s32[1,8,8]{2,1,0:T(8,128)} %ranks.1) | copy-start | bytes 772
  3.2 9.0 %collective-permute-start.3 = (bf16[64,128]{1,0:T(8,128)(2,1)S(1)}, bf16[64,128]{1,0:T(8,128)(2,1)S(1)}, u32[]{:S(2)}, u32[]{:S(2)}) collective-permute-start(bf16[64,128]{1,0:T(8,128)(2,1)S(1)} %get-tuple-element.40), channel_id=1, source_target_pairs={{0,30},{2,20},{4,26},{6,16},{8,18},{10,28},{12,22},{14,24},{16,10}... | collective-permute-start | bytes 49160 | tf_op jit(solution)/shard_map/ppermute | solution.py:289
  8.9 4.1 %collective-permute-start.5 = (bf16[64,128]{1,0:T(8,128)(2,1)S(1)}, bf16[64,128]{1,0:T(8,128)(2,1)S(1)}, u32[]{:S(2)}, u32[]{:S(2)}) collective-permute-start(bf16[64,128]{1,0:T(8,128)(2,1)S(1)} %get-tuple-element.47), channel_id=1, source_target_pairs={{0,6},{2,12},{4,2},{6,20},{8,22},{10,24},{12,18},{14,28},{16,14},{... | collective-permute-start | bytes 49160 | tf_op jit(solution)/shard_map/ppermute | solution.py:289
  8.9 4.3 %collective-permute-start.1 = (bf16[64,128]{1,0:T(8,128)(2,1)S(1)}, bf16[64,128]{1,0:T(8,128)(2,1)S(1)}, u32[]{:S(2)}, u32[]{:S(2)}) collective-permute-start(bf16[64,128]{1,0:T(8,128)(2,1)S(1)} %get-tuple-element.38), channel_id=1, source_target_pairs={{0,26},{2,16},{4,30},{6,8},{8,14},{10,4},{12,10},{14,0},{16,18},{1... | collective-permute-start | bytes 49160 | tf_op jit(solution)/shard_map/ppermute | solution.py:289
  9.6 3.6 %collective-permute-start.2 = (bf16[64,128]{1,0:T(8,128)(2,1)S(1)}, bf16[64,128]{1,0:T(8,128)(2,1)S(1)}, u32[]{:S(2)}, u32[]{:S(2)}) collective-permute-start(bf16[64,128]{1,0:T(8,128)(2,1)S(1)} %get-tuple-element.39), channel_id=1, source_target_pairs={{0,2},{2,8},{4,6},{6,12},{8,10},{10,0},{12,14},{14,4},{16,22},{18,... | collective-permute-start | bytes 49160 | tf_op jit(solution)/shard_map/ppermute | solution.py:289
  10.9 1.3 %copy-start = (bf16[1,256,8,128]{3,2,1,0:T(8,128)(2,1)S(1)}, bf16[1,256,8,128]{3,2,1,0:T(8,128)(2,1)}, u32[]{:S(2)}) copy-start(bf16[1,256,8,128]{3,2,1,0:T(8,128)(2,1)} %param.6) | copy-start | bytes 1572868
  12.2 7.8 %collective-permute-start.8 = (bf16[2048,128]{1,0:T(8,128)(2,1)S(1)}, bf16[2048,128]{1,0:T(8,128)(2,1)S(1)}, u32[]{:S(2)}, u32[]{:S(2)}) collective-permute-start(bf16[2048,128]{1,0:T(8,128)(2,1)S(1)} %bitcast.6), channel_id=1, source_target_pairs={{0,2},{2,0},{4,6},{6,4},{8,10},{10,8},{12,14},{14,12},{16,18},{18,... | collective-permute-start | bytes 1572872 | tf_op jit(solution)/shard_map/ppermute | solution.py:272
  13.4 1.9 %collective-permute-start.6 = (f32[128,512]{1,0:T(8,128)S(1)}, f32[128,512]{1,0:T(8,128)S(1)}, u32[]{:S(2)}, u32[]{:S(2)}) collective-permute-start(f32[128,512]{1,0:T(8,128)S(1)} %image.1.here), channel_id=1, source_target_pairs={{0,2},{2,0},{4,6},{6,4},{8,10},{10,8},{12,14},{14,12},{16,18},{18,... | collective-permute-start | bytes 786440 | tf_op jit(solution)/shard_map/ppermute | solution.py:272
  13.8 7.0 %collective-permute-start.9 = (f32[256,128]{1,0:T(8,128)S(1)}, f32[256,128]{1,0:T(8,128)S(1)}, u32[]{:S(2)}, u32[]{:S(2)}) collective-permute-start(f32[256,128]{1,0:T(8,128)S(1)} %get-tuple-element.53.here), channel_id=1, source_target_pairs={{0,1},{1,0},{2,3},{3,2},{4,5},{5,4},{6,7},{7,6},{8,9},{9,8},{10,11... | collective-permute-start | bytes 393224 | tf_op jit(solution)/shard_map/ppermute | solution.py:356
  15.6 5.9 %collective-permute-start.7 = (bf16[64,128]{1,0:T(8,128)(2,1)S(1)}, bf16[64,128]{1,0:T(8,128)(2,1)S(1)}, u32[]{:S(2)}, u32[]{:S(2)}) collective-permute-start(bf16[64,128]{1,0:T(8,128)(2,1)S(1)} %get-tuple-element.49), channel_id=1, source_target_pairs={{0,14},{2,28},{4,10},{6,24},{8,30},{10,16},{12,26},{14,12},{16,6},... | collective-permute-start | bytes 49160 | tf_op jit(solution)/shard_map/ppermute | solution.py:289
  16.1 5.5 %collective-permute-start.10 = (bf16[64,128]{1,0:T(8,128)(2,1)S(1)}, bf16[64,128]{1,0:T(8,128)(2,1)S(1)}, u32[]{:S(2)}, u32[]{:S(2)}) collective-permute-start(bf16[64,128]{1,0:T(8,128)(2,1)S(1)} %get-tuple-element.55), channel_id=1, source_target_pairs={{0,22},{2,4},{4,18},{6,28},{8,6},{10,20},{12,2},{14,16},{16,26},{1... | collective-permute-start | bytes 49160 | tf_op jit(solution)/shard_map/ppermute | solution.py:289
  18.2 3.4 %collective-permute-start.11 = (bf16[64,128]{1,0:T(8,128)(2,1)S(1)}, bf16[64,128]{1,0:T(8,128)(2,1)S(1)}, u32[]{:S(2)}, u32[]{:S(2)}) collective-permute-start(bf16[64,128]{1,0:T(8,128)(2,1)S(1)} %get-tuple-element.56), channel_id=1, source_target_pairs={{0,18},{2,24},{4,22},{6,0},{8,26},{10,8},{12,30},{14,20},{16,2},{1... | collective-permute-start | bytes 49160 | tf_op jit(solution)/shard_map/ppermute | solution.py:289
  20.0 1.9 %collective-permute-start.12 = (bf16[64,128]{1,0:T(8,128)(2,1)S(1)}, bf16[64,128]{1,0:T(8,128)(2,1)S(1)}, u32[]{:S(2)}, u32[]{:S(2)}) collective-permute-start(bf16[64,128]{1,0:T(8,128)(2,1)S(1)} %get-tuple-element.57), channel_id=1, source_target_pairs={{0,10},{2,0},{4,14},{6,4},{8,2},{10,12},{12,6},{14,8},{16,30},{18,... | collective-permute-start | bytes 49160 | tf_op jit(solution)/shard_map/ppermute | solution.py:289
  21.8 1.3 %collective-permute-start.13 = (bf16[4,64,128]{2,1,0:T(8,128)(2,1)S(1)}, bf16[4,64,128]{2,1,0:T(8,128)(2,1)S(1)}, u32[]{:S(2)}, u32[]{:S(2)}) collective-permute-start(bf16[4,64,128]{2,1,0:T(8,128)(2,1)S(1)} %pack.1.blocks), channel_id=1, source_target_pairs={{0,2},{2,0},{4,6},{6,4},{8,10},{10,8},{12,14},{14,12},{16,18},{18,... | collective-permute-start | bytes 196616 | tf_op jit(solution)/shard_map/ppermute | solution.py:272
  23.4 4.0 %collective-permute-start.14 = (bf16[256,128]{1,0:T(8,128)(2,1)S(1)}, bf16[256,128]{1,0:T(8,128)(2,1)S(1)}, u32[]{:S(2)}, u32[]{:S(2)}) collective-permute-start(bf16[256,128]{1,0:T(8,128)(2,1)S(1)} %get-tuple-element.59), channel_id=1, source_target_pairs={{0,3},{1,2},{2,1},{3,0},{4,7},{5,6},{6,5},{7,4},{8,11},{9,10},{10,... | collective-permute-start | bytes 196616 | tf_op jit(solution)/shard_map/ppermute | solution.py:278

commit v22 on v21

--- a/solution.py
+++ b/solution.py
@@ -116,21 +116,21 @@
     pieces = sems.shape[0] - 1
     rows, columns = separated.shape
     tiles = columns // LANES
-    load_start = pltpu.make_async_copy(start, start_here, sems.at[pieces])
-    load_start.start()
     loads = []
     for piece in range(pieces):
         at = pl.ds(piece * (rows * tiles // pieces), rows * tiles // pieces)
         loads.append(pltpu.make_async_copy(factors.at[at], factors_here.at[at], sems.at[piece]))
         loads[-1].start()
-    load_start.wait()
-    values = start_here[...].T.astype(BF16)
+    load_start = pltpu.make_async_copy(start, start_here, sems.at[pieces])
+    load_start.start()
     for piece, load in enumerate(loads):
         at = pl.ds(piece * (rows * tiles // pieces), rows * tiles // pieces)
         load.wait()
         separate(
             factors_here.at[at], wide.at[at], separated.at[pl.ds(piece * (rows // pieces), rows // pieces)], range(tiles)
         )
+    load_start.wait()
+    values = start_here[...].T.astype(BF16)
     for tile, block in enumerate(adjoint_blocks(values, separated)):
         blocks[tile] = block
     for out, chosen in zip((keep, give), both_tiles(routes)):

time: 28.3 us -> 28.3 us (level)
  no operation moved by 1% of the time
where the time goes in v22:
time: 28.3 us; the launch traced here: 28.1 us
  starting transfers between devices  16.8 us (59%)
  Pallas kernels  5.96 us (21%)
  waiting for transfers between devices  5.17 us (18%)
    ppermute x8, starting transfers between devices, exchange(): arrived.append(lax.ppermute(send, 'tile', sorted(pairs)))  12.5 us
    pallas_call x13, Pallas kernels, call(): pl.pallas_call(kernel, out_shape=outs, in_specs=[pl.BlockSpec(memory_spac...  5.96 us
    ppermute x1, waiting for transfers between devices, across(): return lax.ppermute(value, ('tile', 'freq'), pairs)  1.99 us
    ppermute x8, waiting for transfers between devices, exchange(): arrived.append(lax.ppermute(send, 'tile', sorted(pairs)))  1.73 us
    ppermute x1, starting transfers between devices, body(): lax.ppermute(start, 'freq', [(f, (f - shift) % band) for f in range(band)])  1.52 us
    ppermute x5, waiting for transfers between devices, to_mate(): lax.ppermute(value, 'tile', [(i, i ^ 1) for i in range(lax.axis_size('til...  1.46 us
    ppermute x5, starting transfers between devices, to_mate(): lax.ppermute(value, 'tile', [(i, i ^ 1) for i in range(lax.axis_size('til...  1.39 us
    ppermute x1, starting transfers between devices, across(): return lax.ppermute(value, ('tile', 'freq'), pairs)  1.39 us
  transfers between devices with their start and end apart: 15, of which 6 were waited for; matrix products, arithmetic and copies ran while one was open for 0% of the time, Pallas kernels for 12%

profile of v22, /device:TPU:0, one launch (start us, length us, event | category | flops | bytes accessed | tf_op | source)
XLA Modules:
  0.0 28.1 jit_solution(1667137626786286419)
XLA Ops:
  0.0 1.7 %forward.1 = (bf16[4,64,128]{2,1,0:T(8,128)(2,1)S(1)}, bf16[4,64,128]{2,1,0:T(8,128)(2,1)S(1)}) custom-call(f32[256,128]{1,0:T(8,128)} %bitcast.8, bf16[2048,128]{1,0:T(8,128)(2,1)} %bitcast.5), custom_call_target="tpu_custom_call" | custom-call | flops 67108864 | bytes 786432 | tf_op jit(solution)/shard_map/forward/pallas_call | solution.py:259
  1.7 0.5 %collective-permute-start = (bf16[4,64,128]{2,1,0:T(8,128)(2,1)S(1)}, bf16[4,64,128]{2,1,0:T(8,128)(2,1)S(1)}, u32[]{:S(2)}, u32[]{:S(2)}) collective-permute-start(bf16[4,64,128]{2,1,0:T(8,128)(2,1)S(1)} %get-tuple-element.37), channel_id=1, source_target_pairs={{0,2},{2,0},{4,6},{6,4},{8,10},{10,8},{12,14},{14,12},{16,18},{18,... | collective-permute-start | bytes 196616 | tf_op jit(solution)/shard_map/ppermute | solution.py:272
  2.2 0.1 collective-permute-start.4
  2.3 0.8 %collective-permute-done.arrived = bf16[4,64,128]{2,1,0:T(8,128)(2,1)S(1)} collective-permute-done((bf16[4,64,128]{2,1,0:T(8,128)(2,1)S(1)}, bf16[4,64,128]{2,1,0:T(8,128)(2,1)S(1)}, u32[]{:S(2)}, u32[]{:S(2)}) %collective-permute-start) | collective-permute-done | bytes 65568 | tf_op jit(solution)/shard_map/ppermute | solution.py:272
  3.1 0.0 copy-start.4
  3.2 5.7 %collective-permute-start.3 = (bf16[64,128]{1,0:T(8,128)(2,1)S(1)}, bf16[64,128]{1,0:T(8,128)(2,1)S(1)}, u32[]{:S(2)}, u32[]{:S(2)}) collective-permute-start(bf16[64,128]{1,0:T(8,128)(2,1)S(1)} %get-tuple-element.40), channel_id=1, source_target_pairs={{0,30},{2,20},{4,26},{6,16},{8,18},{10,28},{12,22},{14,24},{16,10}... | collective-permute-start | bytes 49160 | tf_op jit(solution)/shard_map/ppermute | solution.py:289
  8.8 0.7 %collective-permute-start.1 = (bf16[64,128]{1,0:T(8,128)(2,1)S(1)}, bf16[64,128]{1,0:T(8,128)(2,1)S(1)}, u32[]{:S(2)}, u32[]{:S(2)}) collective-permute-start(bf16[64,128]{1,0:T(8,128)(2,1)S(1)} %get-tuple-element.38), channel_id=1, source_target_pairs={{0,26},{2,16},{4,30},{6,8},{8,14},{10,4},{12,10},{14,0},{16,18},{1... | collective-permute-start | bytes 49160 | tf_op jit(solution)/shard_map/ppermute | solution.py:289
  9.6 1.4 %collective-permute-start.2 = (bf16[64,128]{1,0:T(8,128)(2,1)S(1)}, bf16[64,128]{1,0:T(8,128)(2,1)S(1)}, u32[]{:S(2)}, u32[]{:S(2)}) collective-permute-start(bf16[64,128]{1,0:T(8,128)(2,1)S(1)} %get-tuple-element.39), channel_id=1, source_target_pairs={{0,2},{2,8},{4,6},{6,12},{8,10},{10,0},{12,14},{14,4},{16,22},{18,... | collective-permute-start | bytes 49160 | tf_op jit(solution)/shard_map/ppermute | solution.py:289
  10.9 1.2 %rows.1 = (bf16[512,512]{1,0:T(8,128)(2,1)S(1)}, bf16[512,512]{1,0:T(8,128)(2,1)S(1)}, f32[128,256]{1,0:T(8,128)S(1)}, f32[256,128]{1,0:T(8,128)S(1)}) custom-call(s32[1,8,8]{2,1,0:T(8,128)S(1)} %copy-done.4, bf16[2048,128]{1,0:T(8,128)(2,1)S(1)} %bitcast.11, bf16[2048,128]{1,0:T(8,128)(2,1)S(1)} %collective-permute-done.4.mate, f32[256,128]{1,0:T(8,128)S(1)} %bitcast.12, ...), custom_call_target="tpu_custom_call" | custom-call | tf_op jit(solution)/shard_map/rows/pallas_call | solution.py:259
  12.2 0.1 collective-permute-start.8
  12.3 0.6 %collective-permute-done.5.second = bf16[64,128]{1,0:T(8,128)(2,1)S(1)} collective-permute-done((bf16[64,128]{1,0:T(8,128)(2,1)S(1)}, bf16[64,128]{1,0:T(8,128)(2,1)S(1)}, u32[]{:S(2)}, u32[]{:S(2)}) %collective-permute-start.5) | collective-permute-done | bytes 16416 | tf_op jit(solution)/shard_map/ppermute | solution.py:289
  12.9 0.2 early.1.refs_2_
  13.1 0.2 image.1.here
  13.4 0.4 %collective-permute-start.6 = (f32[128,512]{1,0:T(8,128)S(1)}, f32[128,512]{1,0:T(8,128)S(1)}, u32[]{:S(2)}, u32[]{:S(2)}) collective-permute-start(f32[128,512]{1,0:T(8,128)S(1)} %image.1.here), channel_id=1, source_target_pairs={{0,2},{2,0},{4,6},{6,4},{8,10},{10,8},{12,14},{14,12},{16,18},{18,... | collective-permute-start | bytes 786440 | tf_op jit(solution)/shard_map/ppermute | solution.py:272
  13.8 1.5 %collective-permute-start.9 = (f32[256,128]{1,0:T(8,128)S(1)}, f32[256,128]{1,0:T(8,128)S(1)}, u32[]{:S(2)}, u32[]{:S(2)}) collective-permute-start(f32[256,128]{1,0:T(8,128)S(1)} %get-tuple-element.53.here), channel_id=1, source_target_pairs={{0,1},{1,0},{2,3},{3,2},{4,5},{5,4},{6,7},{7,6},{8,9},{9,8},{10,11... | collective-permute-start | bytes 393224 | tf_op jit(solution)/shard_map/ppermute | solution.py:356
  15.3 0.3 %back.1 = (bf16[64,128]{1,0:T(8,128)(2,1)S(1)}, bf16[64,128]{1,0:T(8,128)(2,1)S(1)}, bf16[64,128]{1,0:T(8,128)(2,1)S(1)}, bf16[64,128]{1,0:T(8,128)(2,1)S(1)}) custom-call(f32[128,512]{1,0:T(8,128)S(1)} %image.1.here, f32[128,512]{1,0:T(8,128)S(1)} %collective-permute-done.6.there, bf16[512,512]{1,0:T(8,128)(2,1)S(1)} %get-tuple-element.48.factors), custom_call_target="tpu_custom_call" | custom-call | flops 67108864 | bytes 1114112 | tf_op jit(solution)/shard_map/back/pallas_call | solution.py:259
  15.6 0.4 %collective-permute-start.7 = (bf16[64,128]{1,0:T(8,128)(2,1)S(1)}, bf16[64,128]{1,0:T(8,128)(2,1)S(1)}, u32[]{:S(2)}, u32[]{:S(2)}) collective-permute-start(bf16[64,128]{1,0:T(8,128)(2,1)S(1)} %get-tuple-element.49), channel_id=1, source_target_pairs={{0,14},{2,28},{4,10},{6,24},{8,30},{10,16},{12,26},{14,12},{16,6},... | collective-permute-start | bytes 49160 | tf_op jit(solution)/shard_map/ppermute | solution.py:289
  16.1 2.1 %collective-permute-start.10 = (bf16[64,128]{1,0:T(8,128)(2,1)S(1)}, bf16[64,128]{1,0:T(8,128)(2,1)S(1)}, u32[]{:S(2)}, u32[]{:S(2)}) collective-permute-start(bf16[64,128]{1,0:T(8,128)(2,1)S(1)} %get-tuple-element.55), channel_id=1, source_target_pairs={{0,22},{2,4},{4,18},{6,28},{8,6},{10,20},{12,2},{14,16},{16,26},{1... | collective-permute-start | bytes 49160 | tf_op jit(solution)/shard_map/ppermute | solution.py:289
  18.2 1.8 %collective-permute-start.11 = (bf16[64,128]{1,0:T(8,128)(2,1)S(1)}, bf16[64,128]{1,0:T(8,128)(2,1)S(1)}, u32[]{:S(2)}, u32[]{:S(2)}) collective-permute-start(bf16[64,128]{1,0:T(8,128)(2,1)S(1)} %get-tuple-element.56), channel_id=1, source_target_pairs={{0,18},{2,24},{4,22},{6,0},{8,26},{10,8},{12,30},{14,20},{16,2},{1... | collective-permute-start | bytes 49160 | tf_op jit(solution)/shard_map/ppermute | solution.py:289
  20.0 0.4 %collective-permute-start.12 = (bf16[64,128]{1,0:T(8,128)(2,1)S(1)}, bf16[64,128]{1,0:T(8,128)(2,1)S(1)}, u32[]{:S(2)}, u32[]{:S(2)}) collective-permute-start(bf16[64,128]{1,0:T(8,128)(2,1)S(1)} %get-tuple-element.57), channel_id=1, source_target_pairs={{0,10},{2,0},{4,14},{6,4},{8,2},{10,12},{12,6},{14,8},{16,30},{18,... | collective-permute-start | bytes 49160 | tf_op jit(solution)/shard_map/ppermute | solution.py:289
  20.4 0.3 %columns.2 = (bf16[256,512]{1,0:T(8,128)(2,1)S(1)}, bf16[256,512]{1,0:T(8,128)(2,1)S(1)}) custom-call(bf16[2048,128]{1,0:T(8,128)(2,1)S(1)} %collective-permute-done.8.factors), custom_call_target="tpu_custom_call" | custom-call | tf_op jit(solution)/shard_map/columns/pallas_call | solution.py:259
  20.7 0.8 %collective-permute-done.7.refs_0_ = bf16[64,128]{1,0:T(8,128)(2,1)S(1)} collective-permute-done((bf16[64,128]{1,0:T(8,128)(2,1)S(1)}, bf16[64,128]{1,0:T(8,128)(2,1)S(1)}, u32[]{:S(2)}, u32[]{:S(2)}) %collective-permute-start.7) | collective-permute-done | bytes 16416 | tf_op jit(solution)/shard_map/ppermute | solution.py:289
  21.6 0.3 collective-permute-done.12.refs_3_
  21.8 0.3 %collective-permute-start.13 = (bf16[4,64,128]{2,1,0:T(8,128)(2,1)S(1)}, bf16[4,64,128]{2,1,0:T(8,128)(2,1)S(1)}, u32[]{:S(2)}, u32[]{:S(2)}) collective-permute-start(bf16[4,64,128]{2,1,0:T(8,128)(2,1)S(1)} %pack.1.blocks), channel_id=1, source_target_pairs={{0,2},{2,0},{4,6},{6,4},{8,10},{10,8},{12,14},{14,12},{16,18},{18,... | collective-permute-start | bytes 196616 | tf_op jit(solution)/shard_map/ppermute | solution.py:272
  22.2 0.3 %part.1 = (f32[256,128]{1,0:T(8,128)S(1)}, bf16[128,512]{1,0:T(8,128)(2,1)S(1)}) custom-call(bf16[4,64,128]{2,1,0:T(8,128)(2,1)S(1)} %pack.1.blocks, bf16[256,512]{1,0:T(8,128)(2,1)S(1)} %get-tuple-element.51.factors), custom_call_target="tpu_custom_call" | custom-call | flops 33554432 | bytes 589824 | tf_op jit(solution)/shard_map/part/pallas_call | solution.py:259
  22.4 0.6 %collective-permute-done.13.blocks = bf16[4,64,128]{2,1,0:T(8,128)(2,1)S(1)} collective-permute-done((bf16[4,64,128]{2,1,0:T(8,128)(2,1)S(1)}, bf16[4,64,128]{2,1,0:T(8,128)(2,1)S(1)}, u32[]{:S(2)}, u32[]{:S(2)}) %collective-permute-start.13) | collective-permute-done | bytes 65568 | tf_op jit(solution)/shard_map/ppermute | solution.py:272
  23.1 0.3 %gradient.1 = (bf16[256,128]{1,0:T(8,128)(2,1)S(1)}, bf16[128,512]{1,0:T(8,128)(2,1)S(1)}) custom-call(f32[256,128]{1,0:T(8,128)S(1)} %get-tuple-element.58.part, bf16[4,64,128]{2,1,0:T(8,128)(2,1)S(1)} %collective-permute-done.13.blocks, bf16[256,512]{1,0:T(8,128)(2,1)S(1)} %get-tuple-element.52.factors), custom_call_target="tpu_custom_call" | custom-call | flops 33554432 | bytes 655360 | tf_op jit(solution)/shard_map/gradient/pallas_call | solution.py:259
  23.4 1.4 %collective-permute-start.14 = (bf16[256,128]{1,0:T(8,128)(2,1)S(1)}, bf16[256,128]{1,0:T(8,128)(2,1)S(1)}, u32[]{:S(2)}, u32[]{:S(2)}) collective-permute-start(bf16[256,128]{1,0:T(8,128)(2,1)S(1)} %get-tuple-element.59), channel_id=1, source_target_pairs={{0,3},{1,2},{2,1},{3,0},{4,7},{5,6},{6,5},{7,4},{8,11},{9,10},{10,... | collective-permute-start | bytes 196616 | tf_op jit(solution)/shard_map/ppermute | solution.py:278
  24.8 0.3 %columns.3 = (bf16[256,512]{1,0:T(8,128)(2,1)S(1)}, bf16[256,512]{1,0:T(8,128)(2,1)S(1)}) custom-call(bf16[2048,128]{1,0:T(8,128)(2,1)S(1)} %bitcast.7), custom_call_target="tpu_custom_call" | custom-call | tf_op jit(solution)/shard_map/columns/pallas_call | solution.py:259
  25.1 0.3 %pair.1 = (f32[256,128]{1,0:T(8,128)S(1)}, f32[256,128]{1,0:T(8,128)S(1)}) custom-call(bf16[256,512]{1,0:T(8,128)(2,1)S(1)} %get-tuple-element.61.own, bf16[256,512]{1,0:T(8,128)(2,1)S(1)} %get-tuple-element.62.other, bf16[128,512]{1,0:T(8,128)(2,1)S(1)} %get-tuple-element.63.own_left, bf16[128,512]{1,0:T(8,128)(2,1)S(1)} %get-tuple-element.64.other_left, ...), custom_call_target="tpu_custom_call" | custom-call | flops 67108864 | bytes 1310720 | tf_op jit(solution)/shard_map/pair/pallas_call | solution.py:259
  25.4 2.0 %collective-permute-done.14.gradient = bf16[256,128]{1,0:T(8,128)(2,1)S(1)} collective-permute-done((bf16[256,128]{1,0:T(8,128)(2,1)S(1)}, bf16[256,128]{1,0:T(8,128)(2,1)S(1)}, u32[]{:S(2)}, u32[]{:S(2)}) %collective-permute-start.14) | collective-permute-done | bytes 65568 | tf_op jit(solution)/shard_map/ppermute | solution.py:278
  27.4 0.7 %shrink.1 = f32[256,128]{1,0:T(8,128)} custom-call(f32[256,128]{1,0:T(8,128)S(1)} %get-tuple-element.65.total, f32[256,128]{1,0:T(8,128)S(1)} %get-tuple-element.66.difference, bf16[256,128]{1,0:T(8,128)(2,1)S(1)} %collective-permute-done.14.gradient), custom_call_target="tpu_custom_call" | custom-call | tf_op jit(solution)/shard_map/shrink/pallas_call | solution.py:259
  (21 shorter events, 0.1 us)
Async XLA Ops:
  0.0 2.2 %copy-start.2 = (bf16[1,256,8,128]{3,2,1,0:T(8,128)(2,1)S(1)}, bf16[1,256,8,128]{3,2,1,0:T(8,128)(2,1)}, u32[]{:S(2)}) copy-start(bf16[1,256,8,128]{3,2,1,0:T(8,128)(2,1)} %param.5) | copy-start | bytes 1572868
  1.7 1.4 %collective-permute-start = (bf16[4,64,128]{2,1,0:T(8,128)(2,1)S(1)}, bf16[4,64,128]{2,1,0:T(8,128)(2,1)S(1)}, u32[]{:S(2)}, u32[]{:S(2)}) collective-permute-start(bf16[4,64,128]{2,1,0:T(8,128)(2,1)S(1)} %get-tuple-element.37), channel_id=1, source_target_pairs={{0,2},{2,0},{4,6},{6,4},{8,10},{10,8},{12,14},{14,12},{16,18},{18,... | collective-permute-start | bytes 196616 | tf_op jit(solution)/shard_map/ppermute | solution.py:272
  2.2 8.7 %collective-permute-start.4 = (bf16[2048,128]{1,0:T(8,128)(2,1)S(1)}, bf16[2048,128]{1,0:T(8,128)(2,1)S(1)}, u32[]{:S(2)}, u32[]{:S(2)}) collective-permute-start(bf16[2048,128]{1,0:T(8,128)(2,1)S(1)} %bitcast.10), channel_id=1, source_target_pairs={{0,2},{2,0},{4,6},{6,4},{8,10},{10,8},{12,14},{14,12},{16,18},{18,... | collective-permute-start | bytes 1572872 | tf_op jit(solution)/shard_map/ppermute | solution.py:272
  3.1 7.8 %copy-start.1 = (f32[1,256,128]{2,1,0:T(8,128)S(1)}, f32[1,256,128]{2,1,0:T(8,128)}, u32[]{:S(2)}) copy-start(f32[1,256,128]{2,1,0:T(8,128)} %param.9) | copy-start | bytes 393220
  3.1 7.8 %copy-start.3 = (f32[1,256,128]{2,1,0:T(8,128)S(1)}, f32[1,256,128]{2,1,0:T(8,128)}, u32[]{:S(2)}) copy-start(f32[1,256,128]{2,1,0:T(8,128)} %param.8) | copy-start | bytes 393220
  3.1 7.8 %copy-start.4 = (s32[1,8,8]{2,1,0:T(8,128)S(1)}, s32[1,8,8]{2,1,0:T(8,128)}, u32[]{:S(2)}) copy-start(s32[1,8,8]{2,1,0:T(8,128)} %ranks.1) | copy-start | bytes 772
  3.2 9.0 %collective-permute-start.3 = (bf16[64,128]{1,0:T(8,128)(2,1)S(1)}, bf16[64,128]{1,0:T(8,128)(2,1)S(1)}, u32[]{:S(2)}, u32[]{:S(2)}) collective-permute-start(bf16[64,128]{1,0:T(8,128)(2,1)S(1)} %get-tuple-element.40), channel_id=1, source_target_pairs={{0,30},{2,20},{4,26},{6,16},{8,18},{10,28},{12,22},{14,24},{16,10}... | collective-permute-start | bytes 49160 | tf_op jit(solution)/shard_map/ppermute | solution.py:289
  8.8 4.1 %collective-permute-start.5 = (bf16[64,128]{1,0:T(8,128)(2,1)S(1)}, bf16[64,128]{1,0:T(8,128)(2,1)S(1)}, u32[]{:S(2)}, u32[]{:S(2)}) collective-permute-start(bf16[64,128]{1,0:T(8,128)(2,1)S(1)} %get-tuple-element.47), channel_id=1, source_target_pairs={{0,6},{2,12},{4,2},{6,20},{8,22},{10,24},{12,18},{14,28},{16,14},{... | collective-permute-start | bytes 49160 | tf_op jit(solution)/shard_map/ppermute | solution.py:289
  8.8 4.3 %collective-permute-start.1 = (bf16[64,128]{1,0:T(8,128)(2,1)S(1)}, bf16[64,128]{1,0:T(8,128)(2,1)S(1)}, u32[]{:S(2)}, u32[]{:S(2)}) collective-permute-start(bf16[64,128]{1,0:T(8,128)(2,1)S(1)} %get-tuple-element.38), channel_id=1, source_target_pairs={{0,26},{2,16},{4,30},{6,8},{8,14},{10,4},{12,10},{14,0},{16,18},{1... | collective-permute-start | bytes 49160 | tf_op jit(solution)/shard_map/ppermute | solution.py:289
  9.6 3.6 %collective-permute-start.2 = (bf16[64,128]{1,0:T(8,128)(2,1)S(1)}, bf16[64,128]{1,0:T(8,128)(2,1)S(1)}, u32[]{:S(2)}, u32[]{:S(2)}) collective-permute-start(bf16[64,128]{1,0:T(8,128)(2,1)S(1)} %get-tuple-element.39), channel_id=1, source_target_pairs={{0,2},{2,8},{4,6},{6,12},{8,10},{10,0},{12,14},{14,4},{16,22},{18,... | collective-permute-start | bytes 49160 | tf_op jit(solution)/shard_map/ppermute | solution.py:289
  10.9 1.3 %copy-start = (bf16[1,256,8,128]{3,2,1,0:T(8,128)(2,1)S(1)}, bf16[1,256,8,128]{3,2,1,0:T(8,128)(2,1)}, u32[]{:S(2)}) copy-start(bf16[1,256,8,128]{3,2,1,0:T(8,128)(2,1)} %param.6) | copy-start | bytes 1572868
  12.2 7.8 %collective-permute-start.8 = (bf16[2048,128]{1,0:T(8,128)(2,1)S(1)}, bf16[2048,128]{1,0:T(8,128)(2,1)S(1)}, u32[]{:S(2)}, u32[]{:S(2)}) collective-permute-start(bf16[2048,128]{1,0:T(8,128)(2,1)S(1)} %bitcast.6), channel_id=1, source_target_pairs={{0,2},{2,0},{4,6},{6,4},{8,10},{10,8},{12,14},{14,12},{16,18},{18,... | collective-permute-start | bytes 1572872 | tf_op jit(solution)/shard_map/ppermute | solution.py:272
  13.4 1.9 %collective-permute-start.6 = (f32[128,512]{1,0:T(8,128)S(1)}, f32[128,512]{1,0:T(8,128)S(1)}, u32[]{:S(2)}, u32[]{:S(2)}) collective-permute-start(f32[128,512]{1,0:T(8,128)S(1)} %image.1.here), channel_id=1, source_target_pairs={{0,2},{2,0},{4,6},{6,4},{8,10},{10,8},{12,14},{14,12},{16,18},{18,... | collective-permute-start | bytes 786440 | tf_op jit(solution)/shard_map/ppermute | solution.py:272
  13.8 7.0 %collective-permute-start.9 = (f32[256,128]{1,0:T(8,128)S(1)}, f32[256,128]{1,0:T(8,128)S(1)}, u32[]{:S(2)}, u32[]{:S(2)}) collective-permute-start(f32[256,128]{1,0:T(8,128)S(1)} %get-tuple-element.53.here), channel_id=1, source_target_pairs={{0,1},{1,0},{2,3},{3,2},{4,5},{5,4},{6,7},{7,6},{8,9},{9,8},{10,11... | collective-permute-start | bytes 393224 | tf_op jit(solution)/shard_map/ppermute | solution.py:356
  15.6 5.9 %collective-permute-start.7 = (bf16[64,128]{1,0:T(8,128)(2,1)S(1)}, bf16[64,128]{1,0:T(8,128)(2,1)S(1)}, u32[]{:S(2)}, u32[]{:S(2)}) collective-permute-start(bf16[64,128]{1,0:T(8,128)(2,1)S(1)} %get-tuple-element.49), channel_id=1, source_target_pairs={{0,14},{2,28},{4,10},{6,24},{8,30},{10,16},{12,26},{14,12},{16,6},... | collective-permute-start | bytes 49160 | tf_op jit(solution)/shard_map/ppermute | solution.py:289
  16.1 5.5 %collective-permute-start.10 = (bf16[64,128]{1,0:T(8,128)(2,1)S(1)}, bf16[64,128]{1,0:T(8,128)(2,1)S(1)}, u32[]{:S(2)}, u32[]{:S(2)}) collective-permute-start(bf16[64,128]{1,0:T(8,128)(2,1)S(1)} %get-tuple-element.55), channel_id=1, source_target_pairs={{0,22},{2,4},{4,18},{6,28},{8,6},{10,20},{12,2},{14,16},{16,26},{1... | collective-permute-start | bytes 49160 | tf_op jit(solution)/shard_map/ppermute | solution.py:289
  18.2 3.4 %collective-permute-start.11 = (bf16[64,128]{1,0:T(8,128)(2,1)S(1)}, bf16[64,128]{1,0:T(8,128)(2,1)S(1)}, u32[]{:S(2)}, u32[]{:S(2)}) collective-permute-start(bf16[64,128]{1,0:T(8,128)(2,1)S(1)} %get-tuple-element.56), channel_id=1, source_target_pairs={{0,18},{2,24},{4,22},{6,0},{8,26},{10,8},{12,30},{14,20},{16,2},{1... | collective-permute-start | bytes 49160 | tf_op jit(solution)/shard_map/ppermute | solution.py:289
  20.0 1.9 %collective-permute-start.12 = (bf16[64,128]{1,0:T(8,128)(2,1)S(1)}, bf16[64,128]{1,0:T(8,128)(2,1)S(1)}, u32[]{:S(2)}, u32[]{:S(2)}) collective-permute-start(bf16[64,128]{1,0:T(8,128)(2,1)S(1)} %get-tuple-element.57), channel_id=1, source_target_pairs={{0,10},{2,0},{4,14},{6,4},{8,2},{10,12},{12,6},{14,8},{16,30},{18,... | collective-permute-start | bytes 49160 | tf_op jit(solution)/shard_map/ppermute | solution.py:289
  21.8 1.3 %collective-permute-start.13 = (bf16[4,64,128]{2,1,0:T(8,128)(2,1)S(1)}, bf16[4,64,128]{2,1,0:T(8,128)(2,1)S(1)}, u32[]{:S(2)}, u32[]{:S(2)}) collective-permute-start(bf16[4,64,128]{2,1,0:T(8,128)(2,1)S(1)} %pack.1.blocks), channel_id=1, source_target_pairs={{0,2},{2,0},{4,6},{6,4},{8,10},{10,8},{12,14},{14,12},{16,18},{18,... | collective-permute-start | bytes 196616 | tf_op jit(solution)/shard_map/ppermute | solution.py:272
  23.4 4.0 %collective-permute-start.14 = (bf16[256,128]{1,0:T(8,128)(2,1)S(1)}, bf16[256,128]{1,0:T(8,128)(2,1)S(1)}, u32[]{:S(2)}, u32[]{:S(2)}) collective-permute-start(bf16[256,128]{1,0:T(8,128)(2,1)S(1)} %get-tuple-element.59), channel_id=1, source_target_pairs={{0,3},{1,2},{2,1},{3,0},{4,7},{5,6},{6,5},{7,4},{8,11},{9,10},{10,... | collective-permute-start | bytes 196616 | tf_op jit(solution)/shard_map/ppermute | solution.py:278
